TPU v7x, 32 devices: a whole 2x2x4 slice. The times are simulated.
32 devices in a mesh: groups: 2 (over x), row: 8 (over z, y), col: 2 (over core).
Axes of the slice: x: 2, y: 2, z: 4, core: 2. Of those that a mesh axis runs over, the one named last changes fastest.
Arguments:
- eigvecs: bfloat16 [1024, 512], P(('groups', 'row'), 'col'), parts along dimension 0, may hold values from -0.25 to 0.25
- eigvals: float32 [1024], P(('groups', 'col')), parts along dimension 0, may hold values from 0.05 to 20
- expression: bfloat16 [1024, 1024], P(('groups', 'row')), parts along dimension 0, may hold values from -6 to 6
- dosage: bfloat16 [1024, 1536], P(('groups', 'row')), parts along dimension 0, may hold values from 0 to 2
- delta: float32 [2048], P('groups'), parts along dimension 0, may hold values from 0.1 to 10
- window_start: int32 [2048], P('groups'), parts along dimension 0, may hold values from 0 to 1280
- window_valid: int32 [2048], P('groups'), parts along dimension 0, may hold values from 32 to 256
- gene_owner: int32 [2048], P('groups'), parts along dimension 0, may hold values from 0 to 7, as said below
Outputs:
- zscore: float32 [2048, 256], P(('groups', 'row'), 'col'), parts along dimension 0
There are 2 independent parts, one for each index of `groups`. A program takes and returns all parts, laid end to end along the dimension named above; each array names one. Nothing has to cross between parts.
Inputs may be any that keep to these rules, and one draw needn't show every extreme that they name: `gene_owner`: slice s holds genes s * 128 to (s + 1) * 128 - 1. Every owner holds exactly 128 genes, and the genes of one slice go to one owner in groups of exactly 16 genes or not at all.
All inputs are finite; a program needn't handle non-finite values.
Results may differ from a plain program's by a relative error of at most 0.004.
Values may be sent and summed in bfloat16 or wider, within the bound.
No kernel may reach another device: no remote copies, remote signals or barrier semaphores. Data moves between devices by JAX's collectives and lax.ppermute only.
A program may use at most 64 MiB of HBM per device.

v0:
```python
import jax
import jax.numpy as jnp
from jax import lax
from jax.sharding import PartitionSpec as P

W = 256


def owner_listing(gene_owner):
    total = gene_owner.shape[0]
    return jnp.argsort(gene_owner * total + jnp.arange(total, dtype=jnp.int32))


def earlier_equal(labels):
    places = jnp.arange(labels.shape[0], dtype=jnp.int32)
    same = labels[:, None] == labels[None, :]
    before = places[:, None] > places[None, :]
    return jnp.sum((same & before).astype(jnp.int32), axis=1)


def shift_windows(tables, starts, largest):
    moved_tables = tables
    step_size = 1
    while step_size <= largest:
        bit_set = starts // step_size % 2 == 1
        filler = jnp.zeros(moved_tables.shape[:-1] + (step_size,), moved_tables.dtype)
        moved = jnp.concatenate([moved_tables[..., step_size:], filler], axis=-1)
        moved_tables = jnp.where(bit_set[None, :, None], moved, moved_tables)
        step_size = step_size * 2
    return moved_tables


def body(eigvecs, eigvals, expression, dosage, delta, window_start, window_valid, gene_owner):
    row_count = lax.axis_size("row")
    row_index = lax.axis_index("row")
    genes_all = expression.shape[1]
    own_count = genes_all // row_count
    half_samples = eigvecs.shape[1]
    samples = half_samples * lax.axis_size("col")
    owner_order = owner_listing(gene_owner)
    my_genes = lax.dynamic_slice_in_dim(owner_order, row_index * own_count, own_count)
    expr_panel, dose_panel = (
        lax.all_to_all(expression, "row", split_axis=1, concat_axis=0, tiled=True),
        lax.all_to_all(dosage, "row", split_axis=1, concat_axis=0, tiled=True),
    )
    panel_data = jnp.concatenate([expr_panel, dose_panel], axis=1)
    rotated = lax.dot_general(
        panel_data,
        lax.all_gather(eigvecs, "row", axis=0, tiled=True),
        (((0,), (0,)), ((), ())),
        preferred_element_type=jnp.float32,
    ).astype(jnp.bfloat16)
    rot_expr = rotated[:own_count]
    rot_dose = rotated[own_count:]
    dose_all = lax.all_gather(rot_dose, "row", axis=0, tiled=True)
    capacity = max(2, own_count // row_count)
    destination = lax.dynamic_slice_in_dim(gene_owner, row_index * own_count, own_count)
    position = destination * capacity + earlier_equal(destination)
    slot_ids = jnp.arange(row_count * capacity, dtype=jnp.int32)
    placement_map = (slot_ids[:, None] == position[None, :]).astype(jnp.bfloat16)
    buckets = jnp.dot(placement_map, rot_expr, preferred_element_type=jnp.float32).astype(
        jnp.bfloat16
    )
    received = lax.all_to_all(buckets, "row", split_axis=0, concat_axis=0, tiled=True)
    source = my_genes // own_count
    owned_expr = jnp.take(received, source * capacity + earlier_equal(source), axis=0)
    own_delta = jnp.take(delta, my_genes)
    own_start = jnp.take(window_start, my_genes)
    own_valid = jnp.take(window_valid, my_genes)
    weight = 1.0 / (eigvals[None, :] + own_delta[:, None])
    expr_float = owned_expr.astype(jnp.float32)
    expr_power = jnp.sum(weight * expr_float * expr_float, axis=1)
    weighted = (weight * expr_float).astype(jnp.bfloat16)
    weight_low = weight.astype(jnp.bfloat16)
    dose_sq = jnp.square(dose_all.astype(jnp.float32)).astype(jnp.bfloat16)
    slot_index = jnp.arange(W, dtype=jnp.int32)
    contract = (((1,), (1,)), ((), ()))
    cross_all = lax.dot_general(weighted, dose_all, contract, preferred_element_type=jnp.float32)
    power_all = lax.dot_general(weight_low, dose_sq, contract, preferred_element_type=jnp.float32)
    stacked = jnp.stack([cross_all, power_all], axis=0)
    variants = dose_all.shape[0]
    shifted = shift_windows(stacked, own_start, variants - W)
    cross_sum = shifted[0, :, :W]
    dose_power = shifted[1, :, :W]
    cross_sum, dose_power, expr_power = lax.psum((cross_sum, dose_power, expr_power), "col")
    scale = jnp.sqrt(jnp.float32(samples))
    zscore = jnp.where(
        slot_index[None, :] < own_valid[:, None],
        scale * cross_sum / jnp.sqrt(dose_power * expr_power[:, None]),
        0.0,
    )
    width_part = W // lax.axis_size("col")
    return lax.dynamic_slice_in_dim(zscore, lax.axis_index("col") * width_part, width_part, 1)


def solution(mesh):
    placed = (
        P(("groups", "row"), "col"),
        P(("groups", "col")),
        P(("groups", "row"), None),
        P(("groups", "row"), None),
        P("groups"),
        P("groups"),
        P("groups"),
        P("groups"),
    )
    return jax.shard_map(
        body, mesh=mesh, in_specs=placed, out_specs=P(("groups", "row"), "col"), check_vma=False
    )
```

profile of v0, /device:TPU:0, one launch (start us, length us, event | category | flops | bytes accessed | tf_op | source)
XLA Modules:
  0.0 141.3 jit_solution(18025098898955943989)
XLA Ops:
  6.5 0.9 copy-done
  7.4 0.7 copy_bitcast_fusion
  8.1 7.3 %all-to-all-start = ((bf16[64,8,128]{2,0,1:T(8,128)(2,1)}), bf16[64,8,128]{2,0,1:T(8,128)(2,1)S(1)}, u32[]{:S(2)}, u32[]{:S(2)}) async-start(bf16[64,8,128]{2,0,1:T(8,128)(2,1)} %copy_bitcast_fusion), calls=%async_computation | async-start | bytes 262144 | tf_op jit(solution)/shard_map/all_to_all | solution.py:43
  15.4 0.7 iota_add_fusion
  16.1 0.8 dynamic_slice.10
  17.0 4.4 %sort.17 = (s32[1024]{0:T(1024)}, s32[1024]{0:T(1024)S(1)}) sort(s32[1024]{0:T(1024)S(1)} %iota_add_fusion, s32[1024]{0:T(1024)S(1)} %iota.21), dimensions={0}, to_apply=%region_0.0 | sort | flops 10240 | bytes 16384 | tf_op jit(solution)/shard_map/jit(argsort)/sort | solution.py:11
  21.7 1.6 %gather_fusion = f32[128]{0:T(128)S(1)} fusion(f32[1024]{0:T(1024)} %param.14, s32[1024]{0:T(1024)S(1)} %pad_clamp_fusion.1), kind=kCustom, calls=%fused_computation.2 | custom fusion | bytes 1536 | tf_op jit(solution)/shard_map/jit(_take)/gather | solution.py:67
  23.3 0.8 multiply_add_fusion
  24.1 1.6 %gather_fusion.3 = s32[128]{0:T(128)S(1)} fusion(s32[1024]{0:T(1024)} %param.15, s32[1024]{0:T(1024)S(1)} %pad_clamp_fusion.1), kind=kCustom, calls=%fused_computation.1.clone | custom fusion | bytes 1536 | tf_op jit(solution)/shard_map/jit(_take)/gather | solution.py:68
  25.9 0.7 copy.15
  26.7 6.0 %all-to-all-start.1 = ((bf16[64,8,192]{2,0,1:T(8,128)(2,1)}), bf16[64,8,192]{2,0,1:T(8,128)(2,1)S(1)}, u32[]{:S(2)}, u32[]{:S(2)}) async-start(bf16[64,8,192]{2,0,1:T(8,128)(2,1)} %copy.15), calls=%async_computation.1 | async-start | bytes 524288 | tf_op jit(solution)/shard_map/all_to_all | solution.py:44
  32.8 1.0 gather_fusion.2
  33.8 31.7 %all_gather.6 = bf16[512,256]{1,0:T(8,128)(2,1)S(1)} all-gather(bf16[64,256]{1,0:T(8,128)(2,1)S(1)} %copy-done.3), channel_id=1, replica_groups=mesh['groups'=2,'row'=8,'col'=2] {'row'}, dimensions={0}, use_global_device_ids=true | all-gather | bytes 294912 | tf_op jit(solution)/shard_map/all_gather | solution.py:49
  65.9 0.8 convolution_convert_fusion.1
  66.7 5.1 %all-to-all-start.2 = ((bf16[8,16,256]{2,1,0:T(8,128)(2,1)}), bf16[8,16,256]{2,1,0:T(8,128)(2,1)S(1)}, u32[]{:S(2)}, u32[]{:S(2)}) async-start(bf16[8,16,256]{2,1,0:T(8,128)(2,1)} %bitcast.4), calls=%async_computation.2 | async-start | bytes 131072 | tf_op jit(solution)/shard_map/all_to_all | solution.py:64
  71.8 32.6 %all_gather.7 = bf16[1536,256]{1,0:T(8,128)(2,1)S(1)} all-gather(bf16[192,256]{1,0:T(8,128)(2,1)S(1)} %slice.69), channel_id=1, replica_groups=mesh['groups'=2,'row'=8,'col'=2] {'row'}, dimensions={0}, use_global_device_ids=true | all-gather | bytes 884736 | tf_op jit(solution)/shard_map/all_gather | solution.py:55
  104.8 0.8 gather_fusion.1
  106.1 0.5 fusion
  107.4 0.5 pad_select_fusion.9
  108.7 0.5 slice.74
  113.0 0.7 slice_bitcast_fusion
  114.0 2.5 %psum.23 = f32[128]{0:T(128)S(1)} all-reduce(f32[128]{0:T(128)S(1)} %fusion.5), channel_id=1, replica_groups=mesh['groups'=2,'row'=8,'col'=2] {'col'}, use_global_device_ids=true, to_apply=%region_6.8 | all-reduce | flops 128 | bytes 1024 | tf_op jit(solution)/shard_map/psum | solution.py:85
  116.4 16.4 %all-reduce.14.cloned.1.call-done = (f32[128,256]{1,0:T(8,128)}, f32[128,256]{1,0:T(8,128)}) async-done(((f32[128,256]{1,0:T(8,128)}, f32[128,256]{1,0:T(8,128)}), (f32[128,256]{1,0:T(8,128)}, f32[128,256]{1,0:T(8,128)})) %all-reduce.14.cloned.1.call-update) | async-done | bytes 262160 | tf_op jit(solution)/shard_map/psum | solution.py:85
  132.8 1.6 %fusion.11 = f32[128,128]{1,0:T(8,128)} fusion(f32[128,256]{1,0:T(8,128)} %get-tuple-element.8, s32[]{:T(128)S(6)} %select_n.191, f32[128,256]{1,0:T(8,128)} %get-tuple-element.9, s32[128]{0:T(128)S(1)} %broadcast_select_fusion.3, f32[128]{0:T(128)S(1)} %psum.23), kind=kLoop, calls=%fused_computation.39 | loop fusion | flops 98304 | bytes 198656 | tf_op jit(solution)/shard_map/jit(_where)/select_n | solution.py:87
  (50 shorter events, 7.4 us)
Async XLA Ops:
  6.5 0.9 copy-start
  6.5 19.2 %copy-start.2 = (bf16[64,1536]{1,0:T(8,128)(2,1)S(1)}, bf16[64,1536]{1,0:T(8,128)(2,1)}, u32[]{:S(2)}) copy-start(bf16[64,1536]{1,0:T(8,128)(2,1)} %param.13) | copy-start | bytes 589828
  6.5 26.2 %copy-start.1 = (s32[1024]{0:T(1024)S(1)}, s32[1024]{0:T(1024)}, u32[]{:S(2)}) copy-start(s32[1024]{0:T(1024)} %param.16) | copy-start | bytes 12292
  8.1 18.6 %all-to-all-start = ((bf16[64,8,128]{2,0,1:T(8,128)(2,1)}), bf16[64,8,128]{2,0,1:T(8,128)(2,1)S(1)}, u32[]{:S(2)}, u32[]{:S(2)}) async-start(bf16[64,8,128]{2,0,1:T(8,128)(2,1)} %copy_bitcast_fusion), calls=%async_computation | async-start | bytes 262144 | tf_op jit(solution)/shard_map/all_to_all | solution.py:43
  16.1 17.7 %copy-start.3 = (bf16[64,256]{1,0:T(8,128)(2,1)S(1)}, bf16[64,256]{1,0:T(8,128)(2,1)}, u32[]{:S(2)}) copy-start(bf16[64,256]{1,0:T(8,128)(2,1)} %param.10) | copy-start | bytes 98308
  26.7 38.8 %all-to-all-start.1 = ((bf16[64,8,192]{2,0,1:T(8,128)(2,1)}), bf16[64,8,192]{2,0,1:T(8,128)(2,1)S(1)}, u32[]{:S(2)}, u32[]{:S(2)}) async-start(bf16[64,8,192]{2,0,1:T(8,128)(2,1)} %copy.15), calls=%async_computation.1 | async-start | bytes 524288 | tf_op jit(solution)/shard_map/all_to_all | solution.py:44
  33.7 70.7 %copy-start.4 = (f32[256]{0:T(256)S(1)}, f32[256]{0:T(256)}, u32[]{:S(2)}) copy-start(f32[256]{0:T(256)} %param.11) | copy-start | bytes 3076
  66.7 38.2 %all-to-all-start.2 = ((bf16[8,16,256]{2,1,0:T(8,128)(2,1)}), bf16[8,16,256]{2,1,0:T(8,128)(2,1)S(1)}, u32[]{:S(2)}, u32[]{:S(2)}) async-start(bf16[8,16,256]{2,1,0:T(8,128)(2,1)} %bitcast.4), calls=%async_computation.2 | async-start | bytes 131072 | tf_op jit(solution)/shard_map/all_to_all | solution.py:64
  71.8 61.0 %all-reduce.14.cloned.1.call-start = ((), (), s32[]{:S(2)}) async-start(), calls=%async_computation.3 | async-start | bytes 524288 | tf_op jit(solution)/shard_map/psum | solution.py:85
Sparse Core Ops, SparseCore 0:
  113.9 18.8 all-reduce.13
where the time goes:
time: 142 us; the launch traced here: 141 us
  blocking collectives  66.8 us (47%)
  starting transfers between devices  18.5 us (13%)
  waiting for transfers between devices  16.4 us (12%)
  between operations  13.7 us (10%)
  local copies, waits for them, and re-layouts  12.3 us (9%)
  other arithmetic  11.7 us (8%)
  matrix products  1.88 us (1%)
    all_gather x1, blocking collectives, body(): dose_all = lax.all_gather(rot_dose, 'row', axis=0, tiled=True)  32.6 us
    all_gather x1, blocking collectives, body(): lax.all_gather(eigvecs, 'row', axis=0, tiled=True)  31.7 us
    psum x1, waiting for transfers between devices, body(): lax.psum((cross_sum, dose_power, expr_power), 'col')  16.4 us
    all_to_all x1, starting transfers between devices, body(): lax.all_to_all(expression, 'row', split_axis=1, concat_axis=0, tiled=True)  7.28 us
    all_to_all x1, starting transfers between devices, body(): lax.all_to_all(dosage, 'row', split_axis=1, concat_axis=0, tiled=True)  6.01 us
    all_to_all x1, starting transfers between devices, body(): lax.all_to_all(buckets, 'row', split_axis=0, concat_axis=0, tiled=True)  5.13 us
    sort x1, other arithmetic, owner_listing(): return jnp.argsort(gene_owner * total + jnp.arange(total, dtype=jnp.int32))  4.37 us
    slice x10, local copies, waits for them, and re-layouts, shift_windows(): moved = jnp.concatenate([moved_tables[..., step_size:], filler], axis=-1)  3.17 us
  transfers between devices with their start and end apart: 4, of which 1 were waited for; matrix products, arithmetic and copies ran while one was open for 9% of the time, Pallas kernels for 0%

commit v1 on v0

--- a/solution.py
+++ b/solution.py
@@ -1,9 +1,16 @@
 import jax
 import jax.numpy as jnp
 from jax import lax
+from jax.experimental import pallas as pl
+from jax.experimental.pallas import tpu as pltpu
 from jax.sharding import PartitionSpec as P
 
 W = 256
+LANES = 128
+VMEM_LIMIT = 32 * 1024 * 1024
+NT = (((1,), (1,)), ((), ()))
+f32 = jnp.float32
+bf16 = jnp.bfloat16
 
 
 def owner_listing(gene_owner):
@@ -30,7 +37,7 @@
     return moved_tables
 
 
-def body(eigvecs, eigvals, expression, dosage, delta, window_start, window_valid, gene_owner):
+def wide_body(eigvecs, eigvals, expression, dosage, delta, window_start, window_valid, gene_owner):
     row_count = lax.axis_size("row")
     row_index = lax.axis_index("row")
     genes_all = expression.shape[1]
@@ -93,6 +100,190 @@
     return lax.dynamic_slice_in_dim(zscore, lax.axis_index("col") * width_part, width_part, 1)
 
 
+def route_kernel(place_ref, owner_ref, delta_ref, start_ref, valid_ref, vecs_ref, expr_ref, send_ref, gene_ref):
+    slices = owner_ref.shape[0]
+    capacity = LANES // slices
+    half = vecs_ref.shape[1]
+    owner = owner_ref[...]
+    before = lax.broadcasted_iota(jnp.int32, (LANES, LANES), 0) < lax.broadcasted_iota(
+        jnp.int32, (LANES, LANES), 1
+    )
+    before = before.astype(bf16)
+    rank = jnp.zeros(owner.shape, f32)
+    for o in range(slices):
+        same = (owner == o).astype(f32)
+        rank += same * jnp.dot(same.astype(bf16), before, preferred_element_type=f32)
+    bucket = owner * capacity + rank.astype(jnp.int32)
+    slot = lax.broadcasted_iota(jnp.int32, (LANES, LANES), 0)
+    own_slot = lax.broadcasted_iota(jnp.int32, (capacity, LANES), 0) + place_ref[0] * capacity
+    lane = lax.broadcasted_iota(jnp.int32, (capacity, LANES), 1)
+    sorted_slices = []
+    for s in range(slices):
+        here = bucket[s : s + 1, :]
+        pick = (slot == here).astype(bf16)
+        sorted_slices.append(
+            lax.dot_general(pick, expr_ref[:, s * LANES : (s + 1) * LANES], NT, preferred_element_type=f32)
+        )
+        mine = (own_slot == here).astype(f32)
+        figures = jnp.zeros((capacity, LANES), f32)
+        for i, ref in enumerate((delta_ref, start_ref, valid_ref)):
+            row = ref[s : s + 1, :].astype(f32)
+            figures = jnp.where(lane == i, jnp.sum(mine * row, axis=1, keepdims=True), figures)
+        gene_ref[s * capacity : (s + 1) * capacity, :] = figures
+    for o in range(slices):
+        rows = jnp.concatenate([x[o * capacity : (o + 1) * capacity, :] for x in sorted_slices], axis=0)
+        send_ref[o, :, :half] = vecs_ref[...]
+        send_ref[o, :, half:] = rows.T.astype(bf16)
+
+
+def weight_kernel(place_ref, recv_ref, other_ref, vals_ref, gene_ref, turned_ref, weighted_ref, low_ref, power_ref):
+    rows, samples, _ = recv_ref.shape
+    half = other_ref.shape[2]
+    row = place_ref[0]
+    for m in range(rows):
+        r = row ^ m
+        cols = pl.ds(m * samples, samples)
+        turned_ref[:half, cols] = recv_ref[r, :, :half].astype(f32).T.astype(bf16)
+        turned_ref[half:, cols] = other_ref[r].astype(f32).T.astype(bf16)
+    data = jnp.concatenate([recv_ref[r, :, half:] for r in range(rows)], axis=0)
+    data = data.astype(f32).T.astype(bf16)
+    delta = gene_ref[:, 0:1]
+    total = jnp.zeros((data.shape[0], 1), f32)
+    for c in range(2):
+        if c == 0:
+            vecs = jnp.concatenate([recv_ref[r, :, :half] for r in range(rows)], axis=0)
+        else:
+            vecs = jnp.concatenate([other_ref[r] for r in range(rows)], axis=0)
+        cols = pl.ds(c * half, half)
+        rotated = jnp.dot(data, vecs, preferred_element_type=f32).astype(bf16).astype(f32)
+        weight = 1.0 / (vals_ref[:, cols] + delta)
+        total += jnp.sum(weight * rotated * rotated, axis=1, keepdims=True)
+        weighted_ref[:, cols] = (weight * rotated).astype(bf16)
+        low_ref[:, cols] = weight.astype(bf16)
+    power_ref[...] = jnp.broadcast_to(total, power_ref.shape)
+
+
+def score_kernel(place_ref, gene_ref, power_ref, turned_ref, weighted_ref, low_ref, *refs):
+    *dose_refs, keep_ref, pass_ref, dose_scr = refs
+    samples, variants = dose_refs[0].shape
+    for m, ref in enumerate(dose_refs):
+        dose_scr[m * samples : (m + 1) * samples, :] = ref[...]
+    rotated = jnp.dot(turned_ref[...], dose_scr[...], preferred_element_type=f32).astype(bf16)
+    squared = jnp.square(rotated.astype(f32)).astype(bf16)
+    cross = jnp.dot(weighted_ref[...], rotated, preferred_element_type=f32)
+    power = jnp.dot(low_ref[...], squared, preferred_element_type=f32)
+    core = place_ref[1]
+    start = gene_ref[:, 1:2].astype(jnp.int32)
+    valid = gene_ref[:, 2:3].astype(jnp.int32)
+    genes = cross.shape[0]
+    lane = lax.broadcasted_iota(jnp.int32, (genes, LANES), 1)
+    own_power = power_ref[...]
+    scale = jnp.sqrt(f32(samples * len(dose_refs)))
+    blocks = variants // LANES
+    for out_ref, half in ((keep_ref, core), (pass_ref, 1 - core)):
+        offset = start + half * LANES - core * variants
+        block = offset >> 7
+        shift = offset & (LANES - 1)
+        at = lane + shift
+        wrapped = at >= LANES
+        at = at & (LANES - 1)
+        here = block + wrapped.astype(jnp.int32)
+        picked = []
+        for array in (cross, power):
+            low = jnp.zeros((genes, LANES), f32)
+            high = low
+            for b in range(blocks):
+                part = array[:, b * LANES : (b + 1) * LANES]
+                low = jnp.where(block == b, part, low)
+                high = jnp.where(block + 1 == b, part, high)
+            low = jnp.take_along_axis(low, at, axis=1)
+            high = jnp.take_along_axis(high, at, axis=1)
+            picked.append(jnp.where(wrapped, high, low))
+        live = (here >= 0) & (here < blocks) & (lane + half * LANES < valid)
+        score = scale * picked[0] / jnp.sqrt(picked[1] * own_power)
+        out_ref[...] = jnp.where(live, score, 0.0)
+
+
+def call(kernel, outs, scratch=(), smem=1, count=0):
+    vmem = pl.BlockSpec(memory_space=pltpu.VMEM)
+    return pl.pallas_call(
+        kernel,
+        out_shape=[jax.ShapeDtypeStruct(*o) for o in outs],
+        in_specs=[pl.BlockSpec(memory_space=pltpu.SMEM)] * smem + [vmem] * (count - smem),
+        out_specs=[vmem] * len(outs),
+        scratch_shapes=list(scratch),
+        compiler_params=pltpu.CompilerParams(vmem_limit_bytes=VMEM_LIMIT),
+    )
+
+
+def near_body(eigvecs, eigvals, expression, dosage, delta, window_start, window_valid, gene_owner):
+    rows = lax.axis_size("row")
+    row = lax.axis_index("row")
+    core = lax.axis_index("col")
+    panel, half = eigvecs.shape
+    samples = panel * rows
+    variants = dosage.shape[1] // 2
+    place = jnp.stack([row, core]).astype(jnp.int32)
+
+    def swap(x, m):
+        return lax.ppermute(x, "row", [(i, i ^ m) for i in range(rows)])
+
+    def other_core(x):
+        return lax.ppermute(x, "col", [(0, 1), (1, 0)])
+
+    chunks = [None] * rows
+    chunks[0] = lax.dynamic_slice_in_dim(dosage, core * variants, variants, 1)
+    for m in range(2, rows, 2):
+        chunks[m] = swap(chunks[0], m)
+    for m in range(0, rows, 2):
+        chunks[m + 1] = swap(chunks[m], 1)
+    vals = jnp.concatenate([eigvals, other_core(eigvals)])[None, :]
+    send, gene = call(
+        route_kernel,
+        [((rows, panel, half + LANES), bf16), ((LANES, LANES), f32)],
+        count=7,
+    )(
+        place,
+        gene_owner.reshape(rows, LANES),
+        delta.reshape(rows, LANES),
+        window_start.reshape(rows, LANES),
+        window_valid.reshape(rows, LANES),
+        eigvecs,
+        expression,
+    )
+    received = lax.all_to_all(send, "row", split_axis=0, concat_axis=0, tiled=True)
+    other = other_core(received[:, :, :half])
+    turned, weighted, low, power = call(
+        weight_kernel,
+        [((2 * half, samples), bf16), ((LANES, 2 * half), bf16), ((LANES, 2 * half), bf16), ((LANES, LANES), f32)],
+        count=5,
+    )(place, received, other, vals, gene)
+    keep, passed = call(
+        score_kernel,
+        [((LANES, LANES), f32)] * 2,
+        scratch=[pltpu.VMEM((samples, variants), bf16)],
+        count=6 + rows,
+    )(place, gene, power, turned, weighted, low, *chunks)
+    return keep + other_core(passed)
+
+
+def body(eigvecs, eigvals, expression, dosage, delta, window_start, window_valid, gene_owner):
+    rows = lax.axis_size("row")
+    samples = eigvecs.shape[0] * rows
+    own = expression.shape[1] // rows
+    fits = (
+        lax.axis_size("col") == 2
+        and own == LANES
+        and W == 2 * LANES
+        and rows & (rows - 1) == 0
+        and own // rows % 16 == 0
+        and dosage.shape[1] % (2 * LANES) == 0
+        and samples * (samples + dosage.shape[1]) <= VMEM_LIMIT // 16
+    )
+    run = near_body if fits else wide_body
+    return run(eigvecs, eigvals, expression, dosage, delta, window_start, window_valid, gene_owner)
+
+
 def solution(mesh):
     placed = (
         P(("groups", "row"), "col"),

time: 142 us -> 44.8 us (0.32)
  blocking collectives: 66.8 us -> 0 us
  between operations: 13.7 us -> 0.1 us
  other arithmetic: 11.7 us -> 0.72 us
  local copies, waits for them, and re-layouts: 12.3 us -> 2.4 us
  Pallas kernels: 0 us -> 5 us
  waiting for transfers between devices: 16.4 us -> 20.1 us
  starting transfers between devices: 18.5 us -> 16.2 us
  matrix products: 1.88 us -> 0 us
    all_gather x2 -> x0, blocking collectives: 64.3 us -> none  [the longest x1 32.6 us: body(): dose_all = lax.all_gather(rot_dose, 'row', axis=0, tiled=True)]
    psum x1 -> x0, waiting for transfers between devices: 16.4 us -> none  [body(): lax.psum((cross_sum, dose_power, expr_power), 'col')]
    all_to_all x3 -> x1, waiting for transfers between devices: 0.01 us -> 11.7 us  [near_body(): lax.all_to_all(send, 'row', split_axis=0, concat_axis=0, tiled=True)]
    all_to_all x3 -> x1, starting transfers between devices: 18.4 us -> 7.29 us  [near_body(): lax.all_to_all(send, 'row', split_axis=0, concat_axis=0, tiled=True)]
    ppermute x0 -> x10, starting transfers between devices: none -> 8.87 us  [the longest x7 8.72 us: swap(): return lax.ppermute(x, 'row', [(i, i ^ m) for i in range(rows)])]
    ppermute x0 -> x10, waiting for transfers between devices: none -> 8.39 us  [the longest x7 6.01 us: swap(): return lax.ppermute(x, 'row', [(i, i ^ m) for i in range(rows)])]
    gather x4 -> x0, local copies, waits for them, and re-layouts: 5.05 us -> none  [the longest x1 1.62 us: body(): own_delta = jnp.take(delta, my_genes)]
    pallas_call x0 -> x3, Pallas kernels: none -> 5 us  [the longest x1 1.83 us: near_body(): call(score_kernel, [((LANES, LANES), f32)] * 2, scratch=[pltpu.VMEM((samp...]
  transfers between devices with their start and end apart: 4 -> 11, of which waited for: 1 -> 6; matrix products, arithmetic and copies ran while one was open for 9% -> 0% of each run, Pallas kernels for 0% -> 3%
where the time goes in v1:
time: 44.8 us; the launch traced here: 44.5 us
  waiting for transfers between devices  20.1 us (45%)
  starting transfers between devices  16.2 us (36%)
  Pallas kernels  5 us (11%)
  local copies, waits for them, and re-layouts  2.4 us (5%)
  other arithmetic  0.72 us (2%)
    all_to_all x1, waiting for transfers between devices, near_body(): lax.all_to_all(send, 'row', split_axis=0, concat_axis=0, tiled=True)  11.7 us
    ppermute x7, starting transfers between devices, swap(): return lax.ppermute(x, 'row', [(i, i ^ m) for i in range(rows)])  8.72 us
    all_to_all x1, starting transfers between devices, near_body(): lax.all_to_all(send, 'row', split_axis=0, concat_axis=0, tiled=True)  7.29 us
    ppermute x7, waiting for transfers between devices, swap(): return lax.ppermute(x, 'row', [(i, i ^ m) for i in range(rows)])  6.01 us
    ppermute x3, waiting for transfers between devices, other_core(): return lax.ppermute(x, 'col', [(0, 1), (1, 0)])  2.38 us
    unnamed x16, local copies, waits for them, and re-layouts  2.36 us
    pallas_call x1, Pallas kernels, near_body(): call(score_kernel, [((LANES, LANES), f32)] * 2, scratch=[pltpu.VMEM((samp...  1.83 us
    pallas_call x1, Pallas kernels, near_body(): call(route_kernel, [((rows, panel, half + LANES), bf16), ((LANES, LANES),...  1.77 us
  transfers between devices with their start and end apart: 11, of which 6 were waited for; matrix products, arithmetic and copies ran while one was open for 0% of the time, Pallas kernels for 3%

profile of v1, /device:TPU:0, one launch (start us, length us, event | category | flops | bytes accessed | tf_op | source)
XLA Modules:
  0.0 44.5 jit_solution(16890470063819423147)
XLA Ops:
  0.0 0.1 pad_add_fusion.place_ref
  0.1 0.6 %copy-done.6 = s32[1024]{0:T(1024)S(1)} copy-done((s32[1024]{0:T(1024)S(1)}, s32[1024]{0:T(1024)}, u32[]{:S(2)}) %copy-start.6) | copy-done | bytes 4120
  0.8 0.9 %copy-done.1 = bf16[64,1024]{1,0:T(8,128)(2,1)S(1)} copy-done((bf16[64,1024]{1,0:T(8,128)(2,1)S(1)}, bf16[64,1024]{1,0:T(8,128)(2,1)}, u32[]{:S(2)}) %copy-start.1) | copy-done | bytes 131096
  1.7 0.8 %copy-done.2 = bf16[64,256]{1,0:T(8,128)(2,1)S(1)} copy-done((bf16[64,256]{1,0:T(8,128)(2,1)S(1)}, bf16[64,256]{1,0:T(8,128)(2,1)}, u32[]{:S(2)}) %copy-start.2) | copy-done | bytes 32792
  2.4 1.8 %shard_map.82 = (bf16[8,64,384]{2,1,0:T(8,128)(2,1)}, f32[128,128]{1,0:T(8,128)S(1)}) custom-call(s32[2]{0:T(128)S(1)} %pad_add_fusion.place_ref, s32[8,128]{1,0:T(8,128)S(1)} %bitcast.8, f32[8,128]{1,0:T(8,128)S(1)} %bitcast.9, s32[8,128]{1,0:T(8,128)S(1)} %bitcast.10, s32[8,128]{1,0:T(8,128)S(1)} %bitcast.11, bf16[64,256]{1,0:T(8,128)(2,1)S(1)} %copy-done.2, ...), custom_call_target="tpu_custom_call" | custom-call | tf_op jit(solution)/shard_map/pallas_call | solution.py:241
  4.2 7.3 %all-to-all-start = ((bf16[8,64,384]{2,1,0:T(8,128)(2,1)}), bf16[8,64,384]{2,1,0:T(8,128)(2,1)S(1)}, u32[]{:S(2)}, u32[]{:S(2)}) async-start(bf16[8,64,384]{2,1,0:T(8,128)(2,1)} %get-tuple-element.14), calls=%async_computation | async-start | bytes 786432 | tf_op jit(solution)/shard_map/all_to_all | solution.py:254
  11.5 11.7 %all-to-all-done.recv_ref = bf16[8,64,384]{2,1,0:T(8,128)(2,1)S(1)} async-done(((bf16[8,64,384]{2,1,0:T(8,128)(2,1)}), bf16[8,64,384]{2,1,0:T(8,128)(2,1)S(1)}, u32[]{:S(2)}, u32[]{:S(2)}) %all-to-all-start) | async-done | bytes 393248 | tf_op jit(solution)/shard_map/all_to_all | solution.py:254
  23.2 0.1 collective-permute-start
  23.3 1.0 %collective-permute-start.3 = (bf16[64,768]{1,0:T(8,128)(2,1)S(1)}, bf16[64,768]{1,0:T(8,128)(2,1)S(1)}, u32[]{:S(2)}, u32[]{:S(2)}) collective-permute-start(bf16[64,768]{1,0:T(8,128)(2,1)S(1)} %constant_dynamic-slice_fusion.refs_0_), channel_id=1, source_target_pairs={{0,4},{2,6},{4,0},{6,2},{8,12},{10,14},{12,8},{14,10},{1,5},{3,7},... | collective-permute-start | bytes 294920 | tf_op jit(solution)/shard_map/ppermute | solution.py:229
  24.3 0.8 %collective-permute-start.5 = (bf16[64,768]{1,0:T(8,128)(2,1)S(1)}, bf16[64,768]{1,0:T(8,128)(2,1)S(1)}, u32[]{:S(2)}, u32[]{:S(2)}) collective-permute-start(bf16[64,768]{1,0:T(8,128)(2,1)S(1)} %constant_dynamic-slice_fusion.refs_0_), channel_id=1, source_target_pairs={{0,8},{2,10},{4,12},{6,14},{8,0},{10,2},{12,4},{14,6},{1,9},{3,11}... | collective-permute-start | bytes 294920 | tf_op jit(solution)/shard_map/ppermute | solution.py:229
  25.1 2.7 %collective-permute-start.7 = (bf16[64,768]{1,0:T(8,128)(2,1)S(1)}, bf16[64,768]{1,0:T(8,128)(2,1)S(1)}, u32[]{:S(2)}, u32[]{:S(2)}) collective-permute-start(bf16[64,768]{1,0:T(8,128)(2,1)S(1)} %constant_dynamic-slice_fusion.refs_0_), channel_id=1, source_target_pairs={{0,12},{2,14},{4,8},{6,10},{8,4},{10,6},{12,0},{14,2},{1,13},{3,15... | collective-permute-start | bytes 294920 | tf_op jit(solution)/shard_map/ppermute | solution.py:229
  27.8 1.1 %collective-permute-done.1 = f32[256]{0:T(256)S(1)} collective-permute-done((f32[256]{0:T(256)S(1)}, f32[256]{0:T(256)S(1)}, u32[]{:S(2)}, u32[]{:S(2)}) %collective-permute-start.1) | collective-permute-done | bytes 1056 | tf_op jit(solution)/shard_map/ppermute | solution.py:232
  28.9 1.4 %collective-permute-start.2 = (bf16[64,768]{1,0:T(8,128)(2,1)S(1)}, bf16[64,768]{1,0:T(8,128)(2,1)S(1)}, u32[]{:S(2)}, u32[]{:S(2)}) collective-permute-start(bf16[64,768]{1,0:T(8,128)(2,1)S(1)} %constant_dynamic-slice_fusion.refs_0_), channel_id=1, source_target_pairs={{0,2},{2,0},{4,6},{6,4},{8,10},{10,8},{12,14},{14,12},{1,3},{3,1},... | collective-permute-start | bytes 294920 | tf_op jit(solution)/shard_map/ppermute | solution.py:229
  30.4 0.8 %collective-permute-start.4 = (bf16[64,768]{1,0:T(8,128)(2,1)S(1)}, bf16[64,768]{1,0:T(8,128)(2,1)S(1)}, u32[]{:S(2)}, u32[]{:S(2)}) collective-permute-start(bf16[64,768]{1,0:T(8,128)(2,1)S(1)} %collective-permute-done.3.refs_2_), channel_id=1, source_target_pairs={{0,2},{2,0},{4,6},{6,4},{8,10},{10,8},{12,14},{14,12},{1,3},{3,1},... | collective-permute-start | bytes 294920 | tf_op jit(solution)/shard_map/ppermute | solution.py:229
  31.2 3.8 %collective-permute-done.5.refs_4_ = bf16[64,768]{1,0:T(8,128)(2,1)S(1)} collective-permute-done((bf16[64,768]{1,0:T(8,128)(2,1)S(1)}, bf16[64,768]{1,0:T(8,128)(2,1)S(1)}, u32[]{:S(2)}, u32[]{:S(2)}) %collective-permute-start.5) | collective-permute-done | bytes 98336 | tf_op jit(solution)/shard_map/ppermute | solution.py:229
  35.0 0.7 %collective-permute-start.6 = (bf16[64,768]{1,0:T(8,128)(2,1)S(1)}, bf16[64,768]{1,0:T(8,128)(2,1)S(1)}, u32[]{:S(2)}, u32[]{:S(2)}) collective-permute-start(bf16[64,768]{1,0:T(8,128)(2,1)S(1)} %collective-permute-done.5.refs_4_), channel_id=1, source_target_pairs={{0,2},{2,0},{4,6},{6,4},{8,10},{10,8},{12,14},{14,12},{1,3},{3,1},... | collective-permute-start | bytes 294920 | tf_op jit(solution)/shard_map/ppermute | solution.py:229
  35.7 1.3 %collective-permute-start.8 = (bf16[64,768]{1,0:T(8,128)(2,1)S(1)}, bf16[64,768]{1,0:T(8,128)(2,1)S(1)}, u32[]{:S(2)}, u32[]{:S(2)}) collective-permute-start(bf16[64,768]{1,0:T(8,128)(2,1)S(1)} %collective-permute-done.7.refs_6_), channel_id=1, source_target_pairs={{0,2},{2,0},{4,6},{6,4},{8,10},{10,8},{12,14},{14,12},{1,3},{3,1},... | collective-permute-start | bytes 294920 | tf_op jit(solution)/shard_map/ppermute | solution.py:229
  37.0 1.4 %shard_map.83 = (bf16[512,512]{1,0:T(8,128)(2,1)S(1)}, bf16[128,512]{1,0:T(8,128)(2,1)S(1)}, bf16[128,512]{1,0:T(8,128)(2,1)S(1)}, f32[128,128]{1,0:T(8,128)S(1)}) custom-call(s32[2]{0:T(128)S(1)} %pad_add_fusion.place_ref, bf16[8,64,384]{2,1,0:T(8,128)(2,1)S(1)} %all-to-all-done.recv_ref, bf16[8,64,256]{2,1,0:T(8,128)(2,1)S(1)} %collective-permute-done.other_ref, ...), custom_call_target="tpu_custom_call" | custom-call | tf_op jit(solution)/shard_map/pallas_call | solution.py:256
  38.4 1.2 %collective-permute-done.6.refs_5_ = bf16[64,768]{1,0:T(8,128)(2,1)S(1)} collective-permute-done((bf16[64,768]{1,0:T(8,128)(2,1)S(1)}, bf16[64,768]{1,0:T(8,128)(2,1)S(1)}, u32[]{:S(2)}, u32[]{:S(2)}) %collective-permute-start.6) | collective-permute-done | bytes 98336 | tf_op jit(solution)/shard_map/ppermute | solution.py:229
  39.6 1.1 %collective-permute-done.8.refs_7_ = bf16[64,768]{1,0:T(8,128)(2,1)S(1)} collective-permute-done((bf16[64,768]{1,0:T(8,128)(2,1)S(1)}, bf16[64,768]{1,0:T(8,128)(2,1)S(1)}, u32[]{:S(2)}, u32[]{:S(2)}) %collective-permute-start.8) | collective-permute-done | bytes 98336 | tf_op jit(solution)/shard_map/ppermute | solution.py:229
  40.6 1.8 %shard_map.84 = (f32[128,128]{1,0:T(8,128)S(1)}, f32[128,128]{1,0:T(8,128)S(1)}) custom-call(s32[2]{0:T(128)S(1)} %pad_add_fusion.place_ref, f32[128,128]{1,0:T(8,128)S(1)} %get-tuple-element.13.gene_ref, f32[128,128]{1,0:T(8,128)S(1)} %get-tuple-element.15.power_ref, bf16[512,512]{1,0:T(8,128)(2,1)S(1)} %get-tuple-element.16.turned_ref, ...), custom_call_target="tpu_custom_call" | custom-call | tf_op jit(solution)/shard_map/pallas_call | solution.py:261
  42.5 0.1 collective-permute-start.9
  42.6 1.2 %collective-permute-done.9 = f32[128,128]{1,0:T(8,128)S(1)} collective-permute-done((f32[128,128]{1,0:T(8,128)S(1)}, f32[128,128]{1,0:T(8,128)S(1)}, u32[]{:S(2)}, u32[]{:S(2)}) %collective-permute-start.9) | collective-permute-done | bytes 65568 | tf_op jit(solution)/shard_map/ppermute | solution.py:232
  43.8 0.6 %add.7 = f32[128,128]{1,0:T(8,128)} add(f32[128,128]{1,0:T(8,128)S(1)} %get-tuple-element.19, f32[128,128]{1,0:T(8,128)S(1)} %collective-permute-done.9) | non-fusion elementwise | flops 16384 | bytes 196608 | tf_op jit(solution)/shard_map/add | solution.py:267
  (22 shorter events, 0.1 us)
Async XLA Ops:
  0.0 23.3 %copy-start = (bf16[64,1536]{1,0:T(8,128)(2,1)S(1)}, bf16[64,1536]{1,0:T(8,128)(2,1)}, u32[]{:S(2)}) copy-start(bf16[64,1536]{1,0:T(8,128)(2,1)} %param.11) | copy-start | bytes 589828
  0.0 0.7 %copy-start.6 = (s32[1024]{0:T(1024)S(1)}, s32[1024]{0:T(1024)}, u32[]{:S(2)}) copy-start(s32[1024]{0:T(1024)} %param.14) | copy-start | bytes 12292
  0.0 0.7 %copy-start.5 = (s32[1024]{0:T(1024)S(1)}, s32[1024]{0:T(1024)}, u32[]{:S(2)}) copy-start(s32[1024]{0:T(1024)} %param.13) | copy-start | bytes 12292
  0.0 0.8 %copy-start.4 = (f32[1024]{0:T(1024)S(1)}, f32[1024]{0:T(1024)}, u32[]{:S(2)}) copy-start(f32[1024]{0:T(1024)} %param.12) | copy-start | bytes 12292
  0.1 0.7 %copy-start.3 = (s32[1024]{0:T(1024)S(1)}, s32[1024]{0:T(1024)}, u32[]{:S(2)}) copy-start(s32[1024]{0:T(1024)} %param.15) | copy-start | bytes 12292
  0.8 0.9 %copy-start.1 = (bf16[64,1024]{1,0:T(8,128)(2,1)S(1)}, bf16[64,1024]{1,0:T(8,128)(2,1)}, u32[]{:S(2)}) copy-start(bf16[64,1024]{1,0:T(8,128)(2,1)} %expr_ref.1) | copy-start | bytes 393220
  1.7 0.8 %copy-start.2 = (bf16[64,256]{1,0:T(8,128)(2,1)S(1)}, bf16[64,256]{1,0:T(8,128)(2,1)}, u32[]{:S(2)}) copy-start(bf16[64,256]{1,0:T(8,128)(2,1)} %vecs_ref.1) | copy-start | bytes 98308
  4.2 19.0 %all-to-all-start = ((bf16[8,64,384]{2,1,0:T(8,128)(2,1)}), bf16[8,64,384]{2,1,0:T(8,128)(2,1)S(1)}, u32[]{:S(2)}, u32[]{:S(2)}) async-start(bf16[8,64,384]{2,1,0:T(8,128)(2,1)} %get-tuple-element.14), calls=%async_computation | async-start | bytes 786432 | tf_op jit(solution)/shard_map/all_to_all | solution.py:254
  23.2 4.6 %copy-start.7 = (f32[256]{0:T(256)S(1)}, f32[256]{0:T(256)}, u32[]{:S(2)}) copy-start(f32[256]{0:T(256)} %param.9) | copy-start | bytes 3076
  23.2 13.8 %collective-permute-start = (bf16[8,64,256]{2,1,0:T(8,128)(2,1)S(1)}, bf16[8,64,256]{2,1,0:T(8,128)(2,1)S(1)}, u32[]{:S(2)}, u32[]{:S(2)}) collective-permute-start(bf16[8,64,256]{2,1,0:T(8,128)(2,1)S(1)} %slice.4), channel_id=1, source_target_pairs={{0,1},{1,0},{2,3},{3,2},{4,5},{5,4},{6,7},{7,6},{8,9},{9,8},{10,11... | collective-permute-start | bytes 786440 | tf_op jit(solution)/shard_map/ppermute | solution.py:232
  23.3 7.0 %collective-permute-start.3 = (bf16[64,768]{1,0:T(8,128)(2,1)S(1)}, bf16[64,768]{1,0:T(8,128)(2,1)S(1)}, u32[]{:S(2)}, u32[]{:S(2)}) collective-permute-start(bf16[64,768]{1,0:T(8,128)(2,1)S(1)} %constant_dynamic-slice_fusion.refs_0_), channel_id=1, source_target_pairs={{0,4},{2,6},{4,0},{6,2},{8,12},{10,14},{12,8},{14,10},{1,5},{3,7},... | collective-permute-start | bytes 294920 | tf_op jit(solution)/shard_map/ppermute | solution.py:229
  24.3 10.6 %collective-permute-start.5 = (bf16[64,768]{1,0:T(8,128)(2,1)S(1)}, bf16[64,768]{1,0:T(8,128)(2,1)S(1)}, u32[]{:S(2)}, u32[]{:S(2)}) collective-permute-start(bf16[64,768]{1,0:T(8,128)(2,1)S(1)} %constant_dynamic-slice_fusion.refs_0_), channel_id=1, source_target_pairs={{0,8},{2,10},{4,12},{6,14},{8,0},{10,2},{12,4},{14,6},{1,9},{3,11}... | collective-permute-start | bytes 294920 | tf_op jit(solution)/shard_map/ppermute | solution.py:229
  25.1 10.6 %collective-permute-start.7 = (bf16[64,768]{1,0:T(8,128)(2,1)S(1)}, bf16[64,768]{1,0:T(8,128)(2,1)S(1)}, u32[]{:S(2)}, u32[]{:S(2)}) collective-permute-start(bf16[64,768]{1,0:T(8,128)(2,1)S(1)} %constant_dynamic-slice_fusion.refs_0_), channel_id=1, source_target_pairs={{0,12},{2,14},{4,8},{6,10},{8,4},{10,6},{12,0},{14,2},{1,13},{3,15... | collective-permute-start | bytes 294920 | tf_op jit(solution)/shard_map/ppermute | solution.py:229
  27.8 1.1 %collective-permute-start.1 = (f32[256]{0:T(256)S(1)}, f32[256]{0:T(256)S(1)}, u32[]{:S(2)}, u32[]{:S(2)}) collective-permute-start(f32[256]{0:T(256)S(1)} %copy-done.7), channel_id=1, source_target_pairs={{0,1},{1,0},{2,3},{3,2},{4,5},{5,4},{6,7},{7,6},{8,9},{9,8},{10,11... | collective-permute-start | bytes 3080 | tf_op jit(solution)/shard_map/ppermute | solution.py:232
  28.9 9.5 %collective-permute-start.2 = (bf16[64,768]{1,0:T(8,128)(2,1)S(1)}, bf16[64,768]{1,0:T(8,128)(2,1)S(1)}, u32[]{:S(2)}, u32[]{:S(2)}) collective-permute-start(bf16[64,768]{1,0:T(8,128)(2,1)S(1)} %constant_dynamic-slice_fusion.refs_0_), channel_id=1, source_target_pairs={{0,2},{2,0},{4,6},{6,4},{8,10},{10,8},{12,14},{14,12},{1,3},{3,1},... | collective-permute-start | bytes 294920 | tf_op jit(solution)/shard_map/ppermute | solution.py:229
  30.4 8.0 %collective-permute-start.4 = (bf16[64,768]{1,0:T(8,128)(2,1)S(1)}, bf16[64,768]{1,0:T(8,128)(2,1)S(1)}, u32[]{:S(2)}, u32[]{:S(2)}) collective-permute-start(bf16[64,768]{1,0:T(8,128)(2,1)S(1)} %collective-permute-done.3.refs_2_), channel_id=1, source_target_pairs={{0,2},{2,0},{4,6},{6,4},{8,10},{10,8},{12,14},{14,12},{1,3},{3,1},... | collective-permute-start | bytes 294920 | tf_op jit(solution)/shard_map/ppermute | solution.py:229
  35.0 4.6 %collective-permute-start.6 = (bf16[64,768]{1,0:T(8,128)(2,1)S(1)}, bf16[64,768]{1,0:T(8,128)(2,1)S(1)}, u32[]{:S(2)}, u32[]{:S(2)}) collective-permute-start(bf16[64,768]{1,0:T(8,128)(2,1)S(1)} %collective-permute-done.5.refs_4_), channel_id=1, source_target_pairs={{0,2},{2,0},{4,6},{6,4},{8,10},{10,8},{12,14},{14,12},{1,3},{3,1},... | collective-permute-start | bytes 294920 | tf_op jit(solution)/shard_map/ppermute | solution.py:229
  35.7 5.0 %collective-permute-start.8 = (bf16[64,768]{1,0:T(8,128)(2,1)S(1)}, bf16[64,768]{1,0:T(8,128)(2,1)S(1)}, u32[]{:S(2)}, u32[]{:S(2)}) collective-permute-start(bf16[64,768]{1,0:T(8,128)(2,1)S(1)} %collective-permute-done.7.refs_6_), channel_id=1, source_target_pairs={{0,2},{2,0},{4,6},{6,4},{8,10},{10,8},{12,14},{14,12},{1,3},{3,1},... | collective-permute-start | bytes 294920 | tf_op jit(solution)/shard_map/ppermute | solution.py:229
  42.5 1.3 %collective-permute-start.9 = (f32[128,128]{1,0:T(8,128)S(1)}, f32[128,128]{1,0:T(8,128)S(1)}, u32[]{:S(2)}, u32[]{:S(2)}) collective-permute-start(f32[128,128]{1,0:T(8,128)S(1)} %get-tuple-element.20), channel_id=1, source_target_pairs={{0,1},{1,0},{2,3},{3,2},{4,5},{5,4},{6,7},{7,6},{8,9},{9,8},{10,11... | collective-permute-start | bytes 196616 | tf_op jit(solution)/shard_map/ppermute | solution.py:232

commit v2 on v1

--- a/solution.py
+++ b/solution.py
@@ -100,10 +100,12 @@
     return lax.dynamic_slice_in_dim(zscore, lax.axis_index("col") * width_part, width_part, 1)
 
 
-def route_kernel(place_ref, owner_ref, delta_ref, start_ref, valid_ref, vecs_ref, expr_ref, send_ref, gene_ref):
+def route_kernel(place_ref, owner_ref, delta_ref, start_ref, valid_ref, vecs_ref, expr_ref, far_ref, e2_ref, e1_ref, e0_ref, gene_ref):
     slices = owner_ref.shape[0]
     capacity = LANES // slices
     half = vecs_ref.shape[1]
+    part = expr_ref.shape[0] // 2
+    row, core = place_ref[0], place_ref[1]
     owner = owner_ref[...]
     before = lax.broadcasted_iota(jnp.int32, (LANES, LANES), 0) < lax.broadcasted_iota(
         jnp.int32, (LANES, LANES), 1
@@ -113,48 +115,65 @@
     for o in range(slices):
         same = (owner == o).astype(f32)
         rank += same * jnp.dot(same.astype(bf16), before, preferred_element_type=f32)
-    bucket = owner * capacity + rank.astype(jnp.int32)
+    bucket = (owner ^ row) * capacity + rank.astype(jnp.int32)
     slot = lax.broadcasted_iota(jnp.int32, (LANES, LANES), 0)
-    own_slot = lax.broadcasted_iota(jnp.int32, (capacity, LANES), 0) + place_ref[0] * capacity
+    own_slot = lax.broadcasted_iota(jnp.int32, (capacity, LANES), 0)
     lane = lax.broadcasted_iota(jnp.int32, (capacity, LANES), 1)
+    rows = pl.ds(pl.multiple_of(core * part, part), part)
     sorted_slices = []
     for s in range(slices):
         here = bucket[s : s + 1, :]
         pick = (slot == here).astype(bf16)
         sorted_slices.append(
-            lax.dot_general(pick, expr_ref[:, s * LANES : (s + 1) * LANES], NT, preferred_element_type=f32)
+            lax.dot_general(pick, expr_ref[rows, s * LANES : (s + 1) * LANES], NT, preferred_element_type=f32)
         )
         mine = (own_slot == here).astype(f32)
         figures = jnp.zeros((capacity, LANES), f32)
         for i, ref in enumerate((delta_ref, start_ref, valid_ref)):
-            row = ref[s : s + 1, :].astype(f32)
-            figures = jnp.where(lane == i, jnp.sum(mine * row, axis=1, keepdims=True), figures)
+            line = ref[s : s + 1, :].astype(f32)
+            figures = jnp.where(lane == i, jnp.sum(mine * line, axis=1, keepdims=True), figures)
         gene_ref[s * capacity : (s + 1) * capacity, :] = figures
-    for o in range(slices):
-        rows = jnp.concatenate([x[o * capacity : (o + 1) * capacity, :] for x in sorted_slices], axis=0)
-        send_ref[o, :, :half] = vecs_ref[...]
-        send_ref[o, :, half:] = rows.T.astype(bf16)
-
-
-def weight_kernel(place_ref, recv_ref, other_ref, vals_ref, gene_ref, turned_ref, weighted_ref, low_ref, power_ref):
-    rows, samples, _ = recv_ref.shape
-    half = other_ref.shape[2]
-    row = place_ref[0]
-    for m in range(rows):
-        r = row ^ m
-        cols = pl.ds(m * samples, samples)
-        turned_ref[:half, cols] = recv_ref[r, :, :half].astype(f32).T.astype(bf16)
-        turned_ref[half:, cols] = other_ref[r].astype(f32).T.astype(bf16)
-    data = jnp.concatenate([recv_ref[r, :, half:] for r in range(rows)], axis=0)
-    data = data.astype(f32).T.astype(bf16)
+    far_ref[:, :half] = vecs_ref[...]
+    for m in range(slices):
+        block = jnp.concatenate([x[m * capacity : (m + 1) * capacity, :] for x in sorted_slices], axis=0)
+        block = block.T.astype(bf16)
+        side = slice(half + m % 2 * LANES, half + (m % 2 + 1) * LANES)
+        if m >= 4:
+            far_ref[(m - 4) // 2 * part : ((m - 4) // 2 + 1) * part, side] = block
+        elif m >= 2:
+            e2_ref[:, m % 2 * LANES : (m % 2 + 1) * LANES] = block
+        elif m == 1:
+            e1_ref[...] = block
+        else:
+            e0_ref[...] = block
+
+
+def weight_kernel(place_ref, kept_ref, near_ref, kept2_ref, near2_ref, vals_ref, gene_ref, turned_ref, weighted_ref, low_ref, power_ref, data_scr):
+    samples = kept_ref.shape[0]
+    half = vals_ref.shape[1] // 2
+    part = samples // 2
+    core = place_ref[1]
+    sources = ((kept_ref, kept2_ref), (near_ref, near2_ref))
+    for n, pair in enumerate(sources):
+        for c, ref in enumerate(pair):
+            side = core if c == 0 else 1 - core
+            for i in range(4):
+                first = (n * 4 + i) * samples
+                turned_ref[c * half : (c + 1) * half, first : first + samples] = (
+                    ref[:, i * half : (i + 1) * half].astype(f32).T.astype(bf16)
+                )
+                at = 4 * half + i % 2 * LANES
+                data_scr[pl.ds(pl.multiple_of(first + side * part, part), part), :] = ref[
+                    i // 2 * part : (i // 2 + 1) * part, at : at + LANES
+                ]
+    data = data_scr[...].astype(f32).T.astype(bf16)
     delta = gene_ref[:, 0:1]
     total = jnp.zeros((data.shape[0], 1), f32)
     for c in range(2):
-        if c == 0:
-            vecs = jnp.concatenate([recv_ref[r, :, :half] for r in range(rows)], axis=0)
-        else:
-            vecs = jnp.concatenate([other_ref[r] for r in range(rows)], axis=0)
-        cols = pl.ds(c * half, half)
+        vecs = jnp.concatenate(
+            [pair[c][:, i * half : (i + 1) * half] for pair in sources for i in range(4)], axis=0
+        )
+        cols = slice(c * half, (c + 1) * half)
         rotated = jnp.dot(data, vecs, preferred_element_type=f32).astype(bf16).astype(f32)
         weight = 1.0 / (vals_ref[:, cols] + delta)
         total += jnp.sum(weight * rotated * rotated, axis=1, keepdims=True)
@@ -221,6 +240,7 @@
     row = lax.axis_index("row")
     core = lax.axis_index("col")
     panel, half = eigvecs.shape
+    part = panel // 2
     samples = panel * rows
     variants = dosage.shape[1] // 2
     place = jnp.stack([row, core]).astype(jnp.int32)
@@ -231,16 +251,20 @@
     def other_core(x):
         return lax.ppermute(x, "col", [(0, 1), (1, 0)])
 
-    chunks = [None] * rows
-    chunks[0] = lax.dynamic_slice_in_dim(dosage, core * variants, variants, 1)
-    for m in range(2, rows, 2):
-        chunks[m] = swap(chunks[0], m)
-    for m in range(0, rows, 2):
-        chunks[m + 1] = swap(chunks[m], 1)
+    dose = {0: lax.dynamic_slice_in_dim(dosage, core * variants, variants, 1)}
+    dose[4] = swap(dose[0], 4)
+    dose[1] = swap(dose[0], 1)
+    dose[2] = swap(dose[0], 2)
     vals = jnp.concatenate([eigvals, other_core(eigvals)])[None, :]
-    send, gene = call(
+    far, e2, e1, e0, gene = call(
         route_kernel,
-        [((rows, panel, half + LANES), bf16), ((LANES, LANES), f32)],
+        [
+            ((panel, half + 2 * LANES), bf16),
+            ((part, 2 * LANES), bf16),
+            ((part, LANES), bf16),
+            ((part, LANES), bf16),
+            ((LANES, LANES), f32),
+        ],
         count=7,
     )(
         place,
@@ -251,19 +275,34 @@
         eigvecs,
         expression,
     )
-    received = lax.all_to_all(send, "row", split_axis=0, concat_axis=0, tiled=True)
-    other = other_core(received[:, :, :half])
+    r4 = swap(far, 4)
+    mid = jnp.concatenate([e2, r4[part:, half:]], axis=0)
+    r2 = swap(jnp.concatenate([eigvecs, r4[:, :half], mid], axis=1), 2)
+    vecs = [eigvecs, r4[:, :half], r2[:, :half], r2[:, half : 2 * half]]
+
+    def joined(mine, at):
+        upper = jnp.concatenate([mine, r4[:part, half + at : half + at + LANES]], axis=1)
+        right = r2[:, 2 * half + at : 2 * half + at + LANES]
+        lower = jnp.concatenate([right[:part], right[part:]], axis=1)
+        return jnp.concatenate(vecs + [jnp.concatenate([upper, lower], axis=0)], axis=1)
+
+    near = swap(joined(e1, LANES), 1)
+    kept = joined(e0, 0)
+    dose[6] = swap(dose[4], 2)
+    for m in (4, 2, 6):
+        dose[m + 1] = swap(dose[m], 1)
     turned, weighted, low, power = call(
         weight_kernel,
         [((2 * half, samples), bf16), ((LANES, 2 * half), bf16), ((LANES, 2 * half), bf16), ((LANES, LANES), f32)],
-        count=5,
-    )(place, received, other, vals, gene)
+        scratch=[pltpu.VMEM((samples, LANES), bf16)],
+        count=7,
+    )(place, kept, near, other_core(kept), other_core(near), vals, gene)
     keep, passed = call(
         score_kernel,
         [((LANES, LANES), f32)] * 2,
         scratch=[pltpu.VMEM((samples, variants), bf16)],
         count=6 + rows,
-    )(place, gene, power, turned, weighted, low, *chunks)
+    )(place, gene, power, turned, weighted, low, *[dose[m] for m in (0, 4, 2, 6, 1, 5, 3, 7)])
     return keep + other_core(passed)
 
 
@@ -275,8 +314,7 @@
         lax.axis_size("col") == 2
         and own == LANES
         and W == 2 * LANES
-        and rows & (rows - 1) == 0
-        and own // rows % 16 == 0
+        and rows == 8
         and dosage.shape[1] % (2 * LANES) == 0
         and samples * (samples + dosage.shape[1]) <= VMEM_LIMIT // 16
     )

time: 44.8 us -> 42 us (0.938)
  waiting for transfers between devices: 20.1 us -> 18.6 us
  starting transfers between devices: 16.2 us -> 15 us
  Pallas kernels: 5 us -> 4.22 us
  local copies, waits for them, and re-layouts: 2.4 us -> 3.14 us
    all_to_all x1 -> x0, waiting for transfers between devices: 11.7 us -> none  [near_body(): lax.all_to_all(send, 'row', split_axis=0, concat_axis=0, tiled=True)]
    ppermute x7 -> x10, waiting for transfers between devices: 6.01 us -> 16.4 us  [swap(): return lax.ppermute(x, 'row', [(i, i ^ m) for i in range(rows)])]
    all_to_all x1 -> x0, starting transfers between devices: 7.29 us -> none  [near_body(): lax.all_to_all(send, 'row', split_axis=0, concat_axis=0, tiled=True)]
    ppermute x7 -> x10, starting transfers between devices: 8.72 us -> 14.4 us  [swap(): return lax.ppermute(x, 'row', [(i, i ^ m) for i in range(rows)])]
    pallas_call x1, Pallas kernels: 1.77 us -> 1 us  [near_body(): call(route_kernel, [((panel, half + 2 * LANES), bf16), ((part, 2 * LANES)...]
    unnamed x16 -> x18, local copies, waits for them, and re-layouts: 2.36 us -> 3.12 us
    ppermute x3 -> x4, waiting for transfers between devices: 2.38 us -> 2.13 us  [other_core(): return lax.ppermute(x, 'col', [(0, 1), (1, 0)])]
  transfers between devices with their start and end apart: 11 -> 14, of which waited for: 6 -> 9; matrix products, arithmetic and copies ran while one was open for 0% -> 0% of each run, Pallas kernels for 3% -> 3%
where the time goes in v2:
time: 42 us; the launch traced here: 41.8 us
  waiting for transfers between devices  18.6 us (44%)
  starting transfers between devices  15 us (36%)
  Pallas kernels  4.22 us (10%)
  local copies, waits for them, and re-layouts  3.14 us (7%)
  other arithmetic  0.76 us (2%)
    ppermute x10, waiting for transfers between devices, swap(): return lax.ppermute(x, 'row', [(i, i ^ m) for i in range(rows)])  16.4 us
    ppermute x10, starting transfers between devices, swap(): return lax.ppermute(x, 'row', [(i, i ^ m) for i in range(rows)])  14.4 us
    unnamed x18, local copies, waits for them, and re-layouts  3.12 us
    ppermute x4, waiting for transfers between devices, other_core(): return lax.ppermute(x, 'col', [(0, 1), (1, 0)])  2.13 us
    pallas_call x1, Pallas kernels, near_body(): call(score_kernel, [((LANES, LANES), f32)] * 2, scratch=[pltpu.VMEM((samp...  1.83 us
    pallas_call x1, Pallas kernels, near_body(): call(weight_kernel, [((2 * half, samples), bf16), ((LANES, 2 * half), bf1...  1.39 us
    pallas_call x1, Pallas kernels, near_body(): call(route_kernel, [((panel, half + 2 * LANES), bf16), ((part, 2 * LANES)...  1 us
  transfers between devices with their start and end apart: 14, of which 9 were waited for; matrix products, arithmetic and copies ran while one was open for 0% of the time, Pallas kernels for 3%

profile of v2, /device:TPU:0, one launch (start us, length us, event | category | flops | bytes accessed | tf_op | source)
XLA Modules:
  0.0 41.8 jit_solution(11538903760609297061)
XLA Ops:
  0.1 0.6 %copy-done.7 = s32[1024]{0:T(1024)S(1)} copy-done((s32[1024]{0:T(1024)S(1)}, s32[1024]{0:T(1024)}, u32[]{:S(2)}) %copy-start.7) | copy-done | bytes 4120
  0.8 0.8 %copy-done.1 = bf16[64,256]{1,0:T(8,128)(2,1)S(1)} copy-done((bf16[64,256]{1,0:T(8,128)(2,1)S(1)}, bf16[64,256]{1,0:T(8,128)(2,1)}, u32[]{:S(2)}) %copy-start.1) | copy-done | bytes 32792
  1.5 0.9 %copy-done.3 = bf16[64,1024]{1,0:T(8,128)(2,1)S(1)} copy-done((bf16[64,1024]{1,0:T(8,128)(2,1)S(1)}, bf16[64,1024]{1,0:T(8,128)(2,1)}, u32[]{:S(2)}) %copy-start.3) | copy-done | bytes 131096
  2.4 1.0 %shard_map.82 = (bf16[64,512]{1,0:T(8,128)(2,1)S(1)}, bf16[32,256]{1,0:T(8,128)(2,1)S(1)}, bf16[32,128]{1,0:T(8,128)(2,1)S(1)}, bf16[32,128]{1,0:T(8,128)(2,1)S(1)}, f32[128,128]{1,0:T(8,128)S(1)}) custom-call(s32[2]{0:T(128)S(1)} %pad_add_fusion.place_ref, s32[8,128]{1,0:T(8,128)S(1)} %bitcast.8, f32[8,128]{1,0:T(8,128)S(1)} %bitcast.9, ...), custom_call_target="tpu_custom_call" | custom-call | tf_op jit(solution)/shard_map/pallas_call | solution.py:259
  3.5 4.1 %collective-permute-start = (bf16[64,512]{1,0:T(8,128)(2,1)S(1)}, bf16[64,512]{1,0:T(8,128)(2,1)S(1)}, u32[]{:S(2)}, u32[]{:S(2)}) collective-permute-start(bf16[64,512]{1,0:T(8,128)(2,1)S(1)} %get-tuple-element.17), channel_id=1, source_target_pairs={{0,8},{2,10},{4,12},{6,14},{8,0},{10,2},{12,4},{14,6},{1,9},{3,11}... | collective-permute-start | bytes 196616 | tf_op jit(solution)/shard_map/ppermute | solution.py:249
  7.6 3.6 %collective-permute-done = bf16[64,512]{1,0:T(8,128)(2,1)S(1)} collective-permute-done((bf16[64,512]{1,0:T(8,128)(2,1)S(1)}, bf16[64,512]{1,0:T(8,128)(2,1)S(1)}, u32[]{:S(2)}, u32[]{:S(2)}) %collective-permute-start) | collective-permute-done | bytes 65568 | tf_op jit(solution)/shard_map/ppermute | solution.py:249
  11.2 0.8 %copy-done.2 = bf16[64,256]{1,0:T(8,128)(2,1)S(1)} copy-done((bf16[64,256]{1,0:T(8,128)(2,1)S(1)}, bf16[64,256]{1,0:T(8,128)(2,1)}, u32[]{:S(2)}) %copy-start.2) | copy-done | bytes 32792
  12.6 4.0 %collective-permute-done.1 = bf16[64,768]{1,0:T(8,128)(2,1)S(1)} collective-permute-done((bf16[64,768]{1,0:T(8,128)(2,1)S(1)}, bf16[64,768]{1,0:T(8,128)(2,1)S(1)}, u32[]{:S(2)}, u32[]{:S(2)}) %collective-permute-start.1) | collective-permute-done | bytes 98336 | tf_op jit(solution)/shard_map/ppermute | solution.py:249
  16.7 1.8 %collective-permute-start.2 = (bf16[64,1280]{1,0:T(8,128)(2,1)S(1)}, bf16[64,1280]{1,0:T(8,128)(2,1)S(1)}, u32[]{:S(2)}, u32[]{:S(2)}) collective-permute-start(bf16[64,1280]{1,0:T(8,128)(2,1)S(1)} %get-tuple-element.27), channel_id=1, source_target_pairs={{0,2},{2,0},{4,6},{6,4},{8,10},{10,8},{12,14},{14,12},{1,3},{3,1},... | collective-permute-start | bytes 491528 | tf_op jit(solution)/shard_map/ppermute | solution.py:249
  18.5 1.8 %collective-permute-start.6 = (bf16[64,768]{1,0:T(8,128)(2,1)S(1)}, bf16[64,768]{1,0:T(8,128)(2,1)S(1)}, u32[]{:S(2)}, u32[]{:S(2)}) collective-permute-start(bf16[64,768]{1,0:T(8,128)(2,1)S(1)} %constant_dynamic-slice_fusion.refs_0_), channel_id=1, source_target_pairs={{0,8},{2,10},{4,12},{6,14},{8,0},{10,2},{12,4},{14,6},{1,9},{3,11}... | collective-permute-start | bytes 294920 | tf_op jit(solution)/shard_map/ppermute | solution.py:249
  20.3 2.0 %collective-permute-start.7 = (bf16[64,768]{1,0:T(8,128)(2,1)S(1)}, bf16[64,768]{1,0:T(8,128)(2,1)S(1)}, u32[]{:S(2)}, u32[]{:S(2)}) collective-permute-start(bf16[64,768]{1,0:T(8,128)(2,1)S(1)} %constant_dynamic-slice_fusion.refs_0_), channel_id=1, source_target_pairs={{0,4},{2,6},{4,0},{6,2},{8,12},{10,14},{12,8},{14,10},{1,5},{3,7},... | collective-permute-start | bytes 294920 | tf_op jit(solution)/shard_map/ppermute | solution.py:249
  22.3 2.9 %collective-permute-done.6.refs_1_ = bf16[64,768]{1,0:T(8,128)(2,1)S(1)} collective-permute-done((bf16[64,768]{1,0:T(8,128)(2,1)S(1)}, bf16[64,768]{1,0:T(8,128)(2,1)S(1)}, u32[]{:S(2)}, u32[]{:S(2)}) %collective-permute-start.6) | collective-permute-done | bytes 98336 | tf_op jit(solution)/shard_map/ppermute | solution.py:249
  25.8 0.9 %collective-permute-done.5 = f32[256]{0:T(256)S(1)} collective-permute-done((f32[256]{0:T(256)S(1)}, f32[256]{0:T(256)S(1)}, u32[]{:S(2)}, u32[]{:S(2)}) %collective-permute-start.5) | collective-permute-done | bytes 1056 | tf_op jit(solution)/shard_map/ppermute | solution.py:252
  26.7 0.7 %collective-permute-start.9 = (bf16[64,768]{1,0:T(8,128)(2,1)S(1)}, bf16[64,768]{1,0:T(8,128)(2,1)S(1)}, u32[]{:S(2)}, u32[]{:S(2)}) collective-permute-start(bf16[64,768]{1,0:T(8,128)(2,1)S(1)} %constant_dynamic-slice_fusion.refs_0_), channel_id=1, source_target_pairs={{0,2},{2,0},{4,6},{6,4},{8,10},{10,8},{12,14},{14,12},{1,3},{3,1},... | collective-permute-start | bytes 294920 | tf_op jit(solution)/shard_map/ppermute | solution.py:249
  27.4 1.3 %collective-permute-start.10 = (bf16[64,768]{1,0:T(8,128)(2,1)S(1)}, bf16[64,768]{1,0:T(8,128)(2,1)S(1)}, u32[]{:S(2)}, u32[]{:S(2)}) collective-permute-start(bf16[64,768]{1,0:T(8,128)(2,1)S(1)} %collective-permute-done.6.refs_1_), channel_id=1, source_target_pairs={{0,2},{2,0},{4,6},{6,4},{8,10},{10,8},{12,14},{14,12},{1,3},{3,1},... | collective-permute-start | bytes 294920 | tf_op jit(solution)/shard_map/ppermute | solution.py:249
  28.7 1.2 %collective-permute-done.8.refs_3_ = bf16[64,768]{1,0:T(8,128)(2,1)S(1)} collective-permute-done((bf16[64,768]{1,0:T(8,128)(2,1)S(1)}, bf16[64,768]{1,0:T(8,128)(2,1)S(1)}, u32[]{:S(2)}, u32[]{:S(2)}) %collective-permute-start.8) | collective-permute-done | bytes 98336 | tf_op jit(solution)/shard_map/ppermute | solution.py:249
  30.1 1.8 %collective-permute-start.12 = (bf16[64,768]{1,0:T(8,128)(2,1)S(1)}, bf16[64,768]{1,0:T(8,128)(2,1)S(1)}, u32[]{:S(2)}, u32[]{:S(2)}) collective-permute-start(bf16[64,768]{1,0:T(8,128)(2,1)S(1)} %collective-permute-done.8.refs_3_), channel_id=1, source_target_pairs={{0,2},{2,0},{4,6},{6,4},{8,10},{10,8},{12,14},{14,12},{1,3},{3,1},... | collective-permute-start | bytes 294920 | tf_op jit(solution)/shard_map/ppermute | solution.py:249
  31.9 1.4 %shard_map.83 = (bf16[512,512]{1,0:T(8,128)(2,1)S(1)}, bf16[128,512]{1,0:T(8,128)(2,1)S(1)}, bf16[128,512]{1,0:T(8,128)(2,1)S(1)}, f32[128,128]{1,0:T(8,128)S(1)}) custom-call(s32[2]{0:T(128)S(1)} %pad_add_fusion.place_ref, bf16[64,1280]{1,0:T(8,128)(2,1)S(1)} %get-tuple-element.28.kept_ref, bf16[64,1280]{1,0:T(8,128)(2,1)S(1)} %collective-permute-done.2.near_ref, ...), custom_call_target="tpu_custom_call" | custom-call | tf_op jit(solution)/shard_map/pallas_call | solution.py:294
  33.3 1.1 %collective-permute-done.10.refs_5_ = bf16[64,768]{1,0:T(8,128)(2,1)S(1)} collective-permute-done((bf16[64,768]{1,0:T(8,128)(2,1)S(1)}, bf16[64,768]{1,0:T(8,128)(2,1)S(1)}, u32[]{:S(2)}, u32[]{:S(2)}) %collective-permute-start.10) | collective-permute-done | bytes 98336 | tf_op jit(solution)/shard_map/ppermute | solution.py:249
  34.4 2.1 %collective-permute-done.11.refs_6_ = bf16[64,768]{1,0:T(8,128)(2,1)S(1)} collective-permute-done((bf16[64,768]{1,0:T(8,128)(2,1)S(1)}, bf16[64,768]{1,0:T(8,128)(2,1)S(1)}, u32[]{:S(2)}, u32[]{:S(2)}) %collective-permute-start.11) | collective-permute-done | bytes 98336 | tf_op jit(solution)/shard_map/ppermute | solution.py:249
  36.5 1.4 %collective-permute-done.12.refs_7_ = bf16[64,768]{1,0:T(8,128)(2,1)S(1)} collective-permute-done((bf16[64,768]{1,0:T(8,128)(2,1)S(1)}, bf16[64,768]{1,0:T(8,128)(2,1)S(1)}, u32[]{:S(2)}, u32[]{:S(2)}) %collective-permute-start.12) | collective-permute-done | bytes 98336 | tf_op jit(solution)/shard_map/ppermute | solution.py:249
  38.0 1.8 %shard_map.84 = (f32[128,128]{1,0:T(8,128)S(1)}, f32[128,128]{1,0:T(8,128)S(1)}) custom-call(s32[2]{0:T(128)S(1)} %pad_add_fusion.place_ref, f32[128,128]{1,0:T(8,128)S(1)} %get-tuple-element.16.gene_ref, f32[128,128]{1,0:T(8,128)S(1)} %get-tuple-element.21.power_ref, bf16[512,512]{1,0:T(8,128)(2,1)S(1)} %get-tuple-element.22.turned_ref, ...), custom_call_target="tpu_custom_call" | custom-call | tf_op jit(solution)/shard_map/pallas_call | solution.py:300
  39.9 1.2 %collective-permute-done.13 = f32[128,128]{1,0:T(8,128)S(1)} collective-permute-done((f32[128,128]{1,0:T(8,128)S(1)}, f32[128,128]{1,0:T(8,128)S(1)}, u32[]{:S(2)}, u32[]{:S(2)}) %collective-permute-start.13) | collective-permute-done | bytes 65568 | tf_op jit(solution)/shard_map/ppermute | solution.py:252
  41.1 0.6 %add.7 = f32[128,128]{1,0:T(8,128)} add(f32[128,128]{1,0:T(8,128)S(1)} %get-tuple-element.25, f32[128,128]{1,0:T(8,128)S(1)} %collective-permute-done.13) | non-fusion elementwise | flops 16384 | bytes 196608 | tf_op jit(solution)/shard_map/add | solution.py:306
  (36 shorter events, 1.6 us)
Async XLA Ops:
  0.0 18.5 %copy-start = (bf16[64,1536]{1,0:T(8,128)(2,1)S(1)}, bf16[64,1536]{1,0:T(8,128)(2,1)}, u32[]{:S(2)}) copy-start(bf16[64,1536]{1,0:T(8,128)(2,1)} %param.11) | copy-start | bytes 589828
  0.0 0.7 %copy-start.7 = (s32[1024]{0:T(1024)S(1)}, s32[1024]{0:T(1024)}, u32[]{:S(2)}) copy-start(s32[1024]{0:T(1024)} %param.14) | copy-start | bytes 12292
  0.0 0.7 %copy-start.6 = (s32[1024]{0:T(1024)S(1)}, s32[1024]{0:T(1024)}, u32[]{:S(2)}) copy-start(s32[1024]{0:T(1024)} %param.13) | copy-start | bytes 12292
  0.0 0.8 %copy-start.5 = (f32[1024]{0:T(1024)S(1)}, f32[1024]{0:T(1024)}, u32[]{:S(2)}) copy-start(f32[1024]{0:T(1024)} %param.12) | copy-start | bytes 12292
  0.1 0.7 %copy-start.4 = (s32[1024]{0:T(1024)S(1)}, s32[1024]{0:T(1024)}, u32[]{:S(2)}) copy-start(s32[1024]{0:T(1024)} %param.15) | copy-start | bytes 12292
  0.8 0.8 %copy-start.1 = (bf16[64,256]{1,0:T(8,128)(2,1)S(1)}, bf16[64,256]{1,0:T(8,128)(2,1)}, u32[]{:S(2)}) copy-start(bf16[64,256]{1,0:T(8,128)(2,1)} %vecs_ref.1) | copy-start | bytes 98308
  1.5 0.9 %copy-start.3 = (bf16[64,1024]{1,0:T(8,128)(2,1)S(1)}, bf16[64,1024]{1,0:T(8,128)(2,1)}, u32[]{:S(2)}) copy-start(bf16[64,1024]{1,0:T(8,128)(2,1)} %expr_ref.1) | copy-start | bytes 393220
  3.5 7.8 %collective-permute-start = (bf16[64,512]{1,0:T(8,128)(2,1)S(1)}, bf16[64,512]{1,0:T(8,128)(2,1)S(1)}, u32[]{:S(2)}, u32[]{:S(2)}) collective-permute-start(bf16[64,512]{1,0:T(8,128)(2,1)S(1)} %get-tuple-element.17), channel_id=1, source_target_pairs={{0,8},{2,10},{4,12},{6,14},{8,0},{10,2},{12,4},{14,6},{1,9},{3,11}... | collective-permute-start | bytes 196616 | tf_op jit(solution)/shard_map/ppermute | solution.py:249
  11.2 0.8 %copy-start.2 = (bf16[64,256]{1,0:T(8,128)(2,1)S(1)}, bf16[64,256]{1,0:T(8,128)(2,1)}, u32[]{:S(2)}) copy-start(bf16[64,256]{1,0:T(8,128)(2,1)} %vecs_ref.1) | copy-start | bytes 98308
  12.0 4.7 %collective-permute-start.1 = (bf16[64,768]{1,0:T(8,128)(2,1)S(1)}, bf16[64,768]{1,0:T(8,128)(2,1)S(1)}, u32[]{:S(2)}, u32[]{:S(2)}) collective-permute-start(bf16[64,768]{1,0:T(8,128)(2,1)S(1)} %maximum_maximum_fusion.2), channel_id=1, source_target_pairs={{0,4},{2,6},{4,0},{6,2},{8,12},{10,14},{12,8},{14,10},{1,5},{3,7},... | collective-permute-start | bytes 294920 | tf_op jit(solution)/shard_map/ppermute | solution.py:249
  16.7 8.6 %collective-permute-start.2 = (bf16[64,1280]{1,0:T(8,128)(2,1)S(1)}, bf16[64,1280]{1,0:T(8,128)(2,1)S(1)}, u32[]{:S(2)}, u32[]{:S(2)}) collective-permute-start(bf16[64,1280]{1,0:T(8,128)(2,1)S(1)} %get-tuple-element.27), channel_id=1, source_target_pairs={{0,2},{2,0},{4,6},{6,4},{8,10},{10,8},{12,14},{14,12},{1,3},{3,1},... | collective-permute-start | bytes 491528 | tf_op jit(solution)/shard_map/ppermute | solution.py:249
  18.5 6.8 %copy-start.8 = (f32[256]{0:T(256)S(1)}, f32[256]{0:T(256)}, u32[]{:S(2)}) copy-start(f32[256]{0:T(256)} %param.9) | copy-start | bytes 3076
  18.5 6.7 %collective-permute-start.6 = (bf16[64,768]{1,0:T(8,128)(2,1)S(1)}, bf16[64,768]{1,0:T(8,128)(2,1)S(1)}, u32[]{:S(2)}, u32[]{:S(2)}) collective-permute-start(bf16[64,768]{1,0:T(8,128)(2,1)S(1)} %constant_dynamic-slice_fusion.refs_0_), channel_id=1, source_target_pairs={{0,8},{2,10},{4,12},{6,14},{8,0},{10,2},{12,4},{14,6},{1,9},{3,11}... | collective-permute-start | bytes 294920 | tf_op jit(solution)/shard_map/ppermute | solution.py:249
  20.3 9.7 %collective-permute-start.3 = (bf16[64,1280]{1,0:T(8,128)(2,1)S(1)}, bf16[64,1280]{1,0:T(8,128)(2,1)S(1)}, u32[]{:S(2)}, u32[]{:S(2)}) collective-permute-start(bf16[64,1280]{1,0:T(8,128)(2,1)S(1)} %get-tuple-element.28.kept_ref), channel_id=1, source_target_pairs={{0,1},{1,0},{2,3},{3,2},{4,5},{5,4},{6,7},{7,6},{8,9},{9,8},{10,11... | collective-permute-start | bytes 491528 | tf_op jit(solution)/shard_map/ppermute | solution.py:252
  20.3 7.1 %collective-permute-start.7 = (bf16[64,768]{1,0:T(8,128)(2,1)S(1)}, bf16[64,768]{1,0:T(8,128)(2,1)S(1)}, u32[]{:S(2)}, u32[]{:S(2)}) collective-permute-start(bf16[64,768]{1,0:T(8,128)(2,1)S(1)} %constant_dynamic-slice_fusion.refs_0_), channel_id=1, source_target_pairs={{0,4},{2,6},{4,0},{6,2},{8,12},{10,14},{12,8},{14,10},{1,5},{3,7},... | collective-permute-start | bytes 294920 | tf_op jit(solution)/shard_map/ppermute | solution.py:249
  25.3 4.6 %collective-permute-start.8 = (bf16[64,768]{1,0:T(8,128)(2,1)S(1)}, bf16[64,768]{1,0:T(8,128)(2,1)S(1)}, u32[]{:S(2)}, u32[]{:S(2)}) collective-permute-start(bf16[64,768]{1,0:T(8,128)(2,1)S(1)} %collective-permute-done.6.refs_1_), channel_id=1, source_target_pairs={{0,4},{2,6},{4,0},{6,2},{8,12},{10,14},{12,8},{14,10},{1,5},{3,7},... | collective-permute-start | bytes 294920 | tf_op jit(solution)/shard_map/ppermute | solution.py:249
  25.3 6.6 %collective-permute-start.4 = (bf16[64,1280]{1,0:T(8,128)(2,1)S(1)}, bf16[64,1280]{1,0:T(8,128)(2,1)S(1)}, u32[]{:S(2)}, u32[]{:S(2)}) collective-permute-start(bf16[64,1280]{1,0:T(8,128)(2,1)S(1)} %collective-permute-done.2.near_ref), channel_id=1, source_target_pairs={{0,1},{1,0},{2,3},{3,2},{4,5},{5,4},{6,7},{7,6},{8,9},{9,8},{10,11... | collective-permute-start | bytes 491528 | tf_op jit(solution)/shard_map/ppermute | solution.py:252
  25.3 1.4 %collective-permute-start.5 = (f32[256]{0:T(256)S(1)}, f32[256]{0:T(256)S(1)}, u32[]{:S(2)}, u32[]{:S(2)}) collective-permute-start(f32[256]{0:T(256)S(1)} %copy-done.8), channel_id=1, source_target_pairs={{0,1},{1,0},{2,3},{3,2},{4,5},{5,4},{6,7},{7,6},{8,9},{9,8},{10,11... | collective-permute-start | bytes 3080 | tf_op jit(solution)/shard_map/ppermute | solution.py:252
  26.7 6.6 %collective-permute-start.9 = (bf16[64,768]{1,0:T(8,128)(2,1)S(1)}, bf16[64,768]{1,0:T(8,128)(2,1)S(1)}, u32[]{:S(2)}, u32[]{:S(2)}) collective-permute-start(bf16[64,768]{1,0:T(8,128)(2,1)S(1)} %constant_dynamic-slice_fusion.refs_0_), channel_id=1, source_target_pairs={{0,2},{2,0},{4,6},{6,4},{8,10},{10,8},{12,14},{14,12},{1,3},{3,1},... | collective-permute-start | bytes 294920 | tf_op jit(solution)/shard_map/ppermute | solution.py:249
  27.4 7.0 %collective-permute-start.10 = (bf16[64,768]{1,0:T(8,128)(2,1)S(1)}, bf16[64,768]{1,0:T(8,128)(2,1)S(1)}, u32[]{:S(2)}, u32[]{:S(2)}) collective-permute-start(bf16[64,768]{1,0:T(8,128)(2,1)S(1)} %collective-permute-done.6.refs_1_), channel_id=1, source_target_pairs={{0,2},{2,0},{4,6},{6,4},{8,10},{10,8},{12,14},{14,12},{1,3},{3,1},... | collective-permute-start | bytes 294920 | tf_op jit(solution)/shard_map/ppermute | solution.py:249
  29.9 6.6 %collective-permute-start.11 = (bf16[64,768]{1,0:T(8,128)(2,1)S(1)}, bf16[64,768]{1,0:T(8,128)(2,1)S(1)}, u32[]{:S(2)}, u32[]{:S(2)}) collective-permute-start(bf16[64,768]{1,0:T(8,128)(2,1)S(1)} %collective-permute-done.7.refs_2_), channel_id=1, source_target_pairs={{0,2},{2,0},{4,6},{6,4},{8,10},{10,8},{12,14},{14,12},{1,3},{3,1},... | collective-permute-start | bytes 294920 | tf_op jit(solution)/shard_map/ppermute | solution.py:249
  30.1 7.9 %collective-permute-start.12 = (bf16[64,768]{1,0:T(8,128)(2,1)S(1)}, bf16[64,768]{1,0:T(8,128)(2,1)S(1)}, u32[]{:S(2)}, u32[]{:S(2)}) collective-permute-start(bf16[64,768]{1,0:T(8,128)(2,1)S(1)} %collective-permute-done.8.refs_3_), channel_id=1, source_target_pairs={{0,2},{2,0},{4,6},{6,4},{8,10},{10,8},{12,14},{14,12},{1,3},{3,1},... | collective-permute-start | bytes 294920 | tf_op jit(solution)/shard_map/ppermute | solution.py:249
  39.8 1.3 %collective-permute-start.13 = (f32[128,128]{1,0:T(8,128)S(1)}, f32[128,128]{1,0:T(8,128)S(1)}, u32[]{:S(2)}, u32[]{:S(2)}) collective-permute-start(f32[128,128]{1,0:T(8,128)S(1)} %get-tuple-element.26), channel_id=1, source_target_pairs={{0,1},{1,0},{2,3},{3,2},{4,5},{5,4},{6,7},{7,6},{8,9},{9,8},{10,11... | collective-permute-start | bytes 196616 | tf_op jit(solution)/shard_map/ppermute | solution.py:252

commit v3 on v2

--- a/solution.py
+++ b/solution.py
@@ -100,32 +100,48 @@
     return lax.dynamic_slice_in_dim(zscore, lax.axis_index("col") * width_part, width_part, 1)
 
 
-def route_kernel(place_ref, owner_ref, delta_ref, start_ref, valid_ref, vecs_ref, expr_ref, far_ref, e2_ref, e1_ref, e0_ref, gene_ref):
+def route_kernel(
+    place_ref, owner_any, delta_any, start_any, valid_any, expr_any,
+    e4_ref, e2_ref, e1_ref, e0_ref, gene_ref,
+    owner_ref, delta_ref, start_ref, valid_ref, expr_ref, sems,
+):
+    row, core = place_ref[0], place_ref[1]
+    part = expr_ref.shape[0]
+    rows = pl.ds(pl.multiple_of(core * part, part), part)
+    pairs = (
+        (owner_any, owner_ref),
+        (expr_any.at[rows], expr_ref),
+        (delta_any, delta_ref),
+        (start_any, start_ref),
+        (valid_any, valid_ref),
+    )
+    copies = [pltpu.make_async_copy(a, b, sems.at[i]) for i, (a, b) in enumerate(pairs)]
+    for copy in copies:
+        copy.start()
     slices = owner_ref.shape[0]
     capacity = LANES // slices
-    half = vecs_ref.shape[1]
-    part = expr_ref.shape[0] // 2
-    row, core = place_ref[0], place_ref[1]
-    owner = owner_ref[...]
     before = lax.broadcasted_iota(jnp.int32, (LANES, LANES), 0) < lax.broadcasted_iota(
         jnp.int32, (LANES, LANES), 1
     )
     before = before.astype(bf16)
+    slot = lax.broadcasted_iota(jnp.int32, (LANES, LANES), 0)
+    own_slot = lax.broadcasted_iota(jnp.int32, (capacity, LANES), 0)
+    lane = lax.broadcasted_iota(jnp.int32, (capacity, LANES), 1)
+    copies[0].wait()
+    owner = owner_ref[...]
     rank = jnp.zeros(owner.shape, f32)
     for o in range(slices):
         same = (owner == o).astype(f32)
         rank += same * jnp.dot(same.astype(bf16), before, preferred_element_type=f32)
     bucket = (owner ^ row) * capacity + rank.astype(jnp.int32)
-    slot = lax.broadcasted_iota(jnp.int32, (LANES, LANES), 0)
-    own_slot = lax.broadcasted_iota(jnp.int32, (capacity, LANES), 0)
-    lane = lax.broadcasted_iota(jnp.int32, (capacity, LANES), 1)
-    rows = pl.ds(pl.multiple_of(core * part, part), part)
+    for copy in copies[1:]:
+        copy.wait()
     sorted_slices = []
     for s in range(slices):
         here = bucket[s : s + 1, :]
         pick = (slot == here).astype(bf16)
         sorted_slices.append(
-            lax.dot_general(pick, expr_ref[rows, s * LANES : (s + 1) * LANES], NT, preferred_element_type=f32)
+            lax.dot_general(pick, expr_ref[:, s * LANES : (s + 1) * LANES], NT, preferred_element_type=f32)
         )
         mine = (own_slot == here).astype(f32)
         figures = jnp.zeros((capacity, LANES), f32)
@@ -133,61 +149,78 @@
             line = ref[s : s + 1, :].astype(f32)
             figures = jnp.where(lane == i, jnp.sum(mine * line, axis=1, keepdims=True), figures)
         gene_ref[s * capacity : (s + 1) * capacity, :] = figures
-    far_ref[:, :half] = vecs_ref[...]
     for m in range(slices):
         block = jnp.concatenate([x[m * capacity : (m + 1) * capacity, :] for x in sorted_slices], axis=0)
         block = block.T.astype(bf16)
-        side = slice(half + m % 2 * LANES, half + (m % 2 + 1) * LANES)
+        side = slice(m % 2 * LANES, (m % 2 + 1) * LANES)
         if m >= 4:
-            far_ref[(m - 4) // 2 * part : ((m - 4) // 2 + 1) * part, side] = block
+            e4_ref[(m - 4) // 2 * part : ((m - 4) // 2 + 1) * part, side] = block
         elif m >= 2:
-            e2_ref[:, m % 2 * LANES : (m % 2 + 1) * LANES] = block
+            e2_ref[:, side] = block
         elif m == 1:
             e1_ref[...] = block
         else:
             e0_ref[...] = block
 
 
-def weight_kernel(place_ref, kept_ref, near_ref, kept2_ref, near2_ref, vals_ref, gene_ref, turned_ref, weighted_ref, low_ref, power_ref, data_scr):
+def turn(refs, out_ref):
+    samples = refs[0].shape[0]
+    half = refs[0].shape[1] // 4
+    for c, ref in enumerate(refs):
+        for i in range(4):
+            out_ref[c * half : (c + 1) * half, i * samples : (i + 1) * samples] = (
+                ref[:, i * half : (i + 1) * half].astype(f32).T.astype(bf16)
+            )
+
+
+def line_kernel(vecs_ref, vecs2_ref, *refs):
+    *dose_refs, part_ref, turned_scr, dose_scr = refs
+    turn((vecs_ref, vecs2_ref), turned_scr)
+    samples = dose_refs[0].shape[0]
+    for m, ref in enumerate(dose_refs):
+        dose_scr[m * samples : (m + 1) * samples, :] = ref[...]
+    part_ref[...] = jnp.dot(turned_scr[...], dose_scr[...], preferred_element_type=f32)
+
+
+def weight_kernel(
+    place_ref, kept_ref, kept2_ref, near_ref, near2_ref, expr_ref, expr2_ref, vals_ref, vals2_ref, gene_ref,
+    turned_ref, weighted_ref, low_ref, power_ref, data_scr,
+):
     samples = kept_ref.shape[0]
-    half = vals_ref.shape[1] // 2
+    half = vals_ref.shape[1]
     part = samples // 2
     core = place_ref[1]
-    sources = ((kept_ref, kept2_ref), (near_ref, near2_ref))
-    for n, pair in enumerate(sources):
-        for c, ref in enumerate(pair):
-            side = core if c == 0 else 1 - core
-            for i in range(4):
-                first = (n * 4 + i) * samples
-                turned_ref[c * half : (c + 1) * half, first : first + samples] = (
-                    ref[:, i * half : (i + 1) * half].astype(f32).T.astype(bf16)
-                )
-                at = 4 * half + i % 2 * LANES
-                data_scr[pl.ds(pl.multiple_of(first + side * part, part), part), :] = ref[
-                    i // 2 * part : (i // 2 + 1) * part, at : at + LANES
-                ]
+    turn((near_ref, near2_ref), turned_ref)
+    for ref, side in ((expr_ref, core), (expr2_ref, 1 - core)):
+        for i in range(8):
+            at = i // 4 * 2 * LANES + i % 2 * LANES
+            data_scr[pl.ds(pl.multiple_of(i * samples + side * part, part), part), :] = ref[
+                i // 2 % 2 * part : (i // 2 % 2 + 1) * part, at : at + LANES
+            ]
     data = data_scr[...].astype(f32).T.astype(bf16)
     delta = gene_ref[:, 0:1]
     total = jnp.zeros((data.shape[0], 1), f32)
-    for c in range(2):
+    sources = ((kept_ref, near_ref, vals_ref), (kept2_ref, near2_ref, vals2_ref))
+    for c, (first, second, vals) in enumerate(sources):
         vecs = jnp.concatenate(
-            [pair[c][:, i * half : (i + 1) * half] for pair in sources for i in range(4)], axis=0
+            [ref[:, i * half : (i + 1) * half] for ref in (first, second) for i in range(4)], axis=0
         )
         cols = slice(c * half, (c + 1) * half)
         rotated = jnp.dot(data, vecs, preferred_element_type=f32).astype(bf16).astype(f32)
-        weight = 1.0 / (vals_ref[:, cols] + delta)
+        weight = 1.0 / (vals[...] + delta)
         total += jnp.sum(weight * rotated * rotated, axis=1, keepdims=True)
         weighted_ref[:, cols] = (weight * rotated).astype(bf16)
         low_ref[:, cols] = weight.astype(bf16)
     power_ref[...] = jnp.broadcast_to(total, power_ref.shape)
 
 
-def score_kernel(place_ref, gene_ref, power_ref, turned_ref, weighted_ref, low_ref, *refs):
+def score_kernel(place_ref, gene_ref, power_ref, part_ref, turned_ref, weighted_ref, low_ref, *refs):
     *dose_refs, keep_ref, pass_ref, dose_scr = refs
     samples, variants = dose_refs[0].shape
     for m, ref in enumerate(dose_refs):
         dose_scr[m * samples : (m + 1) * samples, :] = ref[...]
-    rotated = jnp.dot(turned_ref[...], dose_scr[...], preferred_element_type=f32).astype(bf16)
+    rotated = part_ref[...] + jnp.dot(turned_ref[...], dose_scr[...], preferred_element_type=f32)
+    rotated = rotated.astype(bf16)
     squared = jnp.square(rotated.astype(f32)).astype(bf16)
     cross = jnp.dot(weighted_ref[...], rotated, preferred_element_type=f32)
     power = jnp.dot(low_ref[...], squared, preferred_element_type=f32)
@@ -197,7 +230,7 @@
     genes = cross.shape[0]
     lane = lax.broadcasted_iota(jnp.int32, (genes, LANES), 1)
     own_power = power_ref[...]
-    scale = jnp.sqrt(f32(samples * len(dose_refs)))
+    scale = jnp.sqrt(f32(part_ref.shape[0]))
     blocks = variants // LANES
     for out_ref, half in ((keep_ref, core), (pass_ref, 1 - core)):
         offset = start + half * LANES - core * variants
@@ -223,15 +256,17 @@
         out_ref[...] = jnp.where(live, score, 0.0)
 
 
-def call(kernel, outs, scratch=(), smem=1, count=0):
+def call(kernel, outs, count, scratch=(), smem=1, anywhere=0, flops=0):
     vmem = pl.BlockSpec(memory_space=pltpu.VMEM)
+    inputs = [pl.BlockSpec(memory_space=pltpu.SMEM)] * smem + [pl.BlockSpec(memory_space=pltpu.HBM)] * anywhere
     return pl.pallas_call(
         kernel,
         out_shape=[jax.ShapeDtypeStruct(*o) for o in outs],
-        in_specs=[pl.BlockSpec(memory_space=pltpu.SMEM)] * smem + [vmem] * (count - smem),
+        in_specs=inputs + [vmem] * (count - len(inputs)),
         out_specs=[vmem] * len(outs),
         scratch_shapes=list(scratch),
         compiler_params=pltpu.CompilerParams(vmem_limit_bytes=VMEM_LIMIT),
+        cost_estimate=pl.CostEstimate(flops=flops, bytes_accessed=1 << 20, transcendentals=0),
     )
 
 
@@ -241,68 +276,92 @@
     core = lax.axis_index("col")
     panel, half = eigvecs.shape
     part = panel // 2
-    samples = panel * rows
+    line = panel * rows // 2
+    vectors = 2 * half
     variants = dosage.shape[1] // 2
     place = jnp.stack([row, core]).astype(jnp.int32)
+    ints = (rows, LANES)
 
     def swap(x, m):
         return lax.ppermute(x, "row", [(i, i ^ m) for i in range(rows)])
 
     def other_core(x):
         return lax.ppermute(x, "col", [(0, 1), (1, 0)])
+
+    def beside(*xs):
+        return jnp.concatenate(xs, axis=1)
+
+    def below(*xs):
+        return jnp.concatenate(xs, axis=0)
 
     dose = {0: lax.dynamic_slice_in_dim(dosage, core * variants, variants, 1)}
     dose[4] = swap(dose[0], 4)
     dose[1] = swap(dose[0], 1)
     dose[2] = swap(dose[0], 2)
-    vals = jnp.concatenate([eigvals, other_core(eigvals)])[None, :]
-    far, e2, e1, e0, gene = call(
+    dose[6] = swap(dose[4], 2)
+    for m in (4, 2, 6):
+        dose[m + 1] = swap(dose[m], 1)
+    vals = eigvals[None, :]
+    u4 = swap(eigvecs, 4)
+    u2 = swap(beside(eigvecs, u4), 2)
+    kept = beside(eigvecs, u4, u2)
+    near = swap(kept, 1)
+    kept2 = other_core(kept)
+    near2 = other_core(near)
+    e4, e2, e1, e0, gene = call(
         route_kernel,
         [
-            ((panel, half + 2 * LANES), bf16),
+            ((panel, 2 * LANES), bf16),
             ((part, 2 * LANES), bf16),
             ((part, LANES), bf16),
             ((part, LANES), bf16),
             ((LANES, LANES), f32),
         ],
-        count=7,
+        6,
+        scratch=[
+            pltpu.VMEM(ints, jnp.int32),
+            pltpu.VMEM(ints, f32),
+            pltpu.VMEM(ints, jnp.int32),
+            pltpu.VMEM(ints, jnp.int32),
+            pltpu.VMEM((part, expression.shape[1]), bf16),
+            pltpu.SemaphoreType.DMA((5,)),
+        ],
+        anywhere=5,
     )(
         place,
-        gene_owner.reshape(rows, LANES),
-        delta.reshape(rows, LANES),
-        window_start.reshape(rows, LANES),
-        window_valid.reshape(rows, LANES),
-        eigvecs,
+        gene_owner.reshape(ints),
+        delta.reshape(ints),
+        window_start.reshape(ints),
+        window_valid.reshape(ints),
         expression,
     )
-    r4 = swap(far, 4)
-    mid = jnp.concatenate([e2, r4[part:, half:]], axis=0)
-    r2 = swap(jnp.concatenate([eigvecs, r4[:, :half], mid], axis=1), 2)
-    vecs = [eigvecs, r4[:, :half], r2[:, :half], r2[:, half : 2 * half]]
+    r4 = swap(e4, 4)
+    r2 = swap(below(e2, r4[part:]), 2)
 
     def joined(mine, at):
-        upper = jnp.concatenate([mine, r4[:part, half + at : half + at + LANES]], axis=1)
-        right = r2[:, 2 * half + at : 2 * half + at + LANES]
-        lower = jnp.concatenate([right[:part], right[part:]], axis=1)
-        return jnp.concatenate(vecs + [jnp.concatenate([upper, lower], axis=0)], axis=1)
-
-    near = swap(joined(e1, LANES), 1)
-    kept = joined(e0, 0)
-    dose[6] = swap(dose[4], 2)
-    for m in (4, 2, 6):
-        dose[m + 1] = swap(dose[m], 1)
+        return below(beside(mine, r4[:part, at : at + LANES]), beside(r2[:part, at : at + LANES], r2[part:, at : at + LANES]))
+
+    data = beside(joined(e0, 0), swap(joined(e1, LANES), 1))
+    first = call(
+        line_kernel,
+        [((vectors, variants), f32)],
+        6,
+        scratch=[pltpu.VMEM((vectors, line), bf16), pltpu.VMEM((line, variants), bf16)],
+        smem=0,
+        flops=2 * vectors * line * variants,
+    )(kept, kept2, *[dose[m] for m in (0, 4, 2, 6)])[0]
     turned, weighted, low, power = call(
         weight_kernel,
-        [((2 * half, samples), bf16), ((LANES, 2 * half), bf16), ((LANES, 2 * half), bf16), ((LANES, LANES), f32)],
-        scratch=[pltpu.VMEM((samples, LANES), bf16)],
-        count=7,
-    )(place, kept, near, other_core(kept), other_core(near), vals, gene)
+        [((vectors, line), bf16), ((LANES, vectors), bf16), ((LANES, vectors), bf16), ((LANES, LANES), f32)],
+        10,
+        scratch=[pltpu.VMEM((2 * line, LANES), bf16)],
+    )(place, kept, kept2, near, near2, data, other_core(data), vals, other_core(vals), gene)
     keep, passed = call(
         score_kernel,
         [((LANES, LANES), f32)] * 2,
-        scratch=[pltpu.VMEM((samples, variants), bf16)],
-        count=6 + rows,
-    )(place, gene, power, turned, weighted, low, *[dose[m] for m in (0, 4, 2, 6, 1, 5, 3, 7)])
+        11,
+        scratch=[pltpu.VMEM((line, variants), bf16)],
+    )(place, gene, power, first, turned, weighted, low, *[dose[m] for m in (1, 5, 3, 7)])
     return keep + other_core(passed)
 
 

time: 42 us -> 43.2 us (1.029)
  waiting for transfers between devices: 18.6 us -> 12.7 us
  starting transfers between devices: 15 us -> 18.4 us
  local copies, waits for them, and re-layouts: 3.14 us -> 5.4 us
  other arithmetic: 0.76 us -> 1.49 us
  Pallas kernels: 4.22 us -> 4.66 us
    ppermute x10 -> x13, waiting for transfers between devices: 16.4 us -> 11.4 us  [swap(): return lax.ppermute(x, 'row', [(i, i ^ m) for i in range(rows)])]
    ppermute x10 -> x13, starting transfers between devices: 14.4 us -> 18.1 us  [swap(): return lax.ppermute(x, 'row', [(i, i ^ m) for i in range(rows)])]
    unnamed x18 -> x16, local copies, waits for them, and re-layouts: 3.12 us -> 5.37 us
    ppermute x4 -> x5, waiting for transfers between devices: 2.13 us -> 1.25 us  [other_core(): return lax.ppermute(x, 'col', [(0, 1), (1, 0)])]
    concatenate x3 -> x4, other arithmetic: 0.04 us -> 0.78 us  [the longest x2 0.77 us: beside(): return jnp.concatenate(xs, axis=1)]
    pallas_call x3 -> x4, Pallas kernels: 4.22 us -> 4.66 us  [the longest x1 1.7 us: near_body(): call(score_kernel, [((LANES, LANES), f32)] * 2, 11, scratch=[pltpu.VMEM((...]
  transfers between devices with their start and end apart: 14 -> 18, of which waited for: 9 -> 10; matrix products, arithmetic and copies ran while one was open for 0% -> 4% of each run, Pallas kernels for 3% -> 7%
where the time goes in v3:
time: 43.2 us; the launch traced here: 42.8 us
  starting transfers between devices  18.4 us (43%)
  waiting for transfers between devices  12.7 us (29%)
  local copies, waits for them, and re-layouts  5.4 us (12%)
  Pallas kernels  4.66 us (11%)
  other arithmetic  1.49 us (3%)
    ppermute x13, starting transfers between devices, swap(): return lax.ppermute(x, 'row', [(i, i ^ m) for i in range(rows)])  18.1 us
    ppermute x13, waiting for transfers between devices, swap(): return lax.ppermute(x, 'row', [(i, i ^ m) for i in range(rows)])  11.4 us
    unnamed x16, local copies, waits for them, and re-layouts  5.37 us
    pallas_call x1, Pallas kernels, near_body(): call(score_kernel, [((LANES, LANES), f32)] * 2, 11, scratch=[pltpu.VMEM((...  1.7 us
    ppermute x5, waiting for transfers between devices, other_core(): return lax.ppermute(x, 'col', [(0, 1), (1, 0)])  1.25 us
    pallas_call x1, Pallas kernels, near_body(): call(route_kernel, [((panel, 2 * LANES), bf16), ((part, 2 * LANES), bf16)...  1.18 us
    pallas_call x1, Pallas kernels, near_body(): call(weight_kernel, [((vectors, line), bf16), ((LANES, vectors), bf16), (...  1.11 us
  transfers between devices with their start and end apart: 18, of which 10 were waited for; matrix products, arithmetic and copies ran while one was open for 4% of the time, Pallas kernels for 7%

profile of v3, /device:TPU:0, one launch (start us, length us, event | category | flops | bytes accessed | tf_op | source)
XLA Modules:
  0.0 42.8 jit_solution(8018029326222050221)
XLA Ops:
  0.0 0.9 %copy-done = bf16[64,1536]{1,0:T(8,128)(2,1)S(1)} copy-done((bf16[64,1536]{1,0:T(8,128)(2,1)S(1)}, bf16[64,1536]{1,0:T(8,128)(2,1)}, u32[]{:S(2)}) %copy-start) | copy-done | bytes 196632
  0.9 4.1 %collective-permute-start.10 = (bf16[64,768]{1,0:T(8,128)(2,1)S(1)}, bf16[64,768]{1,0:T(8,128)(2,1)S(1)}, u32[]{:S(2)}, u32[]{:S(2)}) collective-permute-start(bf16[64,768]{1,0:T(8,128)(2,1)S(1)} %constant_dynamic-slice_fusion.refs_0_), channel_id=1, source_target_pairs={{0,8},{2,10},{4,12},{6,14},{8,0},{10,2},{12,4},{14,6},{1,9},{3,11}... | collective-permute-start | bytes 294920 | tf_op jit(solution)/shard_map/ppermute | solution.py:286
  5.0 1.6 %collective-permute-start.11 = (bf16[64,768]{1,0:T(8,128)(2,1)S(1)}, bf16[64,768]{1,0:T(8,128)(2,1)S(1)}, u32[]{:S(2)}, u32[]{:S(2)}) collective-permute-start(bf16[64,768]{1,0:T(8,128)(2,1)S(1)} %constant_dynamic-slice_fusion.refs_0_), channel_id=1, source_target_pairs={{0,4},{2,6},{4,0},{6,2},{8,12},{10,14},{12,8},{14,10},{1,5},{3,7},... | collective-permute-start | bytes 294920 | tf_op jit(solution)/shard_map/ppermute | solution.py:286
  6.7 0.9 %copy-done.1 = bf16[64,1024]{1,0:T(8,128)(2,1)S(1)} copy-done((bf16[64,1024]{1,0:T(8,128)(2,1)S(1)}, bf16[64,1024]{1,0:T(8,128)(2,1)}, u32[]{:S(2)}) %copy-start.1) | copy-done | bytes 131096
  10.3 1.2 %shard_map.82 = (bf16[64,256]{1,0:T(8,128)(2,1)S(1)}, bf16[32,256]{1,0:T(8,128)(2,1)S(1)}, bf16[32,128]{1,0:T(8,128)(2,1)S(1)}, bf16[32,128]{1,0:T(8,128)(2,1)S(1)}, f32[128,128]{1,0:T(8,128)S(1)}) custom-call(s32[2]{0:T(128)S(1)} %pad_add_fusion.place_ref, s32[8,128]{1,0:T(8,128)S(1)} %bitcast.7, f32[8,128]{1,0:T(8,128)S(1)} %bitcast.8, ...), custom_call_target="tpu_custom_call" | custom-call | bytes 1048576 | tf_op jit(solution)/shard_map/pallas_call | solution.py:311
  11.9 2.6 %collective-permute-start = (bf16[64,256]{1,0:T(8,128)(2,1)}, bf16[64,256]{1,0:T(8,128)(2,1)S(1)}, u32[]{:S(2)}, u32[]{:S(2)}) collective-permute-start(bf16[64,256]{1,0:T(8,128)(2,1)} %param.8), channel_id=1, source_target_pairs={{0,8},{2,10},{4,12},{6,14},{8,0},{10,2},{12,4},{14,6},{1,9},{3,11}... | collective-permute-start | bytes 98312 | tf_op jit(solution)/shard_map/ppermute | solution.py:286
  14.5 0.8 %constant_dynamic-update-slice_fusion.2 = bf16[64,1024]{1,0:T(8,128)(2,1)S(1)} fusion(bf16[64,256]{1,0:T(8,128)(2,1)} %param.8), kind=kLoop, calls=%fused_computation.6 | loop fusion | bytes 65536
  15.3 1.7 %collective-permute-done.5 = bf16[64,256]{1,0:T(8,128)(2,1)S(1)} collective-permute-done((bf16[64,256]{1,0:T(8,128)(2,1)S(1)}, bf16[64,256]{1,0:T(8,128)(2,1)S(1)}, u32[]{:S(2)}, u32[]{:S(2)}) %collective-permute-start.5) | collective-permute-done | bytes 32800 | tf_op jit(solution)/shard_map/ppermute | solution.py:286
  17.3 0.8 %pad_maximum_fusion = bf16[64,512]{1,0:T(8,128)(2,1)S(1)} fusion(bf16[64,256]{1,0:T(8,128)(2,1)S(1)} %collective-permute-done, bf16[64,256]{1,0:T(8,128)(2,1)} %param.8), kind=kLoop, calls=%fused_computation | loop fusion | flops 131072 | bytes 131072 | tf_op jit(solution)/shard_map/concatenate | solution.py:292
  18.1 1.7 %collective-permute-start.1 = (bf16[64,512]{1,0:T(8,128)(2,1)S(1)}, bf16[64,512]{1,0:T(8,128)(2,1)S(1)}, u32[]{:S(2)}, u32[]{:S(2)}) collective-permute-start(bf16[64,512]{1,0:T(8,128)(2,1)S(1)} %pad_maximum_fusion), channel_id=1, source_target_pairs={{0,4},{2,6},{4,0},{6,2},{8,12},{10,14},{12,8},{14,10},{1,5},{3,7},... | collective-permute-start | bytes 196616 | tf_op jit(solution)/shard_map/ppermute | solution.py:286
  19.8 1.1 %collective-permute-done.6 = bf16[64,256]{1,0:T(8,128)(2,1)S(1)} collective-permute-done((bf16[64,256]{1,0:T(8,128)(2,1)S(1)}, bf16[64,256]{1,0:T(8,128)(2,1)S(1)}, u32[]{:S(2)}, u32[]{:S(2)}) %collective-permute-start.6) | collective-permute-done | bytes 32800 | tf_op jit(solution)/shard_map/ppermute | solution.py:286
  20.9 1.6 %collective-permute-start.7 = (bf16[64,256]{1,0:T(8,128)(2,1)S(1)}, bf16[64,256]{1,0:T(8,128)(2,1)S(1)}, u32[]{:S(2)}, u32[]{:S(2)}) collective-permute-start(bf16[64,256]{1,0:T(8,128)(2,1)S(1)} %maximum_maximum_fusion), channel_id=1, source_target_pairs={{0,2},{2,0},{4,6},{6,4},{8,10},{10,8},{12,14},{14,12},{1,3},{3,1},... | collective-permute-start | bytes 98312 | tf_op jit(solution)/shard_map/ppermute | solution.py:286
  22.5 1.4 %collective-permute-start.3 = (bf16[64,1024]{1,0:T(8,128)(2,1)S(1)}, bf16[64,1024]{1,0:T(8,128)(2,1)S(1)}, u32[]{:S(2)}, u32[]{:S(2)}) collective-permute-start(bf16[64,1024]{1,0:T(8,128)(2,1)S(1)} %constant_dynamic-update-slice_fusion.kept_ref.vecs_ref), channel_id=1, source_target_pairs={{0,2},{2,0},{4,6},{6,4},{8,10},{10,8},{12,14},{14,12},{1,3},{3,1},... | collective-permute-start | bytes 393224 | tf_op jit(solution)/shard_map/ppermute | solution.py:286
  23.9 1.0 %collective-permute-done.7 = bf16[64,256]{1,0:T(8,128)(2,1)S(1)} collective-permute-done((bf16[64,256]{1,0:T(8,128)(2,1)S(1)}, bf16[64,256]{1,0:T(8,128)(2,1)S(1)}, u32[]{:S(2)}, u32[]{:S(2)}) %collective-permute-start.7) | collective-permute-done | bytes 32800 | tf_op jit(solution)/shard_map/ppermute | solution.py:286
  24.9 0.8 %collective-permute-start.12 = (bf16[64,768]{1,0:T(8,128)(2,1)S(1)}, bf16[64,768]{1,0:T(8,128)(2,1)S(1)}, u32[]{:S(2)}, u32[]{:S(2)}) collective-permute-start(bf16[64,768]{1,0:T(8,128)(2,1)S(1)} %collective-permute-done.10.refs_1_), channel_id=1, source_target_pairs={{0,4},{2,6},{4,0},{6,2},{8,12},{10,14},{12,8},{14,10},{1,5},{3,7},... | collective-permute-start | bytes 294920 | tf_op jit(solution)/shard_map/ppermute | solution.py:286
  25.9 1.7 %collective-permute-done.3.near_ref = bf16[64,1024]{1,0:T(8,128)(2,1)S(1)} collective-permute-done((bf16[64,1024]{1,0:T(8,128)(2,1)S(1)}, bf16[64,1024]{1,0:T(8,128)(2,1)S(1)}, u32[]{:S(2)}, u32[]{:S(2)}) %collective-permute-start.3) | collective-permute-done | bytes 131104 | tf_op jit(solution)/shard_map/ppermute | solution.py:286
  27.6 1.3 %collective-permute-start.13 = (bf16[64,768]{1,0:T(8,128)(2,1)S(1)}, bf16[64,768]{1,0:T(8,128)(2,1)S(1)}, u32[]{:S(2)}, u32[]{:S(2)}) collective-permute-start(bf16[64,768]{1,0:T(8,128)(2,1)S(1)} %constant_dynamic-slice_fusion.refs_0_), channel_id=1, source_target_pairs={{0,2},{2,0},{4,6},{6,4},{8,10},{10,8},{12,14},{14,12},{1,3},{3,1},... | collective-permute-start | bytes 294920 | tf_op jit(solution)/shard_map/ppermute | solution.py:286
  30.1 1.5 %collective-permute-start.15 = (bf16[64,768]{1,0:T(8,128)(2,1)S(1)}, bf16[64,768]{1,0:T(8,128)(2,1)S(1)}, u32[]{:S(2)}, u32[]{:S(2)}) collective-permute-start(bf16[64,768]{1,0:T(8,128)(2,1)S(1)} %collective-permute-done.11.refs_2_), channel_id=1, source_target_pairs={{0,2},{2,0},{4,6},{6,4},{8,10},{10,8},{12,14},{14,12},{1,3},{3,1},... | collective-permute-start | bytes 294920 | tf_op jit(solution)/shard_map/ppermute | solution.py:286
  32.9 1.1 %shard_map.83 = (bf16[512,256]{1,0:T(8,128)(2,1)S(1)}, bf16[128,512]{1,0:T(8,128)(2,1)S(1)}, bf16[128,512]{1,0:T(8,128)(2,1)S(1)}, f32[128,128]{1,0:T(8,128)S(1)}) custom-call(s32[2]{0:T(128)S(1)} %pad_add_fusion.place_ref, bf16[64,1024]{1,0:T(8,128)(2,1)S(1)} %constant_dynamic-update-slice_fusion.kept_ref.vecs_ref, ...), custom_call_target="tpu_custom_call" | custom-call | bytes 1048576 | tf_op jit(solution)/shard_map/pallas_call | solution.py:353
  34.0 1.3 %collective-permute-done.14.refs_1_ = bf16[64,768]{1,0:T(8,128)(2,1)S(1)} collective-permute-done((bf16[64,768]{1,0:T(8,128)(2,1)S(1)}, bf16[64,768]{1,0:T(8,128)(2,1)S(1)}, u32[]{:S(2)}, u32[]{:S(2)}) %collective-permute-start.14) | collective-permute-done | bytes 98336 | tf_op jit(solution)/shard_map/ppermute | solution.py:286
  35.3 2.1 %collective-permute-done.15.refs_2_ = bf16[64,768]{1,0:T(8,128)(2,1)S(1)} collective-permute-done((bf16[64,768]{1,0:T(8,128)(2,1)S(1)}, bf16[64,768]{1,0:T(8,128)(2,1)S(1)}, u32[]{:S(2)}, u32[]{:S(2)}) %collective-permute-start.15) | collective-permute-done | bytes 98336 | tf_op jit(solution)/shard_map/ppermute | solution.py:286
  37.4 1.7 %collective-permute-done.16.refs_3_ = bf16[64,768]{1,0:T(8,128)(2,1)S(1)} collective-permute-done((bf16[64,768]{1,0:T(8,128)(2,1)S(1)}, bf16[64,768]{1,0:T(8,128)(2,1)S(1)}, u32[]{:S(2)}, u32[]{:S(2)}) %collective-permute-start.16) | collective-permute-done | bytes 98336 | tf_op jit(solution)/shard_map/ppermute | solution.py:286
  39.1 1.7 %shard_map.85 = (f32[128,128]{1,0:T(8,128)S(1)}, f32[128,128]{1,0:T(8,128)S(1)}) custom-call(s32[2]{0:T(128)S(1)} %pad_add_fusion.place_ref, f32[128,128]{1,0:T(8,128)S(1)} %get-tuple-element.16.gene_ref, f32[128,128]{1,0:T(8,128)S(1)} %get-tuple-element.21.power_ref, f32[512,768]{1,0:T(8,128)S(1)} %shard_map.84.part_ref, ...), custom_call_target="tpu_custom_call" | custom-call | bytes 1048576 | tf_op jit(solution)/shard_map/pallas_call | solution.py:359
  40.9 1.2 %collective-permute-done.17 = f32[128,128]{1,0:T(8,128)S(1)} collective-permute-done((f32[128,128]{1,0:T(8,128)S(1)}, f32[128,128]{1,0:T(8,128)S(1)}, u32[]{:S(2)}, u32[]{:S(2)}) %collective-permute-start.17) | collective-permute-done | bytes 65568 | tf_op jit(solution)/shard_map/ppermute | solution.py:289
  (43 shorter events, 7.0 us)
Async XLA Ops:
  0.0 0.9 %copy-start = (bf16[64,1536]{1,0:T(8,128)(2,1)S(1)}, bf16[64,1536]{1,0:T(8,128)(2,1)}, u32[]{:S(2)}) copy-start(bf16[64,1536]{1,0:T(8,128)(2,1)} %param.11) | copy-start | bytes 589828
  0.9 24.0 %collective-permute-start.10 = (bf16[64,768]{1,0:T(8,128)(2,1)S(1)}, bf16[64,768]{1,0:T(8,128)(2,1)S(1)}, u32[]{:S(2)}, u32[]{:S(2)}) collective-permute-start(bf16[64,768]{1,0:T(8,128)(2,1)S(1)} %constant_dynamic-slice_fusion.refs_0_), channel_id=1, source_target_pairs={{0,8},{2,10},{4,12},{6,14},{8,0},{10,2},{12,4},{14,6},{1,9},{3,11}... | collective-permute-start | bytes 294920 | tf_op jit(solution)/shard_map/ppermute | solution.py:286
  5.0 22.5 %collective-permute-start.11 = (bf16[64,768]{1,0:T(8,128)(2,1)S(1)}, bf16[64,768]{1,0:T(8,128)(2,1)S(1)}, u32[]{:S(2)}, u32[]{:S(2)}) collective-permute-start(bf16[64,768]{1,0:T(8,128)(2,1)S(1)} %constant_dynamic-slice_fusion.refs_0_), channel_id=1, source_target_pairs={{0,4},{2,6},{4,0},{6,2},{8,12},{10,14},{12,8},{14,10},{1,5},{3,7},... | collective-permute-start | bytes 294920 | tf_op jit(solution)/shard_map/ppermute | solution.py:286
  6.7 0.9 %copy-start.1 = (bf16[64,1024]{1,0:T(8,128)(2,1)S(1)}, bf16[64,1024]{1,0:T(8,128)(2,1)}, u32[]{:S(2)}) copy-start(bf16[64,1024]{1,0:T(8,128)(2,1)} %expr_any.1) | copy-start | bytes 393220
  7.6 0.7 %copy-start.2 = (s32[1024]{0:T(1024)S(1)}, s32[1024]{0:T(1024)}, u32[]{:S(2)}) copy-start(s32[1024]{0:T(1024)} %param.15) | copy-start | bytes 12292
  8.3 0.7 %copy-start.3 = (f32[1024]{0:T(1024)S(1)}, f32[1024]{0:T(1024)}, u32[]{:S(2)}) copy-start(f32[1024]{0:T(1024)} %param.12) | copy-start | bytes 12292
  9.0 0.7 %copy-start.4 = (s32[1024]{0:T(1024)S(1)}, s32[1024]{0:T(1024)}, u32[]{:S(2)}) copy-start(s32[1024]{0:T(1024)} %param.13) | copy-start | bytes 12292
  10.3 22.5 %copy-start.6 = (f32[256]{0:T(256)S(1)}, f32[256]{0:T(256)}, u32[]{:S(2)}) copy-start(f32[256]{0:T(256)} %param.9) | copy-start | bytes 3076
  11.5 5.5 %collective-permute-start.5 = (bf16[64,256]{1,0:T(8,128)(2,1)S(1)}, bf16[64,256]{1,0:T(8,128)(2,1)S(1)}, u32[]{:S(2)}, u32[]{:S(2)}) collective-permute-start(bf16[64,256]{1,0:T(8,128)(2,1)S(1)} %get-tuple-element.18), channel_id=1, source_target_pairs={{0,8},{2,10},{4,12},{6,14},{8,0},{10,2},{12,4},{14,6},{1,9},{3,11}... | collective-permute-start | bytes 98312 | tf_op jit(solution)/shard_map/ppermute | solution.py:286
  11.9 5.4 %collective-permute-start = (bf16[64,256]{1,0:T(8,128)(2,1)}, bf16[64,256]{1,0:T(8,128)(2,1)S(1)}, u32[]{:S(2)}, u32[]{:S(2)}) collective-permute-start(bf16[64,256]{1,0:T(8,128)(2,1)} %param.8), channel_id=1, source_target_pairs={{0,8},{2,10},{4,12},{6,14},{8,0},{10,2},{12,4},{14,6},{1,9},{3,11}... | collective-permute-start | bytes 98312 | tf_op jit(solution)/shard_map/ppermute | solution.py:286
  14.5 11.2 %collective-permute-start.9 = (f32[1,256]{1,0:T(1,128)}, f32[1,256]{1,0:T(1,128)S(1)}, u32[]{:S(2)}, u32[]{:S(2)}) collective-permute-start(f32[1,256]{1,0:T(1,128)} %bitcast.11), channel_id=1, source_target_pairs={{0,1},{1,0},{2,3},{3,2},{4,5},{5,4},{6,7},{7,6},{8,9},{9,8},{10,11... | collective-permute-start | bytes 3080 | tf_op jit(solution)/shard_map/ppermute | solution.py:289
  17.0 3.9 %collective-permute-start.6 = (bf16[64,256]{1,0:T(8,128)(2,1)S(1)}, bf16[64,256]{1,0:T(8,128)(2,1)S(1)}, u32[]{:S(2)}, u32[]{:S(2)}) collective-permute-start(bf16[64,256]{1,0:T(8,128)(2,1)S(1)} %pad_maximum_fusion.2), channel_id=1, source_target_pairs={{0,4},{2,6},{4,0},{6,2},{8,12},{10,14},{12,8},{14,10},{1,5},{3,7},... | collective-permute-start | bytes 98312 | tf_op jit(solution)/shard_map/ppermute | solution.py:286
  18.1 4.4 %collective-permute-start.1 = (bf16[64,512]{1,0:T(8,128)(2,1)S(1)}, bf16[64,512]{1,0:T(8,128)(2,1)S(1)}, u32[]{:S(2)}, u32[]{:S(2)}) collective-permute-start(bf16[64,512]{1,0:T(8,128)(2,1)S(1)} %pad_maximum_fusion), channel_id=1, source_target_pairs={{0,4},{2,6},{4,0},{6,2},{8,12},{10,14},{12,8},{14,10},{1,5},{3,7},... | collective-permute-start | bytes 196616 | tf_op jit(solution)/shard_map/ppermute | solution.py:286
  20.9 4.0 %collective-permute-start.7 = (bf16[64,256]{1,0:T(8,128)(2,1)S(1)}, bf16[64,256]{1,0:T(8,128)(2,1)S(1)}, u32[]{:S(2)}, u32[]{:S(2)}) collective-permute-start(bf16[64,256]{1,0:T(8,128)(2,1)S(1)} %maximum_maximum_fusion), channel_id=1, source_target_pairs={{0,2},{2,0},{4,6},{6,4},{8,10},{10,8},{12,14},{14,12},{1,3},{3,1},... | collective-permute-start | bytes 98312 | tf_op jit(solution)/shard_map/ppermute | solution.py:286
  22.5 5.0 %collective-permute-start.3 = (bf16[64,1024]{1,0:T(8,128)(2,1)S(1)}, bf16[64,1024]{1,0:T(8,128)(2,1)S(1)}, u32[]{:S(2)}, u32[]{:S(2)}) collective-permute-start(bf16[64,1024]{1,0:T(8,128)(2,1)S(1)} %constant_dynamic-update-slice_fusion.kept_ref.vecs_ref), channel_id=1, source_target_pairs={{0,2},{2,0},{4,6},{6,4},{8,10},{10,8},{12,14},{14,12},{1,3},{3,1},... | collective-permute-start | bytes 393224 | tf_op jit(solution)/shard_map/ppermute | solution.py:286
  24.9 6.7 %collective-permute-start.2 = (bf16[64,1024]{1,0:T(8,128)(2,1)S(1)}, bf16[64,1024]{1,0:T(8,128)(2,1)S(1)}, u32[]{:S(2)}, u32[]{:S(2)}) collective-permute-start(bf16[64,1024]{1,0:T(8,128)(2,1)S(1)} %constant_dynamic-update-slice_fusion.kept_ref.vecs_ref), channel_id=1, source_target_pairs={{0,1},{1,0},{2,3},{3,2},{4,5},{5,4},{6,7},{7,6},{8,9},{9,8},{10,11... | collective-permute-start | bytes 393224 | tf_op jit(solution)/shard_map/ppermute | solution.py:289
  24.9 5.2 %collective-permute-start.12 = (bf16[64,768]{1,0:T(8,128)(2,1)S(1)}, bf16[64,768]{1,0:T(8,128)(2,1)S(1)}, u32[]{:S(2)}, u32[]{:S(2)}) collective-permute-start(bf16[64,768]{1,0:T(8,128)(2,1)S(1)} %collective-permute-done.10.refs_1_), channel_id=1, source_target_pairs={{0,4},{2,6},{4,0},{6,2},{8,12},{10,14},{12,8},{14,10},{1,5},{3,7},... | collective-permute-start | bytes 294920 | tf_op jit(solution)/shard_map/ppermute | solution.py:286
  25.7 3.2 %collective-permute-start.8 = (bf16[64,512]{1,0:T(8,128)(2,1)S(1)}, bf16[64,512]{1,0:T(8,128)(2,1)S(1)}, u32[]{:S(2)}, u32[]{:S(2)}) collective-permute-start(bf16[64,512]{1,0:T(8,128)(2,1)S(1)} %pad_maximum_fusion.1.expr_ref), channel_id=1, source_target_pairs={{0,1},{1,0},{2,3},{3,2},{4,5},{5,4},{6,7},{7,6},{8,9},{9,8},{10,11... | collective-permute-start | bytes 196616 | tf_op jit(solution)/shard_map/ppermute | solution.py:289
  27.6 5.3 %collective-permute-start.4 = (bf16[64,1024]{1,0:T(8,128)(2,1)S(1)}, bf16[64,1024]{1,0:T(8,128)(2,1)S(1)}, u32[]{:S(2)}, u32[]{:S(2)}) collective-permute-start(bf16[64,1024]{1,0:T(8,128)(2,1)S(1)} %collective-permute-done.3.near_ref), channel_id=1, source_target_pairs={{0,1},{1,0},{2,3},{3,2},{4,5},{5,4},{6,7},{7,6},{8,9},{9,8},{10,11... | collective-permute-start | bytes 393224 | tf_op jit(solution)/shard_map/ppermute | solution.py:289
  27.6 6.4 %collective-permute-start.13 = (bf16[64,768]{1,0:T(8,128)(2,1)S(1)}, bf16[64,768]{1,0:T(8,128)(2,1)S(1)}, u32[]{:S(2)}, u32[]{:S(2)}) collective-permute-start(bf16[64,768]{1,0:T(8,128)(2,1)S(1)} %constant_dynamic-slice_fusion.refs_0_), channel_id=1, source_target_pairs={{0,2},{2,0},{4,6},{6,4},{8,10},{10,8},{12,14},{14,12},{1,3},{3,1},... | collective-permute-start | bytes 294920 | tf_op jit(solution)/shard_map/ppermute | solution.py:286
  28.9 6.4 %collective-permute-start.14 = (bf16[64,768]{1,0:T(8,128)(2,1)S(1)}, bf16[64,768]{1,0:T(8,128)(2,1)S(1)}, u32[]{:S(2)}, u32[]{:S(2)}) collective-permute-start(bf16[64,768]{1,0:T(8,128)(2,1)S(1)} %collective-permute-done.10.refs_1_), channel_id=1, source_target_pairs={{0,2},{2,0},{4,6},{6,4},{8,10},{10,8},{12,14},{14,12},{1,3},{3,1},... | collective-permute-start | bytes 294920 | tf_op jit(solution)/shard_map/ppermute | solution.py:286
  30.1 7.3 %collective-permute-start.15 = (bf16[64,768]{1,0:T(8,128)(2,1)S(1)}, bf16[64,768]{1,0:T(8,128)(2,1)S(1)}, u32[]{:S(2)}, u32[]{:S(2)}) collective-permute-start(bf16[64,768]{1,0:T(8,128)(2,1)S(1)} %collective-permute-done.11.refs_2_), channel_id=1, source_target_pairs={{0,2},{2,0},{4,6},{6,4},{8,10},{10,8},{12,14},{14,12},{1,3},{3,1},... | collective-permute-start | bytes 294920 | tf_op jit(solution)/shard_map/ppermute | solution.py:286
  31.7 7.4 %collective-permute-start.16 = (bf16[64,768]{1,0:T(8,128)(2,1)S(1)}, bf16[64,768]{1,0:T(8,128)(2,1)S(1)}, u32[]{:S(2)}, u32[]{:S(2)}) collective-permute-start(bf16[64,768]{1,0:T(8,128)(2,1)S(1)} %collective-permute-done.12.refs_3_), channel_id=1, source_target_pairs={{0,2},{2,0},{4,6},{6,4},{8,10},{10,8},{12,14},{14,12},{1,3},{3,1},... | collective-permute-start | bytes 294920 | tf_op jit(solution)/shard_map/ppermute | solution.py:286
  40.8 1.3 %collective-permute-start.17 = (f32[128,128]{1,0:T(8,128)S(1)}, f32[128,128]{1,0:T(8,128)S(1)}, u32[]{:S(2)}, u32[]{:S(2)}) collective-permute-start(f32[128,128]{1,0:T(8,128)S(1)} %get-tuple-element.26), channel_id=1, source_target_pairs={{0,1},{1,0},{2,3},{3,2},{4,5},{5,4},{6,7},{7,6},{8,9},{9,8},{10,11... | collective-permute-start | bytes 196616 | tf_op jit(solution)/shard_map/ppermute | solution.py:289
  (1 other events, 0.7 us)

commit v4 on v2

--- a/solution.py
+++ b/solution.py
@@ -100,7 +100,9 @@
     return lax.dynamic_slice_in_dim(zscore, lax.axis_index("col") * width_part, width_part, 1)
 
 
-def route_kernel(place_ref, owner_ref, delta_ref, start_ref, valid_ref, vecs_ref, expr_ref, far_ref, e2_ref, e1_ref, e0_ref, gene_ref):
+def route_kernel(
+    place_ref, owner_ref, delta_ref, start_ref, valid_ref, vecs_ref, expr_ref, ahead_ref, e46_ref, e2_ref, e0_ref, gene_ref
+):
     slices = owner_ref.shape[0]
     capacity = LANES // slices
     half = vecs_ref.shape[1]
@@ -133,49 +135,89 @@
             line = ref[s : s + 1, :].astype(f32)
             figures = jnp.where(lane == i, jnp.sum(mine * line, axis=1, keepdims=True), figures)
         gene_ref[s * capacity : (s + 1) * capacity, :] = figures
-    far_ref[:, :half] = vecs_ref[...]
-    for m in range(slices):
+    ahead_ref[:, :half] = vecs_ref[...]
+    left, right = slice(0, LANES), slice(LANES, 2 * LANES)
+    upper, lower = slice(0, part), slice(part, 2 * part)
+    targets = {
+        0: (e0_ref, upper, left),
+        1: (ahead_ref, upper, slice(half, half + LANES)),
+        2: (e2_ref, upper, left),
+        3: (ahead_ref, upper, slice(half + LANES, half + 2 * LANES)),
+        4: (e46_ref, upper, left),
+        5: (ahead_ref, lower, slice(half, half + LANES)),
+        6: (e46_ref, upper, right),
+        7: (ahead_ref, lower, slice(half + LANES, half + 2 * LANES)),
+    }
+    for m, (ref, down, side) in targets.items():
         block = jnp.concatenate([x[m * capacity : (m + 1) * capacity, :] for x in sorted_slices], axis=0)
-        block = block.T.astype(bf16)
-        side = slice(half + m % 2 * LANES, half + (m % 2 + 1) * LANES)
-        if m >= 4:
-            far_ref[(m - 4) // 2 * part : ((m - 4) // 2 + 1) * part, side] = block
-        elif m >= 2:
-            e2_ref[:, m % 2 * LANES : (m % 2 + 1) * LANES] = block
-        elif m == 1:
-            e1_ref[...] = block
-        else:
-            e0_ref[...] = block
-
-
-def weight_kernel(place_ref, kept_ref, near_ref, kept2_ref, near2_ref, vals_ref, gene_ref, turned_ref, weighted_ref, low_ref, power_ref, data_scr):
-    samples = kept_ref.shape[0]
-    half = vals_ref.shape[1] // 2
+        ref[down, side] = block.T.astype(bf16)
+
+
+def second_kernel(vecs_ref, r1_ref, e46_ref, d4_any, d1_any, out_ref):
+    half = vecs_ref.shape[1]
+    part = e46_ref.shape[0]
+    out_ref[:, :half] = vecs_ref[...]
+    out_ref[:, half : 2 * half] = r1_ref[:, :half]
+    out_ref[:part, 2 * half :] = e46_ref[...]
+    out_ref[part:, 2 * half :] = r1_ref[part:, half:]
+
+
+def third_kernel(vecs_ref, r1_ref, r4_ref, e2_ref, e0_ref, out_ref, kept_ref):
+    half = vecs_ref.shape[1]
+    part = e0_ref.shape[0]
+    for ref, own, at in ((out_ref, e2_ref, LANES), (kept_ref, e0_ref, 0)):
+        ref[:, :half] = vecs_ref[...]
+        ref[:, half : 2 * half] = r1_ref[:, :half]
+        ref[:, 2 * half : 4 * half] = r4_ref[:, : 2 * half]
+        side = slice(2 * half + at, 2 * half + at + LANES)
+        left, right = slice(4 * half, 4 * half + LANES), slice(4 * half + LANES, 4 * half + 2 * LANES)
+        ref[:part, left] = own[...]
+        ref[:part, right] = r1_ref[:part, half + at : half + at + LANES]
+        ref[part:, left] = r4_ref[:part, side]
+        ref[part:, right] = r4_ref[part:, side]
+
+
+def pack_kernel(kept_ref, far_ref, vals_ref, out_ref):
+    width = kept_ref.shape[1]
+    out_ref[:, :width] = kept_ref[...]
+    out_ref[:, width : 2 * width] = far_ref[...]
+    vals = vals_ref[...]
+    high = vals.astype(bf16).astype(f32)
+    middle = (vals - high).astype(bf16).astype(f32)
+    low = vals - high - middle
+    row = lax.broadcasted_iota(jnp.int32, (out_ref.shape[0], vals.shape[1]), 0)
+    terms = jnp.where(row == 0, high, jnp.where(row == 1, middle, jnp.where(row == 2, low, 0.0)))
+    out_ref[:, 2 * width :] = terms.astype(bf16)
+
+
+def weight_kernel(place_ref, mine_ref, other_ref, gene_ref, turned_ref, weighted_ref, low_ref, power_ref, data_scr):
+    samples = mine_ref.shape[0]
+    half = turned_ref.shape[0] // 2
     part = samples // 2
     core = place_ref[1]
-    sources = ((kept_ref, kept2_ref), (near_ref, near2_ref))
-    for n, pair in enumerate(sources):
-        for c, ref in enumerate(pair):
-            side = core if c == 0 else 1 - core
-            for i in range(4):
-                first = (n * 4 + i) * samples
-                turned_ref[c * half : (c + 1) * half, first : first + samples] = (
-                    ref[:, i * half : (i + 1) * half].astype(f32).T.astype(bf16)
-                )
-                at = 4 * half + i % 2 * LANES
-                data_scr[pl.ds(pl.multiple_of(first + side * part, part), part), :] = ref[
-                    i // 2 * part : (i // 2 + 1) * part, at : at + LANES
-                ]
+    width = 4 * half + 2 * LANES
+    panels = [n * width + i * half for n in range(2) for i in range(4)]
+    for c, ref in enumerate((mine_ref, other_ref)):
+        side = core if c == 0 else 1 - core
+        for m, at in enumerate(panels):
+            turned_ref[c * half : (c + 1) * half, m * samples : (m + 1) * samples] = (
+                ref[:, at : at + half].astype(f32).T.astype(bf16)
+            )
+            n, i = divmod(m, 4)
+            at = n * width + 4 * half + i % 2 * LANES
+            data_scr[pl.ds(pl.multiple_of(m * samples + side * part, part), part), :] = ref[
+                i // 2 * part : (i // 2 + 1) * part, at : at + LANES
+            ]
     data = data_scr[...].astype(f32).T.astype(bf16)
     delta = gene_ref[:, 0:1]
     total = jnp.zeros((data.shape[0], 1), f32)
-    for c in range(2):
-        vecs = jnp.concatenate(
-            [pair[c][:, i * half : (i + 1) * half] for pair in sources for i in range(4)], axis=0
-        )
+    for c, ref in enumerate((mine_ref, other_ref)):
+        vecs = jnp.concatenate([ref[:, at : at + half] for at in panels], axis=0)
         cols = slice(c * half, (c + 1) * half)
+        terms = ref[0:16, 2 * width :].astype(f32)
+        vals = terms[0:1] + terms[1:2] + terms[2:3]
         rotated = jnp.dot(data, vecs, preferred_element_type=f32).astype(bf16).astype(f32)
-        weight = 1.0 / (vals_ref[:, cols] + delta)
+        weight = 1.0 / (vals + delta)
         total += jnp.sum(weight * rotated * rotated, axis=1, keepdims=True)
         weighted_ref[:, cols] = (weight * rotated).astype(bf16)
         low_ref[:, cols] = weight.astype(bf16)
@@ -185,8 +227,10 @@
 def score_kernel(place_ref, gene_ref, power_ref, turned_ref, weighted_ref, low_ref, *refs):
     *dose_refs, keep_ref, pass_ref, dose_scr = refs
     samples, variants = dose_refs[0].shape
-    for m, ref in enumerate(dose_refs):
-        dose_scr[m * samples : (m + 1) * samples, :] = ref[...]
+    chunks = [(ref, at) for ref in dose_refs for at in range(0, ref.shape[1], variants)]
+    order = [0, 1, 2, 5, 3, 6, 4, 7]
+    for m, (ref, at) in enumerate(chunks[i] for i in order):
+        dose_scr[m * samples : (m + 1) * samples, :] = ref[:, at : at + variants]
     rotated = jnp.dot(turned_ref[...], dose_scr[...], preferred_element_type=f32).astype(bf16)
     squared = jnp.square(rotated.astype(f32)).astype(bf16)
     cross = jnp.dot(weighted_ref[...], rotated, preferred_element_type=f32)
@@ -197,7 +241,7 @@
     genes = cross.shape[0]
     lane = lax.broadcasted_iota(jnp.int32, (genes, LANES), 1)
     own_power = power_ref[...]
-    scale = jnp.sqrt(f32(samples * len(dose_refs)))
+    scale = jnp.sqrt(f32(dose_scr.shape[0]))
     blocks = variants // LANES
     for out_ref, half in ((keep_ref, core), (pass_ref, 1 - core)):
         offset = start + half * LANES - core * variants
@@ -223,12 +267,12 @@
         out_ref[...] = jnp.where(live, score, 0.0)
 
 
-def call(kernel, outs, scratch=(), smem=1, count=0):
+def call(kernel, outs, count, scratch=(), smem=1, anywhere=0):
     vmem = pl.BlockSpec(memory_space=pltpu.VMEM)
     return pl.pallas_call(
         kernel,
         out_shape=[jax.ShapeDtypeStruct(*o) for o in outs],
-        in_specs=[pl.BlockSpec(memory_space=pltpu.SMEM)] * smem + [vmem] * (count - smem),
+        in_specs=[pl.BlockSpec(memory_space=pltpu.SMEM)] * smem + [vmem] * (count - smem - anywhere) + [pl.BlockSpec(memory_space=pl.ANY)] * anywhere,
         out_specs=[vmem] * len(outs),
         scratch_shapes=list(scratch),
         compiler_params=pltpu.CompilerParams(vmem_limit_bytes=VMEM_LIMIT),
@@ -251,12 +295,12 @@
     def other_core(x):
         return lax.ppermute(x, "col", [(0, 1), (1, 0)])
 
-    dose = {0: lax.dynamic_slice_in_dim(dosage, core * variants, variants, 1)}
-    dose[4] = swap(dose[0], 4)
-    dose[1] = swap(dose[0], 1)
-    dose[2] = swap(dose[0], 2)
-    vals = jnp.concatenate([eigvals, other_core(eigvals)])[None, :]
-    far, e2, e1, e0, gene = call(
+    d0 = lax.dynamic_slice_in_dim(dosage, core * variants, variants, 1)
+    d4 = swap(d0, 4)
+    d1 = swap(d0, 1)
+    d26 = swap(jnp.concatenate([d0, d4], axis=1), 2)
+    d537 = swap(jnp.concatenate([d4, d26], axis=1), 1)
+    ahead, e46, e2, e0, gene = call(
         route_kernel,
         [
             ((panel, half + 2 * LANES), bf16),
@@ -265,7 +309,7 @@
             ((part, LANES), bf16),
             ((LANES, LANES), f32),
         ],
-        count=7,
+        7,
     )(
         place,
         gene_owner.reshape(rows, LANES),
@@ -275,34 +319,25 @@
         eigvecs,
         expression,
     )
-    r4 = swap(far, 4)
-    mid = jnp.concatenate([e2, r4[part:, half:]], axis=0)
-    r2 = swap(jnp.concatenate([eigvecs, r4[:, :half], mid], axis=1), 2)
-    vecs = [eigvecs, r4[:, :half], r2[:, :half], r2[:, half : 2 * half]]
-
-    def joined(mine, at):
-        upper = jnp.concatenate([mine, r4[:part, half + at : half + at + LANES]], axis=1)
-        right = r2[:, 2 * half + at : 2 * half + at + LANES]
-        lower = jnp.concatenate([right[:part], right[part:]], axis=1)
-        return jnp.concatenate(vecs + [jnp.concatenate([upper, lower], axis=0)], axis=1)
-
-    near = swap(joined(e1, LANES), 1)
-    kept = joined(e0, 0)
-    dose[6] = swap(dose[4], 2)
-    for m in (4, 2, 6):
-        dose[m + 1] = swap(dose[m], 1)
+    r1 = swap(ahead, 1)
+    r4 = swap(
+        call(second_kernel, [((panel, 2 * half + 2 * LANES), bf16)], 5, smem=0, anywhere=2)(eigvecs, r1, e46, d4, d1)[0], 4
+    )
+    width = 4 * half + 2 * LANES
+    out, kept = call(third_kernel, [((panel, width), bf16)] * 2, 5, smem=0)(eigvecs, r1, r4, e2, e0)
+    mine = call(pack_kernel, [((panel, 2 * width + half), bf16)], 3, smem=0)(kept, swap(out, 2), eigvals[None, :])[0]
     turned, weighted, low, power = call(
         weight_kernel,
         [((2 * half, samples), bf16), ((LANES, 2 * half), bf16), ((LANES, 2 * half), bf16), ((LANES, LANES), f32)],
+        4,
         scratch=[pltpu.VMEM((samples, LANES), bf16)],
-        count=7,
-    )(place, kept, near, other_core(kept), other_core(near), vals, gene)
+    )(place, mine, other_core(mine), gene)
     keep, passed = call(
         score_kernel,
         [((LANES, LANES), f32)] * 2,
+        11,
         scratch=[pltpu.VMEM((samples, variants), bf16)],
-        count=6 + rows,
-    )(place, gene, power, turned, weighted, low, *[dose[m] for m in (0, 4, 2, 6, 1, 5, 3, 7)])
+    )(place, gene, power, turned, weighted, low, d0, d1, d4, d26, d537)
     return keep + other_core(passed)
 
 

time: 42 us -> 38.5 us (0.917)
  starting transfers between devices: 15 us -> 11.9 us
  local copies, waits for them, and re-layouts: 3.14 us -> 2.3 us
    ppermute x10 -> x7, starting transfers between devices: 14.4 us -> 11.7 us  [swap(): return lax.ppermute(x, 'row', [(i, i ^ m) for i in range(rows)])]
    unnamed x18 -> x16, local copies, waits for them, and re-layouts: 3.12 us -> 2.3 us
    ppermute x10 -> x7, waiting for transfers between devices: 16.4 us -> 17.1 us  [swap(): return lax.ppermute(x, 'row', [(i, i ^ m) for i in range(rows)])]
    ppermute x4 -> x2, starting transfers between devices: 0.58 us -> 0.14 us  [other_core(): return lax.ppermute(x, 'col', [(0, 1), (1, 0)])]
    ppermute x4 -> x2, waiting for transfers between devices: 2.13 us -> 1.86 us  [other_core(): return lax.ppermute(x, 'col', [(0, 1), (1, 0)])]
    pallas_call x1 -> x4, Pallas kernels: 1.83 us -> 1.91 us  [the longest x1 1.83 us: near_body(): call(score_kernel, [((LANES, LANES), f32)] * 2, 11, scratch=[pltpu.VMEM((...]
  transfers between devices with their start and end apart: 14 -> 9, of which waited for: 9 -> 6; matrix products, arithmetic and copies ran while one was open for 0% -> 0% of each run, Pallas kernels for 3% -> 6%
where the time goes in v4:
time: 38.5 us; the launch traced here: 38.3 us
  waiting for transfers between devices  19 us (49%)
  starting transfers between devices  11.9 us (31%)
  Pallas kernels  4.29 us (11%)
  local copies, waits for them, and re-layouts  2.3 us (6%)
  other arithmetic  0.75 us (2%)
    ppermute x7, waiting for transfers between devices, swap(): return lax.ppermute(x, 'row', [(i, i ^ m) for i in range(rows)])  17.1 us
    ppermute x7, starting transfers between devices, swap(): return lax.ppermute(x, 'row', [(i, i ^ m) for i in range(rows)])  11.7 us
    unnamed x16, local copies, waits for them, and re-layouts  2.3 us
    ppermute x2, waiting for transfers between devices, other_core(): return lax.ppermute(x, 'col', [(0, 1), (1, 0)])  1.86 us
    pallas_call x1, Pallas kernels, near_body(): call(score_kernel, [((LANES, LANES), f32)] * 2, 11, scratch=[pltpu.VMEM((...  1.83 us
    pallas_call x1, Pallas kernels, near_body(): call(weight_kernel, [((2 * half, samples), bf16), ((LANES, 2 * half), bf1...  1.38 us
    pallas_call x1, Pallas kernels, near_body(): call(route_kernel, [((panel, half + 2 * LANES), bf16), ((part, 2 * LANES)...  1 us
  transfers between devices with their start and end apart: 9, of which 6 were waited for; matrix products, arithmetic and copies ran while one was open for 0% of the time, Pallas kernels for 6%

profile of v4, /device:TPU:0, one launch (start us, length us, event | category | flops | bytes accessed | tf_op | source)
XLA Modules:
  0.0 38.3 jit_solution(14899164541653029346)
XLA Ops:
  0.0 0.9 %copy-done = bf16[64,1536]{1,0:T(8,128)(2,1)S(1)} copy-done((bf16[64,1536]{1,0:T(8,128)(2,1)S(1)}, bf16[64,1536]{1,0:T(8,128)(2,1)}, u32[]{:S(2)}) %copy-start) | copy-done | bytes 196632
  0.9 4.1 %collective-permute-start.1 = (bf16[64,768]{1,0:T(8,128)(2,1)S(1)}, bf16[64,768]{1,0:T(8,128)(2,1)S(1)}, u32[]{:S(2)}, u32[]{:S(2)}) collective-permute-start(bf16[64,768]{1,0:T(8,128)(2,1)S(1)} %constant_dynamic-slice_fusion.refs_0_), channel_id=1, source_target_pairs={{0,8},{2,10},{4,12},{6,14},{8,0},{10,2},{12,4},{14,6},{1,9},{3,11}... | collective-permute-start | bytes 294920 | tf_op jit(solution)/shard_map/ppermute | solution.py:293
  5.0 1.5 %collective-permute-start.2 = (bf16[64,768]{1,0:T(8,128)(2,1)S(1)}, bf16[64,768]{1,0:T(8,128)(2,1)S(1)}, u32[]{:S(2)}, u32[]{:S(2)}) collective-permute-start(bf16[64,768]{1,0:T(8,128)(2,1)S(1)} %constant_dynamic-slice_fusion.refs_0_), channel_id=1, source_target_pairs={{0,2},{2,0},{4,6},{6,4},{8,10},{10,8},{12,14},{14,12},{1,3},{3,1},... | collective-permute-start | bytes 294920 | tf_op jit(solution)/shard_map/ppermute | solution.py:293
  6.6 0.1 pad_add_fusion.place_ref
  6.7 0.6 %copy-done.6 = s32[1024]{0:T(1024)S(1)} copy-done((s32[1024]{0:T(1024)S(1)}, s32[1024]{0:T(1024)}, u32[]{:S(2)}) %copy-start.6) | copy-done | bytes 4120
  7.3 0.0 copy-done.3
  7.3 1.0 %shard_map.82 = (bf16[64,512]{1,0:T(8,128)(2,1)S(1)}, bf16[32,256]{1,0:T(8,128)(2,1)S(1)}, bf16[32,128]{1,0:T(8,128)(2,1)S(1)}, bf16[32,128]{1,0:T(8,128)(2,1)S(1)}, f32[128,128]{1,0:T(8,128)S(1)}) custom-call(s32[2]{0:T(128)S(1)} %pad_add_fusion.place_ref, s32[8,128]{1,0:T(8,128)S(1)} %bitcast.7, f32[8,128]{1,0:T(8,128)S(1)} %bitcast.8, ...), custom_call_target="tpu_custom_call" | custom-call | tf_op jit(solution)/shard_map/pallas_call | solution.py:303
  8.3 0.6 %collective-permute-start = (bf16[64,512]{1,0:T(8,128)(2,1)S(1)}, bf16[64,512]{1,0:T(8,128)(2,1)S(1)}, u32[]{:S(2)}, u32[]{:S(2)}) collective-permute-start(bf16[64,512]{1,0:T(8,128)(2,1)S(1)} %get-tuple-element.19), channel_id=1, source_target_pairs={{0,2},{2,0},{4,6},{6,4},{8,10},{10,8},{12,14},{14,12},{1,3},{3,1},... | collective-permute-start | bytes 196616 | tf_op jit(solution)/shard_map/ppermute | solution.py:293
  8.9 3.8 %collective-permute-done.r1_ref = bf16[64,512]{1,0:T(8,128)(2,1)S(1)} collective-permute-done((bf16[64,512]{1,0:T(8,128)(2,1)S(1)}, bf16[64,512]{1,0:T(8,128)(2,1)S(1)}, u32[]{:S(2)}, u32[]{:S(2)}) %collective-permute-start) | collective-permute-done | bytes 65568 | tf_op jit(solution)/shard_map/ppermute | solution.py:293
  12.7 0.4 %collective-permute-start.3 = (bf16[64,768]{1,0:T(8,128)(2,1)S(1)}, bf16[64,768]{1,0:T(8,128)(2,1)S(1)}, u32[]{:S(2)}, u32[]{:S(2)}) collective-permute-start(bf16[64,768]{1,0:T(8,128)(2,1)S(1)} %shard_map.83), channel_id=1, source_target_pairs={{0,8},{2,10},{4,12},{6,14},{8,0},{10,2},{12,4},{14,6},{1,9},{3,11}... | collective-permute-start | bytes 294920 | tf_op jit(solution)/shard_map/ppermute | solution.py:293
  13.1 1.6 %collective-permute-start.6 = (bf16[64,1536]{1,0:T(8,128)(2,1)S(1)}, bf16[64,1536]{1,0:T(8,128)(2,1)S(1)}, u32[]{:S(2)}, u32[]{:S(2)}) collective-permute-start(bf16[64,1536]{1,0:T(8,128)(2,1)S(1)} %pad_maximum_fusion.1), channel_id=1, source_target_pairs={{0,4},{2,6},{4,0},{6,2},{8,12},{10,14},{12,8},{14,10},{1,5},{3,7},... | collective-permute-start | bytes 589832 | tf_op jit(solution)/shard_map/ppermute | solution.py:293
  14.8 3.6 %collective-permute-done.3.r4_ref = bf16[64,768]{1,0:T(8,128)(2,1)S(1)} collective-permute-done((bf16[64,768]{1,0:T(8,128)(2,1)S(1)}, bf16[64,768]{1,0:T(8,128)(2,1)S(1)}, u32[]{:S(2)}, u32[]{:S(2)}) %collective-permute-start.3) | collective-permute-done | bytes 98336 | tf_op jit(solution)/shard_map/ppermute | solution.py:293
  18.4 2.5 %collective-permute-start.4 = (bf16[64,1280]{1,0:T(8,128)(2,1)S(1)}, bf16[64,1280]{1,0:T(8,128)(2,1)S(1)}, u32[]{:S(2)}, u32[]{:S(2)}) collective-permute-start(bf16[64,1280]{1,0:T(8,128)(2,1)S(1)} %get-tuple-element.24), channel_id=1, source_target_pairs={{0,4},{2,6},{4,0},{6,2},{8,12},{10,14},{12,8},{14,10},{1,5},{3,7},... | collective-permute-start | bytes 491528 | tf_op jit(solution)/shard_map/ppermute | solution.py:293
  20.9 3.3 %collective-permute-done.4.far_ref = bf16[64,1280]{1,0:T(8,128)(2,1)S(1)} collective-permute-done((bf16[64,1280]{1,0:T(8,128)(2,1)S(1)}, bf16[64,1280]{1,0:T(8,128)(2,1)S(1)}, u32[]{:S(2)}, u32[]{:S(2)}) %collective-permute-start.4) | collective-permute-done | bytes 163872 | tf_op jit(solution)/shard_map/ppermute | solution.py:293
  24.2 0.7 %copy-done.7 = f32[256]{0:T(256)S(1)} copy-done((f32[256]{0:T(256)S(1)}, f32[256]{0:T(256)}, u32[]{:S(2)}) %copy-start.7) | copy-done | bytes 1048
  24.9 0.1 collective-permute-start.5
  25.0 1.0 %collective-permute-start.7 = (bf16[64,2304]{1,0:T(8,128)(2,1)S(1)}, bf16[64,2304]{1,0:T(8,128)(2,1)S(1)}, u32[]{:S(2)}, u32[]{:S(2)}) collective-permute-start(bf16[64,2304]{1,0:T(8,128)(2,1)S(1)} %pad_maximum_fusion), channel_id=1, source_target_pairs={{0,2},{2,0},{4,6},{6,4},{8,10},{10,8},{12,14},{14,12},{1,3},{3,1},... | collective-permute-start | bytes 884744 | tf_op jit(solution)/shard_map/ppermute | solution.py:293
  26.0 0.6 %collective-permute-done.5.other_ref = bf16[64,2816]{1,0:T(8,128)(2,1)S(1)} collective-permute-done((bf16[64,2816]{1,0:T(8,128)(2,1)S(1)}, bf16[64,2816]{1,0:T(8,128)(2,1)S(1)}, u32[]{:S(2)}, u32[]{:S(2)}) %collective-permute-start.5) | collective-permute-done | bytes 360480 | tf_op jit(solution)/shard_map/ppermute | solution.py:296
  26.7 1.4 %shard_map.86 = (bf16[512,512]{1,0:T(8,128)(2,1)S(1)}, bf16[128,512]{1,0:T(8,128)(2,1)S(1)}, bf16[128,512]{1,0:T(8,128)(2,1)S(1)}, f32[128,128]{1,0:T(8,128)S(1)}) custom-call(s32[2]{0:T(128)S(1)} %pad_add_fusion.place_ref, bf16[64,2816]{1,0:T(8,128)(2,1)S(1)} %shard_map.85.mine_ref, bf16[64,2816]{1,0:T(8,128)(2,1)S(1)} %collective-permute-done.5.other_ref, ...), custom_call_target="tpu_custom_call" | custom-call | tf_op jit(solution)/shard_map/pallas_call | solution.py:329
  28.1 6.5 %collective-permute-done.7.refs_4_ = bf16[64,2304]{1,0:T(8,128)(2,1)S(1)} collective-permute-done((bf16[64,2304]{1,0:T(8,128)(2,1)S(1)}, bf16[64,2304]{1,0:T(8,128)(2,1)S(1)}, u32[]{:S(2)}, u32[]{:S(2)}) %collective-permute-start.7) | collective-permute-done | bytes 294944 | tf_op jit(solution)/shard_map/ppermute | solution.py:293
  34.5 1.8 %shard_map.87 = (f32[128,128]{1,0:T(8,128)S(1)}, f32[128,128]{1,0:T(8,128)S(1)}) custom-call(s32[2]{0:T(128)S(1)} %pad_add_fusion.place_ref, f32[128,128]{1,0:T(8,128)S(1)} %get-tuple-element.18.gene_ref, f32[128,128]{1,0:T(8,128)S(1)} %get-tuple-element.25.power_ref, bf16[512,512]{1,0:T(8,128)(2,1)S(1)} %get-tuple-element.26.turned_ref, ...), custom_call_target="tpu_custom_call" | custom-call | tf_op jit(solution)/shard_map/pallas_call | solution.py:335
  36.3 0.1 collective-permute-start.8
  36.4 1.2 %collective-permute-done.8 = f32[128,128]{1,0:T(8,128)S(1)} collective-permute-done((f32[128,128]{1,0:T(8,128)S(1)}, f32[128,128]{1,0:T(8,128)S(1)}, u32[]{:S(2)}, u32[]{:S(2)}) %collective-permute-start.8) | collective-permute-done | bytes 65568 | tf_op jit(solution)/shard_map/ppermute | solution.py:296
  37.7 0.6 %add.7 = f32[128,128]{1,0:T(8,128)} add(f32[128,128]{1,0:T(8,128)S(1)} %get-tuple-element.29, f32[128,128]{1,0:T(8,128)S(1)} %collective-permute-done.8) | non-fusion elementwise | flops 16384 | bytes 196608 | tf_op jit(solution)/shard_map/add | solution.py:341
  (21 shorter events, 0.2 us)
Async XLA Ops:
  0.0 0.9 %copy-start = (bf16[64,1536]{1,0:T(8,128)(2,1)S(1)}, bf16[64,1536]{1,0:T(8,128)(2,1)}, u32[]{:S(2)}) copy-start(bf16[64,1536]{1,0:T(8,128)(2,1)} %param.11) | copy-start | bytes 589828
  0.0 6.6 %copy-start.2 = (bf16[64,1024]{1,0:T(8,128)(2,1)S(1)}, bf16[64,1024]{1,0:T(8,128)(2,1)}, u32[]{:S(2)}) copy-start(bf16[64,1024]{1,0:T(8,128)(2,1)} %expr_ref.1) | copy-start | bytes 393220
  0.9 5.7 %copy-start.1 = (bf16[64,256]{1,0:T(8,128)(2,1)S(1)}, bf16[64,256]{1,0:T(8,128)(2,1)}, u32[]{:S(2)}) copy-start(bf16[64,256]{1,0:T(8,128)(2,1)} %vecs_ref.5) | copy-start | bytes 98308
  0.9 11.7 %collective-permute-start.1 = (bf16[64,768]{1,0:T(8,128)(2,1)S(1)}, bf16[64,768]{1,0:T(8,128)(2,1)S(1)}, u32[]{:S(2)}, u32[]{:S(2)}) collective-permute-start(bf16[64,768]{1,0:T(8,128)(2,1)S(1)} %constant_dynamic-slice_fusion.refs_0_), channel_id=1, source_target_pairs={{0,8},{2,10},{4,12},{6,14},{8,0},{10,2},{12,4},{14,6},{1,9},{3,11}... | collective-permute-start | bytes 294920 | tf_op jit(solution)/shard_map/ppermute | solution.py:293
  5.0 7.6 %collective-permute-start.2 = (bf16[64,768]{1,0:T(8,128)(2,1)S(1)}, bf16[64,768]{1,0:T(8,128)(2,1)S(1)}, u32[]{:S(2)}, u32[]{:S(2)}) collective-permute-start(bf16[64,768]{1,0:T(8,128)(2,1)S(1)} %constant_dynamic-slice_fusion.refs_0_), channel_id=1, source_target_pairs={{0,2},{2,0},{4,6},{6,4},{8,10},{10,8},{12,14},{14,12},{1,3},{3,1},... | collective-permute-start | bytes 294920 | tf_op jit(solution)/shard_map/ppermute | solution.py:293
  6.6 0.7 %copy-start.6 = (s32[1024]{0:T(1024)S(1)}, s32[1024]{0:T(1024)}, u32[]{:S(2)}) copy-start(s32[1024]{0:T(1024)} %param.14) | copy-start | bytes 12292
  6.6 0.7 %copy-start.5 = (s32[1024]{0:T(1024)S(1)}, s32[1024]{0:T(1024)}, u32[]{:S(2)}) copy-start(s32[1024]{0:T(1024)} %param.13) | copy-start | bytes 12292
  6.6 0.7 %copy-start.4 = (f32[1024]{0:T(1024)S(1)}, f32[1024]{0:T(1024)}, u32[]{:S(2)}) copy-start(f32[1024]{0:T(1024)} %param.12) | copy-start | bytes 12292
  6.6 0.7 %copy-start.3 = (s32[1024]{0:T(1024)S(1)}, s32[1024]{0:T(1024)}, u32[]{:S(2)}) copy-start(s32[1024]{0:T(1024)} %param.15) | copy-start | bytes 12292
  8.3 4.3 %collective-permute-start = (bf16[64,512]{1,0:T(8,128)(2,1)S(1)}, bf16[64,512]{1,0:T(8,128)(2,1)S(1)}, u32[]{:S(2)}, u32[]{:S(2)}) collective-permute-start(bf16[64,512]{1,0:T(8,128)(2,1)S(1)} %get-tuple-element.19), channel_id=1, source_target_pairs={{0,2},{2,0},{4,6},{6,4},{8,10},{10,8},{12,14},{14,12},{1,3},{3,1},... | collective-permute-start | bytes 196616 | tf_op jit(solution)/shard_map/ppermute | solution.py:293
  12.7 5.7 %collective-permute-start.3 = (bf16[64,768]{1,0:T(8,128)(2,1)S(1)}, bf16[64,768]{1,0:T(8,128)(2,1)S(1)}, u32[]{:S(2)}, u32[]{:S(2)}) collective-permute-start(bf16[64,768]{1,0:T(8,128)(2,1)S(1)} %shard_map.83), channel_id=1, source_target_pairs={{0,8},{2,10},{4,12},{6,14},{8,0},{10,2},{12,4},{14,6},{1,9},{3,11}... | collective-permute-start | bytes 294920 | tf_op jit(solution)/shard_map/ppermute | solution.py:293
  13.1 11.9 %collective-permute-start.6 = (bf16[64,1536]{1,0:T(8,128)(2,1)S(1)}, bf16[64,1536]{1,0:T(8,128)(2,1)S(1)}, u32[]{:S(2)}, u32[]{:S(2)}) collective-permute-start(bf16[64,1536]{1,0:T(8,128)(2,1)S(1)} %pad_maximum_fusion.1), channel_id=1, source_target_pairs={{0,4},{2,6},{4,0},{6,2},{8,12},{10,14},{12,8},{14,10},{1,5},{3,7},... | collective-permute-start | bytes 589832 | tf_op jit(solution)/shard_map/ppermute | solution.py:293
  18.4 5.8 %collective-permute-start.4 = (bf16[64,1280]{1,0:T(8,128)(2,1)S(1)}, bf16[64,1280]{1,0:T(8,128)(2,1)S(1)}, u32[]{:S(2)}, u32[]{:S(2)}) collective-permute-start(bf16[64,1280]{1,0:T(8,128)(2,1)S(1)} %get-tuple-element.24), channel_id=1, source_target_pairs={{0,4},{2,6},{4,0},{6,2},{8,12},{10,14},{12,8},{14,10},{1,5},{3,7},... | collective-permute-start | bytes 491528 | tf_op jit(solution)/shard_map/ppermute | solution.py:293
  24.2 0.7 %copy-start.7 = (f32[256]{0:T(256)S(1)}, f32[256]{0:T(256)}, u32[]{:S(2)}) copy-start(f32[256]{0:T(256)} %param.9) | copy-start | bytes 3076
  24.9 1.7 %collective-permute-start.5 = (bf16[64,2816]{1,0:T(8,128)(2,1)S(1)}, bf16[64,2816]{1,0:T(8,128)(2,1)S(1)}, u32[]{:S(2)}, u32[]{:S(2)}) collective-permute-start(bf16[64,2816]{1,0:T(8,128)(2,1)S(1)} %shard_map.85.mine_ref), channel_id=1, source_target_pairs={{0,1},{1,0},{2,3},{3,2},{4,5},{5,4},{6,7},{7,6},{8,9},{9,8},{10,11... | collective-permute-start | bytes 1081352 | tf_op jit(solution)/shard_map/ppermute | solution.py:296
  25.0 9.5 %collective-permute-start.7 = (bf16[64,2304]{1,0:T(8,128)(2,1)S(1)}, bf16[64,2304]{1,0:T(8,128)(2,1)S(1)}, u32[]{:S(2)}, u32[]{:S(2)}) collective-permute-start(bf16[64,2304]{1,0:T(8,128)(2,1)S(1)} %pad_maximum_fusion), channel_id=1, source_target_pairs={{0,2},{2,0},{4,6},{6,4},{8,10},{10,8},{12,14},{14,12},{1,3},{3,1},... | collective-permute-start | bytes 884744 | tf_op jit(solution)/shard_map/ppermute | solution.py:293
  36.3 1.3 %collective-permute-start.8 = (f32[128,128]{1,0:T(8,128)S(1)}, f32[128,128]{1,0:T(8,128)S(1)}, u32[]{:S(2)}, u32[]{:S(2)}) collective-permute-start(f32[128,128]{1,0:T(8,128)S(1)} %get-tuple-element.30), channel_id=1, source_target_pairs={{0,1},{1,0},{2,3},{3,2},{4,5},{5,4},{6,7},{7,6},{8,9},{9,8},{10,11... | collective-permute-start | bytes 196616 | tf_op jit(solution)/shard_map/ppermute | solution.py:296

commit v5 on v4

--- a/solution.py
+++ b/solution.py
@@ -101,7 +101,8 @@
 
 
 def route_kernel(
-    place_ref, owner_ref, delta_ref, start_ref, valid_ref, vecs_ref, expr_ref, ahead_ref, e46_ref, e2_ref, e0_ref, gene_ref
+    place_ref, owner_ref, delta_ref, start_ref, valid_ref, vals_ref, vecs_ref, expr_ref,
+    ahead_ref, e46_ref, e2_ref, e0_ref, gene_ref, terms_ref,
 ):
     slices = owner_ref.shape[0]
     capacity = LANES // slices
@@ -135,6 +136,12 @@
             line = ref[s : s + 1, :].astype(f32)
             figures = jnp.where(lane == i, jnp.sum(mine * line, axis=1, keepdims=True), figures)
         gene_ref[s * capacity : (s + 1) * capacity, :] = figures
+    vals = vals_ref[...]
+    high = vals.astype(bf16).astype(f32)
+    middle = (vals - high).astype(bf16).astype(f32)
+    term = lax.broadcasted_iota(jnp.int32, terms_ref.shape, 0)
+    terms = jnp.where(term == 0, high, jnp.where(term == 1, middle, jnp.where(term == 2, vals - high - middle, 0.0)))
+    terms_ref[...] = terms.astype(bf16)
     ahead_ref[:, :half] = vecs_ref[...]
     left, right = slice(0, LANES), slice(LANES, 2 * LANES)
     upper, lower = slice(0, part), slice(part, 2 * part)
@@ -153,7 +160,7 @@
         ref[down, side] = block.T.astype(bf16)
 
 
-def second_kernel(vecs_ref, r1_ref, e46_ref, d4_any, d1_any, out_ref):
+def second_kernel(vecs_ref, r1_ref, e46_ref, d4_any, d1_any, d2_any, out_ref):
     half = vecs_ref.shape[1]
     part = e46_ref.shape[0]
     out_ref[:, :half] = vecs_ref[...]
@@ -162,7 +169,7 @@
     out_ref[part:, 2 * half :] = r1_ref[part:, half:]
 
 
-def third_kernel(vecs_ref, r1_ref, r4_ref, e2_ref, e0_ref, out_ref, kept_ref):
+def third_kernel(vecs_ref, r1_ref, r4_ref, e2_ref, e0_ref, d6_any, d5_any, d3_any, out_ref, kept_ref):
     half = vecs_ref.shape[1]
     part = e0_ref.shape[0]
     for ref, own, at in ((out_ref, e2_ref, LANES), (kept_ref, e0_ref, 0)):
@@ -177,17 +184,12 @@
         ref[part:, right] = r4_ref[part:, side]
 
 
-def pack_kernel(kept_ref, far_ref, vals_ref, out_ref):
+def pack_kernel(kept_ref, far_ref, terms_ref, d7_any, out_ref):
     width = kept_ref.shape[1]
     out_ref[:, :width] = kept_ref[...]
     out_ref[:, width : 2 * width] = far_ref[...]
-    vals = vals_ref[...]
-    high = vals.astype(bf16).astype(f32)
-    middle = (vals - high).astype(bf16).astype(f32)
-    low = vals - high - middle
-    row = lax.broadcasted_iota(jnp.int32, (out_ref.shape[0], vals.shape[1]), 0)
-    terms = jnp.where(row == 0, high, jnp.where(row == 1, middle, jnp.where(row == 2, low, 0.0)))
-    out_ref[:, 2 * width :] = terms.astype(bf16)
+    out_ref[: terms_ref.shape[0], 2 * width :] = terms_ref[...]
+    out_ref[terms_ref.shape[0] :, 2 * width :] = jnp.zeros_like(out_ref[terms_ref.shape[0] :, 2 * width :])
 
 
 def weight_kernel(place_ref, mine_ref, other_ref, gene_ref, turned_ref, weighted_ref, low_ref, power_ref, data_scr):
@@ -228,7 +230,7 @@
     *dose_refs, keep_ref, pass_ref, dose_scr = refs
     samples, variants = dose_refs[0].shape
     chunks = [(ref, at) for ref in dose_refs for at in range(0, ref.shape[1], variants)]
-    order = [0, 1, 2, 5, 3, 6, 4, 7]
+    order = range(8)
     for m, (ref, at) in enumerate(chunks[i] for i in order):
         dose_scr[m * samples : (m + 1) * samples, :] = ref[:, at : at + variants]
     rotated = jnp.dot(turned_ref[...], dose_scr[...], preferred_element_type=f32).astype(bf16)
@@ -298,9 +300,8 @@
     d0 = lax.dynamic_slice_in_dim(dosage, core * variants, variants, 1)
     d4 = swap(d0, 4)
     d1 = swap(d0, 1)
-    d26 = swap(jnp.concatenate([d0, d4], axis=1), 2)
-    d537 = swap(jnp.concatenate([d4, d26], axis=1), 1)
-    ahead, e46, e2, e0, gene = call(
+    d2 = swap(d0, 2)
+    ahead, e46, e2, e0, gene, terms = call(
         route_kernel,
         [
             ((panel, half + 2 * LANES), bf16),
@@ -308,24 +309,35 @@
             ((part, LANES), bf16),
             ((part, LANES), bf16),
             ((LANES, LANES), f32),
+            ((16, half), bf16),
         ],
-        7,
+        8,
     )(
         place,
         gene_owner.reshape(rows, LANES),
         delta.reshape(rows, LANES),
         window_start.reshape(rows, LANES),
         window_valid.reshape(rows, LANES),
+        eigvals[None, :],
         eigvecs,
         expression,
     )
     r1 = swap(ahead, 1)
     r4 = swap(
-        call(second_kernel, [((panel, 2 * half + 2 * LANES), bf16)], 5, smem=0, anywhere=2)(eigvecs, r1, e46, d4, d1)[0], 4
-    )
+        call(second_kernel, [((panel, 2 * half + 2 * LANES), bf16)], 6, smem=0, anywhere=3)(
+            eigvecs, r1, e46, d4, d1, d2
+        )[0],
+        4,
+    )
+    d6 = swap(d4, 2)
+    d5 = swap(d4, 1)
+    d3 = swap(d2, 1)
+    d7 = swap(d6, 1)
     width = 4 * half + 2 * LANES
-    out, kept = call(third_kernel, [((panel, width), bf16)] * 2, 5, smem=0)(eigvecs, r1, r4, e2, e0)
-    mine = call(pack_kernel, [((panel, 2 * width + half), bf16)], 3, smem=0)(kept, swap(out, 2), eigvals[None, :])[0]
+    out, kept = call(third_kernel, [((panel, width), bf16)] * 2, 8, smem=0, anywhere=3)(
+        eigvecs, r1, r4, e2, e0, d6, d5, d3
+    )
+    mine = call(pack_kernel, [((panel, 2 * width + half), bf16)], 4, smem=0, anywhere=1)(kept, swap(out, 2), terms, d7)[0]
     turned, weighted, low, power = call(
         weight_kernel,
         [((2 * half, samples), bf16), ((LANES, 2 * half), bf16), ((LANES, 2 * half), bf16), ((LANES, LANES), f32)],
@@ -335,9 +347,9 @@
     keep, passed = call(
         score_kernel,
         [((LANES, LANES), f32)] * 2,
-        11,
+        14,
         scratch=[pltpu.VMEM((samples, variants), bf16)],
-    )(place, gene, power, turned, weighted, low, d0, d1, d4, d26, d537)
+    )(place, gene, power, turned, weighted, low, d0, d1, d4, d5, d2, d3, d6, d7)
     return keep + other_core(passed)
 
 

time: 38.5 us -> 34.7 us (0.901)
  waiting for transfers between devices: 19 us -> 11.4 us
  starting transfers between devices: 11.9 us -> 16.5 us
  local copies, waits for them, and re-layouts: 2.3 us -> 1.64 us
    ppermute x7 -> x10, waiting for transfers between devices: 17.1 us -> 8.56 us  [swap(): return lax.ppermute(x, 'row', [(i, i ^ m) for i in range(rows)])]
    ppermute x7 -> x10, starting transfers between devices: 11.7 us -> 16.3 us  [swap(): return lax.ppermute(x, 'row', [(i, i ^ m) for i in range(rows)])]
    ppermute x2, waiting for transfers between devices: 1.86 us -> 2.79 us  [other_core(): return lax.ppermute(x, 'col', [(0, 1), (1, 0)])]
    unnamed x16, local copies, waits for them, and re-layouts: 2.3 us -> 1.63 us
  transfers between devices with their start and end apart: 9 -> 12, of which waited for: 6 -> 7; matrix products, arithmetic and copies ran while one was open for 0% -> 0% of each run, Pallas kernels for 6% -> 3%
where the time goes in v5:
time: 34.7 us; the launch traced here: 34.6 us
  starting transfers between devices  16.5 us (48%)
  waiting for transfers between devices  11.4 us (33%)
  Pallas kernels  4.28 us (12%)
  local copies, waits for them, and re-layouts  1.64 us (5%)
  other arithmetic  0.71 us (2%)
    ppermute x10, starting transfers between devices, swap(): return lax.ppermute(x, 'row', [(i, i ^ m) for i in range(rows)])  16.3 us
    ppermute x10, waiting for transfers between devices, swap(): return lax.ppermute(x, 'row', [(i, i ^ m) for i in range(rows)])  8.56 us
    ppermute x2, waiting for transfers between devices, other_core(): return lax.ppermute(x, 'col', [(0, 1), (1, 0)])  2.79 us
    pallas_call x1, Pallas kernels, near_body(): call(score_kernel, [((LANES, LANES), f32)] * 2, 14, scratch=[pltpu.VMEM((...  1.84 us
    unnamed x16, local copies, waits for them, and re-layouts  1.63 us
    pallas_call x1, Pallas kernels, near_body(): call(weight_kernel, [((2 * half, samples), bf16), ((LANES, 2 * half), bf1...  1.39 us
    pallas_call x1, Pallas kernels, near_body(): call(route_kernel, [((panel, half + 2 * LANES), bf16), ((part, 2 * LANES)...  1 us
  transfers between devices with their start and end apart: 12, of which 7 were waited for; matrix products, arithmetic and copies ran while one was open for 0% of the time, Pallas kernels for 3%

profile of v5, /device:TPU:0, one launch (start us, length us, event | category | flops | bytes accessed | tf_op | source)
XLA Modules:
  0.0 34.6 jit_solution(991856205985505821)
XLA Ops:
  0.0 0.9 %copy-done = bf16[64,1536]{1,0:T(8,128)(2,1)S(1)} copy-done((bf16[64,1536]{1,0:T(8,128)(2,1)S(1)}, bf16[64,1536]{1,0:T(8,128)(2,1)}, u32[]{:S(2)}) %copy-start) | copy-done | bytes 196632
  0.9 3.1 %collective-permute-start.3 = (bf16[64,768]{1,0:T(8,128)(2,1)S(1)}, bf16[64,768]{1,0:T(8,128)(2,1)S(1)}, u32[]{:S(2)}, u32[]{:S(2)}) collective-permute-start(bf16[64,768]{1,0:T(8,128)(2,1)S(1)} %constant_dynamic-slice_fusion.refs_0_), channel_id=1, source_target_pairs={{0,4},{2,6},{4,0},{6,2},{8,12},{10,14},{12,8},{14,10},{1,5},{3,7},... | collective-permute-start | bytes 294920 | tf_op jit(solution)/shard_map/ppermute | solution.py:295
  4.0 1.5 %collective-permute-start.2 = (bf16[64,768]{1,0:T(8,128)(2,1)S(1)}, bf16[64,768]{1,0:T(8,128)(2,1)S(1)}, u32[]{:S(2)}, u32[]{:S(2)}) collective-permute-start(bf16[64,768]{1,0:T(8,128)(2,1)S(1)} %constant_dynamic-slice_fusion.refs_0_), channel_id=1, source_target_pairs={{0,2},{2,0},{4,6},{6,4},{8,10},{10,8},{12,14},{14,12},{1,3},{3,1},... | collective-permute-start | bytes 294920 | tf_op jit(solution)/shard_map/ppermute | solution.py:295
  5.6 2.6 %collective-permute-start.1 = (bf16[64,768]{1,0:T(8,128)(2,1)S(1)}, bf16[64,768]{1,0:T(8,128)(2,1)S(1)}, u32[]{:S(2)}, u32[]{:S(2)}) collective-permute-start(bf16[64,768]{1,0:T(8,128)(2,1)S(1)} %constant_dynamic-slice_fusion.refs_0_), channel_id=1, source_target_pairs={{0,8},{2,10},{4,12},{6,14},{8,0},{10,2},{12,4},{14,6},{1,9},{3,11}... | collective-permute-start | bytes 294920 | tf_op jit(solution)/shard_map/ppermute | solution.py:295
  8.2 0.6 %copy-done.6 = s32[1024]{0:T(1024)S(1)} copy-done((s32[1024]{0:T(1024)S(1)}, s32[1024]{0:T(1024)}, u32[]{:S(2)}) %copy-start.6) | copy-done | bytes 4120
  8.9 1.0 %shard_map.82 = (bf16[64,512]{1,0:T(8,128)(2,1)S(1)}, bf16[32,256]{1,0:T(8,128)(2,1)S(1)}, bf16[32,128]{1,0:T(8,128)(2,1)S(1)}, bf16[32,128]{1,0:T(8,128)(2,1)S(...) custom-call(s32[2]{0:T(128)S(1)} %pad_add_fusion.place_ref, s32[8,128]{1,0:T(8,128)S(1)} %bitcast.7, ...), custom_call_target="tpu_custom_call" | custom-call | tf_op jit(solution)/shard_map/pallas_call | solution.py:304
  9.9 0.6 %collective-permute-start = (bf16[64,512]{1,0:T(8,128)(2,1)S(1)}, bf16[64,512]{1,0:T(8,128)(2,1)S(1)}, u32[]{:S(2)}, u32[]{:S(2)}) collective-permute-start(bf16[64,512]{1,0:T(8,128)(2,1)S(1)} %get-tuple-element.20), channel_id=1, source_target_pairs={{0,2},{2,0},{4,6},{6,4},{8,10},{10,8},{12,14},{14,12},{1,3},{3,1},... | collective-permute-start | bytes 196616 | tf_op jit(solution)/shard_map/ppermute | solution.py:295
  10.5 2.0 %collective-permute-done.1.d4_any.refs_2_ = bf16[64,768]{1,0:T(8,128)(2,1)S(1)} collective-permute-done((bf16[64,768]{1,0:T(8,128)(2,1)S(1)}, bf16[64,768]{1,0:T(8,128)(2,1)S(1)}, u32[]{:S(2)}, u32[]{:S(2)}) %collective-permute-start.1) | collective-permute-done | bytes 98336 | tf_op jit(solution)/shard_map/ppermute | solution.py:295
  12.5 0.6 %collective-permute-start.6 = (bf16[64,768]{1,0:T(8,128)(2,1)S(1)}, bf16[64,768]{1,0:T(8,128)(2,1)S(1)}, u32[]{:S(2)}, u32[]{:S(2)}) collective-permute-start(bf16[64,768]{1,0:T(8,128)(2,1)S(1)} %collective-permute-done.1.d4_any.refs_2_), channel_id=1, source_target_pairs={{0,2},{2,0},{4,6},{6,4},{8,10},{10,8},{12,14},{14,12},{1,3},{3,1},... | collective-permute-start | bytes 294920 | tf_op jit(solution)/shard_map/ppermute | solution.py:295
  13.1 0.1 collective-permute-start.5
  13.2 1.3 %collective-permute-start.7 = (bf16[64,768]{1,0:T(8,128)(2,1)S(1)}, bf16[64,768]{1,0:T(8,128)(2,1)S(1)}, u32[]{:S(2)}, u32[]{:S(2)}) collective-permute-start(bf16[64,768]{1,0:T(8,128)(2,1)S(1)} %collective-permute-done.3.d2_any.refs_4_), channel_id=1, source_target_pairs={{0,2},{2,0},{4,6},{6,4},{8,10},{10,8},{12,14},{14,12},{1,3},{3,1},... | collective-permute-start | bytes 294920 | tf_op jit(solution)/shard_map/ppermute | solution.py:295
  14.5 3.3 %collective-permute-start.4 = (bf16[64,768]{1,0:T(8,128)(2,1)S(1)}, bf16[64,768]{1,0:T(8,128)(2,1)S(1)}, u32[]{:S(2)}, u32[]{:S(2)}) collective-permute-start(bf16[64,768]{1,0:T(8,128)(2,1)S(1)} %shard_map.83), channel_id=1, source_target_pairs={{0,8},{2,10},{4,12},{6,14},{8,0},{10,2},{12,4},{14,6},{1,9},{3,11}... | collective-permute-start | bytes 294920 | tf_op jit(solution)/shard_map/ppermute | solution.py:295
  17.8 0.7 %collective-permute-done.7.d3_any.refs_5_ = bf16[64,768]{1,0:T(8,128)(2,1)S(1)} collective-permute-done((bf16[64,768]{1,0:T(8,128)(2,1)S(1)}, bf16[64,768]{1,0:T(8,128)(2,1)S(1)}, u32[]{:S(2)}, u32[]{:S(2)}) %collective-permute-start.7) | collective-permute-done | bytes 98336 | tf_op jit(solution)/shard_map/ppermute | solution.py:295
  18.5 0.3 collective-permute-done.5.d6_any.refs_6_
  18.8 1.6 %collective-permute-done.4.r4_ref = bf16[64,768]{1,0:T(8,128)(2,1)S(1)} collective-permute-done((bf16[64,768]{1,0:T(8,128)(2,1)S(1)}, bf16[64,768]{1,0:T(8,128)(2,1)S(1)}, u32[]{:S(2)}, u32[]{:S(2)}) %collective-permute-start.4) | collective-permute-done | bytes 98336 | tf_op jit(solution)/shard_map/ppermute | solution.py:295
  20.5 2.5 %collective-permute-start.8 = (bf16[64,1280]{1,0:T(8,128)(2,1)S(1)}, bf16[64,1280]{1,0:T(8,128)(2,1)S(1)}, u32[]{:S(2)}, u32[]{:S(2)}) collective-permute-start(bf16[64,1280]{1,0:T(8,128)(2,1)S(1)} %get-tuple-element.25), channel_id=1, source_target_pairs={{0,4},{2,6},{4,0},{6,2},{8,12},{10,14},{12,8},{14,10},{1,5},{3,7},... | collective-permute-start | bytes 491528 | tf_op jit(solution)/shard_map/ppermute | solution.py:295
  23.0 0.7 %collective-permute-start.9 = (bf16[64,768]{1,0:T(8,128)(2,1)S(1)}, bf16[64,768]{1,0:T(8,128)(2,1)S(1)}, u32[]{:S(2)}, u32[]{:S(2)}) collective-permute-start(bf16[64,768]{1,0:T(8,128)(2,1)S(1)} %collective-permute-done.5.d6_any.refs_6_), channel_id=1, source_target_pairs={{0,2},{2,0},{4,6},{6,4},{8,10},{10,8},{12,14},{14,12},{1,3},{3,1},... | collective-permute-start | bytes 294920 | tf_op jit(solution)/shard_map/ppermute | solution.py:295
  23.7 4.0 %collective-permute-done.9.d7_any.refs_7_ = bf16[64,768]{1,0:T(8,128)(2,1)S(1)} collective-permute-done((bf16[64,768]{1,0:T(8,128)(2,1)S(1)}, bf16[64,768]{1,0:T(8,128)(2,1)S(1)}, u32[]{:S(2)}, u32[]{:S(2)}) %collective-permute-start.9) | collective-permute-done | bytes 98336 | tf_op jit(solution)/shard_map/ppermute | solution.py:295
  27.7 1.7 %collective-permute-done.10.other_ref = bf16[64,2816]{1,0:T(8,128)(2,1)S(1)} collective-permute-done((bf16[64,2816]{1,0:T(8,128)(2,1)S(1)}, bf16[64,2816]{1,0:T(8,128)(2,1)S(1)}, u32[]{:S(2)}, u32[]{:S(2)}) %collective-permute-start.10) | collective-permute-done | bytes 360480 | tf_op jit(solution)/shard_map/ppermute | solution.py:298
  29.4 1.4 %shard_map.86 = (bf16[512,512]{1,0:T(8,128)(2,1)S(1)}, bf16[128,512]{1,0:T(8,128)(2,1)S(1)}, bf16[128,512]{1,0:T(8,128)(2,1)S(1)}, f32[128,128]{1,0:T(8,128)S(1)}) custom-call(s32[2]{0:T(128)S(1)} %pad_add_fusion.place_ref, bf16[64,2816]{1,0:T(8,128)(2,1)S(1)} %shard_map.85.mine_ref, bf16[64,2816]{1,0:T(8,128)(2,1)S(1)} %collective-permute-done.10.other_ref, ...), custom_call_target="tpu_custom_call" | custom-call | tf_op jit(solution)/shard_map/pallas_call | solution.py:341
  30.8 1.8 %shard_map.87 = (f32[128,128]{1,0:T(8,128)S(1)}, f32[128,128]{1,0:T(8,128)S(1)}) custom-call(s32[2]{0:T(128)S(1)} %pad_add_fusion.place_ref, f32[128,128]{1,0:T(8,128)S(1)} %get-tuple-element.19.gene_ref, f32[128,128]{1,0:T(8,128)S(1)} %get-tuple-element.27.power_ref, bf16[512,512]{1,0:T(8,128)(2,1)S(1)} %get-tuple-element.28.turned_ref, ...), custom_call_target="tpu_custom_call" | custom-call | tf_op jit(solution)/shard_map/pallas_call | solution.py:347
  32.6 0.2 collective-permute-start.11
  32.8 1.1 %collective-permute-done.11 = f32[128,128]{1,0:T(8,128)S(1)} collective-permute-done((f32[128,128]{1,0:T(8,128)S(1)}, f32[128,128]{1,0:T(8,128)S(1)}, u32[]{:S(2)}, u32[]{:S(2)}) %collective-permute-start.11) | collective-permute-done | bytes 65568 | tf_op jit(solution)/shard_map/ppermute | solution.py:298
  33.9 0.6 %add.7 = f32[128,128]{1,0:T(8,128)} add(f32[128,128]{1,0:T(8,128)S(1)} %get-tuple-element.31, f32[128,128]{1,0:T(8,128)S(1)} %collective-permute-done.11) | non-fusion elementwise | flops 16384 | bytes 196608 | tf_op jit(solution)/shard_map/add | solution.py:353
  (25 shorter events, 0.3 us)
Async XLA Ops:
  0.0 0.9 %copy-start = (bf16[64,1536]{1,0:T(8,128)(2,1)S(1)}, bf16[64,1536]{1,0:T(8,128)(2,1)}, u32[]{:S(2)}) copy-start(bf16[64,1536]{1,0:T(8,128)(2,1)} %param.11) | copy-start | bytes 589828
  0.0 8.2 %copy-start.2 = (bf16[64,1024]{1,0:T(8,128)(2,1)S(1)}, bf16[64,1024]{1,0:T(8,128)(2,1)}, u32[]{:S(2)}) copy-start(bf16[64,1024]{1,0:T(8,128)(2,1)} %expr_ref.1) | copy-start | bytes 393220
  0.9 7.3 %copy-start.1 = (bf16[64,256]{1,0:T(8,128)(2,1)S(1)}, bf16[64,256]{1,0:T(8,128)(2,1)}, u32[]{:S(2)}) copy-start(bf16[64,256]{1,0:T(8,128)(2,1)} %vecs_ref.5) | copy-start | bytes 98308
  0.9 12.3 %collective-permute-start.3 = (bf16[64,768]{1,0:T(8,128)(2,1)S(1)}, bf16[64,768]{1,0:T(8,128)(2,1)S(1)}, u32[]{:S(2)}, u32[]{:S(2)}) collective-permute-start(bf16[64,768]{1,0:T(8,128)(2,1)S(1)} %constant_dynamic-slice_fusion.refs_0_), channel_id=1, source_target_pairs={{0,4},{2,6},{4,0},{6,2},{8,12},{10,14},{12,8},{14,10},{1,5},{3,7},... | collective-permute-start | bytes 294920 | tf_op jit(solution)/shard_map/ppermute | solution.py:295
  4.0 10.5 %collective-permute-start.2 = (bf16[64,768]{1,0:T(8,128)(2,1)S(1)}, bf16[64,768]{1,0:T(8,128)(2,1)S(1)}, u32[]{:S(2)}, u32[]{:S(2)}) collective-permute-start(bf16[64,768]{1,0:T(8,128)(2,1)S(1)} %constant_dynamic-slice_fusion.refs_0_), channel_id=1, source_target_pairs={{0,2},{2,0},{4,6},{6,4},{8,10},{10,8},{12,14},{14,12},{1,3},{3,1},... | collective-permute-start | bytes 294920 | tf_op jit(solution)/shard_map/ppermute | solution.py:295
  5.6 6.9 %collective-permute-start.1 = (bf16[64,768]{1,0:T(8,128)(2,1)S(1)}, bf16[64,768]{1,0:T(8,128)(2,1)S(1)}, u32[]{:S(2)}, u32[]{:S(2)}) collective-permute-start(bf16[64,768]{1,0:T(8,128)(2,1)S(1)} %constant_dynamic-slice_fusion.refs_0_), channel_id=1, source_target_pairs={{0,8},{2,10},{4,12},{6,14},{8,0},{10,2},{12,4},{14,6},{1,9},{3,11}... | collective-permute-start | bytes 294920 | tf_op jit(solution)/shard_map/ppermute | solution.py:295
  8.1 0.7 %copy-start.6 = (s32[1024]{0:T(1024)S(1)}, s32[1024]{0:T(1024)}, u32[]{:S(2)}) copy-start(s32[1024]{0:T(1024)} %param.14) | copy-start | bytes 12292
  8.1 0.7 %copy-start.5 = (s32[1024]{0:T(1024)S(1)}, s32[1024]{0:T(1024)}, u32[]{:S(2)}) copy-start(s32[1024]{0:T(1024)} %param.13) | copy-start | bytes 12292
  8.2 0.7 %copy-start.4 = (f32[1024]{0:T(1024)S(1)}, f32[1024]{0:T(1024)}, u32[]{:S(2)}) copy-start(f32[1024]{0:T(1024)} %param.12) | copy-start | bytes 12292
  8.2 0.7 %copy-start.3 = (s32[1024]{0:T(1024)S(1)}, s32[1024]{0:T(1024)}, u32[]{:S(2)}) copy-start(s32[1024]{0:T(1024)} %param.15) | copy-start | bytes 12292
  8.2 0.7 %copy-start.7 = (f32[256]{0:T(256)S(1)}, f32[256]{0:T(256)}, u32[]{:S(2)}) copy-start(f32[256]{0:T(256)} %param.9) | copy-start | bytes 3076
  9.9 4.6 %collective-permute-start = (bf16[64,512]{1,0:T(8,128)(2,1)S(1)}, bf16[64,512]{1,0:T(8,128)(2,1)S(1)}, u32[]{:S(2)}, u32[]{:S(2)}) collective-permute-start(bf16[64,512]{1,0:T(8,128)(2,1)S(1)} %get-tuple-element.20), channel_id=1, source_target_pairs={{0,2},{2,0},{4,6},{6,4},{8,10},{10,8},{12,14},{14,12},{1,3},{3,1},... | collective-permute-start | bytes 196616 | tf_op jit(solution)/shard_map/ppermute | solution.py:295
  12.5 6.0 %collective-permute-start.6 = (bf16[64,768]{1,0:T(8,128)(2,1)S(1)}, bf16[64,768]{1,0:T(8,128)(2,1)S(1)}, u32[]{:S(2)}, u32[]{:S(2)}) collective-permute-start(bf16[64,768]{1,0:T(8,128)(2,1)S(1)} %collective-permute-done.1.d4_any.refs_2_), channel_id=1, source_target_pairs={{0,2},{2,0},{4,6},{6,4},{8,10},{10,8},{12,14},{14,12},{1,3},{3,1},... | collective-permute-start | bytes 294920 | tf_op jit(solution)/shard_map/ppermute | solution.py:295
  13.1 5.7 %collective-permute-start.5 = (bf16[64,768]{1,0:T(8,128)(2,1)S(1)}, bf16[64,768]{1,0:T(8,128)(2,1)S(1)}, u32[]{:S(2)}, u32[]{:S(2)}) collective-permute-start(bf16[64,768]{1,0:T(8,128)(2,1)S(1)} %collective-permute-done.1.d4_any.refs_2_), channel_id=1, source_target_pairs={{0,4},{2,6},{4,0},{6,2},{8,12},{10,14},{12,8},{14,10},{1,5},{3,7},... | collective-permute-start | bytes 294920 | tf_op jit(solution)/shard_map/ppermute | solution.py:295
  13.2 5.3 %collective-permute-start.7 = (bf16[64,768]{1,0:T(8,128)(2,1)S(1)}, bf16[64,768]{1,0:T(8,128)(2,1)S(1)}, u32[]{:S(2)}, u32[]{:S(2)}) collective-permute-start(bf16[64,768]{1,0:T(8,128)(2,1)S(1)} %collective-permute-done.3.d2_any.refs_4_), channel_id=1, source_target_pairs={{0,2},{2,0},{4,6},{6,4},{8,10},{10,8},{12,14},{14,12},{1,3},{3,1},... | collective-permute-start | bytes 294920 | tf_op jit(solution)/shard_map/ppermute | solution.py:295
  14.5 5.9 %collective-permute-start.4 = (bf16[64,768]{1,0:T(8,128)(2,1)S(1)}, bf16[64,768]{1,0:T(8,128)(2,1)S(1)}, u32[]{:S(2)}, u32[]{:S(2)}) collective-permute-start(bf16[64,768]{1,0:T(8,128)(2,1)S(1)} %shard_map.83), channel_id=1, source_target_pairs={{0,8},{2,10},{4,12},{6,14},{8,0},{10,2},{12,4},{14,6},{1,9},{3,11}... | collective-permute-start | bytes 294920 | tf_op jit(solution)/shard_map/ppermute | solution.py:295
  20.5 7.2 %collective-permute-start.8 = (bf16[64,1280]{1,0:T(8,128)(2,1)S(1)}, bf16[64,1280]{1,0:T(8,128)(2,1)S(1)}, u32[]{:S(2)}, u32[]{:S(2)}) collective-permute-start(bf16[64,1280]{1,0:T(8,128)(2,1)S(1)} %get-tuple-element.25), channel_id=1, source_target_pairs={{0,4},{2,6},{4,0},{6,2},{8,12},{10,14},{12,8},{14,10},{1,5},{3,7},... | collective-permute-start | bytes 491528 | tf_op jit(solution)/shard_map/ppermute | solution.py:295
  23.0 4.6 %collective-permute-start.9 = (bf16[64,768]{1,0:T(8,128)(2,1)S(1)}, bf16[64,768]{1,0:T(8,128)(2,1)S(1)}, u32[]{:S(2)}, u32[]{:S(2)}) collective-permute-start(bf16[64,768]{1,0:T(8,128)(2,1)S(1)} %collective-permute-done.5.d6_any.refs_6_), channel_id=1, source_target_pairs={{0,2},{2,0},{4,6},{6,4},{8,10},{10,8},{12,14},{14,12},{1,3},{3,1},... | collective-permute-start | bytes 294920 | tf_op jit(solution)/shard_map/ppermute | solution.py:295
  27.6 1.7 %collective-permute-start.10 = (bf16[64,2816]{1,0:T(8,128)(2,1)S(1)}, bf16[64,2816]{1,0:T(8,128)(2,1)S(1)}, u32[]{:S(2)}, u32[]{:S(2)}) collective-permute-start(bf16[64,2816]{1,0:T(8,128)(2,1)S(1)} %shard_map.85.mine_ref), channel_id=1, source_target_pairs={{0,1},{1,0},{2,3},{3,2},{4,5},{5,4},{6,7},{7,6},{8,9},{9,8},{10,11... | collective-permute-start | bytes 1081352 | tf_op jit(solution)/shard_map/ppermute | solution.py:298
  32.6 1.3 %collective-permute-start.11 = (f32[128,128]{1,0:T(8,128)S(1)}, f32[128,128]{1,0:T(8,128)S(1)}, u32[]{:S(2)}, u32[]{:S(2)}) collective-permute-start(f32[128,128]{1,0:T(8,128)S(1)} %get-tuple-element.32), channel_id=1, source_target_pairs={{0,1},{1,0},{2,3},{3,2},{4,5},{5,4},{6,7},{7,6},{8,9},{9,8},{10,11... | collective-permute-start | bytes 196616 | tf_op jit(solution)/shard_map/ppermute | solution.py:298

commit v6 on v5

--- a/solution.py
+++ b/solution.py
@@ -101,8 +101,8 @@
 
 
 def route_kernel(
-    place_ref, owner_ref, delta_ref, start_ref, valid_ref, vals_ref, vecs_ref, expr_ref,
-    ahead_ref, e46_ref, e2_ref, e0_ref, gene_ref, terms_ref,
+    place_ref, owner_ref, delta_ref, start_ref, valid_ref, vals_ref, vecs_ref, expr_ref, dose_ref,
+    ahead_ref, e46_ref, e2_ref, e0_ref, gene_ref, terms_ref, again_ref,
 ):
     slices = owner_ref.shape[0]
     capacity = LANES // slices
@@ -142,6 +142,7 @@
     term = lax.broadcasted_iota(jnp.int32, terms_ref.shape, 0)
     terms = jnp.where(term == 0, high, jnp.where(term == 1, middle, jnp.where(term == 2, vals - high - middle, 0.0)))
     terms_ref[...] = terms.astype(bf16)
+    again_ref[...] = dose_ref[...]
     ahead_ref[:, :half] = vecs_ref[...]
     left, right = slice(0, LANES), slice(LANES, 2 * LANES)
     upper, lower = slice(0, part), slice(part, 2 * part)
@@ -160,16 +161,20 @@
         ref[down, side] = block.T.astype(bf16)
 
 
-def second_kernel(vecs_ref, r1_ref, e46_ref, d4_any, d1_any, d2_any, out_ref):
+def second_kernel(vecs_ref, r1_ref, e46_ref, d0_ref, d4_ref, d2_ref, out_ref, dose_ref, again_ref):
     half = vecs_ref.shape[1]
     part = e46_ref.shape[0]
+    variants = d0_ref.shape[1]
     out_ref[:, :half] = vecs_ref[...]
     out_ref[:, half : 2 * half] = r1_ref[:, :half]
     out_ref[:part, 2 * half :] = e46_ref[...]
     out_ref[part:, 2 * half :] = r1_ref[part:, half:]
-
-
-def third_kernel(vecs_ref, r1_ref, r4_ref, e2_ref, e0_ref, d6_any, d5_any, d3_any, out_ref, kept_ref):
+    for i, ref in enumerate((d0_ref, d4_ref, d2_ref)):
+        dose_ref[:, i * variants : (i + 1) * variants] = ref[...]
+    again_ref[...] = d4_ref[...]
+
+
+def third_kernel(vecs_ref, r1_ref, r4_ref, e2_ref, e0_ref, out_ref, kept_ref):
     half = vecs_ref.shape[1]
     part = e0_ref.shape[0]
     for ref, own, at in ((out_ref, e2_ref, LANES), (kept_ref, e0_ref, 0)):
@@ -184,7 +189,7 @@
         ref[part:, right] = r4_ref[part:, side]
 
 
-def pack_kernel(kept_ref, far_ref, terms_ref, d7_any, out_ref):
+def pack_kernel(kept_ref, far_ref, terms_ref, d153_any, d7_any, out_ref):
     width = kept_ref.shape[1]
     out_ref[:, :width] = kept_ref[...]
     out_ref[:, width : 2 * width] = far_ref[...]
@@ -230,7 +235,7 @@
     *dose_refs, keep_ref, pass_ref, dose_scr = refs
     samples, variants = dose_refs[0].shape
     chunks = [(ref, at) for ref in dose_refs for at in range(0, ref.shape[1], variants)]
-    order = range(8)
+    order = [0, 3, 1, 4, 2, 5, 6, 7]
     for m, (ref, at) in enumerate(chunks[i] for i in order):
         dose_scr[m * samples : (m + 1) * samples, :] = ref[:, at : at + variants]
     rotated = jnp.dot(turned_ref[...], dose_scr[...], preferred_element_type=f32).astype(bf16)
@@ -299,9 +304,7 @@
 
     d0 = lax.dynamic_slice_in_dim(dosage, core * variants, variants, 1)
     d4 = swap(d0, 4)
-    d1 = swap(d0, 1)
-    d2 = swap(d0, 2)
-    ahead, e46, e2, e0, gene, terms = call(
+    ahead, e46, e2, e0, gene, terms, again = call(
         route_kernel,
         [
             ((panel, half + 2 * LANES), bf16),
@@ -310,8 +313,9 @@
             ((part, LANES), bf16),
             ((LANES, LANES), f32),
             ((16, half), bf16),
+            ((panel, variants), bf16),
         ],
-        8,
+        9,
     )(
         place,
         gene_owner.reshape(rows, LANES),
@@ -321,23 +325,25 @@
         eigvals[None, :],
         eigvecs,
         expression,
+        d0,
     )
     r1 = swap(ahead, 1)
-    r4 = swap(
-        call(second_kernel, [((panel, 2 * half + 2 * LANES), bf16)], 6, smem=0, anywhere=3)(
-            eigvecs, r1, e46, d4, d1, d2
-        )[0],
-        4,
-    )
-    d6 = swap(d4, 2)
-    d5 = swap(d4, 1)
-    d3 = swap(d2, 1)
+    d2 = swap(again, 2)
+    to4, three, again4 = call(
+        second_kernel,
+        [((panel, 2 * half + 2 * LANES), bf16), ((panel, 3 * variants), bf16), ((panel, variants), bf16)],
+        6,
+        smem=0,
+    )(eigvecs, r1, e46, d0, d4, d2)
+    r4 = swap(to4, 4)
+    d6 = swap(again4, 2)
+    d153 = swap(three, 1)
     d7 = swap(d6, 1)
     width = 4 * half + 2 * LANES
-    out, kept = call(third_kernel, [((panel, width), bf16)] * 2, 8, smem=0, anywhere=3)(
-        eigvecs, r1, r4, e2, e0, d6, d5, d3
-    )
-    mine = call(pack_kernel, [((panel, 2 * width + half), bf16)], 4, smem=0, anywhere=1)(kept, swap(out, 2), terms, d7)[0]
+    out, kept = call(third_kernel, [((panel, width), bf16)] * 2, 5, smem=0)(eigvecs, r1, r4, e2, e0)
+    mine = call(pack_kernel, [((panel, 2 * width + half), bf16)], 5, smem=0, anywhere=2)(
+        kept, swap(out, 2), terms, d153, d7
+    )[0]
     turned, weighted, low, power = call(
         weight_kernel,
         [((2 * half, samples), bf16), ((LANES, 2 * half), bf16), ((LANES, 2 * half), bf16), ((LANES, LANES), f32)],
@@ -347,9 +353,9 @@
     keep, passed = call(
         score_kernel,
         [((LANES, LANES), f32)] * 2,
-        14,
+        12,
         scratch=[pltpu.VMEM((samples, variants), bf16)],
-    )(place, gene, power, turned, weighted, low, d0, d1, d4, d5, d2, d3, d6, d7)
+    )(place, gene, power, turned, weighted, low, d0, d4, d2, d153, d6, d7)
     return keep + other_core(passed)
 
 

time: 34.7 us -> 33.4 us (0.963)
  starting transfers between devices: 16.5 us -> 12.1 us
  waiting for transfers between devices: 11.4 us -> 14.4 us
    ppermute x10 -> x8, starting transfers between devices: 16.3 us -> 11.8 us  [swap(): return lax.ppermute(x, 'row', [(i, i ^ m) for i in range(rows)])]
    ppermute x10 -> x8, waiting for transfers between devices: 8.56 us -> 11.6 us  [swap(): return lax.ppermute(x, 'row', [(i, i ^ m) for i in range(rows)])]
  transfers between devices with their start and end apart: 12 -> 10, of which waited for: 7 -> 6; matrix products, arithmetic and copies ran while one was open for 0% -> 0% of each run, Pallas kernels for 3% -> 3%
where the time goes in v6:
time: 33.4 us; the launch traced here: 33.2 us
  waiting for transfers between devices  14.4 us (43%)
  starting transfers between devices  12.1 us (36%)
  Pallas kernels  4.3 us (13%)
  local copies, waits for them, and re-layouts  1.64 us (5%)
  other arithmetic  0.71 us (2%)
    ppermute x8, starting transfers between devices, swap(): return lax.ppermute(x, 'row', [(i, i ^ m) for i in range(rows)])  11.8 us
    ppermute x8, waiting for transfers between devices, swap(): return lax.ppermute(x, 'row', [(i, i ^ m) for i in range(rows)])  11.6 us
    ppermute x2, waiting for transfers between devices, other_core(): return lax.ppermute(x, 'col', [(0, 1), (1, 0)])  2.78 us
    pallas_call x1, Pallas kernels, near_body(): call(score_kernel, [((LANES, LANES), f32)] * 2, 12, scratch=[pltpu.VMEM((...  1.83 us
    unnamed x16, local copies, waits for them, and re-layouts  1.63 us
    pallas_call x1, Pallas kernels, near_body(): call(weight_kernel, [((2 * half, samples), bf16), ((LANES, 2 * half), bf1...  1.39 us
    pallas_call x1, Pallas kernels, near_body(): call(route_kernel, [((panel, half + 2 * LANES), bf16), ((part, 2 * LANES)...  1 us
  transfers between devices with their start and end apart: 10, of which 6 were waited for; matrix products, arithmetic and copies ran while one was open for 0% of the time, Pallas kernels for 3%

profile of v6, /device:TPU:0, one launch (start us, length us, event | category | flops | bytes accessed | tf_op | source)
XLA Modules:
  0.0 33.2 jit_solution(17136966684654740496)
XLA Ops:
  0.0 0.9 %copy-done = bf16[64,1536]{1,0:T(8,128)(2,1)S(1)} copy-done((bf16[64,1536]{1,0:T(8,128)(2,1)S(1)}, bf16[64,1536]{1,0:T(8,128)(2,1)}, u32[]{:S(2)}) %copy-start) | copy-done | bytes 196632
  0.9 4.1 %collective-permute-start.1 = (bf16[64,768]{1,0:T(8,128)(2,1)S(1)}, bf16[64,768]{1,0:T(8,128)(2,1)S(1)}, u32[]{:S(2)}, u32[]{:S(2)}) collective-permute-start(bf16[64,768]{1,0:T(8,128)(2,1)S(1)} %constant_dynamic-slice_fusion.dose_ref.d0_ref.refs_0_), channel_id=1, source_target_pairs={{0,8},{2,10},{4,12},{6,14},{8,0},{10,2},{12,4},{14,6},{1,9},{3,11}... | collective-permute-start | bytes 294920 | tf_op jit(solution)/shard_map/ppermute | solution.py:300
  5.0 0.1 pad_add_fusion.place_ref
  5.1 0.6 %copy-done.6 = s32[1024]{0:T(1024)S(1)} copy-done((s32[1024]{0:T(1024)S(1)}, s32[1024]{0:T(1024)}, u32[]{:S(2)}) %copy-start.6) | copy-done | bytes 4120
  5.7 0.1 copy-done.4
  5.8 1.0 %shard_map.82 = (bf16[64,512]{1,0:T(8,128)(2,1)S(1)}, bf16[32,256]{1,0:T(8,128)(2,1)S(1)}, bf16[32,128]{1,0:T(8,128)(2,1)S(1)}, bf16[32,128]{1,0:T(8,128)(2,1)S(...) custom-call(s32[2]{0:T(128)S(1)} %pad_add_fusion.place_ref, ...), custom_call_target="tpu_custom_call" | custom-call | tf_op jit(solution)/shard_map/pallas_call | solution.py:307
  6.8 1.6 %collective-permute-start.2 = (bf16[64,768]{1,0:T(8,128)(2,1)S(1)}, bf16[64,768]{1,0:T(8,128)(2,1)S(1)}, u32[]{:S(2)}, u32[]{:S(2)}) collective-permute-start(bf16[64,768]{1,0:T(8,128)(2,1)S(1)} %get-tuple-element.26), channel_id=1, source_target_pairs={{0,4},{2,6},{4,0},{6,2},{8,12},{10,14},{12,8},{14,10},{1,5},{3,7},... | collective-permute-start | bytes 294920 | tf_op jit(solution)/shard_map/ppermute | solution.py:300
  8.5 1.5 %collective-permute-start = (bf16[64,512]{1,0:T(8,128)(2,1)S(1)}, bf16[64,512]{1,0:T(8,128)(2,1)S(1)}, u32[]{:S(2)}, u32[]{:S(2)}) collective-permute-start(bf16[64,512]{1,0:T(8,128)(2,1)S(1)} %get-tuple-element.24), channel_id=1, source_target_pairs={{0,2},{2,0},{4,6},{6,4},{8,10},{10,8},{12,14},{14,12},{1,3},{3,1},... | collective-permute-start | bytes 196616 | tf_op jit(solution)/shard_map/ppermute | solution.py:300
  10.0 2.7 %collective-permute-done.r1_ref = bf16[64,512]{1,0:T(8,128)(2,1)S(1)} collective-permute-done((bf16[64,512]{1,0:T(8,128)(2,1)S(1)}, bf16[64,512]{1,0:T(8,128)(2,1)S(1)}, u32[]{:S(2)}, u32[]{:S(2)}) %collective-permute-start) | collective-permute-done | bytes 65568 | tf_op jit(solution)/shard_map/ppermute | solution.py:300
  12.8 1.6 %collective-permute-start.5 = (bf16[64,2304]{1,0:T(8,128)(2,1)S(1)}, bf16[64,2304]{1,0:T(8,128)(2,1)S(1)}, u32[]{:S(2)}, u32[]{:S(2)}) collective-permute-start(bf16[64,2304]{1,0:T(8,128)(2,1)S(1)} %get-tuple-element.33), channel_id=1, source_target_pairs={{0,2},{2,0},{4,6},{6,4},{8,10},{10,8},{12,14},{14,12},{1,3},{3,1},... | collective-permute-start | bytes 884744 | tf_op jit(solution)/shard_map/ppermute | solution.py:300
  14.4 0.3 %collective-permute-start.3 = (bf16[64,768]{1,0:T(8,128)(2,1)S(1)}, bf16[64,768]{1,0:T(8,128)(2,1)S(1)}, u32[]{:S(2)}, u32[]{:S(2)}) collective-permute-start(bf16[64,768]{1,0:T(8,128)(2,1)S(1)} %get-tuple-element.27), channel_id=1, source_target_pairs={{0,8},{2,10},{4,12},{6,14},{8,0},{10,2},{12,4},{14,6},{1,9},{3,11}... | collective-permute-start | bytes 294920 | tf_op jit(solution)/shard_map/ppermute | solution.py:300
  14.7 2.0 %collective-permute-start.6 = (bf16[64,768]{1,0:T(8,128)(2,1)S(1)}, bf16[64,768]{1,0:T(8,128)(2,1)S(1)}, u32[]{:S(2)}, u32[]{:S(2)}) collective-permute-start(bf16[64,768]{1,0:T(8,128)(2,1)S(1)} %get-tuple-element.34), channel_id=1, source_target_pairs={{0,4},{2,6},{4,0},{6,2},{8,12},{10,14},{12,8},{14,10},{1,5},{3,7},... | collective-permute-start | bytes 294920 | tf_op jit(solution)/shard_map/ppermute | solution.py:300
  16.7 4.2 %collective-permute-done.3.r4_ref = bf16[64,768]{1,0:T(8,128)(2,1)S(1)} collective-permute-done((bf16[64,768]{1,0:T(8,128)(2,1)S(1)}, bf16[64,768]{1,0:T(8,128)(2,1)S(1)}, u32[]{:S(2)}, u32[]{:S(2)}) %collective-permute-start.3) | collective-permute-done | bytes 98336 | tf_op jit(solution)/shard_map/ppermute | solution.py:300
  20.9 0.1 collective-permute-start.4
  21.0 0.6 %collective-permute-start.7 = (bf16[64,768]{1,0:T(8,128)(2,1)S(1)}, bf16[64,768]{1,0:T(8,128)(2,1)S(1)}, u32[]{:S(2)}, u32[]{:S(2)}) collective-permute-start(bf16[64,768]{1,0:T(8,128)(2,1)S(1)} %collective-permute-done.6.refs_4_), channel_id=1, source_target_pairs={{0,2},{2,0},{4,6},{6,4},{8,10},{10,8},{12,14},{14,12},{1,3},{3,1},... | collective-permute-start | bytes 294920 | tf_op jit(solution)/shard_map/ppermute | solution.py:300
  21.6 4.1 %collective-permute-done.7.d7_any.refs_5_ = bf16[64,768]{1,0:T(8,128)(2,1)S(1)} collective-permute-done((bf16[64,768]{1,0:T(8,128)(2,1)S(1)}, bf16[64,768]{1,0:T(8,128)(2,1)S(1)}, u32[]{:S(2)}, u32[]{:S(2)}) %collective-permute-start.7) | collective-permute-done | bytes 98336 | tf_op jit(solution)/shard_map/ppermute | solution.py:300
  25.7 0.6 %collective-permute-done.4.far_ref = bf16[64,1280]{1,0:T(8,128)(2,1)S(1)} collective-permute-done((bf16[64,1280]{1,0:T(8,128)(2,1)S(1)}, bf16[64,1280]{1,0:T(8,128)(2,1)S(1)}, u32[]{:S(2)}, u32[]{:S(2)}) %collective-permute-start.4) | collective-permute-done | bytes 163872 | tf_op jit(solution)/shard_map/ppermute | solution.py:300
  26.3 0.1 collective-permute-start.8
  26.4 1.7 %collective-permute-done.8.other_ref = bf16[64,2816]{1,0:T(8,128)(2,1)S(1)} collective-permute-done((bf16[64,2816]{1,0:T(8,128)(2,1)S(1)}, bf16[64,2816]{1,0:T(8,128)(2,1)S(1)}, u32[]{:S(2)}, u32[]{:S(2)}) %collective-permute-start.8) | collective-permute-done | bytes 360480 | tf_op jit(solution)/shard_map/ppermute | solution.py:303
  28.1 1.4 %shard_map.86 = (bf16[512,512]{1,0:T(8,128)(2,1)S(1)}, bf16[128,512]{1,0:T(8,128)(2,1)S(1)}, bf16[128,512]{1,0:T(8,128)(2,1)S(1)}, f32[128,128]{1,0:T(8,128)S(1)}) custom-call(s32[2]{0:T(128)S(1)} %pad_add_fusion.place_ref, bf16[64,2816]{1,0:T(8,128)(2,1)S(1)} %shard_map.85.mine_ref, bf16[64,2816]{1,0:T(8,128)(2,1)S(1)} %collective-permute-done.8.other_ref, ...), custom_call_target="tpu_custom_call" | custom-call | tf_op jit(solution)/shard_map/pallas_call | solution.py:347
  29.5 1.8 %shard_map.87 = (f32[128,128]{1,0:T(8,128)S(1)}, f32[128,128]{1,0:T(8,128)S(1)}) custom-call(s32[2]{0:T(128)S(1)} %pad_add_fusion.place_ref, f32[128,128]{1,0:T(8,128)S(1)} %get-tuple-element.23.gene_ref, f32[128,128]{1,0:T(8,128)S(1)} %get-tuple-element.35.power_ref, bf16[512,512]{1,0:T(8,128)(2,1)S(1)} %get-tuple-element.36.turned_ref, ...), custom_call_target="tpu_custom_call" | custom-call | tf_op jit(solution)/shard_map/pallas_call | solution.py:353
  31.3 0.2 collective-permute-start.9
  31.5 1.1 %collective-permute-done.9 = f32[128,128]{1,0:T(8,128)S(1)} collective-permute-done((f32[128,128]{1,0:T(8,128)S(1)}, f32[128,128]{1,0:T(8,128)S(1)}, u32[]{:S(2)}, u32[]{:S(2)}) %collective-permute-start.9) | collective-permute-done | bytes 65568 | tf_op jit(solution)/shard_map/ppermute | solution.py:303
  32.6 0.6 %add.7 = f32[128,128]{1,0:T(8,128)} add(f32[128,128]{1,0:T(8,128)S(1)} %get-tuple-element.39, f32[128,128]{1,0:T(8,128)S(1)} %collective-permute-done.9) | non-fusion elementwise | flops 16384 | bytes 196608 | tf_op jit(solution)/shard_map/add | solution.py:359
  (21 shorter events, 0.2 us)
Async XLA Ops:
  0.0 0.9 %copy-start = (bf16[64,1536]{1,0:T(8,128)(2,1)S(1)}, bf16[64,1536]{1,0:T(8,128)(2,1)}, u32[]{:S(2)}) copy-start(bf16[64,1536]{1,0:T(8,128)(2,1)} %param.11) | copy-start | bytes 589828
  0.0 5.1 %copy-start.2 = (bf16[64,1024]{1,0:T(8,128)(2,1)S(1)}, bf16[64,1024]{1,0:T(8,128)(2,1)}, u32[]{:S(2)}) copy-start(bf16[64,1024]{1,0:T(8,128)(2,1)} %expr_ref.1) | copy-start | bytes 393220
  0.9 4.2 %copy-start.1 = (bf16[64,256]{1,0:T(8,128)(2,1)S(1)}, bf16[64,256]{1,0:T(8,128)(2,1)}, u32[]{:S(2)}) copy-start(bf16[64,256]{1,0:T(8,128)(2,1)} %vecs_ref.5) | copy-start | bytes 98308
  0.9 11.8 %collective-permute-start.1 = (bf16[64,768]{1,0:T(8,128)(2,1)S(1)}, bf16[64,768]{1,0:T(8,128)(2,1)S(1)}, u32[]{:S(2)}, u32[]{:S(2)}) collective-permute-start(bf16[64,768]{1,0:T(8,128)(2,1)S(1)} %constant_dynamic-slice_fusion.dose_ref.d0_ref.refs_0_), channel_id=1, source_target_pairs={{0,8},{2,10},{4,12},{6,14},{8,0},{10,2},{12,4},{14,6},{1,9},{3,11}... | collective-permute-start | bytes 294920 | tf_op jit(solution)/shard_map/ppermute | solution.py:300
  5.0 0.7 %copy-start.6 = (s32[1024]{0:T(1024)S(1)}, s32[1024]{0:T(1024)}, u32[]{:S(2)}) copy-start(s32[1024]{0:T(1024)} %param.14) | copy-start | bytes 12292
  5.0 0.7 %copy-start.5 = (s32[1024]{0:T(1024)S(1)}, s32[1024]{0:T(1024)}, u32[]{:S(2)}) copy-start(s32[1024]{0:T(1024)} %param.13) | copy-start | bytes 12292
  5.1 0.7 %copy-start.4 = (f32[1024]{0:T(1024)S(1)}, f32[1024]{0:T(1024)}, u32[]{:S(2)}) copy-start(f32[1024]{0:T(1024)} %param.12) | copy-start | bytes 12292
  5.1 0.7 %copy-start.3 = (s32[1024]{0:T(1024)S(1)}, s32[1024]{0:T(1024)}, u32[]{:S(2)}) copy-start(s32[1024]{0:T(1024)} %param.15) | copy-start | bytes 12292
  5.1 0.7 %copy-start.7 = (f32[256]{0:T(256)S(1)}, f32[256]{0:T(256)}, u32[]{:S(2)}) copy-start(f32[256]{0:T(256)} %param.9) | copy-start | bytes 3076
  6.8 5.9 %collective-permute-start.2 = (bf16[64,768]{1,0:T(8,128)(2,1)S(1)}, bf16[64,768]{1,0:T(8,128)(2,1)S(1)}, u32[]{:S(2)}, u32[]{:S(2)}) collective-permute-start(bf16[64,768]{1,0:T(8,128)(2,1)S(1)} %get-tuple-element.26), channel_id=1, source_target_pairs={{0,4},{2,6},{4,0},{6,2},{8,12},{10,14},{12,8},{14,10},{1,5},{3,7},... | collective-permute-start | bytes 294920 | tf_op jit(solution)/shard_map/ppermute | solution.py:300
  8.5 4.3 %collective-permute-start = (bf16[64,512]{1,0:T(8,128)(2,1)S(1)}, bf16[64,512]{1,0:T(8,128)(2,1)S(1)}, u32[]{:S(2)}, u32[]{:S(2)}) collective-permute-start(bf16[64,512]{1,0:T(8,128)(2,1)S(1)} %get-tuple-element.24), channel_id=1, source_target_pairs={{0,2},{2,0},{4,6},{6,4},{8,10},{10,8},{12,14},{14,12},{1,3},{3,1},... | collective-permute-start | bytes 196616 | tf_op jit(solution)/shard_map/ppermute | solution.py:300
  12.8 13.5 %collective-permute-start.5 = (bf16[64,2304]{1,0:T(8,128)(2,1)S(1)}, bf16[64,2304]{1,0:T(8,128)(2,1)S(1)}, u32[]{:S(2)}, u32[]{:S(2)}) collective-permute-start(bf16[64,2304]{1,0:T(8,128)(2,1)S(1)} %get-tuple-element.33), channel_id=1, source_target_pairs={{0,2},{2,0},{4,6},{6,4},{8,10},{10,8},{12,14},{14,12},{1,3},{3,1},... | collective-permute-start | bytes 884744 | tf_op jit(solution)/shard_map/ppermute | solution.py:300
  14.4 6.5 %collective-permute-start.3 = (bf16[64,768]{1,0:T(8,128)(2,1)S(1)}, bf16[64,768]{1,0:T(8,128)(2,1)S(1)}, u32[]{:S(2)}, u32[]{:S(2)}) collective-permute-start(bf16[64,768]{1,0:T(8,128)(2,1)S(1)} %get-tuple-element.27), channel_id=1, source_target_pairs={{0,8},{2,10},{4,12},{6,14},{8,0},{10,2},{12,4},{14,6},{1,9},{3,11}... | collective-permute-start | bytes 294920 | tf_op jit(solution)/shard_map/ppermute | solution.py:300
  14.7 6.3 %collective-permute-start.6 = (bf16[64,768]{1,0:T(8,128)(2,1)S(1)}, bf16[64,768]{1,0:T(8,128)(2,1)S(1)}, u32[]{:S(2)}, u32[]{:S(2)}) collective-permute-start(bf16[64,768]{1,0:T(8,128)(2,1)S(1)} %get-tuple-element.34), channel_id=1, source_target_pairs={{0,4},{2,6},{4,0},{6,2},{8,12},{10,14},{12,8},{14,10},{1,5},{3,7},... | collective-permute-start | bytes 294920 | tf_op jit(solution)/shard_map/ppermute | solution.py:300
  20.9 5.4 %collective-permute-start.4 = (bf16[64,1280]{1,0:T(8,128)(2,1)S(1)}, bf16[64,1280]{1,0:T(8,128)(2,1)S(1)}, u32[]{:S(2)}, u32[]{:S(2)}) collective-permute-start(bf16[64,1280]{1,0:T(8,128)(2,1)S(1)} %get-tuple-element.31), channel_id=1, source_target_pairs={{0,4},{2,6},{4,0},{6,2},{8,12},{10,14},{12,8},{14,10},{1,5},{3,7},... | collective-permute-start | bytes 491528 | tf_op jit(solution)/shard_map/ppermute | solution.py:300
  21.0 4.7 %collective-permute-start.7 = (bf16[64,768]{1,0:T(8,128)(2,1)S(1)}, bf16[64,768]{1,0:T(8,128)(2,1)S(1)}, u32[]{:S(2)}, u32[]{:S(2)}) collective-permute-start(bf16[64,768]{1,0:T(8,128)(2,1)S(1)} %collective-permute-done.6.refs_4_), channel_id=1, source_target_pairs={{0,2},{2,0},{4,6},{6,4},{8,10},{10,8},{12,14},{14,12},{1,3},{3,1},... | collective-permute-start | bytes 294920 | tf_op jit(solution)/shard_map/ppermute | solution.py:300
  26.3 1.7 %collective-permute-start.8 = (bf16[64,2816]{1,0:T(8,128)(2,1)S(1)}, bf16[64,2816]{1,0:T(8,128)(2,1)S(1)}, u32[]{:S(2)}, u32[]{:S(2)}) collective-permute-start(bf16[64,2816]{1,0:T(8,128)(2,1)S(1)} %shard_map.85.mine_ref), channel_id=1, source_target_pairs={{0,1},{1,0},{2,3},{3,2},{4,5},{5,4},{6,7},{7,6},{8,9},{9,8},{10,11... | collective-permute-start | bytes 1081352 | tf_op jit(solution)/shard_map/ppermute | solution.py:303
  31.3 1.3 %collective-permute-start.9 = (f32[128,128]{1,0:T(8,128)S(1)}, f32[128,128]{1,0:T(8,128)S(1)}, u32[]{:S(2)}, u32[]{:S(2)}) collective-permute-start(f32[128,128]{1,0:T(8,128)S(1)} %get-tuple-element.40), channel_id=1, source_target_pairs={{0,1},{1,0},{2,3},{3,2},{4,5},{5,4},{6,7},{7,6},{8,9},{9,8},{10,11... | collective-permute-start | bytes 196616 | tf_op jit(solution)/shard_map/ppermute | solution.py:303

commit v7 on v6

--- a/solution.py
+++ b/solution.py
@@ -161,20 +161,22 @@
         ref[down, side] = block.T.astype(bf16)
 
 
-def second_kernel(vecs_ref, r1_ref, e46_ref, d0_ref, d4_ref, d2_ref, out_ref, dose_ref, again_ref):
+def second_kernel(vecs_ref, r1_ref, e46_ref, out_ref):
     half = vecs_ref.shape[1]
     part = e46_ref.shape[0]
-    variants = d0_ref.shape[1]
     out_ref[:, :half] = vecs_ref[...]
     out_ref[:, half : 2 * half] = r1_ref[:, :half]
     out_ref[:part, 2 * half :] = e46_ref[...]
     out_ref[part:, 2 * half :] = r1_ref[part:, half:]
-    for i, ref in enumerate((d0_ref, d4_ref, d2_ref)):
-        dose_ref[:, i * variants : (i + 1) * variants] = ref[...]
-    again_ref[...] = d4_ref[...]
-
-
-def third_kernel(vecs_ref, r1_ref, r4_ref, e2_ref, e0_ref, out_ref, kept_ref):
+
+
+def copy_kernel(dose_ref, after_any, out_ref):
+    out_ref[...] = dose_ref[...]
+
+
+def third_kernel(
+    vecs_ref, r1_ref, r4_ref, e2_ref, e0_ref, terms_ref, d4_ref, d2_ref, d6_ref, d1_any, out_ref, kept_ref, dose_ref
+):
     half = vecs_ref.shape[1]
     part = e0_ref.shape[0]
     for ref, own, at in ((out_ref, e2_ref, LANES), (kept_ref, e0_ref, 0)):
@@ -187,43 +189,58 @@
         ref[:part, right] = r1_ref[:part, half + at : half + at + LANES]
         ref[part:, left] = r4_ref[:part, side]
         ref[part:, right] = r4_ref[part:, side]
-
-
-def pack_kernel(kept_ref, far_ref, terms_ref, d153_any, d7_any, out_ref):
-    width = kept_ref.shape[1]
-    out_ref[:, :width] = kept_ref[...]
-    out_ref[:, width : 2 * width] = far_ref[...]
-    out_ref[: terms_ref.shape[0], 2 * width :] = terms_ref[...]
-    out_ref[terms_ref.shape[0] :, 2 * width :] = jnp.zeros_like(out_ref[terms_ref.shape[0] :, 2 * width :])
-
-
-def weight_kernel(place_ref, mine_ref, other_ref, gene_ref, turned_ref, weighted_ref, low_ref, power_ref, data_scr):
-    samples = mine_ref.shape[0]
+    width = out_ref.shape[1]
+    terms = terms_ref.shape[0]
+    kept_ref[:terms, width:] = terms_ref[...]
+    kept_ref[terms:, width:] = jnp.zeros((kept_ref.shape[0] - terms, half), bf16)
+    variants = d4_ref.shape[1]
+    for i, ref in enumerate((d4_ref, d2_ref, d6_ref)):
+        dose_ref[:, i * variants : (i + 1) * variants] = ref[...]
+
+
+def rotate(place_ref, refs, turned_ref, data_scr):
+    samples = refs[0].shape[0]
     half = turned_ref.shape[0] // 2
     part = samples // 2
     core = place_ref[1]
-    width = 4 * half + 2 * LANES
-    panels = [n * width + i * half for n in range(2) for i in range(4)]
-    for c, ref in enumerate((mine_ref, other_ref)):
+    for c, ref in enumerate(refs):
         side = core if c == 0 else 1 - core
-        for m, at in enumerate(panels):
-            turned_ref[c * half : (c + 1) * half, m * samples : (m + 1) * samples] = (
-                ref[:, at : at + half].astype(f32).T.astype(bf16)
+        for i in range(4):
+            turned_ref[c * half : (c + 1) * half, i * samples : (i + 1) * samples] = (
+                ref[:, i * half : (i + 1) * half].astype(f32).T.astype(bf16)
             )
-            n, i = divmod(m, 4)
-            at = n * width + 4 * half + i % 2 * LANES
-            data_scr[pl.ds(pl.multiple_of(m * samples + side * part, part), part), :] = ref[
+            at = 4 * half + i % 2 * LANES
+            data_scr[pl.ds(pl.multiple_of(i * samples + side * part, part), part), :] = ref[
                 i // 2 * part : (i // 2 + 1) * part, at : at + LANES
             ]
     data = data_scr[...].astype(f32).T.astype(bf16)
+    shares = []
+    for ref in refs:
+        vecs = jnp.concatenate([ref[:, i * half : (i + 1) * half] for i in range(4)], axis=0)
+        shares.append(jnp.dot(data, vecs, preferred_element_type=f32))
+    return shares
+
+
+def half_kernel(place_ref, mine_ref, other_ref, turned_ref, share_ref, data_scr):
+    half = turned_ref.shape[0] // 2
+    for c, share in enumerate(rotate(place_ref, (mine_ref, other_ref), turned_ref, data_scr)):
+        share_ref[:, c * half : (c + 1) * half] = share
+
+
+def weight_kernel(
+    place_ref, kept_ref, kept2_ref, mine_ref, other_ref, share_ref, gene_ref, d537_any,
+    turned_ref, weighted_ref, low_ref, power_ref, data_scr,
+):
+    half = turned_ref.shape[0] // 2
     delta = gene_ref[:, 0:1]
-    total = jnp.zeros((data.shape[0], 1), f32)
-    for c, ref in enumerate((mine_ref, other_ref)):
-        vecs = jnp.concatenate([ref[:, at : at + half] for at in panels], axis=0)
+    total = jnp.zeros((delta.shape[0], 1), f32)
+    shares = rotate(place_ref, (mine_ref, other_ref), turned_ref, data_scr)
+    width = mine_ref.shape[1]
+    for c, (share, ref) in enumerate(zip(shares, (kept_ref, kept2_ref))):
         cols = slice(c * half, (c + 1) * half)
-        terms = ref[0:16, 2 * width :].astype(f32)
+        terms = ref[0:16, width:].astype(f32)
         vals = terms[0:1] + terms[1:2] + terms[2:3]
-        rotated = jnp.dot(data, vecs, preferred_element_type=f32).astype(bf16).astype(f32)
+        rotated = (share_ref[:, cols] + share).astype(bf16).astype(f32)
         weight = 1.0 / (vals + delta)
         total += jnp.sum(weight * rotated * rotated, axis=1, keepdims=True)
         weighted_ref[:, cols] = (weight * rotated).astype(bf16)
@@ -231,14 +248,17 @@
     power_ref[...] = jnp.broadcast_to(total, power_ref.shape)
 
 
-def score_kernel(place_ref, gene_ref, power_ref, turned_ref, weighted_ref, low_ref, *refs):
+def score_kernel(place_ref, gene_ref, power_ref, turned_ref, turned2_ref, weighted_ref, low_ref, *refs):
     *dose_refs, keep_ref, pass_ref, dose_scr = refs
     samples, variants = dose_refs[0].shape
     chunks = [(ref, at) for ref in dose_refs for at in range(0, ref.shape[1], variants)]
-    order = [0, 3, 1, 4, 2, 5, 6, 7]
+    order = [0, 1, 2, 3, 6, 4, 7, 5]
     for m, (ref, at) in enumerate(chunks[i] for i in order):
         dose_scr[m * samples : (m + 1) * samples, :] = ref[:, at : at + variants]
-    rotated = jnp.dot(turned_ref[...], dose_scr[...], preferred_element_type=f32).astype(bf16)
+    line = turned_ref.shape[1]
+    rotated = jnp.dot(turned_ref[...], dose_scr[:line], preferred_element_type=f32)
+    rotated += jnp.dot(turned2_ref[...], dose_scr[line:], preferred_element_type=f32)
+    rotated = rotated.astype(bf16)
     squared = jnp.square(rotated.astype(f32)).astype(bf16)
     cross = jnp.dot(weighted_ref[...], rotated, preferred_element_type=f32)
     power = jnp.dot(low_ref[...], squared, preferred_element_type=f32)
@@ -329,33 +349,42 @@
     )
     r1 = swap(ahead, 1)
     d2 = swap(again, 2)
-    to4, three, again4 = call(
-        second_kernel,
-        [((panel, 2 * half + 2 * LANES), bf16), ((panel, 3 * variants), bf16), ((panel, variants), bf16)],
-        6,
+    d1 = swap(again, 1)
+    to4 = call(second_kernel, [((panel, 2 * half + 2 * LANES), bf16)], 3, smem=0)(eigvecs, r1, e46)[0]
+    r4 = swap(to4, 4)
+    d6 = swap(call(copy_kernel, [((panel, variants), bf16)], 2, smem=0, anywhere=1)(d4, to4)[0], 2)
+    width = 4 * half + 2 * LANES
+    out, kept, three = call(
+        third_kernel,
+        [((panel, width), bf16), ((panel, width + half), bf16), ((panel, 3 * variants), bf16)],
+        10,
         smem=0,
-    )(eigvecs, r1, e46, d0, d4, d2)
-    r4 = swap(to4, 4)
-    d6 = swap(again4, 2)
-    d153 = swap(three, 1)
-    d7 = swap(d6, 1)
-    width = 4 * half + 2 * LANES
-    out, kept = call(third_kernel, [((panel, width), bf16)] * 2, 5, smem=0)(eigvecs, r1, r4, e2, e0)
-    mine = call(pack_kernel, [((panel, 2 * width + half), bf16)], 5, smem=0, anywhere=2)(
-        kept, swap(out, 2), terms, d153, d7
-    )[0]
-    turned, weighted, low, power = call(
+        anywhere=1,
+    )(eigvecs, r1, r4, e2, e0, terms, d4, d2, d6, d1)
+    d537 = swap(three, 1)
+    kept2 = other_core(kept)
+    near = swap(out, 2)
+    near2 = other_core(near)
+    shape = ((2 * half, samples // 2), bf16)
+    turned, share = call(
+        half_kernel,
+        [shape, ((LANES, 2 * half), f32)],
+        3,
+        scratch=[pltpu.VMEM((samples // 2, LANES), bf16)],
+    )(place, kept, kept2)
+    turned2, weighted, low, power = call(
         weight_kernel,
-        [((2 * half, samples), bf16), ((LANES, 2 * half), bf16), ((LANES, 2 * half), bf16), ((LANES, LANES), f32)],
-        4,
-        scratch=[pltpu.VMEM((samples, LANES), bf16)],
-    )(place, mine, other_core(mine), gene)
+        [shape, ((LANES, 2 * half), bf16), ((LANES, 2 * half), bf16), ((LANES, LANES), f32)],
+        8,
+        scratch=[pltpu.VMEM((samples // 2, LANES), bf16)],
+        anywhere=1,
+    )(place, kept, kept2, near, near2, share, gene, d537)
     keep, passed = call(
         score_kernel,
         [((LANES, LANES), f32)] * 2,
-        12,
+        13,
         scratch=[pltpu.VMEM((samples, variants), bf16)],
-    )(place, gene, power, turned, weighted, low, d0, d4, d2, d153, d6, d7)
+    )(place, gene, power, turned, turned2, weighted, low, d0, d1, d4, d537, d2, d6)
     return keep + other_core(passed)
 
 

time: 33.4 us -> 31 us (0.928)
  waiting for transfers between devices: 14.4 us -> 11.1 us
  Pallas kernels: 4.3 us -> 4.92 us
    ppermute x8, waiting for transfers between devices: 11.6 us -> 9.84 us  [swap(): return lax.ppermute(x, 'row', [(i, i ^ m) for i in range(rows)])]
    ppermute x2 -> x3, waiting for transfers between devices: 2.78 us -> 1.25 us  [other_core(): return lax.ppermute(x, 'col', [(0, 1), (1, 0)])]
    pallas_call x5 -> x6, Pallas kernels: 3.3 us -> 3.92 us  [the longest x1 1.84 us: near_body(): call(score_kernel, [((LANES, LANES), f32)] * 2, 13, scratch=[pltpu.VMEM((...]
    ppermute x8, starting transfers between devices: 11.8 us -> 12.3 us  [swap(): return lax.ppermute(x, 'row', [(i, i ^ m) for i in range(rows)])]
  transfers between devices with their start and end apart: 10 -> 11, of which waited for: 6 -> 7; matrix products, arithmetic and copies ran while one was open for 0% -> 0% of each run, Pallas kernels for 3% -> 6%
where the time goes in v7:
time: 31 us; the launch traced here: 30.9 us
  starting transfers between devices  12.4 us (40%)
  waiting for transfers between devices  11.1 us (36%)
  Pallas kernels  4.92 us (16%)
  local copies, waits for them, and re-layouts  1.64 us (5%)
  other arithmetic  0.71 us (2%)
    ppermute x8, starting transfers between devices, swap(): return lax.ppermute(x, 'row', [(i, i ^ m) for i in range(rows)])  12.3 us
    ppermute x8, waiting for transfers between devices, swap(): return lax.ppermute(x, 'row', [(i, i ^ m) for i in range(rows)])  9.84 us
    pallas_call x1, Pallas kernels, near_body(): call(score_kernel, [((LANES, LANES), f32)] * 2, 13, scratch=[pltpu.VMEM((...  1.84 us
    unnamed x16, local copies, waits for them, and re-layouts  1.63 us
    ppermute x3, waiting for transfers between devices, other_core(): return lax.ppermute(x, 'col', [(0, 1), (1, 0)])  1.25 us
    pallas_call x1, Pallas kernels, near_body(): call(weight_kernel, [shape, ((LANES, 2 * half), bf16), ((LANES, 2 * half)...  1.08 us
    pallas_call x1, Pallas kernels, near_body(): call(route_kernel, [((panel, half + 2 * LANES), bf16), ((part, 2 * LANES)...  1 us
    pallas_call x1, Pallas kernels, near_body(): call(half_kernel, [shape, ((LANES, 2 * half), f32)], 3, scratch=[pltpu.VM...  0.93 us
  transfers between devices with their start and end apart: 11, of which 7 were waited for; matrix products, arithmetic and copies ran while one was open for 0% of the time, Pallas kernels for 6%

profile of v7, /device:TPU:0, one launch (start us, length us, event | category | flops | bytes accessed | tf_op | source)
XLA Modules:
  0.0 30.9 jit_solution(16038365205738528447)
XLA Ops:
  0.0 0.9 %copy-done = bf16[64,1536]{1,0:T(8,128)(2,1)S(1)} copy-done((bf16[64,1536]{1,0:T(8,128)(2,1)S(1)}, bf16[64,1536]{1,0:T(8,128)(2,1)}, u32[]{:S(2)}) %copy-start) | copy-done | bytes 196632
  0.9 4.1 %collective-permute-start.2 = (bf16[64,768]{1,0:T(8,128)(2,1)S(1)}, bf16[64,768]{1,0:T(8,128)(2,1)S(1)}, u32[]{:S(2)}, u32[]{:S(2)}) collective-permute-start(bf16[64,768]{1,0:T(8,128)(2,1)S(1)} %constant_dynamic-slice_fusion.dose_ref.refs_0_), channel_id=1, source_target_pairs={{0,8},{2,10},{4,12},{6,14},{8,0},{10,2},{12,4},{14,6},{1,9},{3,11}... | collective-permute-start | bytes 294920 | tf_op jit(solution)/shard_map/ppermute | solution.py:320
  5.0 0.1 pad_add_fusion.place_ref
  5.1 0.6 %copy-done.6 = s32[1024]{0:T(1024)S(1)} copy-done((s32[1024]{0:T(1024)S(1)}, s32[1024]{0:T(1024)}, u32[]{:S(2)}) %copy-start.6) | copy-done | bytes 4120
  5.8 1.0 %shard_map.82 = (bf16[64,512]{1,0:T(8,128)(2,1)S(1)}, bf16[32,256]{1,0:T(8,128)(2,1)S(1)}, bf16[32,128]{1,0:T(8,128)(2,1)S(1)}, bf16[32,128]{1,0:T(8,128)(2,1)S(...) custom-call(s32[2]{0:T(128)S(1)} %pad_add_fusion.place_ref, ...), custom_call_target="tpu_custom_call" | custom-call | tf_op jit(solution)/shard_map/pallas_call | solution.py:327
  6.8 1.6 %collective-permute-start = (bf16[64,512]{1,0:T(8,128)(2,1)S(1)}, bf16[64,512]{1,0:T(8,128)(2,1)S(1)}, u32[]{:S(2)}, u32[]{:S(2)}) collective-permute-start(bf16[64,512]{1,0:T(8,128)(2,1)S(1)} %get-tuple-element.24), channel_id=1, source_target_pairs={{0,2},{2,0},{4,6},{6,4},{8,10},{10,8},{12,14},{14,12},{1,3},{3,1},... | collective-permute-start | bytes 196616 | tf_op jit(solution)/shard_map/ppermute | solution.py:320
  8.4 0.5 %collective-permute-start.5 = (bf16[64,768]{1,0:T(8,128)(2,1)S(1)}, bf16[64,768]{1,0:T(8,128)(2,1)S(1)}, u32[]{:S(2)}, u32[]{:S(2)}) collective-permute-start(bf16[64,768]{1,0:T(8,128)(2,1)S(1)} %get-tuple-element.29), channel_id=1, source_target_pairs={{0,2},{2,0},{4,6},{6,4},{8,10},{10,8},{12,14},{14,12},{1,3},{3,1},... | collective-permute-start | bytes 294920 | tf_op jit(solution)/shard_map/ppermute | solution.py:320
  8.9 1.6 %collective-permute-start.3 = (bf16[64,768]{1,0:T(8,128)(2,1)S(1)}, bf16[64,768]{1,0:T(8,128)(2,1)S(1)}, u32[]{:S(2)}, u32[]{:S(2)}) collective-permute-start(bf16[64,768]{1,0:T(8,128)(2,1)S(1)} %get-tuple-element.29), channel_id=1, source_target_pairs={{0,4},{2,6},{4,0},{6,2},{8,12},{10,14},{12,8},{14,10},{1,5},{3,7},... | collective-permute-start | bytes 294920 | tf_op jit(solution)/shard_map/ppermute | solution.py:320
  10.5 1.4 %collective-permute-done.r1_ref = bf16[64,512]{1,0:T(8,128)(2,1)S(1)} collective-permute-done((bf16[64,512]{1,0:T(8,128)(2,1)S(1)}, bf16[64,512]{1,0:T(8,128)(2,1)S(1)}, u32[]{:S(2)}, u32[]{:S(2)}) %collective-permute-start) | collective-permute-done | bytes 65568 | tf_op jit(solution)/shard_map/ppermute | solution.py:320
  11.9 0.1 collective-permute-start.1
  12.0 2.0 %collective-permute-start.4 = (bf16[64,768]{1,0:T(8,128)(2,1)S(1)}, bf16[64,768]{1,0:T(8,128)(2,1)S(1)}, u32[]{:S(2)}, u32[]{:S(2)}) collective-permute-start(bf16[64,768]{1,0:T(8,128)(2,1)S(1)} %shard_map.84), channel_id=1, source_target_pairs={{0,4},{2,6},{4,0},{6,2},{8,12},{10,14},{12,8},{14,10},{1,5},{3,7},... | collective-permute-start | bytes 294920 | tf_op jit(solution)/shard_map/ppermute | solution.py:320
  13.9 1.3 %collective-permute-done.3.d2_ref.refs_4_ = bf16[64,768]{1,0:T(8,128)(2,1)S(1)} collective-permute-done((bf16[64,768]{1,0:T(8,128)(2,1)S(1)}, bf16[64,768]{1,0:T(8,128)(2,1)S(1)}, u32[]{:S(2)}, u32[]{:S(2)}) %collective-permute-start.3) | collective-permute-done | bytes 98336 | tf_op jit(solution)/shard_map/ppermute | solution.py:320
  15.3 2.3 %collective-permute-done.1.r4_ref = bf16[64,768]{1,0:T(8,128)(2,1)S(1)} collective-permute-done((bf16[64,768]{1,0:T(8,128)(2,1)S(1)}, bf16[64,768]{1,0:T(8,128)(2,1)S(1)}, u32[]{:S(2)}, u32[]{:S(2)}) %collective-permute-start.1) | collective-permute-done | bytes 98336 | tf_op jit(solution)/shard_map/ppermute | solution.py:320
  17.6 0.2 collective-permute-done.4.d6_ref.refs_5_
  17.8 1.4 %collective-permute-start.7 = (bf16[64,1280]{1,0:T(8,128)(2,1)S(1)}, bf16[64,1280]{1,0:T(8,128)(2,1)S(1)}, u32[]{:S(2)}, u32[]{:S(2)}) collective-permute-start(bf16[64,1280]{1,0:T(8,128)(2,1)S(1)} %get-tuple-element.31), channel_id=1, source_target_pairs={{0,4},{2,6},{4,0},{6,2},{8,12},{10,14},{12,8},{14,10},{1,5},{3,7},... | collective-permute-start | bytes 491528 | tf_op jit(solution)/shard_map/ppermute | solution.py:320
  19.2 1.1 %collective-permute-start.9 = (bf16[64,2304]{1,0:T(8,128)(2,1)S(1)}, bf16[64,2304]{1,0:T(8,128)(2,1)S(1)}, u32[]{:S(2)}, u32[]{:S(2)}) collective-permute-start(bf16[64,2304]{1,0:T(8,128)(2,1)S(1)} %get-tuple-element.33), channel_id=1, source_target_pairs={{0,2},{2,0},{4,6},{6,4},{8,10},{10,8},{12,14},{14,12},{1,3},{3,1},... | collective-permute-start | bytes 884744 | tf_op jit(solution)/shard_map/ppermute | solution.py:320
  20.4 2.8 %collective-permute-done.7.mine_ref = bf16[64,1280]{1,0:T(8,128)(2,1)S(1)} collective-permute-done((bf16[64,1280]{1,0:T(8,128)(2,1)S(1)}, bf16[64,1280]{1,0:T(8,128)(2,1)S(1)}, u32[]{:S(2)}, u32[]{:S(2)}) %collective-permute-start.7) | collective-permute-done | bytes 163872 | tf_op jit(solution)/shard_map/ppermute | solution.py:320
  23.2 0.9 %shard_map.86 = (bf16[512,256]{1,0:T(8,128)(2,1)S(1)}, f32[128,512]{1,0:T(8,128)S(1)}) custom-call(s32[2]{0:T(128)S(1)} %pad_add_fusion.place_ref, bf16[64,1536]{1,0:T(8,128)(2,1)S(1)} %get-tuple-element.30.mine_ref.kept_ref, bf16[64,1536]{1,0:T(8,128)(2,1)S(1)} %collective-permute-done.6.other_ref.kept2_ref), custom_call_target="tpu_custom_call" | custom-call | tf_op jit(solution)/shard_map/pallas_call | solution.py:369
  24.1 1.8 %collective-permute-done.9.d537_any.refs_3_ = bf16[64,2304]{1,0:T(8,128)(2,1)S(1)} collective-permute-done((bf16[64,2304]{1,0:T(8,128)(2,1)S(1)}, bf16[64,2304]{1,0:T(8,128)(2,1)S(1)}, u32[]{:S(2)}, u32[]{:S(2)}) %collective-permute-start.9) | collective-permute-done | bytes 294944 | tf_op jit(solution)/shard_map/ppermute | solution.py:320
  26.0 1.1 %shard_map.87 = (bf16[512,256]{1,0:T(8,128)(2,1)S(1)}, bf16[128,512]{1,0:T(8,128)(2,1)S(1)}, bf16[128,512]{1,0:T(8,128)(2,1)S(1)}, f32[128,128]{1,0:T(8,128)S(1)}) custom-call(s32[2]{0:T(128)S(1)} %pad_add_fusion.place_ref, bf16[64,1536]{1,0:T(8,128)(2,1)S(1)} %get-tuple-element.30.mine_ref.kept_ref, ...), custom_call_target="tpu_custom_call" | custom-call | tf_op jit(solution)/shard_map/pallas_call | solution.py:375
  27.1 1.8 %shard_map.88 = (f32[128,128]{1,0:T(8,128)S(1)}, f32[128,128]{1,0:T(8,128)S(1)}) custom-call(s32[2]{0:T(128)S(1)} %pad_add_fusion.place_ref, f32[128,128]{1,0:T(8,128)S(1)} %get-tuple-element.23.gene_ref, f32[128,128]{1,0:T(8,128)S(1)} %get-tuple-element.34.power_ref, bf16[512,256]{1,0:T(8,128)(2,1)S(1)} %get-tuple-element.35.turned_ref, ...), custom_call_target="tpu_custom_call" | custom-call | tf_op jit(solution)/shard_map/pallas_call | solution.py:382
  28.9 0.1 collective-permute-start.10
  29.0 1.2 %collective-permute-done.10 = f32[128,128]{1,0:T(8,128)S(1)} collective-permute-done((f32[128,128]{1,0:T(8,128)S(1)}, f32[128,128]{1,0:T(8,128)S(1)}, u32[]{:S(2)}, u32[]{:S(2)}) %collective-permute-start.10) | collective-permute-done | bytes 65568 | tf_op jit(solution)/shard_map/ppermute | solution.py:323
  30.2 0.6 %add.7 = f32[128,128]{1,0:T(8,128)} add(f32[128,128]{1,0:T(8,128)S(1)} %get-tuple-element.39, f32[128,128]{1,0:T(8,128)S(1)} %collective-permute-done.10) | non-fusion elementwise | flops 16384 | bytes 196608 | tf_op jit(solution)/shard_map/add | solution.py:388
  (24 shorter events, 0.2 us)
Async XLA Ops:
  0.0 0.9 %copy-start = (bf16[64,1536]{1,0:T(8,128)(2,1)S(1)}, bf16[64,1536]{1,0:T(8,128)(2,1)}, u32[]{:S(2)}) copy-start(bf16[64,1536]{1,0:T(8,128)(2,1)} %param.11) | copy-start | bytes 589828
  0.0 5.1 %copy-start.2 = (bf16[64,1024]{1,0:T(8,128)(2,1)S(1)}, bf16[64,1024]{1,0:T(8,128)(2,1)}, u32[]{:S(2)}) copy-start(bf16[64,1024]{1,0:T(8,128)(2,1)} %expr_ref.1) | copy-start | bytes 393220
  0.9 4.2 %copy-start.1 = (bf16[64,256]{1,0:T(8,128)(2,1)S(1)}, bf16[64,256]{1,0:T(8,128)(2,1)}, u32[]{:S(2)}) copy-start(bf16[64,256]{1,0:T(8,128)(2,1)} %vecs_ref.5) | copy-start | bytes 98308
  0.9 11.0 %collective-permute-start.2 = (bf16[64,768]{1,0:T(8,128)(2,1)S(1)}, bf16[64,768]{1,0:T(8,128)(2,1)S(1)}, u32[]{:S(2)}, u32[]{:S(2)}) collective-permute-start(bf16[64,768]{1,0:T(8,128)(2,1)S(1)} %constant_dynamic-slice_fusion.dose_ref.refs_0_), channel_id=1, source_target_pairs={{0,8},{2,10},{4,12},{6,14},{8,0},{10,2},{12,4},{14,6},{1,9},{3,11}... | collective-permute-start | bytes 294920 | tf_op jit(solution)/shard_map/ppermute | solution.py:320
  5.0 0.7 %copy-start.6 = (s32[1024]{0:T(1024)S(1)}, s32[1024]{0:T(1024)}, u32[]{:S(2)}) copy-start(s32[1024]{0:T(1024)} %param.14) | copy-start | bytes 12292
  5.0 0.7 %copy-start.5 = (s32[1024]{0:T(1024)S(1)}, s32[1024]{0:T(1024)}, u32[]{:S(2)}) copy-start(s32[1024]{0:T(1024)} %param.13) | copy-start | bytes 12292
  5.1 0.7 %copy-start.4 = (f32[1024]{0:T(1024)S(1)}, f32[1024]{0:T(1024)}, u32[]{:S(2)}) copy-start(f32[1024]{0:T(1024)} %param.12) | copy-start | bytes 12292
  5.1 0.7 %copy-start.3 = (s32[1024]{0:T(1024)S(1)}, s32[1024]{0:T(1024)}, u32[]{:S(2)}) copy-start(s32[1024]{0:T(1024)} %param.15) | copy-start | bytes 12292
  5.1 0.7 %copy-start.7 = (f32[256]{0:T(256)S(1)}, f32[256]{0:T(256)}, u32[]{:S(2)}) copy-start(f32[256]{0:T(256)} %param.9) | copy-start | bytes 3076
  6.8 5.0 %collective-permute-start = (bf16[64,512]{1,0:T(8,128)(2,1)S(1)}, bf16[64,512]{1,0:T(8,128)(2,1)S(1)}, u32[]{:S(2)}, u32[]{:S(2)}) collective-permute-start(bf16[64,512]{1,0:T(8,128)(2,1)S(1)} %get-tuple-element.24), channel_id=1, source_target_pairs={{0,2},{2,0},{4,6},{6,4},{8,10},{10,8},{12,14},{14,12},{1,3},{3,1},... | collective-permute-start | bytes 196616 | tf_op jit(solution)/shard_map/ppermute | solution.py:320
  8.4 5.5 %collective-permute-start.5 = (bf16[64,768]{1,0:T(8,128)(2,1)S(1)}, bf16[64,768]{1,0:T(8,128)(2,1)S(1)}, u32[]{:S(2)}, u32[]{:S(2)}) collective-permute-start(bf16[64,768]{1,0:T(8,128)(2,1)S(1)} %get-tuple-element.29), channel_id=1, source_target_pairs={{0,2},{2,0},{4,6},{6,4},{8,10},{10,8},{12,14},{14,12},{1,3},{3,1},... | collective-permute-start | bytes 294920 | tf_op jit(solution)/shard_map/ppermute | solution.py:320
  8.9 6.3 %collective-permute-start.3 = (bf16[64,768]{1,0:T(8,128)(2,1)S(1)}, bf16[64,768]{1,0:T(8,128)(2,1)S(1)}, u32[]{:S(2)}, u32[]{:S(2)}) collective-permute-start(bf16[64,768]{1,0:T(8,128)(2,1)S(1)} %get-tuple-element.29), channel_id=1, source_target_pairs={{0,4},{2,6},{4,0},{6,2},{8,12},{10,14},{12,8},{14,10},{1,5},{3,7},... | collective-permute-start | bytes 294920 | tf_op jit(solution)/shard_map/ppermute | solution.py:320
  11.9 5.7 %collective-permute-start.1 = (bf16[64,768]{1,0:T(8,128)(2,1)S(1)}, bf16[64,768]{1,0:T(8,128)(2,1)S(1)}, u32[]{:S(2)}, u32[]{:S(2)}) collective-permute-start(bf16[64,768]{1,0:T(8,128)(2,1)S(1)} %shard_map.83.after_any), channel_id=1, source_target_pairs={{0,8},{2,10},{4,12},{6,14},{8,0},{10,2},{12,4},{14,6},{1,9},{3,11}... | collective-permute-start | bytes 294920 | tf_op jit(solution)/shard_map/ppermute | solution.py:320
  12.0 5.8 %collective-permute-start.4 = (bf16[64,768]{1,0:T(8,128)(2,1)S(1)}, bf16[64,768]{1,0:T(8,128)(2,1)S(1)}, u32[]{:S(2)}, u32[]{:S(2)}) collective-permute-start(bf16[64,768]{1,0:T(8,128)(2,1)S(1)} %shard_map.84), channel_id=1, source_target_pairs={{0,4},{2,6},{4,0},{6,2},{8,12},{10,14},{12,8},{14,10},{1,5},{3,7},... | collective-permute-start | bytes 294920 | tf_op jit(solution)/shard_map/ppermute | solution.py:320
  17.8 5.4 %collective-permute-start.7 = (bf16[64,1280]{1,0:T(8,128)(2,1)S(1)}, bf16[64,1280]{1,0:T(8,128)(2,1)S(1)}, u32[]{:S(2)}, u32[]{:S(2)}) collective-permute-start(bf16[64,1280]{1,0:T(8,128)(2,1)S(1)} %get-tuple-element.31), channel_id=1, source_target_pairs={{0,4},{2,6},{4,0},{6,2},{8,12},{10,14},{12,8},{14,10},{1,5},{3,7},... | collective-permute-start | bytes 491528 | tf_op jit(solution)/shard_map/ppermute | solution.py:320
  19.2 6.7 %collective-permute-start.9 = (bf16[64,2304]{1,0:T(8,128)(2,1)S(1)}, bf16[64,2304]{1,0:T(8,128)(2,1)S(1)}, u32[]{:S(2)}, u32[]{:S(2)}) collective-permute-start(bf16[64,2304]{1,0:T(8,128)(2,1)S(1)} %get-tuple-element.33), channel_id=1, source_target_pairs={{0,2},{2,0},{4,6},{6,4},{8,10},{10,8},{12,14},{14,12},{1,3},{3,1},... | collective-permute-start | bytes 884744 | tf_op jit(solution)/shard_map/ppermute | solution.py:320
  20.4 2.8 %collective-permute-start.6 = (bf16[64,1536]{1,0:T(8,128)(2,1)S(1)}, bf16[64,1536]{1,0:T(8,128)(2,1)S(1)}, u32[]{:S(2)}, u32[]{:S(2)}) collective-permute-start(bf16[64,1536]{1,0:T(8,128)(2,1)S(1)} %get-tuple-element.30.mine_ref.kept_ref), channel_id=1, source_target_pairs={{0,1},{1,0},{2,3},{3,2},{4,5},{5,4},{6,7},{7,6},{8,9},{9,8},{10,11... | collective-permute-start | bytes 589832 | tf_op jit(solution)/shard_map/ppermute | solution.py:323
  23.2 2.8 %collective-permute-start.8 = (bf16[64,1280]{1,0:T(8,128)(2,1)S(1)}, bf16[64,1280]{1,0:T(8,128)(2,1)S(1)}, u32[]{:S(2)}, u32[]{:S(2)}) collective-permute-start(bf16[64,1280]{1,0:T(8,128)(2,1)S(1)} %collective-permute-done.7.mine_ref), channel_id=1, source_target_pairs={{0,1},{1,0},{2,3},{3,2},{4,5},{5,4},{6,7},{7,6},{8,9},{9,8},{10,11... | collective-permute-start | bytes 491528 | tf_op jit(solution)/shard_map/ppermute | solution.py:323
  28.9 1.3 %collective-permute-start.10 = (f32[128,128]{1,0:T(8,128)S(1)}, f32[128,128]{1,0:T(8,128)S(1)}, u32[]{:S(2)}, u32[]{:S(2)}) collective-permute-start(f32[128,128]{1,0:T(8,128)S(1)} %get-tuple-element.40), channel_id=1, source_target_pairs={{0,1},{1,0},{2,3},{3,2},{4,5},{5,4},{6,7},{7,6},{8,9},{9,8},{10,11... | collective-permute-start | bytes 196616 | tf_op jit(solution)/shard_map/ppermute | solution.py:323

commit v8 on v7

--- a/solution.py
+++ b/solution.py
@@ -170,8 +170,9 @@
     out_ref[part:, 2 * half :] = r1_ref[part:, half:]
 
 
-def copy_kernel(dose_ref, after_any, out_ref):
-    out_ref[...] = dose_ref[...]
+def copy_kernel(d0_ref, d4_ref, after_any, own_ref, far_ref):
+    own_ref[...] = d0_ref[...]
+    far_ref[...] = d4_ref[...]
 
 
 def third_kernel(
@@ -228,7 +229,7 @@
 
 
 def weight_kernel(
-    place_ref, kept_ref, kept2_ref, mine_ref, other_ref, share_ref, gene_ref, d537_any,
+    place_ref, kept_ref, kept2_ref, mine_ref, other_ref, share_ref, gene_ref,
     turned_ref, weighted_ref, low_ref, power_ref, data_scr,
 ):
     half = turned_ref.shape[0] // 2
@@ -274,24 +275,16 @@
         offset = start + half * LANES - core * variants
         block = offset >> 7
         shift = offset & (LANES - 1)
-        at = lane + shift
-        wrapped = at >= LANES
-        at = at & (LANES - 1)
-        here = block + wrapped.astype(jnp.int32)
-        picked = []
-        for array in (cross, power):
-            low = jnp.zeros((genes, LANES), f32)
-            high = low
-            for b in range(blocks):
-                part = array[:, b * LANES : (b + 1) * LANES]
-                low = jnp.where(block == b, part, low)
-                high = jnp.where(block + 1 == b, part, high)
-            low = jnp.take_along_axis(low, at, axis=1)
-            high = jnp.take_along_axis(high, at, axis=1)
-            picked.append(jnp.where(wrapped, high, low))
-        live = (here >= 0) & (here < blocks) & (lane + half * LANES < valid)
-        score = scale * picked[0] / jnp.sqrt(picked[1] * own_power)
-        out_ref[...] = jnp.where(live, score, 0.0)
+        need = block + (lane < shift).astype(jnp.int32)
+        products = [jnp.zeros((genes, LANES), f32)] * 2
+        for b in range(blocks):
+            here = need == b
+            parts = [array[:, b * LANES : (b + 1) * LANES] for array in (cross, power)]
+            products = [jnp.where(here, part, product) for part, product in zip(parts, products)]
+        inside = (need >= 0) & (need < blocks)
+        score = jnp.where(inside, scale * products[0] / jnp.sqrt(products[1] * own_power), 0.0)
+        score = jnp.take_along_axis(score, (lane + shift) & (LANES - 1), axis=1)
+        out_ref[...] = jnp.where(lane + half * LANES < valid, score, 0.0)
 
 
 def call(kernel, outs, count, scratch=(), smem=1, anywhere=0):
@@ -349,10 +342,11 @@
     )
     r1 = swap(ahead, 1)
     d2 = swap(again, 2)
-    d1 = swap(again, 1)
     to4 = call(second_kernel, [((panel, 2 * half + 2 * LANES), bf16)], 3, smem=0)(eigvecs, r1, e46)[0]
     r4 = swap(to4, 4)
-    d6 = swap(call(copy_kernel, [((panel, variants), bf16)], 2, smem=0, anywhere=1)(d4, to4)[0], 2)
+    own, far = call(copy_kernel, [((panel, variants), bf16)] * 2, 3, smem=0, anywhere=1)(d0, d4, to4)
+    d6 = swap(far, 2)
+    d1 = swap(own, 1)
     width = 4 * half + 2 * LANES
     out, kept, three = call(
         third_kernel,
@@ -375,10 +369,9 @@
     turned2, weighted, low, power = call(
         weight_kernel,
         [shape, ((LANES, 2 * half), bf16), ((LANES, 2 * half), bf16), ((LANES, LANES), f32)],
-        8,
+        7,
         scratch=[pltpu.VMEM((samples // 2, LANES), bf16)],
-        anywhere=1,
-    )(place, kept, kept2, near, near2, share, gene, d537)
+    )(place, kept, kept2, near, near2, share, gene)
     keep, passed = call(
         score_kernel,
         [((LANES, LANES), f32)] * 2,

time: 31 us -> 29.6 us (0.955)
  waiting for transfers between devices: 11.1 us -> 9.11 us
  starting transfers between devices: 12.4 us -> 13.1 us
    ppermute x8, waiting for transfers between devices: 9.84 us -> 7.54 us  [swap(): return lax.ppermute(x, 'row', [(i, i ^ m) for i in range(rows)])]
    ppermute x8, starting transfers between devices: 12.3 us -> 12.9 us  [swap(): return lax.ppermute(x, 'row', [(i, i ^ m) for i in range(rows)])]
    ppermute x3, waiting for transfers between devices: 1.25 us -> 1.57 us  [other_core(): return lax.ppermute(x, 'col', [(0, 1), (1, 0)])]
  transfers between devices with their start and end apart: 11 -> 11, of which waited for: 7 -> 7; matrix products, arithmetic and copies ran while one was open for 0% -> 0% of each run, Pallas kernels for 6% -> 10%
where the time goes in v8:
time: 29.6 us; the launch traced here: 29.5 us
  starting transfers between devices  13.1 us (44%)
  waiting for transfers between devices  9.11 us (31%)
  Pallas kernels  4.8 us (16%)
  local copies, waits for them, and re-layouts  1.64 us (6%)
  other arithmetic  0.71 us (2%)
    ppermute x8, starting transfers between devices, swap(): return lax.ppermute(x, 'row', [(i, i ^ m) for i in range(rows)])  12.9 us
    ppermute x8, waiting for transfers between devices, swap(): return lax.ppermute(x, 'row', [(i, i ^ m) for i in range(rows)])  7.54 us
    pallas_call x1, Pallas kernels, near_body(): call(score_kernel, [((LANES, LANES), f32)] * 2, 13, scratch=[pltpu.VMEM((...  1.72 us
    unnamed x16, local copies, waits for them, and re-layouts  1.63 us
    ppermute x3, waiting for transfers between devices, other_core(): return lax.ppermute(x, 'col', [(0, 1), (1, 0)])  1.57 us
    pallas_call x1, Pallas kernels, near_body(): call(weight_kernel, [shape, ((LANES, 2 * half), bf16), ((LANES, 2 * half)...  1.08 us
    pallas_call x1, Pallas kernels, near_body(): call(route_kernel, [((panel, half + 2 * LANES), bf16), ((part, 2 * LANES)...  1 us
    pallas_call x1, Pallas kernels, near_body(): call(half_kernel, [shape, ((LANES, 2 * half), f32)], 3, scratch=[pltpu.VM...  0.93 us
  transfers between devices with their start and end apart: 11, of which 7 were waited for; matrix products, arithmetic and copies ran while one was open for 0% of the time, Pallas kernels for 10%

profile of v8, /device:TPU:0, one launch (start us, length us, event | category | flops | bytes accessed | tf_op | source)
XLA Modules:
  0.0 29.5 jit_solution(14362732214566165602)
XLA Ops:
  0.0 0.9 %copy-done = bf16[64,1536]{1,0:T(8,128)(2,1)S(1)} copy-done((bf16[64,1536]{1,0:T(8,128)(2,1)S(1)}, bf16[64,1536]{1,0:T(8,128)(2,1)}, u32[]{:S(2)}) %copy-start) | copy-done | bytes 196632
  0.9 4.1 %collective-permute-start.2 = (bf16[64,768]{1,0:T(8,128)(2,1)S(1)}, bf16[64,768]{1,0:T(8,128)(2,1)S(1)}, u32[]{:S(2)}, u32[]{:S(2)}) collective-permute-start(bf16[64,768]{1,0:T(8,128)(2,1)S(1)} %constant_dynamic-slice_fusion.dose_ref.d0_ref.refs_0_), channel_id=1, source_target_pairs={{0,8},{2,10},{4,12},{6,14},{8,0},{10,2},{12,4},{14,6},{1,9},{3,11}... | collective-permute-start | bytes 294920 | tf_op jit(solution)/shard_map/ppermute | solution.py:313
  5.0 0.1 pad_add_fusion.place_ref
  5.1 0.6 %copy-done.6 = s32[1024]{0:T(1024)S(1)} copy-done((s32[1024]{0:T(1024)S(1)}, s32[1024]{0:T(1024)}, u32[]{:S(2)}) %copy-start.6) | copy-done | bytes 4120
  5.8 1.0 %shard_map.82 = (bf16[64,512]{1,0:T(8,128)(2,1)S(1)}, bf16[32,256]{1,0:T(8,128)(2,1)S(1)}, bf16[32,128]{1,0:T(8,128)(2,1)S(1)}, bf16[32,128]{1,0:T(8,128)(2,1)S(...) custom-call(s32[2]{0:T(128)S(1)} %pad_add_fusion.place_ref, ...), custom_call_target="tpu_custom_call" | custom-call | tf_op jit(solution)/shard_map/pallas_call | solution.py:320
  6.8 1.6 %collective-permute-start = (bf16[64,512]{1,0:T(8,128)(2,1)S(1)}, bf16[64,512]{1,0:T(8,128)(2,1)S(1)}, u32[]{:S(2)}, u32[]{:S(2)}) collective-permute-start(bf16[64,512]{1,0:T(8,128)(2,1)S(1)} %get-tuple-element.26), channel_id=1, source_target_pairs={{0,2},{2,0},{4,6},{6,4},{8,10},{10,8},{12,14},{14,12},{1,3},{3,1},... | collective-permute-start | bytes 196616 | tf_op jit(solution)/shard_map/ppermute | solution.py:313
  8.4 1.6 %collective-permute-start.3 = (bf16[64,768]{1,0:T(8,128)(2,1)S(1)}, bf16[64,768]{1,0:T(8,128)(2,1)S(1)}, u32[]{:S(2)}, u32[]{:S(2)}) collective-permute-start(bf16[64,768]{1,0:T(8,128)(2,1)S(1)} %get-tuple-element.31), channel_id=1, source_target_pairs={{0,4},{2,6},{4,0},{6,2},{8,12},{10,14},{12,8},{14,10},{1,5},{3,7},... | collective-permute-start | bytes 294920 | tf_op jit(solution)/shard_map/ppermute | solution.py:313
  10.0 1.2 %collective-permute-done.r1_ref = bf16[64,512]{1,0:T(8,128)(2,1)S(1)} collective-permute-done((bf16[64,512]{1,0:T(8,128)(2,1)S(1)}, bf16[64,512]{1,0:T(8,128)(2,1)S(1)}, u32[]{:S(2)}, u32[]{:S(2)}) %collective-permute-start) | collective-permute-done | bytes 65568 | tf_op jit(solution)/shard_map/ppermute | solution.py:313
  11.2 0.1 collective-permute-start.1
  11.3 1.9 %collective-permute-start.4 = (bf16[64,768]{1,0:T(8,128)(2,1)S(1)}, bf16[64,768]{1,0:T(8,128)(2,1)S(1)}, u32[]{:S(2)}, u32[]{:S(2)}) collective-permute-start(bf16[64,768]{1,0:T(8,128)(2,1)S(1)} %get-tuple-element.32), channel_id=1, source_target_pairs={{0,4},{2,6},{4,0},{6,2},{8,12},{10,14},{12,8},{14,10},{1,5},{3,7},... | collective-permute-start | bytes 294920 | tf_op jit(solution)/shard_map/ppermute | solution.py:313
  13.3 1.5 %collective-permute-start.5 = (bf16[64,768]{1,0:T(8,128)(2,1)S(1)}, bf16[64,768]{1,0:T(8,128)(2,1)S(1)}, u32[]{:S(2)}, u32[]{:S(2)}) collective-permute-start(bf16[64,768]{1,0:T(8,128)(2,1)S(1)} %get-tuple-element.33), channel_id=1, source_target_pairs={{0,2},{2,0},{4,6},{6,4},{8,10},{10,8},{12,14},{14,12},{1,3},{3,1},... | collective-permute-start | bytes 294920 | tf_op jit(solution)/shard_map/ppermute | solution.py:313
  14.8 2.0 %collective-permute-done.1.r4_ref = bf16[64,768]{1,0:T(8,128)(2,1)S(1)} collective-permute-done((bf16[64,768]{1,0:T(8,128)(2,1)S(1)}, bf16[64,768]{1,0:T(8,128)(2,1)S(1)}, u32[]{:S(2)}, u32[]{:S(2)}) %collective-permute-start.1) | collective-permute-done | bytes 98336 | tf_op jit(solution)/shard_map/ppermute | solution.py:313
  16.8 0.5 %collective-permute-done.4.d6_ref.refs_5_ = bf16[64,768]{1,0:T(8,128)(2,1)S(1)} collective-permute-done((bf16[64,768]{1,0:T(8,128)(2,1)S(1)}, bf16[64,768]{1,0:T(8,128)(2,1)S(1)}, u32[]{:S(2)}, u32[]{:S(2)}) %collective-permute-start.4) | collective-permute-done | bytes 98336 | tf_op jit(solution)/shard_map/ppermute | solution.py:313
  17.3 0.6 %collective-permute-done.5.d1_any.refs_1_ = bf16[64,768]{1,0:T(8,128)(2,1)S(1)} collective-permute-done((bf16[64,768]{1,0:T(8,128)(2,1)S(1)}, bf16[64,768]{1,0:T(8,128)(2,1)S(1)}, u32[]{:S(2)}, u32[]{:S(2)}) %collective-permute-start.5) | collective-permute-done | bytes 98336 | tf_op jit(solution)/shard_map/ppermute | solution.py:313
  17.9 0.6 %collective-permute-start.7 = (bf16[64,1280]{1,0:T(8,128)(2,1)S(1)}, bf16[64,1280]{1,0:T(8,128)(2,1)S(1)}, u32[]{:S(2)}, u32[]{:S(2)}) collective-permute-start(bf16[64,1280]{1,0:T(8,128)(2,1)S(1)} %get-tuple-element.35), channel_id=1, source_target_pairs={{0,4},{2,6},{4,0},{6,2},{8,12},{10,14},{12,8},{14,10},{1,5},{3,7},... | collective-permute-start | bytes 491528 | tf_op jit(solution)/shard_map/ppermute | solution.py:313
  18.5 1.5 %collective-permute-start.9 = (bf16[64,2304]{1,0:T(8,128)(2,1)S(1)}, bf16[64,2304]{1,0:T(8,128)(2,1)S(1)}, u32[]{:S(2)}, u32[]{:S(2)}) collective-permute-start(bf16[64,2304]{1,0:T(8,128)(2,1)S(1)} %get-tuple-element.42), channel_id=1, source_target_pairs={{0,2},{2,0},{4,6},{6,4},{8,10},{10,8},{12,14},{14,12},{1,3},{3,1},... | collective-permute-start | bytes 884744 | tf_op jit(solution)/shard_map/ppermute | solution.py:313
  20.0 3.3 %collective-permute-done.7.mine_ref = bf16[64,1280]{1,0:T(8,128)(2,1)S(1)} collective-permute-done((bf16[64,1280]{1,0:T(8,128)(2,1)S(1)}, bf16[64,1280]{1,0:T(8,128)(2,1)S(1)}, u32[]{:S(2)}, u32[]{:S(2)}) %collective-permute-start.7) | collective-permute-done | bytes 163872 | tf_op jit(solution)/shard_map/ppermute | solution.py:313
  23.3 0.9 %shard_map.86 = (bf16[512,256]{1,0:T(8,128)(2,1)S(1)}, f32[128,512]{1,0:T(8,128)S(1)}) custom-call(s32[2]{0:T(128)S(1)} %pad_add_fusion.place_ref, bf16[64,1536]{1,0:T(8,128)(2,1)S(1)} %get-tuple-element.34.mine_ref.kept_ref, bf16[64,1536]{1,0:T(8,128)(2,1)S(1)} %collective-permute-done.6.other_ref.kept2_ref), custom_call_target="tpu_custom_call" | custom-call | tf_op jit(solution)/shard_map/pallas_call | solution.py:363
  24.3 0.5 %collective-permute-done.8.other_ref = bf16[64,1280]{1,0:T(8,128)(2,1)S(1)} collective-permute-done((bf16[64,1280]{1,0:T(8,128)(2,1)S(1)}, bf16[64,1280]{1,0:T(8,128)(2,1)S(1)}, u32[]{:S(2)}, u32[]{:S(2)}) %collective-permute-start.8) | collective-permute-done | bytes 163872 | tf_op jit(solution)/shard_map/ppermute | solution.py:316
  24.7 1.1 %shard_map.87 = (bf16[512,256]{1,0:T(8,128)(2,1)S(1)}, bf16[128,512]{1,0:T(8,128)(2,1)S(1)}, bf16[128,512]{1,0:T(8,128)(2,1)S(1)}, f32[128,128]{1,0:T(8,128)S(1)}) custom-call(s32[2]{0:T(128)S(1)} %pad_add_fusion.place_ref, bf16[64,1536]{1,0:T(8,128)(2,1)S(1)} %get-tuple-element.34.mine_ref.kept_ref, ...), custom_call_target="tpu_custom_call" | custom-call | tf_op jit(solution)/shard_map/pallas_call | solution.py:369
  25.8 1.7 %shard_map.88 = (f32[128,128]{1,0:T(8,128)S(1)}, f32[128,128]{1,0:T(8,128)S(1)}) custom-call(s32[2]{0:T(128)S(1)} %pad_add_fusion.place_ref, f32[128,128]{1,0:T(8,128)S(1)} %get-tuple-element.25.gene_ref, f32[128,128]{1,0:T(8,128)S(1)} %get-tuple-element.37.power_ref, bf16[512,256]{1,0:T(8,128)(2,1)S(1)} %get-tuple-element.38.turned_ref, ...), custom_call_target="tpu_custom_call" | custom-call | tf_op jit(solution)/shard_map/pallas_call | solution.py:375
  27.5 0.2 collective-permute-start.10
  27.7 1.1 %collective-permute-done.10 = f32[128,128]{1,0:T(8,128)S(1)} collective-permute-done((f32[128,128]{1,0:T(8,128)S(1)}, f32[128,128]{1,0:T(8,128)S(1)}, u32[]{:S(2)}, u32[]{:S(2)}) %collective-permute-start.10) | collective-permute-done | bytes 65568 | tf_op jit(solution)/shard_map/ppermute | solution.py:316
  28.8 0.6 %add.7 = f32[128,128]{1,0:T(8,128)} add(f32[128,128]{1,0:T(8,128)S(1)} %get-tuple-element.43, f32[128,128]{1,0:T(8,128)S(1)} %collective-permute-done.10) | non-fusion elementwise | flops 16384 | bytes 196608 | tf_op jit(solution)/shard_map/add | solution.py:381
  (24 shorter events, 0.2 us)
Async XLA Ops:
  0.0 0.9 %copy-start = (bf16[64,1536]{1,0:T(8,128)(2,1)S(1)}, bf16[64,1536]{1,0:T(8,128)(2,1)}, u32[]{:S(2)}) copy-start(bf16[64,1536]{1,0:T(8,128)(2,1)} %param.11) | copy-start | bytes 589828
  0.0 5.1 %copy-start.2 = (bf16[64,1024]{1,0:T(8,128)(2,1)S(1)}, bf16[64,1024]{1,0:T(8,128)(2,1)}, u32[]{:S(2)}) copy-start(bf16[64,1024]{1,0:T(8,128)(2,1)} %expr_ref.1) | copy-start | bytes 393220
  0.9 4.2 %copy-start.1 = (bf16[64,256]{1,0:T(8,128)(2,1)S(1)}, bf16[64,256]{1,0:T(8,128)(2,1)}, u32[]{:S(2)}) copy-start(bf16[64,256]{1,0:T(8,128)(2,1)} %vecs_ref.5) | copy-start | bytes 98308
  0.9 10.4 %collective-permute-start.2 = (bf16[64,768]{1,0:T(8,128)(2,1)S(1)}, bf16[64,768]{1,0:T(8,128)(2,1)S(1)}, u32[]{:S(2)}, u32[]{:S(2)}) collective-permute-start(bf16[64,768]{1,0:T(8,128)(2,1)S(1)} %constant_dynamic-slice_fusion.dose_ref.d0_ref.refs_0_), channel_id=1, source_target_pairs={{0,8},{2,10},{4,12},{6,14},{8,0},{10,2},{12,4},{14,6},{1,9},{3,11}... | collective-permute-start | bytes 294920 | tf_op jit(solution)/shard_map/ppermute | solution.py:313
  5.0 0.7 %copy-start.6 = (s32[1024]{0:T(1024)S(1)}, s32[1024]{0:T(1024)}, u32[]{:S(2)}) copy-start(s32[1024]{0:T(1024)} %param.14) | copy-start | bytes 12292
  5.0 0.7 %copy-start.5 = (s32[1024]{0:T(1024)S(1)}, s32[1024]{0:T(1024)}, u32[]{:S(2)}) copy-start(s32[1024]{0:T(1024)} %param.13) | copy-start | bytes 12292
  5.1 0.7 %copy-start.4 = (f32[1024]{0:T(1024)S(1)}, f32[1024]{0:T(1024)}, u32[]{:S(2)}) copy-start(f32[1024]{0:T(1024)} %param.12) | copy-start | bytes 12292
  5.1 0.7 %copy-start.3 = (s32[1024]{0:T(1024)S(1)}, s32[1024]{0:T(1024)}, u32[]{:S(2)}) copy-start(s32[1024]{0:T(1024)} %param.15) | copy-start | bytes 12292
  5.1 0.7 %copy-start.7 = (f32[256]{0:T(256)S(1)}, f32[256]{0:T(256)}, u32[]{:S(2)}) copy-start(f32[256]{0:T(256)} %param.9) | copy-start | bytes 3076
  6.8 4.3 %collective-permute-start = (bf16[64,512]{1,0:T(8,128)(2,1)S(1)}, bf16[64,512]{1,0:T(8,128)(2,1)S(1)}, u32[]{:S(2)}, u32[]{:S(2)}) collective-permute-start(bf16[64,512]{1,0:T(8,128)(2,1)S(1)} %get-tuple-element.26), channel_id=1, source_target_pairs={{0,2},{2,0},{4,6},{6,4},{8,10},{10,8},{12,14},{14,12},{1,3},{3,1},... | collective-permute-start | bytes 196616 | tf_op jit(solution)/shard_map/ppermute | solution.py:313
  8.4 6.3 %collective-permute-start.3 = (bf16[64,768]{1,0:T(8,128)(2,1)S(1)}, bf16[64,768]{1,0:T(8,128)(2,1)S(1)}, u32[]{:S(2)}, u32[]{:S(2)}) collective-permute-start(bf16[64,768]{1,0:T(8,128)(2,1)S(1)} %get-tuple-element.31), channel_id=1, source_target_pairs={{0,4},{2,6},{4,0},{6,2},{8,12},{10,14},{12,8},{14,10},{1,5},{3,7},... | collective-permute-start | bytes 294920 | tf_op jit(solution)/shard_map/ppermute | solution.py:313
  11.2 5.6 %collective-permute-start.1 = (bf16[64,768]{1,0:T(8,128)(2,1)S(1)}, bf16[64,768]{1,0:T(8,128)(2,1)S(1)}, u32[]{:S(2)}, u32[]{:S(2)}) collective-permute-start(bf16[64,768]{1,0:T(8,128)(2,1)S(1)} %shard_map.83.after_any), channel_id=1, source_target_pairs={{0,8},{2,10},{4,12},{6,14},{8,0},{10,2},{12,4},{14,6},{1,9},{3,11}... | collective-permute-start | bytes 294920 | tf_op jit(solution)/shard_map/ppermute | solution.py:313
  11.3 6.0 %collective-permute-start.4 = (bf16[64,768]{1,0:T(8,128)(2,1)S(1)}, bf16[64,768]{1,0:T(8,128)(2,1)S(1)}, u32[]{:S(2)}, u32[]{:S(2)}) collective-permute-start(bf16[64,768]{1,0:T(8,128)(2,1)S(1)} %get-tuple-element.32), channel_id=1, source_target_pairs={{0,4},{2,6},{4,0},{6,2},{8,12},{10,14},{12,8},{14,10},{1,5},{3,7},... | collective-permute-start | bytes 294920 | tf_op jit(solution)/shard_map/ppermute | solution.py:313
  13.3 4.6 %collective-permute-start.5 = (bf16[64,768]{1,0:T(8,128)(2,1)S(1)}, bf16[64,768]{1,0:T(8,128)(2,1)S(1)}, u32[]{:S(2)}, u32[]{:S(2)}) collective-permute-start(bf16[64,768]{1,0:T(8,128)(2,1)S(1)} %get-tuple-element.33), channel_id=1, source_target_pairs={{0,2},{2,0},{4,6},{6,4},{8,10},{10,8},{12,14},{14,12},{1,3},{3,1},... | collective-permute-start | bytes 294920 | tf_op jit(solution)/shard_map/ppermute | solution.py:313
  17.9 5.4 %collective-permute-start.7 = (bf16[64,1280]{1,0:T(8,128)(2,1)S(1)}, bf16[64,1280]{1,0:T(8,128)(2,1)S(1)}, u32[]{:S(2)}, u32[]{:S(2)}) collective-permute-start(bf16[64,1280]{1,0:T(8,128)(2,1)S(1)} %get-tuple-element.35), channel_id=1, source_target_pairs={{0,4},{2,6},{4,0},{6,2},{8,12},{10,14},{12,8},{14,10},{1,5},{3,7},... | collective-permute-start | bytes 491528 | tf_op jit(solution)/shard_map/ppermute | solution.py:313
  18.5 7.3 %collective-permute-start.9 = (bf16[64,2304]{1,0:T(8,128)(2,1)S(1)}, bf16[64,2304]{1,0:T(8,128)(2,1)S(1)}, u32[]{:S(2)}, u32[]{:S(2)}) collective-permute-start(bf16[64,2304]{1,0:T(8,128)(2,1)S(1)} %get-tuple-element.42), channel_id=1, source_target_pairs={{0,2},{2,0},{4,6},{6,4},{8,10},{10,8},{12,14},{14,12},{1,3},{3,1},... | collective-permute-start | bytes 884744 | tf_op jit(solution)/shard_map/ppermute | solution.py:313
  20.0 3.3 %collective-permute-start.6 = (bf16[64,1536]{1,0:T(8,128)(2,1)S(1)}, bf16[64,1536]{1,0:T(8,128)(2,1)S(1)}, u32[]{:S(2)}, u32[]{:S(2)}) collective-permute-start(bf16[64,1536]{1,0:T(8,128)(2,1)S(1)} %get-tuple-element.34.mine_ref.kept_ref), channel_id=1, source_target_pairs={{0,1},{1,0},{2,3},{3,2},{4,5},{5,4},{6,7},{7,6},{8,9},{9,8},{10,11... | collective-permute-start | bytes 589832 | tf_op jit(solution)/shard_map/ppermute | solution.py:316
  23.3 1.4 %collective-permute-start.8 = (bf16[64,1280]{1,0:T(8,128)(2,1)S(1)}, bf16[64,1280]{1,0:T(8,128)(2,1)S(1)}, u32[]{:S(2)}, u32[]{:S(2)}) collective-permute-start(bf16[64,1280]{1,0:T(8,128)(2,1)S(1)} %collective-permute-done.7.mine_ref), channel_id=1, source_target_pairs={{0,1},{1,0},{2,3},{3,2},{4,5},{5,4},{6,7},{7,6},{8,9},{9,8},{10,11... | collective-permute-start | bytes 491528 | tf_op jit(solution)/shard_map/ppermute | solution.py:316
  27.5 1.3 %collective-permute-start.10 = (f32[128,128]{1,0:T(8,128)S(1)}, f32[128,128]{1,0:T(8,128)S(1)}, u32[]{:S(2)}, u32[]{:S(2)}) collective-permute-start(f32[128,128]{1,0:T(8,128)S(1)} %get-tuple-element.44), channel_id=1, source_target_pairs={{0,1},{1,0},{2,3},{3,2},{4,5},{5,4},{6,7},{7,6},{8,9},{9,8},{10,11... | collective-permute-start | bytes 196616 | tf_op jit(solution)/shard_map/ppermute | solution.py:316

commit v9 on v8

--- a/solution.py
+++ b/solution.py
@@ -8,6 +8,7 @@
 W = 256
 LANES = 128
 VMEM_LIMIT = 32 * 1024 * 1024
+ROUTE_LIMIT = 32 * 1024 * 1024
 NT = (((1,), (1,)), ((), ()))
 f32 = jnp.float32
 bf16 = jnp.bfloat16
@@ -101,34 +102,51 @@
 
 
 def route_kernel(
-    place_ref, owner_ref, delta_ref, start_ref, valid_ref, vals_ref, vecs_ref, expr_ref, dose_ref,
-    ahead_ref, e46_ref, e2_ref, e0_ref, gene_ref, terms_ref, again_ref,
+    place_ref, owner_any, delta_any, start_any, valid_any, vals_any, vecs_any, expr_any, dose_any,
+    ahead_ref, e46_ref, e2_ref, e0_ref, gene_ref, terms_ref, half_ref,
+    owner_ref, delta_ref, start_ref, valid_ref, vals_ref, expr_ref, sems,
 ):
+    row, core = place_ref[0], place_ref[1]
+    half = vecs_any.shape[1]
+    part = expr_ref.shape[0]
+    variants = half_ref.shape[1]
+    pairs = (
+        (owner_any, owner_ref),
+        (expr_any.at[pl.ds(pl.multiple_of(core * part, part), part)], expr_ref),
+        (delta_any, delta_ref),
+        (start_any, start_ref),
+        (valid_any, valid_ref),
+        (vals_any, vals_ref),
+        (vecs_any, ahead_ref.at[:, pl.ds(0, half)]),
+        (dose_any.at[:, pl.ds(pl.multiple_of(core * variants, LANES), variants)], half_ref),
+    )
+    copies = [pltpu.make_async_copy(a, b, sems.at[i]) for i, (a, b) in enumerate(pairs)]
+    for copy in copies:
+        copy.start()
     slices = owner_ref.shape[0]
     capacity = LANES // slices
-    half = vecs_ref.shape[1]
-    part = expr_ref.shape[0] // 2
-    row, core = place_ref[0], place_ref[1]
-    owner = owner_ref[...]
     before = lax.broadcasted_iota(jnp.int32, (LANES, LANES), 0) < lax.broadcasted_iota(
         jnp.int32, (LANES, LANES), 1
     )
     before = before.astype(bf16)
+    slot = lax.broadcasted_iota(jnp.int32, (LANES, LANES), 0)
+    own_slot = lax.broadcasted_iota(jnp.int32, (capacity, LANES), 0)
+    lane = lax.broadcasted_iota(jnp.int32, (capacity, LANES), 1)
+    copies[0].wait()
+    owner = owner_ref[...]
     rank = jnp.zeros(owner.shape, f32)
     for o in range(slices):
         same = (owner == o).astype(f32)
         rank += same * jnp.dot(same.astype(bf16), before, preferred_element_type=f32)
     bucket = (owner ^ row) * capacity + rank.astype(jnp.int32)
-    slot = lax.broadcasted_iota(jnp.int32, (LANES, LANES), 0)
-    own_slot = lax.broadcasted_iota(jnp.int32, (capacity, LANES), 0)
-    lane = lax.broadcasted_iota(jnp.int32, (capacity, LANES), 1)
-    rows = pl.ds(pl.multiple_of(core * part, part), part)
+    for copy in copies[1:]:
+        copy.wait()
     sorted_slices = []
     for s in range(slices):
         here = bucket[s : s + 1, :]
         pick = (slot == here).astype(bf16)
         sorted_slices.append(
-            lax.dot_general(pick, expr_ref[rows, s * LANES : (s + 1) * LANES], NT, preferred_element_type=f32)
+            lax.dot_general(pick, expr_ref[:, s * LANES : (s + 1) * LANES], NT, preferred_element_type=f32)
         )
         mine = (own_slot == here).astype(f32)
         figures = jnp.zeros((capacity, LANES), f32)
@@ -142,8 +160,6 @@
     term = lax.broadcasted_iota(jnp.int32, terms_ref.shape, 0)
     terms = jnp.where(term == 0, high, jnp.where(term == 1, middle, jnp.where(term == 2, vals - high - middle, 0.0)))
     terms_ref[...] = terms.astype(bf16)
-    again_ref[...] = dose_ref[...]
-    ahead_ref[:, :half] = vecs_ref[...]
     left, right = slice(0, LANES), slice(LANES, 2 * LANES)
     upper, lower = slice(0, part), slice(part, 2 * part)
     targets = {
@@ -161,10 +177,10 @@
         ref[down, side] = block.T.astype(bf16)
 
 
-def second_kernel(vecs_ref, r1_ref, e46_ref, out_ref):
-    half = vecs_ref.shape[1]
+def second_kernel(ahead_ref, r1_ref, e46_ref, out_ref):
+    half = out_ref.shape[1] // 2 - LANES
     part = e46_ref.shape[0]
-    out_ref[:, :half] = vecs_ref[...]
+    out_ref[:, :half] = ahead_ref[:, :half]
     out_ref[:, half : 2 * half] = r1_ref[:, :half]
     out_ref[:part, 2 * half :] = e46_ref[...]
     out_ref[part:, 2 * half :] = r1_ref[part:, half:]
@@ -176,12 +192,12 @@
 
 
 def third_kernel(
-    vecs_ref, r1_ref, r4_ref, e2_ref, e0_ref, terms_ref, d4_ref, d2_ref, d6_ref, d1_any, out_ref, kept_ref, dose_ref
+    ahead_ref, r1_ref, r4_ref, e2_ref, e0_ref, terms_ref, d4_ref, d2_ref, d6_ref, d1_any, out_ref, kept_ref, dose_ref
 ):
-    half = vecs_ref.shape[1]
+    half = terms_ref.shape[1]
     part = e0_ref.shape[0]
     for ref, own, at in ((out_ref, e2_ref, LANES), (kept_ref, e0_ref, 0)):
-        ref[:, :half] = vecs_ref[...]
+        ref[:, :half] = ahead_ref[:, :half]
         ref[:, half : 2 * half] = r1_ref[:, :half]
         ref[:, 2 * half : 4 * half] = r4_ref[:, : 2 * half]
         side = slice(2 * half + at, 2 * half + at + LANES)
@@ -287,7 +303,7 @@
         out_ref[...] = jnp.where(lane + half * LANES < valid, score, 0.0)
 
 
-def call(kernel, outs, count, scratch=(), smem=1, anywhere=0):
+def call(kernel, outs, count, scratch=(), smem=1, anywhere=0, limit=VMEM_LIMIT):
     vmem = pl.BlockSpec(memory_space=pltpu.VMEM)
     return pl.pallas_call(
         kernel,
@@ -295,7 +311,7 @@
         in_specs=[pl.BlockSpec(memory_space=pltpu.SMEM)] * smem + [vmem] * (count - smem - anywhere) + [pl.BlockSpec(memory_space=pl.ANY)] * anywhere,
         out_specs=[vmem] * len(outs),
         scratch_shapes=list(scratch),
-        compiler_params=pltpu.CompilerParams(vmem_limit_bytes=VMEM_LIMIT),
+        compiler_params=pltpu.CompilerParams(vmem_limit_bytes=limit),
     )
 
 
@@ -315,9 +331,7 @@
     def other_core(x):
         return lax.ppermute(x, "col", [(0, 1), (1, 0)])
 
-    d0 = lax.dynamic_slice_in_dim(dosage, core * variants, variants, 1)
-    d4 = swap(d0, 4)
-    ahead, e46, e2, e0, gene, terms, again = call(
+    ahead, e46, e2, e0, gene, terms, d0 = call(
         route_kernel,
         [
             ((panel, half + 2 * LANES), bf16),
@@ -329,20 +343,30 @@
             ((panel, variants), bf16),
         ],
         9,
+        scratch=[pltpu.VMEM((rows, LANES), kind) for kind in (jnp.int32, f32, jnp.int32, jnp.int32)]
+        + [pltpu.VMEM((1, half), f32), pltpu.VMEM((part, expression.shape[1]), bf16), pltpu.SemaphoreType.DMA((8,))],
+        anywhere=8,
+        limit=ROUTE_LIMIT,
     )(
         place,
-        gene_owner.reshape(rows, LANES),
-        delta.reshape(rows, LANES),
-        window_start.reshape(rows, LANES),
-        window_valid.reshape(rows, LANES),
-        eigvals[None, :],
-        eigvecs,
-        expression,
-        d0,
+        *[
+            pltpu.with_memory_space_constraint(x, pltpu.HBM)
+            for x in (
+                gene_owner.reshape(rows, LANES),
+                delta.reshape(rows, LANES),
+                window_start.reshape(rows, LANES),
+                window_valid.reshape(rows, LANES),
+                eigvals[None, :],
+                eigvecs,
+                expression,
+                dosage,
+            )
+        ],
     )
     r1 = swap(ahead, 1)
-    d2 = swap(again, 2)
-    to4 = call(second_kernel, [((panel, 2 * half + 2 * LANES), bf16)], 3, smem=0)(eigvecs, r1, e46)[0]
+    d4 = swap(d0, 4)
+    d2 = swap(d0, 2)
+    to4 = call(second_kernel, [((panel, 2 * half + 2 * LANES), bf16)], 3, smem=0)(ahead, r1, e46)[0]
     r4 = swap(to4, 4)
     own, far = call(copy_kernel, [((panel, variants), bf16)] * 2, 3, smem=0, anywhere=1)(d0, d4, to4)
     d6 = swap(far, 2)
@@ -354,7 +378,7 @@
         10,
         smem=0,
         anywhere=1,
-    )(eigvecs, r1, r4, e2, e0, terms, d4, d2, d6, d1)
+    )(ahead, r1, r4, e2, e0, terms, d4, d2, d6, d1)
     d537 = swap(three, 1)
     kept2 = other_core(kept)
     near = swap(out, 2)

time: 29.6 us -> 29.9 us (1.010)
  the two profiles are of different devices: /device:TPU:0 before, /device:TPU:21 now
where the time goes in v9:
time: 29.9 us; the launch traced here: 29.7 us
  starting transfers between devices  16.5 us (55%)
  waiting for transfers between devices  6.73 us (23%)
  Pallas kernels  5.71 us (19%)
  other arithmetic  0.71 us (2%)
    ppermute x8, starting transfers between devices, swap(): return lax.ppermute(x, 'row', [(i, i ^ m) for i in range(rows)])  10.4 us
    ppermute x3, starting transfers between devices, other_core(): return lax.ppermute(x, 'col', [(0, 1), (1, 0)])  6.13 us
    ppermute x8, waiting for transfers between devices, swap(): return lax.ppermute(x, 'row', [(i, i ^ m) for i in range(rows)])  5.74 us
    pallas_call x1, Pallas kernels, near_body(): call(route_kernel, [((panel, half + 2 * LANES), bf16), ((part, 2 * LANES)...  1.93 us
    pallas_call x1, Pallas kernels, near_body(): call(score_kernel, [((LANES, LANES), f32)] * 2, 13, scratch=[pltpu.VMEM((...  1.71 us
    pallas_call x1, Pallas kernels, near_body(): call(weight_kernel, [shape, ((LANES, 2 * half), bf16), ((LANES, 2 * half)...  1.08 us
    ppermute x3, waiting for transfers between devices, other_core(): return lax.ppermute(x, 'col', [(0, 1), (1, 0)])  1 us
    pallas_call x1, Pallas kernels, near_body(): call(half_kernel, [shape, ((LANES, 2 * half), f32)], 3, scratch=[pltpu.VM...  0.93 us
  transfers between devices with their start and end apart: 11, of which 6 were waited for; matrix products, arithmetic and copies ran while one was open for 0% of the time, Pallas kernels for 7%

profile of v9, /device:TPU:21, one launch (start us, length us, event | category | flops | bytes accessed | tf_op | source)
XLA Modules:
  0.0 29.7 jit_solution(15136778435264949701)
XLA Ops:
  0.0 0.1 pad_add_fusion.place_ref
  0.1 1.9 %shard_map.82 = (bf16[64,512]{1,0:T(8,128)(2,1)S(1)}, bf16[32,256]{1,0:T(8,128)(2,1)S(1)}, bf16[32,128]{1,0:T(8,128)(2,1)S(1)}, bf16[32,128]{1,0:T(8,128)(2,1)S(...) custom-call(s32[2]{0:T(128)S(1)} %pad_add_fusion.place_ref, ...), custom_call_target="tpu_custom_call" | custom-call | tf_op jit(solution)/shard_map/pallas_call | solution.py:334
  2.0 0.1 collective-permute-start.2
  2.1 0.2 collective-permute-start
  2.4 1.3 %collective-permute-start.3 = (bf16[64,768]{1,0:T(8,128)(2,1)S(1)}, bf16[64,768]{1,0:T(8,128)(2,1)S(1)}, u32[]{:S(2)}, u32[]{:S(2)}) collective-permute-start(bf16[64,768]{1,0:T(8,128)(2,1)S(1)} %get-tuple-element.31.d0_ref.refs_0_), channel_id=1, source_target_pairs={{0,4},{2,6},{4,0},{6,2},{8,12},{10,14},{12,8},{14,10},{1,5},{3,7},... | collective-permute-start | bytes 294920 | tf_op jit(solution)/shard_map/ppermute | solution.py:329
  3.7 1.6 %collective-permute-done.r1_ref = bf16[64,512]{1,0:T(8,128)(2,1)S(1)} collective-permute-done((bf16[64,512]{1,0:T(8,128)(2,1)S(1)}, bf16[64,512]{1,0:T(8,128)(2,1)S(1)}, u32[]{:S(2)}, u32[]{:S(2)}) %collective-permute-start) | collective-permute-done | bytes 65568 | tf_op jit(solution)/shard_map/ppermute | solution.py:329
  5.3 2.6 %collective-permute-start.1 = (bf16[64,768]{1,0:T(8,128)(2,1)S(1)}, bf16[64,768]{1,0:T(8,128)(2,1)S(1)}, u32[]{:S(2)}, u32[]{:S(2)}) collective-permute-start(bf16[64,768]{1,0:T(8,128)(2,1)S(1)} %shard_map.83.after_any), channel_id=1, source_target_pairs={{0,8},{2,10},{4,12},{6,14},{8,0},{10,2},{12,4},{14,6},{1,9},{3,11}... | collective-permute-start | bytes 294920 | tf_op jit(solution)/shard_map/ppermute | solution.py:329
  8.0 3.7 %collective-permute-start.4 = (bf16[64,768]{1,0:T(8,128)(2,1)S(1)}, bf16[64,768]{1,0:T(8,128)(2,1)S(1)}, u32[]{:S(2)}, u32[]{:S(2)}) collective-permute-start(bf16[64,768]{1,0:T(8,128)(2,1)S(1)} %get-tuple-element.32), channel_id=1, source_target_pairs={{0,4},{2,6},{4,0},{6,2},{8,12},{10,14},{12,8},{14,10},{1,5},{3,7},... | collective-permute-start | bytes 294920 | tf_op jit(solution)/shard_map/ppermute | solution.py:329
  11.7 0.7 %collective-permute-start.5 = (bf16[64,768]{1,0:T(8,128)(2,1)S(1)}, bf16[64,768]{1,0:T(8,128)(2,1)S(1)}, u32[]{:S(2)}, u32[]{:S(2)}) collective-permute-start(bf16[64,768]{1,0:T(8,128)(2,1)S(1)} %get-tuple-element.33), channel_id=1, source_target_pairs={{0,2},{2,0},{4,6},{6,4},{8,10},{10,8},{12,14},{14,12},{1,3},{3,1},... | collective-permute-start | bytes 294920 | tf_op jit(solution)/shard_map/ppermute | solution.py:329
  12.3 0.0 collective-permute-done.3.d2_ref.refs_4_
  12.3 2.7 %collective-permute-done.4.d6_ref.refs_5_ = bf16[64,768]{1,0:T(8,128)(2,1)S(1)} collective-permute-done((bf16[64,768]{1,0:T(8,128)(2,1)S(1)}, bf16[64,768]{1,0:T(8,128)(2,1)S(1)}, u32[]{:S(2)}, u32[]{:S(2)}) %collective-permute-start.4) | collective-permute-done | bytes 98336 | tf_op jit(solution)/shard_map/ppermute | solution.py:329
  15.0 0.4 %collective-permute-done.5.d1_any.refs_1_ = bf16[64,768]{1,0:T(8,128)(2,1)S(1)} collective-permute-done((bf16[64,768]{1,0:T(8,128)(2,1)S(1)}, bf16[64,768]{1,0:T(8,128)(2,1)S(1)}, u32[]{:S(2)}, u32[]{:S(2)}) %collective-permute-start.5) | collective-permute-done | bytes 98336 | tf_op jit(solution)/shard_map/ppermute | solution.py:329
  15.5 1.5 %collective-permute-start.7 = (bf16[64,1280]{1,0:T(8,128)(2,1)S(1)}, bf16[64,1280]{1,0:T(8,128)(2,1)S(1)}, u32[]{:S(2)}, u32[]{:S(2)}) collective-permute-start(bf16[64,1280]{1,0:T(8,128)(2,1)S(1)} %get-tuple-element.35), channel_id=1, source_target_pairs={{0,4},{2,6},{4,0},{6,2},{8,12},{10,14},{12,8},{14,10},{1,5},{3,7},... | collective-permute-start | bytes 491528 | tf_op jit(solution)/shard_map/ppermute | solution.py:329
  17.0 0.2 collective-permute-start.9
  17.2 1.5 %collective-permute-start.6 = (bf16[64,1536]{1,0:T(8,128)(2,1)S(1)}, bf16[64,1536]{1,0:T(8,128)(2,1)S(1)}, u32[]{:S(2)}, u32[]{:S(2)}) collective-permute-start(bf16[64,1536]{1,0:T(8,128)(2,1)S(1)} %get-tuple-element.34.mine_ref.kept_ref), channel_id=1, source_target_pairs={{0,1},{1,0},{2,3},{3,2},{4,5},{5,4},{6,7},{7,6},{8,9},{9,8},{10,11... | collective-permute-start | bytes 589832 | tf_op jit(solution)/shard_map/ppermute | solution.py:332
  18.7 1.0 %collective-permute-done.7.mine_ref = bf16[64,1280]{1,0:T(8,128)(2,1)S(1)} collective-permute-done((bf16[64,1280]{1,0:T(8,128)(2,1)S(1)}, bf16[64,1280]{1,0:T(8,128)(2,1)S(1)}, u32[]{:S(2)}, u32[]{:S(2)}) %collective-permute-start.7) | collective-permute-done | bytes 163872 | tf_op jit(solution)/shard_map/ppermute | solution.py:329
  19.7 3.1 %collective-permute-start.8 = (bf16[64,1280]{1,0:T(8,128)(2,1)S(1)}, bf16[64,1280]{1,0:T(8,128)(2,1)S(1)}, u32[]{:S(2)}, u32[]{:S(2)}) collective-permute-start(bf16[64,1280]{1,0:T(8,128)(2,1)S(1)} %collective-permute-done.7.mine_ref), channel_id=1, source_target_pairs={{0,1},{1,0},{2,3},{3,2},{4,5},{5,4},{6,7},{7,6},{8,9},{9,8},{10,11... | collective-permute-start | bytes 491528 | tf_op jit(solution)/shard_map/ppermute | solution.py:332
  22.8 0.9 %shard_map.86 = (bf16[512,256]{1,0:T(8,128)(2,1)S(1)}, f32[128,512]{1,0:T(8,128)S(1)}) custom-call(s32[2]{0:T(128)S(1)} %pad_add_fusion.place_ref, bf16[64,1536]{1,0:T(8,128)(2,1)S(1)} %get-tuple-element.34.mine_ref.kept_ref, bf16[64,1536]{1,0:T(8,128)(2,1)S(1)} %collective-permute-done.6.other_ref.kept2_ref), custom_call_target="tpu_custom_call" | custom-call | tf_op jit(solution)/shard_map/pallas_call | solution.py:387
  23.7 0.1 collective-permute-done.8.other_ref
  23.8 1.1 %shard_map.87 = (bf16[512,256]{1,0:T(8,128)(2,1)S(1)}, bf16[128,512]{1,0:T(8,128)(2,1)S(1)}, bf16[128,512]{1,0:T(8,128)(2,1)S(1)}, f32[128,128]{1,0:T(8,128)S(1)}) custom-call(s32[2]{0:T(128)S(1)} %pad_add_fusion.place_ref, bf16[64,1536]{1,0:T(8,128)(2,1)S(1)} %get-tuple-element.34.mine_ref.kept_ref, ...), custom_call_target="tpu_custom_call" | custom-call | tf_op jit(solution)/shard_map/pallas_call | solution.py:393
  24.9 1.7 %shard_map.88 = (f32[128,128]{1,0:T(8,128)S(1)}, f32[128,128]{1,0:T(8,128)S(1)}) custom-call(s32[2]{0:T(128)S(1)} %pad_add_fusion.place_ref, f32[128,128]{1,0:T(8,128)S(1)} %get-tuple-element.25.gene_ref, f32[128,128]{1,0:T(8,128)S(1)} %get-tuple-element.37.power_ref, bf16[512,256]{1,0:T(8,128)(2,1)S(1)} %get-tuple-element.38.turned_ref, ...), custom_call_target="tpu_custom_call" | custom-call | tf_op jit(solution)/shard_map/pallas_call | solution.py:399
  26.6 1.5 %collective-permute-start.10 = (f32[128,128]{1,0:T(8,128)S(1)}, f32[128,128]{1,0:T(8,128)S(1)}, u32[]{:S(2)}, u32[]{:S(2)}) collective-permute-start(f32[128,128]{1,0:T(8,128)S(1)} %get-tuple-element.44), channel_id=1, source_target_pairs={{0,1},{1,0},{2,3},{3,2},{4,5},{5,4},{6,7},{7,6},{8,9},{9,8},{10,11... | collective-permute-start | bytes 196616 | tf_op jit(solution)/shard_map/ppermute | solution.py:332
  28.2 0.9 %collective-permute-done.10 = f32[128,128]{1,0:T(8,128)S(1)} collective-permute-done((f32[128,128]{1,0:T(8,128)S(1)}, f32[128,128]{1,0:T(8,128)S(1)}, u32[]{:S(2)}, u32[]{:S(2)}) %collective-permute-start.10) | collective-permute-done | bytes 65568 | tf_op jit(solution)/shard_map/ppermute | solution.py:332
  29.1 0.6 %add.3 = f32[128,128]{1,0:T(8,128)} add(f32[128,128]{1,0:T(8,128)S(1)} %get-tuple-element.43, f32[128,128]{1,0:T(8,128)S(1)} %collective-permute-done.10) | non-fusion elementwise | flops 16384 | bytes 196608 | tf_op jit(solution)/shard_map/add | solution.py:405
  (7 shorter events, 0.1 us)
Async XLA Ops:
  2.0 5.9 %collective-permute-start.2 = (bf16[64,768]{1,0:T(8,128)(2,1)S(1)}, bf16[64,768]{1,0:T(8,128)(2,1)S(1)}, u32[]{:S(2)}, u32[]{:S(2)}) collective-permute-start(bf16[64,768]{1,0:T(8,128)(2,1)S(1)} %get-tuple-element.31.d0_ref.refs_0_), channel_id=1, source_target_pairs={{0,8},{2,10},{4,12},{6,14},{8,0},{10,2},{12,4},{14,6},{1,9},{3,11}... | collective-permute-start | bytes 294920 | tf_op jit(solution)/shard_map/ppermute | solution.py:329
  2.1 3.1 %collective-permute-start = (bf16[64,512]{1,0:T(8,128)(2,1)S(1)}, bf16[64,512]{1,0:T(8,128)(2,1)S(1)}, u32[]{:S(2)}, u32[]{:S(2)}) collective-permute-start(bf16[64,512]{1,0:T(8,128)(2,1)S(1)} %get-tuple-element.26.ahead_ref), channel_id=1, source_target_pairs={{0,2},{2,0},{4,6},{6,4},{8,10},{10,8},{12,14},{14,12},{1,3},{3,1},... | collective-permute-start | bytes 196616 | tf_op jit(solution)/shard_map/ppermute | solution.py:329
  2.4 10.0 %collective-permute-start.3 = (bf16[64,768]{1,0:T(8,128)(2,1)S(1)}, bf16[64,768]{1,0:T(8,128)(2,1)S(1)}, u32[]{:S(2)}, u32[]{:S(2)}) collective-permute-start(bf16[64,768]{1,0:T(8,128)(2,1)S(1)} %get-tuple-element.31.d0_ref.refs_0_), channel_id=1, source_target_pairs={{0,4},{2,6},{4,0},{6,2},{8,12},{10,14},{12,8},{14,10},{1,5},{3,7},... | collective-permute-start | bytes 294920 | tf_op jit(solution)/shard_map/ppermute | solution.py:329
  5.3 7.1 %collective-permute-start.1 = (bf16[64,768]{1,0:T(8,128)(2,1)S(1)}, bf16[64,768]{1,0:T(8,128)(2,1)S(1)}, u32[]{:S(2)}, u32[]{:S(2)}) collective-permute-start(bf16[64,768]{1,0:T(8,128)(2,1)S(1)} %shard_map.83.after_any), channel_id=1, source_target_pairs={{0,8},{2,10},{4,12},{6,14},{8,0},{10,2},{12,4},{14,6},{1,9},{3,11}... | collective-permute-start | bytes 294920 | tf_op jit(solution)/shard_map/ppermute | solution.py:329
  8.0 7.1 %collective-permute-start.4 = (bf16[64,768]{1,0:T(8,128)(2,1)S(1)}, bf16[64,768]{1,0:T(8,128)(2,1)S(1)}, u32[]{:S(2)}, u32[]{:S(2)}) collective-permute-start(bf16[64,768]{1,0:T(8,128)(2,1)S(1)} %get-tuple-element.32), channel_id=1, source_target_pairs={{0,4},{2,6},{4,0},{6,2},{8,12},{10,14},{12,8},{14,10},{1,5},{3,7},... | collective-permute-start | bytes 294920 | tf_op jit(solution)/shard_map/ppermute | solution.py:329
  11.7 3.8 %collective-permute-start.5 = (bf16[64,768]{1,0:T(8,128)(2,1)S(1)}, bf16[64,768]{1,0:T(8,128)(2,1)S(1)}, u32[]{:S(2)}, u32[]{:S(2)}) collective-permute-start(bf16[64,768]{1,0:T(8,128)(2,1)S(1)} %get-tuple-element.33), channel_id=1, source_target_pairs={{0,2},{2,0},{4,6},{6,4},{8,10},{10,8},{12,14},{14,12},{1,3},{3,1},... | collective-permute-start | bytes 294920 | tf_op jit(solution)/shard_map/ppermute | solution.py:329
  15.5 4.2 %collective-permute-start.7 = (bf16[64,1280]{1,0:T(8,128)(2,1)S(1)}, bf16[64,1280]{1,0:T(8,128)(2,1)S(1)}, u32[]{:S(2)}, u32[]{:S(2)}) collective-permute-start(bf16[64,1280]{1,0:T(8,128)(2,1)S(1)} %get-tuple-element.35), channel_id=1, source_target_pairs={{0,4},{2,6},{4,0},{6,2},{8,12},{10,14},{12,8},{14,10},{1,5},{3,7},... | collective-permute-start | bytes 491528 | tf_op jit(solution)/shard_map/ppermute | solution.py:329
  17.0 8.0 %collective-permute-start.9 = (bf16[64,2304]{1,0:T(8,128)(2,1)S(1)}, bf16[64,2304]{1,0:T(8,128)(2,1)S(1)}, u32[]{:S(2)}, u32[]{:S(2)}) collective-permute-start(bf16[64,2304]{1,0:T(8,128)(2,1)S(1)} %get-tuple-element.42), channel_id=1, source_target_pairs={{0,2},{2,0},{4,6},{6,4},{8,10},{10,8},{12,14},{14,12},{1,3},{3,1},... | collective-permute-start | bytes 884744 | tf_op jit(solution)/shard_map/ppermute | solution.py:329
  17.2 5.6 %collective-permute-start.6 = (bf16[64,1536]{1,0:T(8,128)(2,1)S(1)}, bf16[64,1536]{1,0:T(8,128)(2,1)S(1)}, u32[]{:S(2)}, u32[]{:S(2)}) collective-permute-start(bf16[64,1536]{1,0:T(8,128)(2,1)S(1)} %get-tuple-element.34.mine_ref.kept_ref), channel_id=1, source_target_pairs={{0,1},{1,0},{2,3},{3,2},{4,5},{5,4},{6,7},{7,6},{8,9},{9,8},{10,11... | collective-permute-start | bytes 589832 | tf_op jit(solution)/shard_map/ppermute | solution.py:332
  19.7 4.1 %collective-permute-start.8 = (bf16[64,1280]{1,0:T(8,128)(2,1)S(1)}, bf16[64,1280]{1,0:T(8,128)(2,1)S(1)}, u32[]{:S(2)}, u32[]{:S(2)}) collective-permute-start(bf16[64,1280]{1,0:T(8,128)(2,1)S(1)} %collective-permute-done.7.mine_ref), channel_id=1, source_target_pairs={{0,1},{1,0},{2,3},{3,2},{4,5},{5,4},{6,7},{7,6},{8,9},{9,8},{10,11... | collective-permute-start | bytes 491528 | tf_op jit(solution)/shard_map/ppermute | solution.py:332
  26.6 2.4 %collective-permute-start.10 = (f32[128,128]{1,0:T(8,128)S(1)}, f32[128,128]{1,0:T(8,128)S(1)}, u32[]{:S(2)}, u32[]{:S(2)}) collective-permute-start(f32[128,128]{1,0:T(8,128)S(1)} %get-tuple-element.44), channel_id=1, source_target_pairs={{0,1},{1,0},{2,3},{3,2},{4,5},{5,4},{6,7},{7,6},{8,9},{9,8},{10,11... | collective-permute-start | bytes 196616 | tf_op jit(solution)/shard_map/ppermute | solution.py:332

commit v10 on v9

--- a/solution.py
+++ b/solution.py
@@ -186,14 +186,14 @@
     out_ref[part:, 2 * half :] = r1_ref[part:, half:]
 
 
-def copy_kernel(d0_ref, d4_ref, after_any, own_ref, far_ref):
-    own_ref[...] = d0_ref[...]
+def copy_kernel(d0_ref, d4_ref, after_any, pair_ref, far_ref):
+    variants = d0_ref.shape[1]
+    pair_ref[:, :variants] = d0_ref[...]
+    pair_ref[:, variants:] = d4_ref[...]
     far_ref[...] = d4_ref[...]
 
 
-def third_kernel(
-    ahead_ref, r1_ref, r4_ref, e2_ref, e0_ref, terms_ref, d4_ref, d2_ref, d6_ref, d1_any, out_ref, kept_ref, dose_ref
-):
+def third_kernel(ahead_ref, r1_ref, r4_ref, e2_ref, e0_ref, terms_ref, far_any, out_ref, kept_ref):
     half = terms_ref.shape[1]
     part = e0_ref.shape[0]
     for ref, own, at in ((out_ref, e2_ref, LANES), (kept_ref, e0_ref, 0)):
@@ -210,9 +210,6 @@
     terms = terms_ref.shape[0]
     kept_ref[:terms, width:] = terms_ref[...]
     kept_ref[terms:, width:] = jnp.zeros((kept_ref.shape[0] - terms, half), bf16)
-    variants = d4_ref.shape[1]
-    for i, ref in enumerate((d4_ref, d2_ref, d6_ref)):
-        dose_ref[:, i * variants : (i + 1) * variants] = ref[...]
 
 
 def rotate(place_ref, refs, turned_ref, data_scr):
@@ -238,7 +235,7 @@
     return shares
 
 
-def half_kernel(place_ref, mine_ref, other_ref, turned_ref, share_ref, data_scr):
+def half_kernel(place_ref, mine_ref, other_ref, d15_any, turned_ref, share_ref, data_scr):
     half = turned_ref.shape[0] // 2
     for c, share in enumerate(rotate(place_ref, (mine_ref, other_ref), turned_ref, data_scr)):
         share_ref[:, c * half : (c + 1) * half] = share
@@ -269,7 +266,7 @@
     *dose_refs, keep_ref, pass_ref, dose_scr = refs
     samples, variants = dose_refs[0].shape
     chunks = [(ref, at) for ref in dose_refs for at in range(0, ref.shape[1], variants)]
-    order = [0, 1, 2, 3, 6, 4, 7, 5]
+    order = [0, 1, 3, 2, 4, 5, 7, 6]
     for m, (ref, at) in enumerate(chunks[i] for i in order):
         dose_scr[m * samples : (m + 1) * samples, :] = ref[:, at : at + variants]
     line = turned_ref.shape[1]
@@ -368,18 +365,16 @@
     d2 = swap(d0, 2)
     to4 = call(second_kernel, [((panel, 2 * half + 2 * LANES), bf16)], 3, smem=0)(ahead, r1, e46)[0]
     r4 = swap(to4, 4)
-    own, far = call(copy_kernel, [((panel, variants), bf16)] * 2, 3, smem=0, anywhere=1)(d0, d4, to4)
+    pair, far = call(
+        copy_kernel, [((panel, 2 * variants), bf16), ((panel, variants), bf16)], 3, smem=0, anywhere=1
+    )(d0, d4, to4)
     d6 = swap(far, 2)
-    d1 = swap(own, 1)
+    d15 = swap(pair, 1)
+    d37 = swap(jnp.concatenate([d2, d6], axis=1), 1)
     width = 4 * half + 2 * LANES
-    out, kept, three = call(
-        third_kernel,
-        [((panel, width), bf16), ((panel, width + half), bf16), ((panel, 3 * variants), bf16)],
-        10,
-        smem=0,
-        anywhere=1,
-    )(ahead, r1, r4, e2, e0, terms, d4, d2, d6, d1)
-    d537 = swap(three, 1)
+    out, kept = call(
+        third_kernel, [((panel, width), bf16), ((panel, width + half), bf16)], 7, smem=0, anywhere=1
+    )(ahead, r1, r4, e2, e0, terms, far)
     kept2 = other_core(kept)
     near = swap(out, 2)
     near2 = other_core(near)
@@ -387,9 +382,10 @@
     turned, share = call(
         half_kernel,
         [shape, ((LANES, 2 * half), f32)],
-        3,
+        4,
         scratch=[pltpu.VMEM((samples // 2, LANES), bf16)],
-    )(place, kept, kept2)
+        anywhere=1,
+    )(place, kept, kept2, d15)
     turned2, weighted, low, power = call(
         weight_kernel,
         [shape, ((LANES, 2 * half), bf16), ((LANES, 2 * half), bf16), ((LANES, LANES), f32)],
@@ -401,7 +397,7 @@
         [((LANES, LANES), f32)] * 2,
         13,
         scratch=[pltpu.VMEM((samples, variants), bf16)],
-    )(place, gene, power, turned, turned2, weighted, low, d0, d1, d4, d537, d2, d6)
+    )(place, gene, power, turned, turned2, weighted, low, d0, d15, d4, d2, d37, d6)
     return keep + other_core(passed)
 
 

time: 29.9 us -> 29.3 us (0.980)
  the two profiles are of different devices: /device:TPU:21 before, /device:TPU:0 now
where the time goes in v10:
time: 29.3 us; the launch traced here: 29.2 us
  starting transfers between devices  13.6 us (46%)
  waiting for transfers between devices  9.1 us (31%)
  Pallas kernels  5.71 us (19%)
  other arithmetic  0.73 us (2%)
    ppermute x8, starting transfers between devices, swap(): return lax.ppermute(x, 'row', [(i, i ^ m) for i in range(rows)])  13.3 us
    ppermute x8, waiting for transfers between devices, swap(): return lax.ppermute(x, 'row', [(i, i ^ m) for i in range(rows)])  7.54 us
    pallas_call x1, Pallas kernels, near_body(): call(route_kernel, [((panel, half + 2 * LANES), bf16), ((part, 2 * LANES)...  1.93 us
    pallas_call x1, Pallas kernels, near_body(): call(score_kernel, [((LANES, LANES), f32)] * 2, 13, scratch=[pltpu.VMEM((...  1.72 us
    ppermute x3, waiting for transfers between devices, other_core(): return lax.ppermute(x, 'col', [(0, 1), (1, 0)])  1.56 us
    pallas_call x1, Pallas kernels, near_body(): call(weight_kernel, [shape, ((LANES, 2 * half), bf16), ((LANES, 2 * half)...  1.08 us
    pallas_call x1, Pallas kernels, near_body(): call(half_kernel, [shape, ((LANES, 2 * half), f32)], 4, scratch=[pltpu.VM...  0.93 us
    add x1, other arithmetic, near_body(): return keep + other_core(passed)  0.64 us
  transfers between devices with their start and end apart: 11, of which 5 were waited for; matrix products, arithmetic and copies ran while one was open for 0% of the time, Pallas kernels for 7%

profile of v10, /device:TPU:0, one launch (start us, length us, event | category | flops | bytes accessed | tf_op | source)
XLA Modules:
  0.0 29.2 jit_solution(17969212696436418856)
XLA Ops:
  0.0 0.1 pad_add_fusion.place_ref
  0.1 1.9 %shard_map.82 = (bf16[64,512]{1,0:T(8,128)(2,1)S(1)}, bf16[32,256]{1,0:T(8,128)(2,1)S(1)}, bf16[32,128]{1,0:T(8,128)(2,1)S(1)}, bf16[32,128]{1,0:T(8,128)(2,1)S(...) custom-call(s32[2]{0:T(128)S(1)} %pad_add_fusion.place_ref, ...), custom_call_target="tpu_custom_call" | custom-call | tf_op jit(solution)/shard_map/pallas_call | solution.py:331
  2.0 4.1 %collective-permute-start.2 = (bf16[64,768]{1,0:T(8,128)(2,1)S(1)}, bf16[64,768]{1,0:T(8,128)(2,1)S(1)}, u32[]{:S(2)}, u32[]{:S(2)}) collective-permute-start(bf16[64,768]{1,0:T(8,128)(2,1)S(1)} %get-tuple-element.30.d0_ref.refs_0_), channel_id=1, source_target_pairs={{0,8},{2,10},{4,12},{6,14},{8,0},{10,2},{12,4},{14,6},{1,9},{3,11}... | collective-permute-start | bytes 294920 | tf_op jit(solution)/shard_map/ppermute | solution.py:326
  6.1 1.5 %collective-permute-start = (bf16[64,512]{1,0:T(8,128)(2,1)S(1)}, bf16[64,512]{1,0:T(8,128)(2,1)S(1)}, u32[]{:S(2)}, u32[]{:S(2)}) collective-permute-start(bf16[64,512]{1,0:T(8,128)(2,1)S(1)} %get-tuple-element.25.ahead_ref), channel_id=1, source_target_pairs={{0,2},{2,0},{4,6},{6,4},{8,10},{10,8},{12,14},{14,12},{1,3},{3,1},... | collective-permute-start | bytes 196616 | tf_op jit(solution)/shard_map/ppermute | solution.py:326
  7.6 2.7 %collective-permute-done.r1_ref = bf16[64,512]{1,0:T(8,128)(2,1)S(1)} collective-permute-done((bf16[64,512]{1,0:T(8,128)(2,1)S(1)}, bf16[64,512]{1,0:T(8,128)(2,1)S(1)}, u32[]{:S(2)}, u32[]{:S(2)}) %collective-permute-start) | collective-permute-done | bytes 65568 | tf_op jit(solution)/shard_map/ppermute | solution.py:326
  10.4 0.1 collective-permute-start.1
  10.5 1.9 %collective-permute-start.7 = (bf16[64,768]{1,0:T(8,128)(2,1)S(1)}, bf16[64,768]{1,0:T(8,128)(2,1)S(1)}, u32[]{:S(2)}, u32[]{:S(2)}) collective-permute-start(bf16[64,768]{1,0:T(8,128)(2,1)S(1)} %get-tuple-element.30.d0_ref.refs_0_), channel_id=1, source_target_pairs={{0,4},{2,6},{4,0},{6,2},{8,12},{10,14},{12,8},{14,10},{1,5},{3,7},... | collective-permute-start | bytes 294920 | tf_op jit(solution)/shard_map/ppermute | solution.py:326
  12.4 0.0 collective-permute-done.2.d4_ref.refs_2_
  12.4 0.6 %collective-permute-start.8 = (bf16[64,768]{1,0:T(8,128)(2,1)S(1)}, bf16[64,768]{1,0:T(8,128)(2,1)S(1)}, u32[]{:S(2)}, u32[]{:S(2)}) collective-permute-start(bf16[64,768]{1,0:T(8,128)(2,1)S(1)} %get-tuple-element.31.far_any), channel_id=1, source_target_pairs={{0,4},{2,6},{4,0},{6,2},{8,12},{10,14},{12,8},{14,10},{1,5},{3,7},... | collective-permute-start | bytes 294920 | tf_op jit(solution)/shard_map/ppermute | solution.py:326
  13.0 1.5 %collective-permute-start.6 = (bf16[64,1536]{1,0:T(8,128)(2,1)S(1)}, bf16[64,1536]{1,0:T(8,128)(2,1)S(1)}, u32[]{:S(2)}, u32[]{:S(2)}) collective-permute-start(bf16[64,1536]{1,0:T(8,128)(2,1)S(1)} %get-tuple-element.34), channel_id=1, source_target_pairs={{0,2},{2,0},{4,6},{6,4},{8,10},{10,8},{12,14},{14,12},{1,3},{3,1},... | collective-permute-start | bytes 589832 | tf_op jit(solution)/shard_map/ppermute | solution.py:326
  14.5 1.6 %collective-permute-done.1.r4_ref = bf16[64,768]{1,0:T(8,128)(2,1)S(1)} collective-permute-done((bf16[64,768]{1,0:T(8,128)(2,1)S(1)}, bf16[64,768]{1,0:T(8,128)(2,1)S(1)}, u32[]{:S(2)}, u32[]{:S(2)}) %collective-permute-start.1) | collective-permute-done | bytes 98336 | tf_op jit(solution)/shard_map/ppermute | solution.py:326
  16.1 0.1 collective-permute-start.3
  16.2 2.0 %collective-permute-start.4 = (bf16[64,1280]{1,0:T(8,128)(2,1)S(1)}, bf16[64,1280]{1,0:T(8,128)(2,1)S(1)}, u32[]{:S(2)}, u32[]{:S(2)}) collective-permute-start(bf16[64,1280]{1,0:T(8,128)(2,1)S(1)} %get-tuple-element.33), channel_id=1, source_target_pairs={{0,4},{2,6},{4,0},{6,2},{8,12},{10,14},{12,8},{14,10},{1,5},{3,7},... | collective-permute-start | bytes 491528 | tf_op jit(solution)/shard_map/ppermute | solution.py:326
  18.2 0.0 collective-permute-done.7.refs_3_
  18.2 0.0 collective-permute-done.8.refs_5_
  18.2 1.6 %collective-permute-start.9 = (bf16[64,1536]{1,0:T(8,128)(2,1)S(1)}, bf16[64,1536]{1,0:T(8,128)(2,1)S(1)}, u32[]{:S(2)}, u32[]{:S(2)}) collective-permute-start(bf16[64,1536]{1,0:T(8,128)(2,1)S(1)} %pad_maximum_fusion), channel_id=1, source_target_pairs={{0,2},{2,0},{4,6},{6,4},{8,10},{10,8},{12,14},{14,12},{1,3},{3,1},... | collective-permute-start | bytes 589832 | tf_op jit(solution)/shard_map/ppermute | solution.py:326
  19.8 3.2 %collective-permute-done.4.mine_ref = bf16[64,1280]{1,0:T(8,128)(2,1)S(1)} collective-permute-done((bf16[64,1280]{1,0:T(8,128)(2,1)S(1)}, bf16[64,1280]{1,0:T(8,128)(2,1)S(1)}, u32[]{:S(2)}, u32[]{:S(2)}) %collective-permute-start.4) | collective-permute-done | bytes 163872 | tf_op jit(solution)/shard_map/ppermute | solution.py:326
  23.0 0.9 %shard_map.86 = (bf16[512,256]{1,0:T(8,128)(2,1)S(1)}, f32[128,512]{1,0:T(8,128)S(1)}) custom-call(s32[2]{0:T(128)S(1)} %pad_add_fusion.place_ref, bf16[64,1536]{1,0:T(8,128)(2,1)S(1)} %get-tuple-element.32.mine_ref.kept_ref, bf16[64,1536]{1,0:T(8,128)(2,1)S(1)} %collective-permute-done.3.other_ref.kept2_ref, ...), custom_call_target="tpu_custom_call" | custom-call | tf_op jit(solution)/shard_map/pallas_call | solution.py:382
  23.9 0.4 %collective-permute-done.5.other_ref = bf16[64,1280]{1,0:T(8,128)(2,1)S(1)} collective-permute-done((bf16[64,1280]{1,0:T(8,128)(2,1)S(1)}, bf16[64,1280]{1,0:T(8,128)(2,1)S(1)}, u32[]{:S(2)}, u32[]{:S(2)}) %collective-permute-start.5) | collective-permute-done | bytes 163872 | tf_op jit(solution)/shard_map/ppermute | solution.py:329
  24.4 1.1 %shard_map.87 = (bf16[512,256]{1,0:T(8,128)(2,1)S(1)}, bf16[128,512]{1,0:T(8,128)(2,1)S(1)}, bf16[128,512]{1,0:T(8,128)(2,1)S(1)}, f32[128,128]{1,0:T(8,128)S(1)}) custom-call(s32[2]{0:T(128)S(1)} %pad_add_fusion.place_ref, bf16[64,1536]{1,0:T(8,128)(2,1)S(1)} %get-tuple-element.32.mine_ref.kept_ref, ...), custom_call_target="tpu_custom_call" | custom-call | tf_op jit(solution)/shard_map/pallas_call | solution.py:389
  25.5 1.7 %shard_map.88 = (f32[128,128]{1,0:T(8,128)S(1)}, f32[128,128]{1,0:T(8,128)S(1)}) custom-call(s32[2]{0:T(128)S(1)} %pad_add_fusion.place_ref, f32[128,128]{1,0:T(8,128)S(1)} %get-tuple-element.24.gene_ref, f32[128,128]{1,0:T(8,128)S(1)} %get-tuple-element.36.power_ref, bf16[512,256]{1,0:T(8,128)(2,1)S(1)} %get-tuple-element.37.turned_ref, ...), custom_call_target="tpu_custom_call" | custom-call | tf_op jit(solution)/shard_map/pallas_call | solution.py:395
  27.2 0.2 collective-permute-start.10
  27.4 1.1 %collective-permute-done.10 = f32[128,128]{1,0:T(8,128)S(1)} collective-permute-done((f32[128,128]{1,0:T(8,128)S(1)}, f32[128,128]{1,0:T(8,128)S(1)}, u32[]{:S(2)}, u32[]{:S(2)}) %collective-permute-start.10) | collective-permute-done | bytes 65568 | tf_op jit(solution)/shard_map/ppermute | solution.py:329
  28.5 0.6 %add.3 = f32[128,128]{1,0:T(8,128)} add(f32[128,128]{1,0:T(8,128)S(1)} %get-tuple-element.41, f32[128,128]{1,0:T(8,128)S(1)} %collective-permute-done.10) | non-fusion elementwise | flops 16384 | bytes 196608 | tf_op jit(solution)/shard_map/add | solution.py:401
  (8 shorter events, 0.1 us)
Async XLA Ops:
  2.0 10.4 %collective-permute-start.2 = (bf16[64,768]{1,0:T(8,128)(2,1)S(1)}, bf16[64,768]{1,0:T(8,128)(2,1)S(1)}, u32[]{:S(2)}, u32[]{:S(2)}) collective-permute-start(bf16[64,768]{1,0:T(8,128)(2,1)S(1)} %get-tuple-element.30.d0_ref.refs_0_), channel_id=1, source_target_pairs={{0,8},{2,10},{4,12},{6,14},{8,0},{10,2},{12,4},{14,6},{1,9},{3,11}... | collective-permute-start | bytes 294920 | tf_op jit(solution)/shard_map/ppermute | solution.py:326
  6.1 4.3 %collective-permute-start = (bf16[64,512]{1,0:T(8,128)(2,1)S(1)}, bf16[64,512]{1,0:T(8,128)(2,1)S(1)}, u32[]{:S(2)}, u32[]{:S(2)}) collective-permute-start(bf16[64,512]{1,0:T(8,128)(2,1)S(1)} %get-tuple-element.25.ahead_ref), channel_id=1, source_target_pairs={{0,2},{2,0},{4,6},{6,4},{8,10},{10,8},{12,14},{14,12},{1,3},{3,1},... | collective-permute-start | bytes 196616 | tf_op jit(solution)/shard_map/ppermute | solution.py:326
  10.4 5.7 %collective-permute-start.1 = (bf16[64,768]{1,0:T(8,128)(2,1)S(1)}, bf16[64,768]{1,0:T(8,128)(2,1)S(1)}, u32[]{:S(2)}, u32[]{:S(2)}) collective-permute-start(bf16[64,768]{1,0:T(8,128)(2,1)S(1)} %shard_map.83.after_any), channel_id=1, source_target_pairs={{0,8},{2,10},{4,12},{6,14},{8,0},{10,2},{12,4},{14,6},{1,9},{3,11}... | collective-permute-start | bytes 294920 | tf_op jit(solution)/shard_map/ppermute | solution.py:326
  10.5 7.7 %collective-permute-start.7 = (bf16[64,768]{1,0:T(8,128)(2,1)S(1)}, bf16[64,768]{1,0:T(8,128)(2,1)S(1)}, u32[]{:S(2)}, u32[]{:S(2)}) collective-permute-start(bf16[64,768]{1,0:T(8,128)(2,1)S(1)} %get-tuple-element.30.d0_ref.refs_0_), channel_id=1, source_target_pairs={{0,4},{2,6},{4,0},{6,2},{8,12},{10,14},{12,8},{14,10},{1,5},{3,7},... | collective-permute-start | bytes 294920 | tf_op jit(solution)/shard_map/ppermute | solution.py:326
  12.4 5.8 %collective-permute-start.8 = (bf16[64,768]{1,0:T(8,128)(2,1)S(1)}, bf16[64,768]{1,0:T(8,128)(2,1)S(1)}, u32[]{:S(2)}, u32[]{:S(2)}) collective-permute-start(bf16[64,768]{1,0:T(8,128)(2,1)S(1)} %get-tuple-element.31.far_any), channel_id=1, source_target_pairs={{0,4},{2,6},{4,0},{6,2},{8,12},{10,14},{12,8},{14,10},{1,5},{3,7},... | collective-permute-start | bytes 294920 | tf_op jit(solution)/shard_map/ppermute | solution.py:326
  13.0 10.0 %collective-permute-start.6 = (bf16[64,1536]{1,0:T(8,128)(2,1)S(1)}, bf16[64,1536]{1,0:T(8,128)(2,1)S(1)}, u32[]{:S(2)}, u32[]{:S(2)}) collective-permute-start(bf16[64,1536]{1,0:T(8,128)(2,1)S(1)} %get-tuple-element.34), channel_id=1, source_target_pairs={{0,2},{2,0},{4,6},{6,4},{8,10},{10,8},{12,14},{14,12},{1,3},{3,1},... | collective-permute-start | bytes 589832 | tf_op jit(solution)/shard_map/ppermute | solution.py:326
  16.1 6.9 %collective-permute-start.3 = (bf16[64,1536]{1,0:T(8,128)(2,1)S(1)}, bf16[64,1536]{1,0:T(8,128)(2,1)S(1)}, u32[]{:S(2)}, u32[]{:S(2)}) collective-permute-start(bf16[64,1536]{1,0:T(8,128)(2,1)S(1)} %get-tuple-element.32.mine_ref.kept_ref), channel_id=1, source_target_pairs={{0,1},{1,0},{2,3},{3,2},{4,5},{5,4},{6,7},{7,6},{8,9},{9,8},{10,11... | collective-permute-start | bytes 589832 | tf_op jit(solution)/shard_map/ppermute | solution.py:329
  16.2 6.8 %collective-permute-start.4 = (bf16[64,1280]{1,0:T(8,128)(2,1)S(1)}, bf16[64,1280]{1,0:T(8,128)(2,1)S(1)}, u32[]{:S(2)}, u32[]{:S(2)}) collective-permute-start(bf16[64,1280]{1,0:T(8,128)(2,1)S(1)} %get-tuple-element.33), channel_id=1, source_target_pairs={{0,4},{2,6},{4,0},{6,2},{8,12},{10,14},{12,8},{14,10},{1,5},{3,7},... | collective-permute-start | bytes 491528 | tf_op jit(solution)/shard_map/ppermute | solution.py:326
  18.2 7.3 %collective-permute-start.9 = (bf16[64,1536]{1,0:T(8,128)(2,1)S(1)}, bf16[64,1536]{1,0:T(8,128)(2,1)S(1)}, u32[]{:S(2)}, u32[]{:S(2)}) collective-permute-start(bf16[64,1536]{1,0:T(8,128)(2,1)S(1)} %pad_maximum_fusion), channel_id=1, source_target_pairs={{0,2},{2,0},{4,6},{6,4},{8,10},{10,8},{12,14},{14,12},{1,3},{3,1},... | collective-permute-start | bytes 589832 | tf_op jit(solution)/shard_map/ppermute | solution.py:326
  23.0 1.4 %collective-permute-start.5 = (bf16[64,1280]{1,0:T(8,128)(2,1)S(1)}, bf16[64,1280]{1,0:T(8,128)(2,1)S(1)}, u32[]{:S(2)}, u32[]{:S(2)}) collective-permute-start(bf16[64,1280]{1,0:T(8,128)(2,1)S(1)} %collective-permute-done.4.mine_ref), channel_id=1, source_target_pairs={{0,1},{1,0},{2,3},{3,2},{4,5},{5,4},{6,7},{7,6},{8,9},{9,8},{10,11... | collective-permute-start | bytes 491528 | tf_op jit(solution)/shard_map/ppermute | solution.py:329
  27.2 1.3 %collective-permute-start.10 = (f32[128,128]{1,0:T(8,128)S(1)}, f32[128,128]{1,0:T(8,128)S(1)}, u32[]{:S(2)}, u32[]{:S(2)}) collective-permute-start(f32[128,128]{1,0:T(8,128)S(1)} %get-tuple-element.42), channel_id=1, source_target_pairs={{0,1},{1,0},{2,3},{3,2},{4,5},{5,4},{6,7},{7,6},{8,9},{9,8},{10,11... | collective-permute-start | bytes 196616 | tf_op jit(solution)/shard_map/ppermute | solution.py:329

commit v11 on v10

--- a/solution.py
+++ b/solution.py
@@ -103,7 +103,7 @@
 
 def route_kernel(
     place_ref, owner_any, delta_any, start_any, valid_any, vals_any, vecs_any, expr_any, dose_any,
-    ahead_ref, e46_ref, e2_ref, e0_ref, gene_ref, terms_ref, half_ref,
+    ahead_ref, e13_ref, e2_ref, e0_ref, gene_ref, terms_ref, half_ref,
     owner_ref, delta_ref, start_ref, valid_ref, vals_ref, expr_ref, sems,
 ):
     row, core = place_ref[0], place_ref[1]
@@ -164,12 +164,12 @@
     upper, lower = slice(0, part), slice(part, 2 * part)
     targets = {
         0: (e0_ref, upper, left),
-        1: (ahead_ref, upper, slice(half, half + LANES)),
+        1: (e13_ref, upper, left),
         2: (e2_ref, upper, left),
-        3: (ahead_ref, upper, slice(half + LANES, half + 2 * LANES)),
-        4: (e46_ref, upper, left),
+        3: (e13_ref, upper, right),
+        4: (ahead_ref, upper, slice(half, half + LANES)),
         5: (ahead_ref, lower, slice(half, half + LANES)),
-        6: (e46_ref, upper, right),
+        6: (ahead_ref, upper, slice(half + LANES, half + 2 * LANES)),
         7: (ahead_ref, lower, slice(half + LANES, half + 2 * LANES)),
     }
     for m, (ref, down, side) in targets.items():
@@ -177,13 +177,13 @@
         ref[down, side] = block.T.astype(bf16)
 
 
-def second_kernel(ahead_ref, r1_ref, e46_ref, out_ref):
+def second_kernel(ahead_ref, r4_ref, e13_ref, out_ref):
     half = out_ref.shape[1] // 2 - LANES
-    part = e46_ref.shape[0]
+    part = e13_ref.shape[0]
     out_ref[:, :half] = ahead_ref[:, :half]
-    out_ref[:, half : 2 * half] = r1_ref[:, :half]
-    out_ref[:part, 2 * half :] = e46_ref[...]
-    out_ref[part:, 2 * half :] = r1_ref[part:, half:]
+    out_ref[:, half : 2 * half] = r4_ref[:, :half]
+    out_ref[:part, 2 * half :] = e13_ref[...]
+    out_ref[part:, 2 * half :] = r4_ref[part:, half:]
 
 
 def copy_kernel(d0_ref, d4_ref, after_any, pair_ref, far_ref):
@@ -193,19 +193,19 @@
     far_ref[...] = d4_ref[...]
 
 
-def third_kernel(ahead_ref, r1_ref, r4_ref, e2_ref, e0_ref, terms_ref, far_any, out_ref, kept_ref):
+def third_kernel(ahead_ref, r4_ref, r1_ref, e2_ref, e0_ref, terms_ref, far_any, out_ref, kept_ref):
     half = terms_ref.shape[1]
     part = e0_ref.shape[0]
     for ref, own, at in ((out_ref, e2_ref, LANES), (kept_ref, e0_ref, 0)):
         ref[:, :half] = ahead_ref[:, :half]
-        ref[:, half : 2 * half] = r1_ref[:, :half]
-        ref[:, 2 * half : 4 * half] = r4_ref[:, : 2 * half]
+        ref[:, half : 2 * half] = r4_ref[:, :half]
+        ref[:, 2 * half : 4 * half] = r1_ref[:, : 2 * half]
         side = slice(2 * half + at, 2 * half + at + LANES)
         left, right = slice(4 * half, 4 * half + LANES), slice(4 * half + LANES, 4 * half + 2 * LANES)
         ref[:part, left] = own[...]
-        ref[:part, right] = r1_ref[:part, half + at : half + at + LANES]
-        ref[part:, left] = r4_ref[:part, side]
-        ref[part:, right] = r4_ref[part:, side]
+        ref[:part, right] = r4_ref[:part, half + at : half + at + LANES]
+        ref[part:, left] = r1_ref[:part, side]
+        ref[part:, right] = r1_ref[part:, side]
     width = out_ref.shape[1]
     terms = terms_ref.shape[0]
     kept_ref[:terms, width:] = terms_ref[...]
@@ -266,7 +266,7 @@
     *dose_refs, keep_ref, pass_ref, dose_scr = refs
     samples, variants = dose_refs[0].shape
     chunks = [(ref, at) for ref in dose_refs for at in range(0, ref.shape[1], variants)]
-    order = [0, 1, 3, 2, 4, 5, 7, 6]
+    order = [0, 3, 1, 2, 4, 7, 5, 6]
     for m, (ref, at) in enumerate(chunks[i] for i in order):
         dose_scr[m * samples : (m + 1) * samples, :] = ref[:, at : at + variants]
     line = turned_ref.shape[1]
@@ -328,7 +328,7 @@
     def other_core(x):
         return lax.ppermute(x, "col", [(0, 1), (1, 0)])
 
-    ahead, e46, e2, e0, gene, terms, d0 = call(
+    ahead, e13, e2, e0, gene, terms, d0 = call(
         route_kernel,
         [
             ((panel, half + 2 * LANES), bf16),
@@ -360,21 +360,21 @@
             )
         ],
     )
-    r1 = swap(ahead, 1)
+    r4 = swap(ahead, 4)
     d4 = swap(d0, 4)
     d2 = swap(d0, 2)
-    to4 = call(second_kernel, [((panel, 2 * half + 2 * LANES), bf16)], 3, smem=0)(ahead, r1, e46)[0]
-    r4 = swap(to4, 4)
+    to1 = call(second_kernel, [((panel, 2 * half + 2 * LANES), bf16)], 3, smem=0)(ahead, r4, e13)[0]
+    r1 = swap(to1, 1)
     pair, far = call(
         copy_kernel, [((panel, 2 * variants), bf16), ((panel, variants), bf16)], 3, smem=0, anywhere=1
-    )(d0, d4, to4)
+    )(d0, d4, to1)
     d6 = swap(far, 2)
     d15 = swap(pair, 1)
     d37 = swap(jnp.concatenate([d2, d6], axis=1), 1)
     width = 4 * half + 2 * LANES
     out, kept = call(
         third_kernel, [((panel, width), bf16), ((panel, width + half), bf16)], 7, smem=0, anywhere=1
-    )(ahead, r1, r4, e2, e0, terms, far)
+    )(ahead, r4, r1, e2, e0, terms, far)
     kept2 = other_core(kept)
     near = swap(out, 2)
     near2 = other_core(near)

time: 29.3 us -> 31.7 us (1.082)
  waiting for transfers between devices: 9.1 us -> 15.1 us
  starting transfers between devices: 13.6 us -> 9.92 us
    ppermute x8, waiting for transfers between devices: 7.54 us -> 13.5 us  [swap(): return lax.ppermute(x, 'row', [(i, i ^ m) for i in range(rows)])]
    ppermute x8, starting transfers between devices: 13.3 us -> 9.64 us  [swap(): return lax.ppermute(x, 'row', [(i, i ^ m) for i in range(rows)])]
  transfers between devices with their start and end apart: 11 -> 11, of which waited for: 5 -> 7; matrix products, arithmetic and copies ran while one was open for 0% -> 0% of each run, Pallas kernels for 7% -> 7%
where the time goes in v11:
time: 31.7 us; the launch traced here: 31.5 us
  waiting for transfers between devices  15.1 us (48%)
  starting transfers between devices  9.92 us (31%)
  Pallas kernels  5.71 us (18%)
  other arithmetic  0.73 us (2%)
    ppermute x8, waiting for transfers between devices, swap(): return lax.ppermute(x, 'row', [(i, i ^ m) for i in range(rows)])  13.5 us
    ppermute x8, starting transfers between devices, swap(): return lax.ppermute(x, 'row', [(i, i ^ m) for i in range(rows)])  9.64 us
    pallas_call x1, Pallas kernels, near_body(): call(route_kernel, [((panel, half + 2 * LANES), bf16), ((part, 2 * LANES)...  1.93 us
    pallas_call x1, Pallas kernels, near_body(): call(score_kernel, [((LANES, LANES), f32)] * 2, 13, scratch=[pltpu.VMEM((...  1.72 us
    ppermute x3, waiting for transfers between devices, other_core(): return lax.ppermute(x, 'col', [(0, 1), (1, 0)])  1.56 us
    pallas_call x1, Pallas kernels, near_body(): call(weight_kernel, [shape, ((LANES, 2 * half), bf16), ((LANES, 2 * half)...  1.08 us
    pallas_call x1, Pallas kernels, near_body(): call(half_kernel, [shape, ((LANES, 2 * half), f32)], 4, scratch=[pltpu.VM...  0.93 us
    add x1, other arithmetic, near_body(): return keep + other_core(passed)  0.64 us
  transfers between devices with their start and end apart: 11, of which 7 were waited for; matrix products, arithmetic and copies ran while one was open for 0% of the time, Pallas kernels for 7%

profile of v11, /device:TPU:0, one launch (start us, length us, event | category | flops | bytes accessed | tf_op | source)
XLA Modules:
  0.0 31.5 jit_solution(4637714534270001561)
XLA Ops:
  0.0 0.1 pad_add_fusion.place_ref
  0.1 1.9 %shard_map.82 = (bf16[64,512]{1,0:T(8,128)(2,1)S(1)}, bf16[32,256]{1,0:T(8,128)(2,1)S(1)}, bf16[32,128]{1,0:T(8,128)(2,1)S(1)}, bf16[32,128]{1,0:T(8,128)(2,1)S(...) custom-call(s32[2]{0:T(128)S(1)} %pad_add_fusion.place_ref, ...), custom_call_target="tpu_custom_call" | custom-call | tf_op jit(solution)/shard_map/pallas_call | solution.py:331
  2.0 4.1 %collective-permute-start.2 = (bf16[64,768]{1,0:T(8,128)(2,1)S(1)}, bf16[64,768]{1,0:T(8,128)(2,1)S(1)}, u32[]{:S(2)}, u32[]{:S(2)}) collective-permute-start(bf16[64,768]{1,0:T(8,128)(2,1)S(1)} %get-tuple-element.30.d0_ref.refs_0_), channel_id=1, source_target_pairs={{0,8},{2,10},{4,12},{6,14},{8,0},{10,2},{12,4},{14,6},{1,9},{3,11}... | collective-permute-start | bytes 294920 | tf_op jit(solution)/shard_map/ppermute | solution.py:326
  6.1 0.1 collective-permute-start
  6.2 7.6 %collective-permute-done.r4_ref = bf16[64,512]{1,0:T(8,128)(2,1)S(1)} collective-permute-done((bf16[64,512]{1,0:T(8,128)(2,1)S(1)}, bf16[64,512]{1,0:T(8,128)(2,1)S(1)}, u32[]{:S(2)}, u32[]{:S(2)}) %collective-permute-start) | collective-permute-done | bytes 65568 | tf_op jit(solution)/shard_map/ppermute | solution.py:326
  13.8 1.6 %collective-permute-start.1 = (bf16[64,768]{1,0:T(8,128)(2,1)S(1)}, bf16[64,768]{1,0:T(8,128)(2,1)S(1)}, u32[]{:S(2)}, u32[]{:S(2)}) collective-permute-start(bf16[64,768]{1,0:T(8,128)(2,1)S(1)} %shard_map.83.after_any), channel_id=1, source_target_pairs={{0,2},{2,0},{4,6},{6,4},{8,10},{10,8},{12,14},{14,12},{1,3},{3,1},... | collective-permute-start | bytes 294920 | tf_op jit(solution)/shard_map/ppermute | solution.py:326
  15.5 0.6 %collective-permute-start.7 = (bf16[64,768]{1,0:T(8,128)(2,1)S(1)}, bf16[64,768]{1,0:T(8,128)(2,1)S(1)}, u32[]{:S(2)}, u32[]{:S(2)}) collective-permute-start(bf16[64,768]{1,0:T(8,128)(2,1)S(1)} %get-tuple-element.30.d0_ref.refs_0_), channel_id=1, source_target_pairs={{0,4},{2,6},{4,0},{6,2},{8,12},{10,14},{12,8},{14,10},{1,5},{3,7},... | collective-permute-start | bytes 294920 | tf_op jit(solution)/shard_map/ppermute | solution.py:326
  16.1 0.0 collective-permute-done.2.d4_ref.refs_2_
  16.1 1.5 %collective-permute-start.8 = (bf16[64,768]{1,0:T(8,128)(2,1)S(1)}, bf16[64,768]{1,0:T(8,128)(2,1)S(1)}, u32[]{:S(2)}, u32[]{:S(2)}) collective-permute-start(bf16[64,768]{1,0:T(8,128)(2,1)S(1)} %get-tuple-element.31.far_any), channel_id=1, source_target_pairs={{0,4},{2,6},{4,0},{6,2},{8,12},{10,14},{12,8},{14,10},{1,5},{3,7},... | collective-permute-start | bytes 294920 | tf_op jit(solution)/shard_map/ppermute | solution.py:326
  17.6 0.5 %collective-permute-start.6 = (bf16[64,1536]{1,0:T(8,128)(2,1)S(1)}, bf16[64,1536]{1,0:T(8,128)(2,1)S(1)}, u32[]{:S(2)}, u32[]{:S(2)}) collective-permute-start(bf16[64,1536]{1,0:T(8,128)(2,1)S(1)} %get-tuple-element.34), channel_id=1, source_target_pairs={{0,2},{2,0},{4,6},{6,4},{8,10},{10,8},{12,14},{14,12},{1,3},{3,1},... | collective-permute-start | bytes 589832 | tf_op jit(solution)/shard_map/ppermute | solution.py:326
  18.0 0.6 %collective-permute-done.1.r1_ref = bf16[64,768]{1,0:T(8,128)(2,1)S(1)} collective-permute-done((bf16[64,768]{1,0:T(8,128)(2,1)S(1)}, bf16[64,768]{1,0:T(8,128)(2,1)S(1)}, u32[]{:S(2)}, u32[]{:S(2)}) %collective-permute-start.1) | collective-permute-done | bytes 98336 | tf_op jit(solution)/shard_map/ppermute | solution.py:326
  18.7 0.1 collective-permute-start.3
  18.7 0.7 %collective-permute-start.4 = (bf16[64,1280]{1,0:T(8,128)(2,1)S(1)}, bf16[64,1280]{1,0:T(8,128)(2,1)S(1)}, u32[]{:S(2)}, u32[]{:S(2)}) collective-permute-start(bf16[64,1280]{1,0:T(8,128)(2,1)S(1)} %get-tuple-element.33), channel_id=1, source_target_pairs={{0,4},{2,6},{4,0},{6,2},{8,12},{10,14},{12,8},{14,10},{1,5},{3,7},... | collective-permute-start | bytes 491528 | tf_op jit(solution)/shard_map/ppermute | solution.py:326
  19.4 0.9 %collective-permute-done.7.refs_3_ = bf16[64,768]{1,0:T(8,128)(2,1)S(1)} collective-permute-done((bf16[64,768]{1,0:T(8,128)(2,1)S(1)}, bf16[64,768]{1,0:T(8,128)(2,1)S(1)}, u32[]{:S(2)}, u32[]{:S(2)}) %collective-permute-start.7) | collective-permute-done | bytes 98336 | tf_op jit(solution)/shard_map/ppermute | solution.py:326
  20.3 1.1 %collective-permute-done.8.refs_5_ = bf16[64,768]{1,0:T(8,128)(2,1)S(1)} collective-permute-done((bf16[64,768]{1,0:T(8,128)(2,1)S(1)}, bf16[64,768]{1,0:T(8,128)(2,1)S(1)}, u32[]{:S(2)}, u32[]{:S(2)}) %collective-permute-start.8) | collective-permute-done | bytes 98336 | tf_op jit(solution)/shard_map/ppermute | solution.py:326
  21.4 0.6 %collective-permute-start.9 = (bf16[64,1536]{1,0:T(8,128)(2,1)S(1)}, bf16[64,1536]{1,0:T(8,128)(2,1)S(1)}, u32[]{:S(2)}, u32[]{:S(2)}) collective-permute-start(bf16[64,1536]{1,0:T(8,128)(2,1)S(1)} %pad_maximum_fusion), channel_id=1, source_target_pairs={{0,2},{2,0},{4,6},{6,4},{8,10},{10,8},{12,14},{14,12},{1,3},{3,1},... | collective-permute-start | bytes 589832 | tf_op jit(solution)/shard_map/ppermute | solution.py:326
  22.0 3.4 %collective-permute-done.4.mine_ref = bf16[64,1280]{1,0:T(8,128)(2,1)S(1)} collective-permute-done((bf16[64,1280]{1,0:T(8,128)(2,1)S(1)}, bf16[64,1280]{1,0:T(8,128)(2,1)S(1)}, u32[]{:S(2)}, u32[]{:S(2)}) %collective-permute-start.4) | collective-permute-done | bytes 163872 | tf_op jit(solution)/shard_map/ppermute | solution.py:326
  25.4 0.9 %shard_map.86 = (bf16[512,256]{1,0:T(8,128)(2,1)S(1)}, f32[128,512]{1,0:T(8,128)S(1)}) custom-call(s32[2]{0:T(128)S(1)} %pad_add_fusion.place_ref, bf16[64,1536]{1,0:T(8,128)(2,1)S(1)} %get-tuple-element.32.mine_ref.kept_ref, bf16[64,1536]{1,0:T(8,128)(2,1)S(1)} %collective-permute-done.3.other_ref.kept2_ref, ...), custom_call_target="tpu_custom_call" | custom-call | tf_op jit(solution)/shard_map/pallas_call | solution.py:382
  26.3 0.4 %collective-permute-done.5.other_ref = bf16[64,1280]{1,0:T(8,128)(2,1)S(1)} collective-permute-done((bf16[64,1280]{1,0:T(8,128)(2,1)S(1)}, bf16[64,1280]{1,0:T(8,128)(2,1)S(1)}, u32[]{:S(2)}, u32[]{:S(2)}) %collective-permute-start.5) | collective-permute-done | bytes 163872 | tf_op jit(solution)/shard_map/ppermute | solution.py:329
  26.7 1.1 %shard_map.87 = (bf16[512,256]{1,0:T(8,128)(2,1)S(1)}, bf16[128,512]{1,0:T(8,128)(2,1)S(1)}, bf16[128,512]{1,0:T(8,128)(2,1)S(1)}, f32[128,128]{1,0:T(8,128)S(1)}) custom-call(s32[2]{0:T(128)S(1)} %pad_add_fusion.place_ref, bf16[64,1536]{1,0:T(8,128)(2,1)S(1)} %get-tuple-element.32.mine_ref.kept_ref, ...), custom_call_target="tpu_custom_call" | custom-call | tf_op jit(solution)/shard_map/pallas_call | solution.py:389
  27.8 1.7 %shard_map.88 = (f32[128,128]{1,0:T(8,128)S(1)}, f32[128,128]{1,0:T(8,128)S(1)}) custom-call(s32[2]{0:T(128)S(1)} %pad_add_fusion.place_ref, f32[128,128]{1,0:T(8,128)S(1)} %get-tuple-element.24.gene_ref, f32[128,128]{1,0:T(8,128)S(1)} %get-tuple-element.36.power_ref, bf16[512,256]{1,0:T(8,128)(2,1)S(1)} %get-tuple-element.37.turned_ref, ...), custom_call_target="tpu_custom_call" | custom-call | tf_op jit(solution)/shard_map/pallas_call | solution.py:395
  29.6 0.2 collective-permute-start.10
  29.8 1.1 %collective-permute-done.10 = f32[128,128]{1,0:T(8,128)S(1)} collective-permute-done((f32[128,128]{1,0:T(8,128)S(1)}, f32[128,128]{1,0:T(8,128)S(1)}, u32[]{:S(2)}, u32[]{:S(2)}) %collective-permute-start.10) | collective-permute-done | bytes 65568 | tf_op jit(solution)/shard_map/ppermute | solution.py:329
  30.9 0.6 %add.3 = f32[128,128]{1,0:T(8,128)} add(f32[128,128]{1,0:T(8,128)S(1)} %get-tuple-element.41, f32[128,128]{1,0:T(8,128)S(1)} %collective-permute-done.10) | non-fusion elementwise | flops 16384 | bytes 196608 | tf_op jit(solution)/shard_map/add | solution.py:401
  (8 shorter events, 0.1 us)
Async XLA Ops:
  2.0 14.1 %collective-permute-start.2 = (bf16[64,768]{1,0:T(8,128)(2,1)S(1)}, bf16[64,768]{1,0:T(8,128)(2,1)S(1)}, u32[]{:S(2)}, u32[]{:S(2)}) collective-permute-start(bf16[64,768]{1,0:T(8,128)(2,1)S(1)} %get-tuple-element.30.d0_ref.refs_0_), channel_id=1, source_target_pairs={{0,8},{2,10},{4,12},{6,14},{8,0},{10,2},{12,4},{14,6},{1,9},{3,11}... | collective-permute-start | bytes 294920 | tf_op jit(solution)/shard_map/ppermute | solution.py:326
  6.1 7.7 %collective-permute-start = (bf16[64,512]{1,0:T(8,128)(2,1)S(1)}, bf16[64,512]{1,0:T(8,128)(2,1)S(1)}, u32[]{:S(2)}, u32[]{:S(2)}) collective-permute-start(bf16[64,512]{1,0:T(8,128)(2,1)S(1)} %get-tuple-element.25.ahead_ref), channel_id=1, source_target_pairs={{0,8},{2,10},{4,12},{6,14},{8,0},{10,2},{12,4},{14,6},{1,9},{3,11}... | collective-permute-start | bytes 196616 | tf_op jit(solution)/shard_map/ppermute | solution.py:326
  13.8 4.8 %collective-permute-start.1 = (bf16[64,768]{1,0:T(8,128)(2,1)S(1)}, bf16[64,768]{1,0:T(8,128)(2,1)S(1)}, u32[]{:S(2)}, u32[]{:S(2)}) collective-permute-start(bf16[64,768]{1,0:T(8,128)(2,1)S(1)} %shard_map.83.after_any), channel_id=1, source_target_pairs={{0,2},{2,0},{4,6},{6,4},{8,10},{10,8},{12,14},{14,12},{1,3},{3,1},... | collective-permute-start | bytes 294920 | tf_op jit(solution)/shard_map/ppermute | solution.py:326
  15.5 4.9 %collective-permute-start.7 = (bf16[64,768]{1,0:T(8,128)(2,1)S(1)}, bf16[64,768]{1,0:T(8,128)(2,1)S(1)}, u32[]{:S(2)}, u32[]{:S(2)}) collective-permute-start(bf16[64,768]{1,0:T(8,128)(2,1)S(1)} %get-tuple-element.30.d0_ref.refs_0_), channel_id=1, source_target_pairs={{0,4},{2,6},{4,0},{6,2},{8,12},{10,14},{12,8},{14,10},{1,5},{3,7},... | collective-permute-start | bytes 294920 | tf_op jit(solution)/shard_map/ppermute | solution.py:326
  16.1 5.3 %collective-permute-start.8 = (bf16[64,768]{1,0:T(8,128)(2,1)S(1)}, bf16[64,768]{1,0:T(8,128)(2,1)S(1)}, u32[]{:S(2)}, u32[]{:S(2)}) collective-permute-start(bf16[64,768]{1,0:T(8,128)(2,1)S(1)} %get-tuple-element.31.far_any), channel_id=1, source_target_pairs={{0,4},{2,6},{4,0},{6,2},{8,12},{10,14},{12,8},{14,10},{1,5},{3,7},... | collective-permute-start | bytes 294920 | tf_op jit(solution)/shard_map/ppermute | solution.py:326
  17.6 7.8 %collective-permute-start.6 = (bf16[64,1536]{1,0:T(8,128)(2,1)S(1)}, bf16[64,1536]{1,0:T(8,128)(2,1)S(1)}, u32[]{:S(2)}, u32[]{:S(2)}) collective-permute-start(bf16[64,1536]{1,0:T(8,128)(2,1)S(1)} %get-tuple-element.34), channel_id=1, source_target_pairs={{0,2},{2,0},{4,6},{6,4},{8,10},{10,8},{12,14},{14,12},{1,3},{3,1},... | collective-permute-start | bytes 589832 | tf_op jit(solution)/shard_map/ppermute | solution.py:326
  18.7 6.7 %collective-permute-start.3 = (bf16[64,1536]{1,0:T(8,128)(2,1)S(1)}, bf16[64,1536]{1,0:T(8,128)(2,1)S(1)}, u32[]{:S(2)}, u32[]{:S(2)}) collective-permute-start(bf16[64,1536]{1,0:T(8,128)(2,1)S(1)} %get-tuple-element.32.mine_ref.kept_ref), channel_id=1, source_target_pairs={{0,1},{1,0},{2,3},{3,2},{4,5},{5,4},{6,7},{7,6},{8,9},{9,8},{10,11... | collective-permute-start | bytes 589832 | tf_op jit(solution)/shard_map/ppermute | solution.py:329
  18.7 6.6 %collective-permute-start.4 = (bf16[64,1280]{1,0:T(8,128)(2,1)S(1)}, bf16[64,1280]{1,0:T(8,128)(2,1)S(1)}, u32[]{:S(2)}, u32[]{:S(2)}) collective-permute-start(bf16[64,1280]{1,0:T(8,128)(2,1)S(1)} %get-tuple-element.33), channel_id=1, source_target_pairs={{0,4},{2,6},{4,0},{6,2},{8,12},{10,14},{12,8},{14,10},{1,5},{3,7},... | collective-permute-start | bytes 491528 | tf_op jit(solution)/shard_map/ppermute | solution.py:326
  21.4 6.4 %collective-permute-start.9 = (bf16[64,1536]{1,0:T(8,128)(2,1)S(1)}, bf16[64,1536]{1,0:T(8,128)(2,1)S(1)}, u32[]{:S(2)}, u32[]{:S(2)}) collective-permute-start(bf16[64,1536]{1,0:T(8,128)(2,1)S(1)} %pad_maximum_fusion), channel_id=1, source_target_pairs={{0,2},{2,0},{4,6},{6,4},{8,10},{10,8},{12,14},{14,12},{1,3},{3,1},... | collective-permute-start | bytes 589832 | tf_op jit(solution)/shard_map/ppermute | solution.py:326
  25.3 1.4 %collective-permute-start.5 = (bf16[64,1280]{1,0:T(8,128)(2,1)S(1)}, bf16[64,1280]{1,0:T(8,128)(2,1)S(1)}, u32[]{:S(2)}, u32[]{:S(2)}) collective-permute-start(bf16[64,1280]{1,0:T(8,128)(2,1)S(1)} %collective-permute-done.4.mine_ref), channel_id=1, source_target_pairs={{0,1},{1,0},{2,3},{3,2},{4,5},{5,4},{6,7},{7,6},{8,9},{9,8},{10,11... | collective-permute-start | bytes 491528 | tf_op jit(solution)/shard_map/ppermute | solution.py:329
  29.6 1.3 %collective-permute-start.10 = (f32[128,128]{1,0:T(8,128)S(1)}, f32[128,128]{1,0:T(8,128)S(1)}, u32[]{:S(2)}, u32[]{:S(2)}) collective-permute-start(f32[128,128]{1,0:T(8,128)S(1)} %get-tuple-element.42), channel_id=1, source_target_pairs={{0,1},{1,0},{2,3},{3,2},{4,5},{5,4},{6,7},{7,6},{8,9},{9,8},{10,11... | collective-permute-start | bytes 196616 | tf_op jit(solution)/shard_map/ppermute | solution.py:329

commit v12 on v10

--- a/solution.py
+++ b/solution.py
@@ -8,7 +8,6 @@
 W = 256
 LANES = 128
 VMEM_LIMIT = 32 * 1024 * 1024
-ROUTE_LIMIT = 32 * 1024 * 1024
 NT = (((1,), (1,)), ((), ()))
 f32 = jnp.float32
 bf16 = jnp.bfloat16
@@ -102,9 +101,9 @@
 
 
 def route_kernel(
-    place_ref, owner_any, delta_any, start_any, valid_any, vals_any, vecs_any, expr_any, dose_any,
-    ahead_ref, e46_ref, e2_ref, e0_ref, gene_ref, terms_ref, half_ref,
-    owner_ref, delta_ref, start_ref, valid_ref, vals_ref, expr_ref, sems,
+    place_ref, owner_any, expr_any, vecs_any, dose_any,
+    ahead_ref, e46_ref, e2_ref, e0_ref, half_ref, bucket_ref,
+    owner_ref, expr_ref, sems,
 ):
     row, core = place_ref[0], place_ref[1]
     half = vecs_any.shape[1]
@@ -113,10 +112,6 @@
     pairs = (
         (owner_any, owner_ref),
         (expr_any.at[pl.ds(pl.multiple_of(core * part, part), part)], expr_ref),
-        (delta_any, delta_ref),
-        (start_any, start_ref),
-        (valid_any, valid_ref),
-        (vals_any, vals_ref),
         (vecs_any, ahead_ref.at[:, pl.ds(0, half)]),
         (dose_any.at[:, pl.ds(pl.multiple_of(core * variants, LANES), variants)], half_ref),
     )
@@ -130,8 +125,6 @@
     )
     before = before.astype(bf16)
     slot = lax.broadcasted_iota(jnp.int32, (LANES, LANES), 0)
-    own_slot = lax.broadcasted_iota(jnp.int32, (capacity, LANES), 0)
-    lane = lax.broadcasted_iota(jnp.int32, (capacity, LANES), 1)
     copies[0].wait()
     owner = owner_ref[...]
     rank = jnp.zeros(owner.shape, f32)
@@ -139,8 +132,8 @@
         same = (owner == o).astype(f32)
         rank += same * jnp.dot(same.astype(bf16), before, preferred_element_type=f32)
     bucket = (owner ^ row) * capacity + rank.astype(jnp.int32)
-    for copy in copies[1:]:
-        copy.wait()
+    bucket_ref[...] = bucket
+    copies[1].wait()
     sorted_slices = []
     for s in range(slices):
         here = bucket[s : s + 1, :]
@@ -148,18 +141,6 @@
         sorted_slices.append(
             lax.dot_general(pick, expr_ref[:, s * LANES : (s + 1) * LANES], NT, preferred_element_type=f32)
         )
-        mine = (own_slot == here).astype(f32)
-        figures = jnp.zeros((capacity, LANES), f32)
-        for i, ref in enumerate((delta_ref, start_ref, valid_ref)):
-            line = ref[s : s + 1, :].astype(f32)
-            figures = jnp.where(lane == i, jnp.sum(mine * line, axis=1, keepdims=True), figures)
-        gene_ref[s * capacity : (s + 1) * capacity, :] = figures
-    vals = vals_ref[...]
-    high = vals.astype(bf16).astype(f32)
-    middle = (vals - high).astype(bf16).astype(f32)
-    term = lax.broadcasted_iota(jnp.int32, terms_ref.shape, 0)
-    terms = jnp.where(term == 0, high, jnp.where(term == 1, middle, jnp.where(term == 2, vals - high - middle, 0.0)))
-    terms_ref[...] = terms.astype(bf16)
     left, right = slice(0, LANES), slice(LANES, 2 * LANES)
     upper, lower = slice(0, part), slice(part, 2 * part)
     targets = {
@@ -175,6 +156,28 @@
     for m, (ref, down, side) in targets.items():
         block = jnp.concatenate([x[m * capacity : (m + 1) * capacity, :] for x in sorted_slices], axis=0)
         ref[down, side] = block.T.astype(bf16)
+    for copy in copies[2:]:
+        copy.wait()
+
+
+def gene_kernel(bucket_ref, delta_ref, start_ref, valid_ref, vals_ref, gene_ref, terms_ref):
+    slices = bucket_ref.shape[0]
+    capacity = LANES // slices
+    own_slot = lax.broadcasted_iota(jnp.int32, (capacity, LANES), 0)
+    lane = lax.broadcasted_iota(jnp.int32, (capacity, LANES), 1)
+    for s in range(slices):
+        mine = (own_slot == bucket_ref[s : s + 1, :]).astype(f32)
+        figures = jnp.zeros((capacity, LANES), f32)
+        for i, ref in enumerate((delta_ref, start_ref, valid_ref)):
+            line = ref[s : s + 1, :].astype(f32)
+            figures = jnp.where(lane == i, jnp.sum(mine * line, axis=1, keepdims=True), figures)
+        gene_ref[s * capacity : (s + 1) * capacity, :] = figures
+    vals = vals_ref[...]
+    high = vals.astype(bf16).astype(f32)
+    middle = (vals - high).astype(bf16).astype(f32)
+    term = lax.broadcasted_iota(jnp.int32, terms_ref.shape, 0)
+    terms = jnp.where(term == 0, high, jnp.where(term == 1, middle, jnp.where(term == 2, vals - high - middle, 0.0)))
+    terms_ref[...] = terms.astype(bf16)
 
 
 def second_kernel(ahead_ref, r1_ref, e46_ref, out_ref):
@@ -328,37 +331,36 @@
     def other_core(x):
         return lax.ppermute(x, "col", [(0, 1), (1, 0)])
 
-    ahead, e46, e2, e0, gene, terms, d0 = call(
+    ahead, e46, e2, e0, d0, bucket = call(
         route_kernel,
         [
             ((panel, half + 2 * LANES), bf16),
             ((part, 2 * LANES), bf16),
             ((part, LANES), bf16),
             ((part, LANES), bf16),
-            ((LANES, LANES), f32),
-            ((16, half), bf16),
             ((panel, variants), bf16),
+            ((rows, LANES), jnp.int32),
         ],
-        9,
-        scratch=[pltpu.VMEM((rows, LANES), kind) for kind in (jnp.int32, f32, jnp.int32, jnp.int32)]
-        + [pltpu.VMEM((1, half), f32), pltpu.VMEM((part, expression.shape[1]), bf16), pltpu.SemaphoreType.DMA((8,))],
-        anywhere=8,
-        limit=ROUTE_LIMIT,
+        5,
+        scratch=[
+            pltpu.VMEM((rows, LANES), jnp.int32),
+            pltpu.VMEM((part, expression.shape[1]), bf16),
+            pltpu.SemaphoreType.DMA((4,)),
+        ],
+        anywhere=4,
     )(
         place,
         *[
             pltpu.with_memory_space_constraint(x, pltpu.HBM)
-            for x in (
-                gene_owner.reshape(rows, LANES),
-                delta.reshape(rows, LANES),
-                window_start.reshape(rows, LANES),
-                window_valid.reshape(rows, LANES),
-                eigvals[None, :],
-                eigvecs,
-                expression,
-                dosage,
-            )
+            for x in (gene_owner.reshape(rows, LANES), expression, eigvecs, dosage)
         ],
+    )
+    gene, terms = call(gene_kernel, [((LANES, LANES), f32), ((16, half), bf16)], 5, smem=0)(
+        bucket,
+        delta.reshape(rows, LANES),
+        window_start.reshape(rows, LANES),
+        window_valid.reshape(rows, LANES),
+        eigvals[None, :],
     )
     r1 = swap(ahead, 1)
     d4 = swap(d0, 4)

time: 29.3 us -> 29.2 us (level)
  waiting for transfers between devices: 9.1 us -> 8.18 us
  local copies, waits for them, and re-layouts: 0 us -> 0.71 us
    ppermute x8, waiting for transfers between devices: 7.54 us -> 6.62 us  [swap(): return lax.ppermute(x, 'row', [(i, i ^ m) for i in range(rows)])]
    unnamed x0 -> x8, local copies, waits for them, and re-layouts: none -> 0.71 us
  transfers between devices with their start and end apart: 11 -> 11, of which waited for: 5 -> 5; matrix products, arithmetic and copies ran while one was open for 0% -> 0% of each run, Pallas kernels for 7% -> 8%
where the time goes in v12:
time: 29.2 us; the launch traced here: 29 us
  starting transfers between devices  13.6 us (47%)
  waiting for transfers between devices  8.18 us (28%)
  Pallas kernels  5.64 us (19%)
  other arithmetic  0.73 us (2%)
  local copies, waits for them, and re-layouts  0.71 us (2%)
    ppermute x8, starting transfers between devices, swap(): return lax.ppermute(x, 'row', [(i, i ^ m) for i in range(rows)])  13.3 us
    ppermute x8, waiting for transfers between devices, swap(): return lax.ppermute(x, 'row', [(i, i ^ m) for i in range(rows)])  6.62 us
    pallas_call x1, Pallas kernels, near_body(): call(route_kernel, [((panel, half + 2 * LANES), bf16), ((part, 2 * LANES)...  1.73 us
    pallas_call x1, Pallas kernels, near_body(): call(score_kernel, [((LANES, LANES), f32)] * 2, 13, scratch=[pltpu.VMEM((...  1.72 us
    ppermute x3, waiting for transfers between devices, other_core(): return lax.ppermute(x, 'col', [(0, 1), (1, 0)])  1.56 us
    pallas_call x1, Pallas kernels, near_body(): call(weight_kernel, [shape, ((LANES, 2 * half), bf16), ((LANES, 2 * half)...  1.08 us
    pallas_call x1, Pallas kernels, near_body(): call(half_kernel, [shape, ((LANES, 2 * half), f32)], 4, scratch=[pltpu.VM...  0.93 us
    unnamed x8, local copies, waits for them, and re-layouts  0.71 us
  transfers between devices with their start and end apart: 11, of which 5 were waited for; matrix products, arithmetic and copies ran while one was open for 0% of the time, Pallas kernels for 8%

profile of v12, /device:TPU:0, one launch (start us, length us, event | category | flops | bytes accessed | tf_op | source)
XLA Modules:
  0.0 29.0 jit_solution(9580283345021662281)
XLA Ops:
  0.0 0.1 pad_add_fusion.place_ref
  0.1 1.7 %shard_map.82 = (bf16[64,512]{1,0:T(8,128)(2,1)S(1)}, bf16[32,256]{1,0:T(8,128)(2,1)S(1)}, bf16[32,128]{1,0:T(8,128)(2,1)S(1)}, bf16[32,128]{1,0:T(8,128)(2,1)S(...) custom-call(s32[2]{0:T(128)S(1)} %pad_add_fusion.place_ref, s32[8,128]{1,0:T(8,128)} %bitcast.11, ...), custom_call_target="tpu_custom_call" | custom-call | tf_op jit(solution)/shard_map/pallas_call | solution.py:334
  1.8 4.1 %collective-permute-start.2 = (bf16[64,768]{1,0:T(8,128)(2,1)S(1)}, bf16[64,768]{1,0:T(8,128)(2,1)S(1)}, u32[]{:S(2)}, u32[]{:S(2)}) collective-permute-start(bf16[64,768]{1,0:T(8,128)(2,1)S(1)} %get-tuple-element.32.d0_ref.refs_0_), channel_id=1, source_target_pairs={{0,8},{2,10},{4,12},{6,14},{8,0},{10,2},{12,4},{14,6},{1,9},{3,11}... | collective-permute-start | bytes 294920 | tf_op jit(solution)/shard_map/ppermute | solution.py:329
  5.9 1.5 %collective-permute-start = (bf16[64,512]{1,0:T(8,128)(2,1)S(1)}, bf16[64,512]{1,0:T(8,128)(2,1)S(1)}, u32[]{:S(2)}, u32[]{:S(2)}) collective-permute-start(bf16[64,512]{1,0:T(8,128)(2,1)S(1)} %get-tuple-element.27.ahead_ref), channel_id=1, source_target_pairs={{0,2},{2,0},{4,6},{6,4},{8,10},{10,8},{12,14},{14,12},{1,3},{3,1},... | collective-permute-start | bytes 196616 | tf_op jit(solution)/shard_map/ppermute | solution.py:329
  7.4 2.7 %collective-permute-done.r1_ref = bf16[64,512]{1,0:T(8,128)(2,1)S(1)} collective-permute-done((bf16[64,512]{1,0:T(8,128)(2,1)S(1)}, bf16[64,512]{1,0:T(8,128)(2,1)S(1)}, u32[]{:S(2)}, u32[]{:S(2)}) %collective-permute-start) | collective-permute-done | bytes 65568 | tf_op jit(solution)/shard_map/ppermute | solution.py:329
  10.2 0.1 collective-permute-start.1
  10.3 1.9 %collective-permute-start.7 = (bf16[64,768]{1,0:T(8,128)(2,1)S(1)}, bf16[64,768]{1,0:T(8,128)(2,1)S(1)}, u32[]{:S(2)}, u32[]{:S(2)}) collective-permute-start(bf16[64,768]{1,0:T(8,128)(2,1)S(1)} %get-tuple-element.32.d0_ref.refs_0_), channel_id=1, source_target_pairs={{0,4},{2,6},{4,0},{6,2},{8,12},{10,14},{12,8},{14,10},{1,5},{3,7},... | collective-permute-start | bytes 294920 | tf_op jit(solution)/shard_map/ppermute | solution.py:329
  12.2 0.6 %collective-permute-start.8 = (bf16[64,768]{1,0:T(8,128)(2,1)S(1)}, bf16[64,768]{1,0:T(8,128)(2,1)S(1)}, u32[]{:S(2)}, u32[]{:S(2)}) collective-permute-start(bf16[64,768]{1,0:T(8,128)(2,1)S(1)} %get-tuple-element.33.far_any), channel_id=1, source_target_pairs={{0,4},{2,6},{4,0},{6,2},{8,12},{10,14},{12,8},{14,10},{1,5},{3,7},... | collective-permute-start | bytes 294920 | tf_op jit(solution)/shard_map/ppermute | solution.py:329
  12.8 0.1 copy-done.2
  12.9 0.6 %copy-done.1 = s32[1024]{0:T(1024)S(1)} copy-done((s32[1024]{0:T(1024)S(1)}, s32[1024]{0:T(1024)}, u32[]{:S(2)}) %copy-start.1) | copy-done | bytes 4120
  13.5 0.1 shard_map.83
  13.6 1.6 %collective-permute-start.6 = (bf16[64,1536]{1,0:T(8,128)(2,1)S(1)}, bf16[64,1536]{1,0:T(8,128)(2,1)S(1)}, u32[]{:S(2)}, u32[]{:S(2)}) collective-permute-start(bf16[64,1536]{1,0:T(8,128)(2,1)S(1)} %get-tuple-element.36), channel_id=1, source_target_pairs={{0,2},{2,0},{4,6},{6,4},{8,10},{10,8},{12,14},{14,12},{1,3},{3,1},... | collective-permute-start | bytes 589832 | tf_op jit(solution)/shard_map/ppermute | solution.py:329
  15.2 0.7 %collective-permute-done.1.r4_ref = bf16[64,768]{1,0:T(8,128)(2,1)S(1)} collective-permute-done((bf16[64,768]{1,0:T(8,128)(2,1)S(1)}, bf16[64,768]{1,0:T(8,128)(2,1)S(1)}, u32[]{:S(2)}, u32[]{:S(2)}) %collective-permute-start.1) | collective-permute-done | bytes 98336 | tf_op jit(solution)/shard_map/ppermute | solution.py:329
  15.9 0.1 collective-permute-start.3
  16.0 2.0 %collective-permute-start.4 = (bf16[64,1280]{1,0:T(8,128)(2,1)S(1)}, bf16[64,1280]{1,0:T(8,128)(2,1)S(1)}, u32[]{:S(2)}, u32[]{:S(2)}) collective-permute-start(bf16[64,1280]{1,0:T(8,128)(2,1)S(1)} %get-tuple-element.35), channel_id=1, source_target_pairs={{0,4},{2,6},{4,0},{6,2},{8,12},{10,14},{12,8},{14,10},{1,5},{3,7},... | collective-permute-start | bytes 491528 | tf_op jit(solution)/shard_map/ppermute | solution.py:329
  18.0 1.6 %collective-permute-start.9 = (bf16[64,1536]{1,0:T(8,128)(2,1)S(1)}, bf16[64,1536]{1,0:T(8,128)(2,1)S(1)}, u32[]{:S(2)}, u32[]{:S(2)}) collective-permute-start(bf16[64,1536]{1,0:T(8,128)(2,1)S(1)} %pad_maximum_fusion), channel_id=1, source_target_pairs={{0,2},{2,0},{4,6},{6,4},{8,10},{10,8},{12,14},{14,12},{1,3},{3,1},... | collective-permute-start | bytes 589832 | tf_op jit(solution)/shard_map/ppermute | solution.py:329
  19.6 3.2 %collective-permute-done.4.mine_ref = bf16[64,1280]{1,0:T(8,128)(2,1)S(1)} collective-permute-done((bf16[64,1280]{1,0:T(8,128)(2,1)S(1)}, bf16[64,1280]{1,0:T(8,128)(2,1)S(1)}, u32[]{:S(2)}, u32[]{:S(2)}) %collective-permute-start.4) | collective-permute-done | bytes 163872 | tf_op jit(solution)/shard_map/ppermute | solution.py:329
  22.8 0.9 %shard_map.87 = (bf16[512,256]{1,0:T(8,128)(2,1)S(1)}, f32[128,512]{1,0:T(8,128)S(1)}) custom-call(s32[2]{0:T(128)S(1)} %pad_add_fusion.place_ref, bf16[64,1536]{1,0:T(8,128)(2,1)S(1)} %get-tuple-element.34.mine_ref.kept_ref, bf16[64,1536]{1,0:T(8,128)(2,1)S(1)} %collective-permute-done.3.other_ref.kept2_ref, ...), custom_call_target="tpu_custom_call" | custom-call | tf_op jit(solution)/shard_map/pallas_call | solution.py:384
  23.7 0.4 %collective-permute-done.5.other_ref = bf16[64,1280]{1,0:T(8,128)(2,1)S(1)} collective-permute-done((bf16[64,1280]{1,0:T(8,128)(2,1)S(1)}, bf16[64,1280]{1,0:T(8,128)(2,1)S(1)}, u32[]{:S(2)}, u32[]{:S(2)}) %collective-permute-start.5) | collective-permute-done | bytes 163872 | tf_op jit(solution)/shard_map/ppermute | solution.py:332
  24.2 1.1 %shard_map.88 = (bf16[512,256]{1,0:T(8,128)(2,1)S(1)}, bf16[128,512]{1,0:T(8,128)(2,1)S(1)}, bf16[128,512]{1,0:T(8,128)(2,1)S(1)}, f32[128,128]{1,0:T(8,128)S(1)}) custom-call(s32[2]{0:T(128)S(1)} %pad_add_fusion.place_ref, bf16[64,1536]{1,0:T(8,128)(2,1)S(1)} %get-tuple-element.34.mine_ref.kept_ref, ...), custom_call_target="tpu_custom_call" | custom-call | tf_op jit(solution)/shard_map/pallas_call | solution.py:391
  25.3 1.7 %shard_map.89 = (f32[128,128]{1,0:T(8,128)S(1)}, f32[128,128]{1,0:T(8,128)S(1)}) custom-call(s32[2]{0:T(128)S(1)} %pad_add_fusion.place_ref, f32[128,128]{1,0:T(8,128)S(1)} %get-tuple-element.26.gene_ref, f32[128,128]{1,0:T(8,128)S(1)} %get-tuple-element.38.power_ref, bf16[512,256]{1,0:T(8,128)(2,1)S(1)} %get-tuple-element.39.turned_ref, ...), custom_call_target="tpu_custom_call" | custom-call | tf_op jit(solution)/shard_map/pallas_call | solution.py:397
  27.0 0.2 collective-permute-start.10
  27.2 1.1 %collective-permute-done.10 = f32[128,128]{1,0:T(8,128)S(1)} collective-permute-done((f32[128,128]{1,0:T(8,128)S(1)}, f32[128,128]{1,0:T(8,128)S(1)}, u32[]{:S(2)}, u32[]{:S(2)}) %collective-permute-start.10) | collective-permute-done | bytes 65568 | tf_op jit(solution)/shard_map/ppermute | solution.py:332
  28.3 0.6 %add.3 = f32[128,128]{1,0:T(8,128)} add(f32[128,128]{1,0:T(8,128)S(1)} %get-tuple-element.43, f32[128,128]{1,0:T(8,128)S(1)} %collective-permute-done.10) | non-fusion elementwise | flops 16384 | bytes 196608 | tf_op jit(solution)/shard_map/add | solution.py:403
  (17 shorter events, 0.1 us)
Async XLA Ops:
  1.8 10.4 %collective-permute-start.2 = (bf16[64,768]{1,0:T(8,128)(2,1)S(1)}, bf16[64,768]{1,0:T(8,128)(2,1)S(1)}, u32[]{:S(2)}, u32[]{:S(2)}) collective-permute-start(bf16[64,768]{1,0:T(8,128)(2,1)S(1)} %get-tuple-element.32.d0_ref.refs_0_), channel_id=1, source_target_pairs={{0,8},{2,10},{4,12},{6,14},{8,0},{10,2},{12,4},{14,6},{1,9},{3,11}... | collective-permute-start | bytes 294920 | tf_op jit(solution)/shard_map/ppermute | solution.py:329
  5.9 4.3 %collective-permute-start = (bf16[64,512]{1,0:T(8,128)(2,1)S(1)}, bf16[64,512]{1,0:T(8,128)(2,1)S(1)}, u32[]{:S(2)}, u32[]{:S(2)}) collective-permute-start(bf16[64,512]{1,0:T(8,128)(2,1)S(1)} %get-tuple-element.27.ahead_ref), channel_id=1, source_target_pairs={{0,2},{2,0},{4,6},{6,4},{8,10},{10,8},{12,14},{14,12},{1,3},{3,1},... | collective-permute-start | bytes 196616 | tf_op jit(solution)/shard_map/ppermute | solution.py:329
  10.2 5.7 %collective-permute-start.1 = (bf16[64,768]{1,0:T(8,128)(2,1)S(1)}, bf16[64,768]{1,0:T(8,128)(2,1)S(1)}, u32[]{:S(2)}, u32[]{:S(2)}) collective-permute-start(bf16[64,768]{1,0:T(8,128)(2,1)S(1)} %shard_map.84.after_any), channel_id=1, source_target_pairs={{0,8},{2,10},{4,12},{6,14},{8,0},{10,2},{12,4},{14,6},{1,9},{3,11}... | collective-permute-start | bytes 294920 | tf_op jit(solution)/shard_map/ppermute | solution.py:329
  10.3 7.7 %collective-permute-start.7 = (bf16[64,768]{1,0:T(8,128)(2,1)S(1)}, bf16[64,768]{1,0:T(8,128)(2,1)S(1)}, u32[]{:S(2)}, u32[]{:S(2)}) collective-permute-start(bf16[64,768]{1,0:T(8,128)(2,1)S(1)} %get-tuple-element.32.d0_ref.refs_0_), channel_id=1, source_target_pairs={{0,4},{2,6},{4,0},{6,2},{8,12},{10,14},{12,8},{14,10},{1,5},{3,7},... | collective-permute-start | bytes 294920 | tf_op jit(solution)/shard_map/ppermute | solution.py:329
  12.2 0.7 %copy-start.2 = (s32[1024]{0:T(1024)S(1)}, s32[1024]{0:T(1024)}, u32[]{:S(2)}) copy-start(s32[1024]{0:T(1024)} %param.14) | copy-start | bytes 12292
  12.2 5.8 %collective-permute-start.8 = (bf16[64,768]{1,0:T(8,128)(2,1)S(1)}, bf16[64,768]{1,0:T(8,128)(2,1)S(1)}, u32[]{:S(2)}, u32[]{:S(2)}) collective-permute-start(bf16[64,768]{1,0:T(8,128)(2,1)S(1)} %get-tuple-element.33.far_any), channel_id=1, source_target_pairs={{0,4},{2,6},{4,0},{6,2},{8,12},{10,14},{12,8},{14,10},{1,5},{3,7},... | collective-permute-start | bytes 294920 | tf_op jit(solution)/shard_map/ppermute | solution.py:329
  12.8 0.7 %copy-start.1 = (s32[1024]{0:T(1024)S(1)}, s32[1024]{0:T(1024)}, u32[]{:S(2)}) copy-start(s32[1024]{0:T(1024)} %param.13) | copy-start | bytes 12292
  12.8 0.7 %copy-start = (f32[1024]{0:T(1024)S(1)}, f32[1024]{0:T(1024)}, u32[]{:S(2)}) copy-start(f32[1024]{0:T(1024)} %param.12) | copy-start | bytes 12292
  12.8 0.7 %copy-start.3 = (f32[256]{0:T(256)S(1)}, f32[256]{0:T(256)}, u32[]{:S(2)}) copy-start(f32[256]{0:T(256)} %param.9) | copy-start | bytes 3076
  13.6 9.2 %collective-permute-start.6 = (bf16[64,1536]{1,0:T(8,128)(2,1)S(1)}, bf16[64,1536]{1,0:T(8,128)(2,1)S(1)}, u32[]{:S(2)}, u32[]{:S(2)}) collective-permute-start(bf16[64,1536]{1,0:T(8,128)(2,1)S(1)} %get-tuple-element.36), channel_id=1, source_target_pairs={{0,2},{2,0},{4,6},{6,4},{8,10},{10,8},{12,14},{14,12},{1,3},{3,1},... | collective-permute-start | bytes 589832 | tf_op jit(solution)/shard_map/ppermute | solution.py:329
  15.9 6.9 %collective-permute-start.3 = (bf16[64,1536]{1,0:T(8,128)(2,1)S(1)}, bf16[64,1536]{1,0:T(8,128)(2,1)S(1)}, u32[]{:S(2)}, u32[]{:S(2)}) collective-permute-start(bf16[64,1536]{1,0:T(8,128)(2,1)S(1)} %get-tuple-element.34.mine_ref.kept_ref), channel_id=1, source_target_pairs={{0,1},{1,0},{2,3},{3,2},{4,5},{5,4},{6,7},{7,6},{8,9},{9,8},{10,11... | collective-permute-start | bytes 589832 | tf_op jit(solution)/shard_map/ppermute | solution.py:332
  16.0 6.8 %collective-permute-start.4 = (bf16[64,1280]{1,0:T(8,128)(2,1)S(1)}, bf16[64,1280]{1,0:T(8,128)(2,1)S(1)}, u32[]{:S(2)}, u32[]{:S(2)}) collective-permute-start(bf16[64,1280]{1,0:T(8,128)(2,1)S(1)} %get-tuple-element.35), channel_id=1, source_target_pairs={{0,4},{2,6},{4,0},{6,2},{8,12},{10,14},{12,8},{14,10},{1,5},{3,7},... | collective-permute-start | bytes 491528 | tf_op jit(solution)/shard_map/ppermute | solution.py:329
  18.0 7.3 %collective-permute-start.9 = (bf16[64,1536]{1,0:T(8,128)(2,1)S(1)}, bf16[64,1536]{1,0:T(8,128)(2,1)S(1)}, u32[]{:S(2)}, u32[]{:S(2)}) collective-permute-start(bf16[64,1536]{1,0:T(8,128)(2,1)S(1)} %pad_maximum_fusion), channel_id=1, source_target_pairs={{0,2},{2,0},{4,6},{6,4},{8,10},{10,8},{12,14},{14,12},{1,3},{3,1},... | collective-permute-start | bytes 589832 | tf_op jit(solution)/shard_map/ppermute | solution.py:329
  22.8 1.4 %collective-permute-start.5 = (bf16[64,1280]{1,0:T(8,128)(2,1)S(1)}, bf16[64,1280]{1,0:T(8,128)(2,1)S(1)}, u32[]{:S(2)}, u32[]{:S(2)}) collective-permute-start(bf16[64,1280]{1,0:T(8,128)(2,1)S(1)} %collective-permute-done.4.mine_ref), channel_id=1, source_target_pairs={{0,1},{1,0},{2,3},{3,2},{4,5},{5,4},{6,7},{7,6},{8,9},{9,8},{10,11... | collective-permute-start | bytes 491528 | tf_op jit(solution)/shard_map/ppermute | solution.py:332
  27.0 1.3 %collective-permute-start.10 = (f32[128,128]{1,0:T(8,128)S(1)}, f32[128,128]{1,0:T(8,128)S(1)}, u32[]{:S(2)}, u32[]{:S(2)}) collective-permute-start(f32[128,128]{1,0:T(8,128)S(1)} %get-tuple-element.44), channel_id=1, source_target_pairs={{0,1},{1,0},{2,3},{3,2},{4,5},{5,4},{6,7},{7,6},{8,9},{9,8},{10,11... | collective-permute-start | bytes 196616 | tf_op jit(solution)/shard_map/ppermute | solution.py:332

commit v13 on v12

--- a/solution.py
+++ b/solution.py
@@ -1,3 +1,5 @@
+import functools
+
 import jax
 import jax.numpy as jnp
 from jax import lax
@@ -196,7 +198,7 @@
     far_ref[...] = d4_ref[...]
 
 
-def third_kernel(ahead_ref, r1_ref, r4_ref, e2_ref, e0_ref, terms_ref, far_any, out_ref, kept_ref):
+def third_kernel(ahead_ref, r1_ref, r4_ref, e2_ref, e0_ref, terms_ref, far_any, d2_any, out_ref, kept_ref):
     half = terms_ref.shape[1]
     part = e0_ref.shape[0]
     for ref, own, at in ((out_ref, e2_ref, LANES), (kept_ref, e0_ref, 0)):
@@ -265,8 +267,33 @@
     power_ref[...] = jnp.broadcast_to(total, power_ref.shape)
 
 
+def window(place_ref, gene_ref, power_ref, cross, power, half, samples):
+    core = place_ref[1]
+    start = gene_ref[:, 1:2].astype(jnp.int32)
+    valid = gene_ref[:, 2:3].astype(jnp.int32)
+    genes = cross.shape[0]
+    lane = lax.broadcasted_iota(jnp.int32, (genes, LANES), 1)
+    own_power = power_ref[...]
+    scale = jnp.sqrt(f32(samples))
+    variants = cross.shape[1]
+    blocks = variants // LANES
+    offset = start + half * LANES - core * variants
+    block = offset >> 7
+    shift = offset & (LANES - 1)
+    need = block + (lane < shift).astype(jnp.int32)
+    products = [jnp.zeros((genes, LANES), f32)] * 2
+    for b in range(blocks):
+        here = need == b
+        parts = [array[:, b * LANES : (b + 1) * LANES] for array in (cross, power)]
+        products = [jnp.where(here, part, product) for part, product in zip(parts, products)]
+    inside = (need >= 0) & (need < blocks)
+    score = jnp.where(inside, scale * products[0] / jnp.sqrt(products[1] * own_power), 0.0)
+    score = jnp.take_along_axis(score, (lane + shift) & (LANES - 1), axis=1)
+    return jnp.where(lane + half * LANES < valid, score, 0.0)
+
+
 def score_kernel(place_ref, gene_ref, power_ref, turned_ref, turned2_ref, weighted_ref, low_ref, *refs):
-    *dose_refs, keep_ref, pass_ref, dose_scr = refs
+    *dose_refs, cross_ref, product_ref, pass_ref, dose_scr = refs
     samples, variants = dose_refs[0].shape
     chunks = [(ref, at) for ref in dose_refs for at in range(0, ref.shape[1], variants)]
     order = [0, 1, 3, 2, 4, 5, 7, 6]
@@ -279,28 +306,15 @@
     squared = jnp.square(rotated.astype(f32)).astype(bf16)
     cross = jnp.dot(weighted_ref[...], rotated, preferred_element_type=f32)
     power = jnp.dot(low_ref[...], squared, preferred_element_type=f32)
-    core = place_ref[1]
-    start = gene_ref[:, 1:2].astype(jnp.int32)
-    valid = gene_ref[:, 2:3].astype(jnp.int32)
-    genes = cross.shape[0]
-    lane = lax.broadcasted_iota(jnp.int32, (genes, LANES), 1)
-    own_power = power_ref[...]
-    scale = jnp.sqrt(f32(dose_scr.shape[0]))
-    blocks = variants // LANES
-    for out_ref, half in ((keep_ref, core), (pass_ref, 1 - core)):
-        offset = start + half * LANES - core * variants
-        block = offset >> 7
-        shift = offset & (LANES - 1)
-        need = block + (lane < shift).astype(jnp.int32)
-        products = [jnp.zeros((genes, LANES), f32)] * 2
-        for b in range(blocks):
-            here = need == b
-            parts = [array[:, b * LANES : (b + 1) * LANES] for array in (cross, power)]
-            products = [jnp.where(here, part, product) for part, product in zip(parts, products)]
-        inside = (need >= 0) & (need < blocks)
-        score = jnp.where(inside, scale * products[0] / jnp.sqrt(products[1] * own_power), 0.0)
-        score = jnp.take_along_axis(score, (lane + shift) & (LANES - 1), axis=1)
-        out_ref[...] = jnp.where(lane + half * LANES < valid, score, 0.0)
+    cross_ref[...] = cross
+    product_ref[...] = power
+    pass_ref[...] = window(place_ref, gene_ref, power_ref, cross, power, 1 - place_ref[1], dose_scr.shape[0])
+
+
+def keep_kernel(place_ref, gene_ref, power_ref, cross_ref, product_ref, keep_ref, *, samples):
+    keep_ref[...] = window(
+        place_ref, gene_ref, power_ref, cross_ref[...], product_ref[...], place_ref[1], samples
+    )
 
 
 def call(kernel, outs, count, scratch=(), smem=1, anywhere=0, limit=VMEM_LIMIT):
@@ -375,8 +389,8 @@
     d37 = swap(jnp.concatenate([d2, d6], axis=1), 1)
     width = 4 * half + 2 * LANES
     out, kept = call(
-        third_kernel, [((panel, width), bf16), ((panel, width + half), bf16)], 7, smem=0, anywhere=1
-    )(ahead, r1, r4, e2, e0, terms, far)
+        third_kernel, [((panel, width), bf16), ((panel, width + half), bf16)], 8, smem=0, anywhere=2
+    )(ahead, r1, r4, e2, e0, terms, far, d2)
     kept2 = other_core(kept)
     near = swap(out, 2)
     near2 = other_core(near)
@@ -394,12 +408,15 @@
         7,
         scratch=[pltpu.VMEM((samples // 2, LANES), bf16)],
     )(place, kept, kept2, near, near2, share, gene)
-    keep, passed = call(
+    cross, product, passed = call(
         score_kernel,
-        [((LANES, LANES), f32)] * 2,
+        [((LANES, variants), f32)] * 2 + [((LANES, LANES), f32)],
         13,
         scratch=[pltpu.VMEM((samples, variants), bf16)],
     )(place, gene, power, turned, turned2, weighted, low, d0, d15, d4, d2, d37, d6)
+    keep = call(functools.partial(keep_kernel, samples=samples), [((LANES, LANES), f32)], 5)(
+        place, gene, power, cross, product
+    )[0]
     return keep + other_core(passed)
 
 

time: 29.2 us -> 29 us (level)
  waiting for transfers between devices: 8.18 us -> 6.48 us
  starting transfers between devices: 13.6 us -> 14.5 us
  Pallas kernels: 5.64 us -> 6.33 us
    ppermute x8, waiting for transfers between devices: 6.62 us -> 5.7 us  [swap(): return lax.ppermute(x, 'row', [(i, i ^ m) for i in range(rows)])]
    ppermute x8, starting transfers between devices: 13.3 us -> 14.2 us  [swap(): return lax.ppermute(x, 'row', [(i, i ^ m) for i in range(rows)])]
    ppermute x3, waiting for transfers between devices: 1.56 us -> 0.78 us  [other_core(): return lax.ppermute(x, 'col', [(0, 1), (1, 0)])]
    pallas_call x1 -> x2, Pallas kernels: 1.72 us -> 2.42 us  [the longest x1 1.64 us: near_body(): call(score_kernel, [((LANES, variants), f32)] * 2 + [((LANES, LANES), f32...]
  transfers between devices with their start and end apart: 11 -> 11, of which waited for: 5 -> 6; matrix products, arithmetic and copies ran while one was open for 0% -> 0% of each run, Pallas kernels for 8% -> 10%
where the time goes in v13:
time: 29 us; the launch traced here: 28.8 us
  starting transfers between devices  14.5 us (50%)
  waiting for transfers between devices  6.48 us (22%)
  Pallas kernels  6.33 us (22%)
  other arithmetic  0.73 us (3%)
  local copies, waits for them, and re-layouts  0.71 us (2%)
    ppermute x8, starting transfers between devices, swap(): return lax.ppermute(x, 'row', [(i, i ^ m) for i in range(rows)])  14.2 us
    ppermute x8, waiting for transfers between devices, swap(): return lax.ppermute(x, 'row', [(i, i ^ m) for i in range(rows)])  5.7 us
    pallas_call x1, Pallas kernels, near_body(): call(route_kernel, [((panel, half + 2 * LANES), bf16), ((part, 2 * LANES)...  1.73 us
    pallas_call x1, Pallas kernels, near_body(): call(score_kernel, [((LANES, variants), f32)] * 2 + [((LANES, LANES), f32...  1.64 us
    pallas_call x1, Pallas kernels, near_body(): call(weight_kernel, [shape, ((LANES, 2 * half), bf16), ((LANES, 2 * half)...  1.08 us
    pallas_call x1, Pallas kernels, near_body(): call(half_kernel, [shape, ((LANES, 2 * half), f32)], 4, scratch=[pltpu.VM...  0.93 us
    ppermute x3, waiting for transfers between devices, other_core(): return lax.ppermute(x, 'col', [(0, 1), (1, 0)])  0.78 us
    pallas_call x1, Pallas kernels, near_body(): call(functools.partial(keep_kernel, samples=samples), [((LANES, LANES), f...  0.78 us
  transfers between devices with their start and end apart: 11, of which 6 were waited for; matrix products, arithmetic and copies ran while one was open for 0% of the time, Pallas kernels for 10%

profile of v13, /device:TPU:0, one launch (start us, length us, event | category | flops | bytes accessed | tf_op | source)
XLA Modules:
  0.0 28.8 jit_solution(7865774210477077337)
XLA Ops:
  0.0 0.1 pad_add_fusion.place_ref
  0.1 1.7 %shard_map.82 = (bf16[64,512]{1,0:T(8,128)(2,1)S(1)}, bf16[32,256]{1,0:T(8,128)(2,1)S(1)}, bf16[32,128]{1,0:T(8,128)(2,1)S(1)}, bf16[32,128]{1,0:T(8,128)(2,1)S(...) custom-call(s32[2]{0:T(128)S(1)} %pad_add_fusion.place_ref, s32[8,128]{1,0:T(8,128)} %bitcast.11, ...), custom_call_target="tpu_custom_call" | custom-call | tf_op jit(solution)/shard_map/pallas_call | solution.py:348
  1.8 4.1 %collective-permute-start.2 = (bf16[64,768]{1,0:T(8,128)(2,1)S(1)}, bf16[64,768]{1,0:T(8,128)(2,1)S(1)}, u32[]{:S(2)}, u32[]{:S(2)}) collective-permute-start(bf16[64,768]{1,0:T(8,128)(2,1)S(1)} %get-tuple-element.33.d0_ref.refs_0_), channel_id=1, source_target_pairs={{0,8},{2,10},{4,12},{6,14},{8,0},{10,2},{12,4},{14,6},{1,9},{3,11}... | collective-permute-start | bytes 294920 | tf_op jit(solution)/shard_map/ppermute | solution.py:343
  5.9 1.5 %collective-permute-start = (bf16[64,512]{1,0:T(8,128)(2,1)S(1)}, bf16[64,512]{1,0:T(8,128)(2,1)S(1)}, u32[]{:S(2)}, u32[]{:S(2)}) collective-permute-start(bf16[64,512]{1,0:T(8,128)(2,1)S(1)} %get-tuple-element.28.ahead_ref), channel_id=1, source_target_pairs={{0,2},{2,0},{4,6},{6,4},{8,10},{10,8},{12,14},{14,12},{1,3},{3,1},... | collective-permute-start | bytes 196616 | tf_op jit(solution)/shard_map/ppermute | solution.py:343
  7.4 1.6 %collective-permute-start.3 = (bf16[64,768]{1,0:T(8,128)(2,1)S(1)}, bf16[64,768]{1,0:T(8,128)(2,1)S(1)}, u32[]{:S(2)}, u32[]{:S(2)}) collective-permute-start(bf16[64,768]{1,0:T(8,128)(2,1)S(1)} %get-tuple-element.33.d0_ref.refs_0_), channel_id=1, source_target_pairs={{0,4},{2,6},{4,0},{6,2},{8,12},{10,14},{12,8},{14,10},{1,5},{3,7},... | collective-permute-start | bytes 294920 | tf_op jit(solution)/shard_map/ppermute | solution.py:343
  9.0 1.2 %collective-permute-done.r1_ref = bf16[64,512]{1,0:T(8,128)(2,1)S(1)} collective-permute-done((bf16[64,512]{1,0:T(8,128)(2,1)S(1)}, bf16[64,512]{1,0:T(8,128)(2,1)S(1)}, u32[]{:S(2)}, u32[]{:S(2)}) %collective-permute-start) | collective-permute-done | bytes 65568 | tf_op jit(solution)/shard_map/ppermute | solution.py:343
  10.2 0.1 collective-permute-start.1
  10.3 0.6 %collective-permute-done.2.d4_ref.refs_2_ = bf16[64,768]{1,0:T(8,128)(2,1)S(1)} collective-permute-done((bf16[64,768]{1,0:T(8,128)(2,1)S(1)}, bf16[64,768]{1,0:T(8,128)(2,1)S(1)}, u32[]{:S(2)}, u32[]{:S(2)}) %collective-permute-start.2) | collective-permute-done | bytes 98336 | tf_op jit(solution)/shard_map/ppermute | solution.py:343
  10.9 1.8 %collective-permute-start.8 = (bf16[64,768]{1,0:T(8,128)(2,1)S(1)}, bf16[64,768]{1,0:T(8,128)(2,1)S(1)}, u32[]{:S(2)}, u32[]{:S(2)}) collective-permute-start(bf16[64,768]{1,0:T(8,128)(2,1)S(1)} %get-tuple-element.34.far_any), channel_id=1, source_target_pairs={{0,4},{2,6},{4,0},{6,2},{8,12},{10,14},{12,8},{14,10},{1,5},{3,7},... | collective-permute-start | bytes 294920 | tf_op jit(solution)/shard_map/ppermute | solution.py:343
  12.8 0.7 %copy-done.1 = s32[1024]{0:T(1024)S(1)} copy-done((s32[1024]{0:T(1024)S(1)}, s32[1024]{0:T(1024)}, u32[]{:S(2)}) %copy-start.1) | copy-done | bytes 4120
  13.5 0.1 shard_map.83
  13.6 1.1 %collective-permute-start.7 = (bf16[64,1536]{1,0:T(8,128)(2,1)S(1)}, bf16[64,1536]{1,0:T(8,128)(2,1)S(1)}, u32[]{:S(2)}, u32[]{:S(2)}) collective-permute-start(bf16[64,1536]{1,0:T(8,128)(2,1)S(1)} %get-tuple-element.37), channel_id=1, source_target_pairs={{0,2},{2,0},{4,6},{6,4},{8,10},{10,8},{12,14},{14,12},{1,3},{3,1},... | collective-permute-start | bytes 589832 | tf_op jit(solution)/shard_map/ppermute | solution.py:343
  14.7 1.2 %collective-permute-done.1.r4_ref = bf16[64,768]{1,0:T(8,128)(2,1)S(1)} collective-permute-done((bf16[64,768]{1,0:T(8,128)(2,1)S(1)}, bf16[64,768]{1,0:T(8,128)(2,1)S(1)}, u32[]{:S(2)}, u32[]{:S(2)}) %collective-permute-start.1) | collective-permute-done | bytes 98336 | tf_op jit(solution)/shard_map/ppermute | solution.py:343
  16.0 1.9 %collective-permute-start.5 = (bf16[64,1280]{1,0:T(8,128)(2,1)S(1)}, bf16[64,1280]{1,0:T(8,128)(2,1)S(1)}, u32[]{:S(2)}, u32[]{:S(2)}) collective-permute-start(bf16[64,1280]{1,0:T(8,128)(2,1)S(1)} %get-tuple-element.36), channel_id=1, source_target_pairs={{0,4},{2,6},{4,0},{6,2},{8,12},{10,14},{12,8},{14,10},{1,5},{3,7},... | collective-permute-start | bytes 491528 | tf_op jit(solution)/shard_map/ppermute | solution.py:343
  18.0 2.0 %collective-permute-start.9 = (bf16[64,1536]{1,0:T(8,128)(2,1)S(1)}, bf16[64,1536]{1,0:T(8,128)(2,1)S(1)}, u32[]{:S(2)}, u32[]{:S(2)}) collective-permute-start(bf16[64,1536]{1,0:T(8,128)(2,1)S(1)} %pad_maximum_fusion), channel_id=1, source_target_pairs={{0,2},{2,0},{4,6},{6,4},{8,10},{10,8},{12,14},{14,12},{1,3},{3,1},... | collective-permute-start | bytes 589832 | tf_op jit(solution)/shard_map/ppermute | solution.py:343
  20.0 2.7 %collective-permute-done.5.mine_ref = bf16[64,1280]{1,0:T(8,128)(2,1)S(1)} collective-permute-done((bf16[64,1280]{1,0:T(8,128)(2,1)S(1)}, bf16[64,1280]{1,0:T(8,128)(2,1)S(1)}, u32[]{:S(2)}, u32[]{:S(2)}) %collective-permute-start.5) | collective-permute-done | bytes 163872 | tf_op jit(solution)/shard_map/ppermute | solution.py:343
  22.7 0.9 %shard_map.87 = (bf16[512,256]{1,0:T(8,128)(2,1)S(1)}, f32[128,512]{1,0:T(8,128)S(1)}) custom-call(s32[2]{0:T(128)S(1)} %pad_add_fusion.place_ref, bf16[64,1536]{1,0:T(8,128)(2,1)S(1)} %get-tuple-element.35.mine_ref.kept_ref, bf16[64,1536]{1,0:T(8,128)(2,1)S(1)} %collective-permute-done.4.other_ref.kept2_ref, ...), custom_call_target="tpu_custom_call" | custom-call | tf_op jit(solution)/shard_map/pallas_call | solution.py:398
  23.7 0.4 %collective-permute-done.6.other_ref = bf16[64,1280]{1,0:T(8,128)(2,1)S(1)} collective-permute-done((bf16[64,1280]{1,0:T(8,128)(2,1)S(1)}, bf16[64,1280]{1,0:T(8,128)(2,1)S(1)}, u32[]{:S(2)}, u32[]{:S(2)}) %collective-permute-start.6) | collective-permute-done | bytes 163872 | tf_op jit(solution)/shard_map/ppermute | solution.py:346
  24.1 1.1 %shard_map.88 = (bf16[512,256]{1,0:T(8,128)(2,1)S(1)}, bf16[128,512]{1,0:T(8,128)(2,1)S(1)}, bf16[128,512]{1,0:T(8,128)(2,1)S(1)}, f32[128,128]{1,0:T(8,128)S(1)}) custom-call(s32[2]{0:T(128)S(1)} %pad_add_fusion.place_ref, bf16[64,1536]{1,0:T(8,128)(2,1)S(1)} %get-tuple-element.35.mine_ref.kept_ref, ...), custom_call_target="tpu_custom_call" | custom-call | tf_op jit(solution)/shard_map/pallas_call | solution.py:405
  25.2 1.6 %shard_map.89 = (f32[128,768]{1,0:T(8,128)S(1)}, f32[128,768]{1,0:T(8,128)S(1)}, f32[128,128]{1,0:T(8,128)S(1)}) custom-call(s32[2]{0:T(128)S(1)} %pad_add_fusion.place_ref, f32[128,128]{1,0:T(8,128)S(1)} %get-tuple-element.27.gene_ref, f32[128,128]{1,0:T(8,128)S(1)} %get-tuple-element.39.power_ref, bf16[512,256]{1,0:T(8,128)(2,1)S(1)} %get-tuple-element.40.turned_ref, ...), custom_call_target="tpu_custom_call" | custom-call | tf_op jit(solution)/shard_map/pallas_call | solution.py:411
  26.9 0.2 collective-permute-start.10
  27.1 0.8 %shard_map.90 = f32[128,128]{1,0:T(8,128)S(1)} custom-call(s32[2]{0:T(128)S(1)} %pad_add_fusion.place_ref, f32[128,128]{1,0:T(8,128)S(1)} %get-tuple-element.27.gene_ref, f32[128,128]{1,0:T(8,128)S(1)} %get-tuple-element.39.power_ref, f32[128,768]{1,0:T(8,128)S(1)} %get-tuple-element.44.cross_ref, f32[128,768]{1,0:T(8,128)S(1)} %get-tuple-element.45.product_ref), custom_call_target="tpu_custom_call" | custom-call | tf_op jit(solution)/shard_map/pallas_call | solution.py:417
  27.9 0.3 %collective-permute-done.10 = f32[128,128]{1,0:T(8,128)S(1)} collective-permute-done((f32[128,128]{1,0:T(8,128)S(1)}, f32[128,128]{1,0:T(8,128)S(1)}, u32[]{:S(2)}, u32[]{:S(2)}) %collective-permute-start.10) | collective-permute-done | bytes 65568 | tf_op jit(solution)/shard_map/ppermute | solution.py:346
  28.2 0.6 %add.3 = f32[128,128]{1,0:T(8,128)} add(f32[128,128]{1,0:T(8,128)S(1)} %shard_map.90, f32[128,128]{1,0:T(8,128)S(1)} %collective-permute-done.10) | non-fusion elementwise | flops 16384 | bytes 196608 | tf_op jit(solution)/shard_map/add | solution.py:420
  (18 shorter events, 0.2 us)
Async XLA Ops:
  1.8 9.1 %collective-permute-start.2 = (bf16[64,768]{1,0:T(8,128)(2,1)S(1)}, bf16[64,768]{1,0:T(8,128)(2,1)S(1)}, u32[]{:S(2)}, u32[]{:S(2)}) collective-permute-start(bf16[64,768]{1,0:T(8,128)(2,1)S(1)} %get-tuple-element.33.d0_ref.refs_0_), channel_id=1, source_target_pairs={{0,8},{2,10},{4,12},{6,14},{8,0},{10,2},{12,4},{14,6},{1,9},{3,11}... | collective-permute-start | bytes 294920 | tf_op jit(solution)/shard_map/ppermute | solution.py:343
  5.9 4.3 %collective-permute-start = (bf16[64,512]{1,0:T(8,128)(2,1)S(1)}, bf16[64,512]{1,0:T(8,128)(2,1)S(1)}, u32[]{:S(2)}, u32[]{:S(2)}) collective-permute-start(bf16[64,512]{1,0:T(8,128)(2,1)S(1)} %get-tuple-element.28.ahead_ref), channel_id=1, source_target_pairs={{0,2},{2,0},{4,6},{6,4},{8,10},{10,8},{12,14},{14,12},{1,3},{3,1},... | collective-permute-start | bytes 196616 | tf_op jit(solution)/shard_map/ppermute | solution.py:343
  7.4 7.3 %collective-permute-start.3 = (bf16[64,768]{1,0:T(8,128)(2,1)S(1)}, bf16[64,768]{1,0:T(8,128)(2,1)S(1)}, u32[]{:S(2)}, u32[]{:S(2)}) collective-permute-start(bf16[64,768]{1,0:T(8,128)(2,1)S(1)} %get-tuple-element.33.d0_ref.refs_0_), channel_id=1, source_target_pairs={{0,4},{2,6},{4,0},{6,2},{8,12},{10,14},{12,8},{14,10},{1,5},{3,7},... | collective-permute-start | bytes 294920 | tf_op jit(solution)/shard_map/ppermute | solution.py:343
  10.2 5.7 %collective-permute-start.1 = (bf16[64,768]{1,0:T(8,128)(2,1)S(1)}, bf16[64,768]{1,0:T(8,128)(2,1)S(1)}, u32[]{:S(2)}, u32[]{:S(2)}) collective-permute-start(bf16[64,768]{1,0:T(8,128)(2,1)S(1)} %shard_map.84.after_any), channel_id=1, source_target_pairs={{0,8},{2,10},{4,12},{6,14},{8,0},{10,2},{12,4},{14,6},{1,9},{3,11}... | collective-permute-start | bytes 294920 | tf_op jit(solution)/shard_map/ppermute | solution.py:343
  10.9 1.9 %copy-start.2 = (s32[1024]{0:T(1024)S(1)}, s32[1024]{0:T(1024)}, u32[]{:S(2)}) copy-start(s32[1024]{0:T(1024)} %param.14) | copy-start | bytes 12292
  10.9 7.0 %collective-permute-start.8 = (bf16[64,768]{1,0:T(8,128)(2,1)S(1)}, bf16[64,768]{1,0:T(8,128)(2,1)S(1)}, u32[]{:S(2)}, u32[]{:S(2)}) collective-permute-start(bf16[64,768]{1,0:T(8,128)(2,1)S(1)} %get-tuple-element.34.far_any), channel_id=1, source_target_pairs={{0,4},{2,6},{4,0},{6,2},{8,12},{10,14},{12,8},{14,10},{1,5},{3,7},... | collective-permute-start | bytes 294920 | tf_op jit(solution)/shard_map/ppermute | solution.py:343
  12.8 0.7 %copy-start.1 = (s32[1024]{0:T(1024)S(1)}, s32[1024]{0:T(1024)}, u32[]{:S(2)}) copy-start(s32[1024]{0:T(1024)} %param.13) | copy-start | bytes 12292
  12.8 0.7 %copy-start = (f32[1024]{0:T(1024)S(1)}, f32[1024]{0:T(1024)}, u32[]{:S(2)}) copy-start(f32[1024]{0:T(1024)} %param.12) | copy-start | bytes 12292
  12.8 0.7 %copy-start.3 = (f32[256]{0:T(256)S(1)}, f32[256]{0:T(256)}, u32[]{:S(2)}) copy-start(f32[256]{0:T(256)} %param.9) | copy-start | bytes 3076
  13.6 9.1 %collective-permute-start.7 = (bf16[64,1536]{1,0:T(8,128)(2,1)S(1)}, bf16[64,1536]{1,0:T(8,128)(2,1)S(1)}, u32[]{:S(2)}, u32[]{:S(2)}) collective-permute-start(bf16[64,1536]{1,0:T(8,128)(2,1)S(1)} %get-tuple-element.37), channel_id=1, source_target_pairs={{0,2},{2,0},{4,6},{6,4},{8,10},{10,8},{12,14},{14,12},{1,3},{3,1},... | collective-permute-start | bytes 589832 | tf_op jit(solution)/shard_map/ppermute | solution.py:343
  15.9 6.8 %collective-permute-start.4 = (bf16[64,1536]{1,0:T(8,128)(2,1)S(1)}, bf16[64,1536]{1,0:T(8,128)(2,1)S(1)}, u32[]{:S(2)}, u32[]{:S(2)}) collective-permute-start(bf16[64,1536]{1,0:T(8,128)(2,1)S(1)} %get-tuple-element.35.mine_ref.kept_ref), channel_id=1, source_target_pairs={{0,1},{1,0},{2,3},{3,2},{4,5},{5,4},{6,7},{7,6},{8,9},{9,8},{10,11... | collective-permute-start | bytes 589832 | tf_op jit(solution)/shard_map/ppermute | solution.py:346
  16.0 6.7 %collective-permute-start.5 = (bf16[64,1280]{1,0:T(8,128)(2,1)S(1)}, bf16[64,1280]{1,0:T(8,128)(2,1)S(1)}, u32[]{:S(2)}, u32[]{:S(2)}) collective-permute-start(bf16[64,1280]{1,0:T(8,128)(2,1)S(1)} %get-tuple-element.36), channel_id=1, source_target_pairs={{0,4},{2,6},{4,0},{6,2},{8,12},{10,14},{12,8},{14,10},{1,5},{3,7},... | collective-permute-start | bytes 491528 | tf_op jit(solution)/shard_map/ppermute | solution.py:343
  18.0 7.3 %collective-permute-start.9 = (bf16[64,1536]{1,0:T(8,128)(2,1)S(1)}, bf16[64,1536]{1,0:T(8,128)(2,1)S(1)}, u32[]{:S(2)}, u32[]{:S(2)}) collective-permute-start(bf16[64,1536]{1,0:T(8,128)(2,1)S(1)} %pad_maximum_fusion), channel_id=1, source_target_pairs={{0,2},{2,0},{4,6},{6,4},{8,10},{10,8},{12,14},{14,12},{1,3},{3,1},... | collective-permute-start | bytes 589832 | tf_op jit(solution)/shard_map/ppermute | solution.py:343
  22.7 1.4 %collective-permute-start.6 = (bf16[64,1280]{1,0:T(8,128)(2,1)S(1)}, bf16[64,1280]{1,0:T(8,128)(2,1)S(1)}, u32[]{:S(2)}, u32[]{:S(2)}) collective-permute-start(bf16[64,1280]{1,0:T(8,128)(2,1)S(1)} %collective-permute-done.5.mine_ref), channel_id=1, source_target_pairs={{0,1},{1,0},{2,3},{3,2},{4,5},{5,4},{6,7},{7,6},{8,9},{9,8},{10,11... | collective-permute-start | bytes 491528 | tf_op jit(solution)/shard_map/ppermute | solution.py:346
  26.9 1.3 %collective-permute-start.10 = (f32[128,128]{1,0:T(8,128)S(1)}, f32[128,128]{1,0:T(8,128)S(1)}, u32[]{:S(2)}, u32[]{:S(2)}) collective-permute-start(f32[128,128]{1,0:T(8,128)S(1)} %get-tuple-element.46), channel_id=1, source_target_pairs={{0,1},{1,0},{2,3},{3,2},{4,5},{5,4},{6,7},{7,6},{8,9},{9,8},{10,11... | collective-permute-start | bytes 196616 | tf_op jit(solution)/shard_map/ppermute | solution.py:346

commit v14 on v13

--- a/solution.py
+++ b/solution.py
@@ -191,11 +191,8 @@
     out_ref[part:, 2 * half :] = r1_ref[part:, half:]
 
 
-def copy_kernel(d0_ref, d4_ref, after_any, pair_ref, far_ref):
-    variants = d0_ref.shape[1]
-    pair_ref[:, :variants] = d0_ref[...]
-    pair_ref[:, variants:] = d4_ref[...]
-    far_ref[...] = d4_ref[...]
+def copy_kernel(dose_ref, after_any, out_ref):
+    out_ref[...] = dose_ref[...]
 
 
 def third_kernel(ahead_ref, r1_ref, r4_ref, e2_ref, e0_ref, terms_ref, far_any, d2_any, out_ref, kept_ref):
@@ -240,7 +237,7 @@
     return shares
 
 
-def half_kernel(place_ref, mine_ref, other_ref, d15_any, turned_ref, share_ref, data_scr):
+def half_kernel(place_ref, mine_ref, other_ref, d153_any, turned_ref, share_ref, data_scr):
     half = turned_ref.shape[0] // 2
     for c, share in enumerate(rotate(place_ref, (mine_ref, other_ref), turned_ref, data_scr)):
         share_ref[:, c * half : (c + 1) * half] = share
@@ -296,7 +293,7 @@
     *dose_refs, cross_ref, product_ref, pass_ref, dose_scr = refs
     samples, variants = dose_refs[0].shape
     chunks = [(ref, at) for ref in dose_refs for at in range(0, ref.shape[1], variants)]
-    order = [0, 1, 3, 2, 4, 5, 7, 6]
+    order = [0, 1, 4, 2, 5, 3, 6, 7]
     for m, (ref, at) in enumerate(chunks[i] for i in order):
         dose_scr[m * samples : (m + 1) * samples, :] = ref[:, at : at + variants]
     line = turned_ref.shape[1]
@@ -381,12 +378,10 @@
     d2 = swap(d0, 2)
     to4 = call(second_kernel, [((panel, 2 * half + 2 * LANES), bf16)], 3, smem=0)(ahead, r1, e46)[0]
     r4 = swap(to4, 4)
-    pair, far = call(
-        copy_kernel, [((panel, 2 * variants), bf16), ((panel, variants), bf16)], 3, smem=0, anywhere=1
-    )(d0, d4, to4)
+    far = call(copy_kernel, [((panel, variants), bf16)], 2, smem=0, anywhere=1)(d4, to4)[0]
     d6 = swap(far, 2)
-    d15 = swap(pair, 1)
-    d37 = swap(jnp.concatenate([d2, d6], axis=1), 1)
+    d153 = swap(jnp.concatenate([d0, d4, d2], axis=1), 1)
+    d7 = swap(d6, 1)
     width = 4 * half + 2 * LANES
     out, kept = call(
         third_kernel, [((panel, width), bf16), ((panel, width + half), bf16)], 8, smem=0, anywhere=2
@@ -401,7 +396,7 @@
         4,
         scratch=[pltpu.VMEM((samples // 2, LANES), bf16)],
         anywhere=1,
-    )(place, kept, kept2, d15)
+    )(place, kept, kept2, d153)
     turned2, weighted, low, power = call(
         weight_kernel,
         [shape, ((LANES, 2 * half), bf16), ((LANES, 2 * half), bf16), ((LANES, LANES), f32)],
@@ -413,7 +408,7 @@
         [((LANES, variants), f32)] * 2 + [((LANES, LANES), f32)],
         13,
         scratch=[pltpu.VMEM((samples, variants), bf16)],
-    )(place, gene, power, turned, turned2, weighted, low, d0, d15, d4, d2, d37, d6)
+    )(place, gene, power, turned, turned2, weighted, low, d0, d153, d4, d2, d6, d7)
     keep = call(functools.partial(keep_kernel, samples=samples), [((LANES, LANES), f32)], 5)(
         place, gene, power, cross, product
     )[0]

time: 29 us -> 32.6 us (1.12)
  waiting for transfers between devices: 6.48 us -> 13.1 us
  starting transfers between devices: 14.5 us -> 11.4 us
    ppermute x8, waiting for transfers between devices: 5.7 us -> 12.7 us  [swap(): return lax.ppermute(x, 'row', [(i, i ^ m) for i in range(rows)])]
    ppermute x8, starting transfers between devices: 14.2 us -> 11.3 us  [swap(): return lax.ppermute(x, 'row', [(i, i ^ m) for i in range(rows)])]
  transfers between devices with their start and end apart: 11 -> 11, of which waited for: 6 -> 7; matrix products, arithmetic and copies ran while one was open for 0% -> 0% of each run, Pallas kernels for 10% -> 9%
where the time goes in v14:
time: 32.6 us; the launch traced here: 32.4 us
  waiting for transfers between devices  13.1 us (40%)
  starting transfers between devices  11.4 us (35%)
  Pallas kernels  6.32 us (19%)
  other arithmetic  0.73 us (2%)
  local copies, waits for them, and re-layouts  0.71 us (2%)
    ppermute x8, waiting for transfers between devices, swap(): return lax.ppermute(x, 'row', [(i, i ^ m) for i in range(rows)])  12.7 us
    ppermute x8, starting transfers between devices, swap(): return lax.ppermute(x, 'row', [(i, i ^ m) for i in range(rows)])  11.3 us
    pallas_call x1, Pallas kernels, near_body(): call(route_kernel, [((panel, half + 2 * LANES), bf16), ((part, 2 * LANES)...  1.73 us
    pallas_call x1, Pallas kernels, near_body(): call(score_kernel, [((LANES, variants), f32)] * 2 + [((LANES, LANES), f32...  1.64 us
    pallas_call x1, Pallas kernels, near_body(): call(weight_kernel, [shape, ((LANES, 2 * half), bf16), ((LANES, 2 * half)...  1.08 us
    pallas_call x1, Pallas kernels, near_body(): call(half_kernel, [shape, ((LANES, 2 * half), f32)], 4, scratch=[pltpu.VM...  0.93 us
    pallas_call x1, Pallas kernels, near_body(): call(functools.partial(keep_kernel, samples=samples), [((LANES, LANES), f...  0.78 us
    unnamed x8, local copies, waits for them, and re-layouts  0.71 us
  transfers between devices with their start and end apart: 11, of which 7 were waited for; matrix products, arithmetic and copies ran while one was open for 0% of the time, Pallas kernels for 9%

profile of v14, /device:TPU:0, one launch (start us, length us, event | category | flops | bytes accessed | tf_op | source)
XLA Modules:
  0.0 32.4 jit_solution(11851503474038632274)
XLA Ops:
  0.0 0.1 pad_add_fusion.place_ref
  0.1 1.7 %shard_map.82 = (bf16[64,512]{1,0:T(8,128)(2,1)S(1)}, bf16[32,256]{1,0:T(8,128)(2,1)S(1)}, bf16[32,128]{1,0:T(8,128)(2,1)S(1)}, bf16[32,128]{1,0:T(8,128)(2,1)S(...) custom-call(s32[2]{0:T(128)S(1)} %pad_add_fusion.place_ref, s32[8,128]{1,0:T(8,128)} %bitcast.11, ...), custom_call_target="tpu_custom_call" | custom-call | tf_op jit(solution)/shard_map/pallas_call | solution.py:345
  1.8 3.0 %collective-permute-start = (bf16[64,512]{1,0:T(8,128)(2,1)S(1)}, bf16[64,512]{1,0:T(8,128)(2,1)S(1)}, u32[]{:S(2)}, u32[]{:S(2)}) collective-permute-start(bf16[64,512]{1,0:T(8,128)(2,1)S(1)} %get-tuple-element.26.ahead_ref), channel_id=1, source_target_pairs={{0,2},{2,0},{4,6},{6,4},{8,10},{10,8},{12,14},{14,12},{1,3},{3,1},... | collective-permute-start | bytes 196616 | tf_op jit(solution)/shard_map/ppermute | solution.py:340
  4.8 2.6 %collective-permute-start.2 = (bf16[64,768]{1,0:T(8,128)(2,1)S(1)}, bf16[64,768]{1,0:T(8,128)(2,1)S(1)}, u32[]{:S(2)}, u32[]{:S(2)}) collective-permute-start(bf16[64,768]{1,0:T(8,128)(2,1)S(1)} %get-tuple-element.31.refs_0_), channel_id=1, source_target_pairs={{0,8},{2,10},{4,12},{6,14},{8,0},{10,2},{12,4},{14,6},{1,9},{3,11}... | collective-permute-start | bytes 294920 | tf_op jit(solution)/shard_map/ppermute | solution.py:340
  7.4 1.6 %collective-permute-start.3 = (bf16[64,768]{1,0:T(8,128)(2,1)S(1)}, bf16[64,768]{1,0:T(8,128)(2,1)S(1)}, u32[]{:S(2)}, u32[]{:S(2)}) collective-permute-start(bf16[64,768]{1,0:T(8,128)(2,1)S(1)} %get-tuple-element.31.refs_0_), channel_id=1, source_target_pairs={{0,4},{2,6},{4,0},{6,2},{8,12},{10,14},{12,8},{14,10},{1,5},{3,7},... | collective-permute-start | bytes 294920 | tf_op jit(solution)/shard_map/ppermute | solution.py:340
  9.0 1.2 %collective-permute-start.1 = (bf16[64,768]{1,0:T(8,128)(2,1)S(1)}, bf16[64,768]{1,0:T(8,128)(2,1)S(1)}, u32[]{:S(2)}, u32[]{:S(2)}) collective-permute-start(bf16[64,768]{1,0:T(8,128)(2,1)S(1)} %shard_map.84.after_any), channel_id=1, source_target_pairs={{0,8},{2,10},{4,12},{6,14},{8,0},{10,2},{12,4},{14,6},{1,9},{3,11}... | collective-permute-start | bytes 294920 | tf_op jit(solution)/shard_map/ppermute | solution.py:340
  10.3 0.7 %copy-done.1 = s32[1024]{0:T(1024)S(1)} copy-done((s32[1024]{0:T(1024)S(1)}, s32[1024]{0:T(1024)}, u32[]{:S(2)}) %copy-start.1) | copy-done | bytes 4120
  11.0 0.1 shard_map.83
  11.1 1.5 %collective-permute-done.2.dose_ref.refs_2_ = bf16[64,768]{1,0:T(8,128)(2,1)S(1)} collective-permute-done((bf16[64,768]{1,0:T(8,128)(2,1)S(1)}, bf16[64,768]{1,0:T(8,128)(2,1)S(1)}, u32[]{:S(2)}, u32[]{:S(2)}) %collective-permute-start.2) | collective-permute-done | bytes 98336 | tf_op jit(solution)/shard_map/ppermute | solution.py:340
  12.6 3.7 %collective-permute-done.1.r4_ref = bf16[64,768]{1,0:T(8,128)(2,1)S(1)} collective-permute-done((bf16[64,768]{1,0:T(8,128)(2,1)S(1)}, bf16[64,768]{1,0:T(8,128)(2,1)S(1)}, u32[]{:S(2)}, u32[]{:S(2)}) %collective-permute-start.1) | collective-permute-done | bytes 98336 | tf_op jit(solution)/shard_map/ppermute | solution.py:340
  16.4 0.7 %collective-permute-start.5 = (bf16[64,1280]{1,0:T(8,128)(2,1)S(1)}, bf16[64,1280]{1,0:T(8,128)(2,1)S(1)}, u32[]{:S(2)}, u32[]{:S(2)}) collective-permute-start(bf16[64,1280]{1,0:T(8,128)(2,1)S(1)} %get-tuple-element.33), channel_id=1, source_target_pairs={{0,4},{2,6},{4,0},{6,2},{8,12},{10,14},{12,8},{14,10},{1,5},{3,7},... | collective-permute-start | bytes 491528 | tf_op jit(solution)/shard_map/ppermute | solution.py:340
  17.1 0.6 %collective-permute-start.7 = (bf16[64,2304]{1,0:T(8,128)(2,1)S(1)}, bf16[64,2304]{1,0:T(8,128)(2,1)S(1)}, u32[]{:S(2)}, u32[]{:S(2)}) collective-permute-start(bf16[64,2304]{1,0:T(8,128)(2,1)S(1)} %pad_maximum_fusion), channel_id=1, source_target_pairs={{0,2},{2,0},{4,6},{6,4},{8,10},{10,8},{12,14},{14,12},{1,3},{3,1},... | collective-permute-start | bytes 884744 | tf_op jit(solution)/shard_map/ppermute | solution.py:340
  17.7 1.3 %collective-permute-start.8 = (bf16[64,768]{1,0:T(8,128)(2,1)S(1)}, bf16[64,768]{1,0:T(8,128)(2,1)S(1)}, u32[]{:S(2)}, u32[]{:S(2)}) collective-permute-start(bf16[64,768]{1,0:T(8,128)(2,1)S(1)} %shard_map.85.far_any), channel_id=1, source_target_pairs={{0,4},{2,6},{4,0},{6,2},{8,12},{10,14},{12,8},{14,10},{1,5},{3,7},... | collective-permute-start | bytes 294920 | tf_op jit(solution)/shard_map/ppermute | solution.py:340
  19.0 4.1 %collective-permute-done.5.mine_ref = bf16[64,1280]{1,0:T(8,128)(2,1)S(1)} collective-permute-done((bf16[64,1280]{1,0:T(8,128)(2,1)S(1)}, bf16[64,1280]{1,0:T(8,128)(2,1)S(1)}, u32[]{:S(2)}, u32[]{:S(2)}) %collective-permute-start.5) | collective-permute-done | bytes 163872 | tf_op jit(solution)/shard_map/ppermute | solution.py:340
  23.1 1.0 %collective-permute-done.8.refs_4_ = bf16[64,768]{1,0:T(8,128)(2,1)S(1)} collective-permute-done((bf16[64,768]{1,0:T(8,128)(2,1)S(1)}, bf16[64,768]{1,0:T(8,128)(2,1)S(1)}, u32[]{:S(2)}, u32[]{:S(2)}) %collective-permute-start.8) | collective-permute-done | bytes 98336 | tf_op jit(solution)/shard_map/ppermute | solution.py:340
  24.2 0.3 collective-permute-start.9
  24.5 1.0 %collective-permute-done.7.d153_any.refs_1_ = bf16[64,2304]{1,0:T(8,128)(2,1)S(1)} collective-permute-done((bf16[64,2304]{1,0:T(8,128)(2,1)S(1)}, bf16[64,2304]{1,0:T(8,128)(2,1)S(1)}, u32[]{:S(2)}, u32[]{:S(2)}) %collective-permute-start.7) | collective-permute-done | bytes 294944 | tf_op jit(solution)/shard_map/ppermute | solution.py:340
  25.5 0.9 %shard_map.87 = (bf16[512,256]{1,0:T(8,128)(2,1)S(1)}, f32[128,512]{1,0:T(8,128)S(1)}) custom-call(s32[2]{0:T(128)S(1)} %pad_add_fusion.place_ref, bf16[64,1536]{1,0:T(8,128)(2,1)S(1)} %get-tuple-element.32.mine_ref.kept_ref, bf16[64,1536]{1,0:T(8,128)(2,1)S(1)} %collective-permute-done.4.other_ref.kept2_ref, ...), custom_call_target="tpu_custom_call" | custom-call | tf_op jit(solution)/shard_map/pallas_call | solution.py:393
  26.4 1.1 %shard_map.88 = (bf16[512,256]{1,0:T(8,128)(2,1)S(1)}, bf16[128,512]{1,0:T(8,128)(2,1)S(1)}, bf16[128,512]{1,0:T(8,128)(2,1)S(1)}, f32[128,128]{1,0:T(8,128)S(1)}) custom-call(s32[2]{0:T(128)S(1)} %pad_add_fusion.place_ref, bf16[64,1536]{1,0:T(8,128)(2,1)S(1)} %get-tuple-element.32.mine_ref.kept_ref, ...), custom_call_target="tpu_custom_call" | custom-call | tf_op jit(solution)/shard_map/pallas_call | solution.py:400
  27.5 1.3 %collective-permute-done.9.refs_5_ = bf16[64,768]{1,0:T(8,128)(2,1)S(1)} collective-permute-done((bf16[64,768]{1,0:T(8,128)(2,1)S(1)}, bf16[64,768]{1,0:T(8,128)(2,1)S(1)}, u32[]{:S(2)}, u32[]{:S(2)}) %collective-permute-start.9) | collective-permute-done | bytes 98336 | tf_op jit(solution)/shard_map/ppermute | solution.py:340
  28.8 1.6 %shard_map.89 = (f32[128,768]{1,0:T(8,128)S(1)}, f32[128,768]{1,0:T(8,128)S(1)}, f32[128,128]{1,0:T(8,128)S(1)}) custom-call(s32[2]{0:T(128)S(1)} %pad_add_fusion.place_ref, f32[128,128]{1,0:T(8,128)S(1)} %get-tuple-element.25.gene_ref, f32[128,128]{1,0:T(8,128)S(1)} %get-tuple-element.35.power_ref, bf16[512,256]{1,0:T(8,128)(2,1)S(1)} %get-tuple-element.36.turned_ref, ...), custom_call_target="tpu_custom_call" | custom-call | tf_op jit(solution)/shard_map/pallas_call | solution.py:406
  30.5 0.8 %shard_map.90 = f32[128,128]{1,0:T(8,128)S(1)} custom-call(s32[2]{0:T(128)S(1)} %pad_add_fusion.place_ref, f32[128,128]{1,0:T(8,128)S(1)} %get-tuple-element.25.gene_ref, f32[128,128]{1,0:T(8,128)S(1)} %get-tuple-element.35.power_ref, f32[128,768]{1,0:T(8,128)S(1)} %get-tuple-element.40.cross_ref, f32[128,768]{1,0:T(8,128)S(1)} %get-tuple-element.41.product_ref), custom_call_target="tpu_custom_call" | custom-call | tf_op jit(solution)/shard_map/pallas_call | solution.py:412
  31.3 0.5 %collective-permute-done.10 = f32[128,128]{1,0:T(8,128)S(1)} collective-permute-done((f32[128,128]{1,0:T(8,128)S(1)}, f32[128,128]{1,0:T(8,128)S(1)}, u32[]{:S(2)}, u32[]{:S(2)}) %collective-permute-start.10) | collective-permute-done | bytes 65568 | tf_op jit(solution)/shard_map/ppermute | solution.py:343
  31.8 0.6 %add.3 = f32[128,128]{1,0:T(8,128)} add(f32[128,128]{1,0:T(8,128)S(1)} %shard_map.90, f32[128,128]{1,0:T(8,128)S(1)} %collective-permute-done.10) | non-fusion elementwise | flops 16384 | bytes 196608 | tf_op jit(solution)/shard_map/add | solution.py:415
  (18 shorter events, 0.2 us)
Async XLA Ops:
  1.8 7.2 %collective-permute-start = (bf16[64,512]{1,0:T(8,128)(2,1)S(1)}, bf16[64,512]{1,0:T(8,128)(2,1)S(1)}, u32[]{:S(2)}, u32[]{:S(2)}) collective-permute-start(bf16[64,512]{1,0:T(8,128)(2,1)S(1)} %get-tuple-element.26.ahead_ref), channel_id=1, source_target_pairs={{0,2},{2,0},{4,6},{6,4},{8,10},{10,8},{12,14},{14,12},{1,3},{3,1},... | collective-permute-start | bytes 196616 | tf_op jit(solution)/shard_map/ppermute | solution.py:340
  4.8 7.7 %collective-permute-start.2 = (bf16[64,768]{1,0:T(8,128)(2,1)S(1)}, bf16[64,768]{1,0:T(8,128)(2,1)S(1)}, u32[]{:S(2)}, u32[]{:S(2)}) collective-permute-start(bf16[64,768]{1,0:T(8,128)(2,1)S(1)} %get-tuple-element.31.refs_0_), channel_id=1, source_target_pairs={{0,8},{2,10},{4,12},{6,14},{8,0},{10,2},{12,4},{14,6},{1,9},{3,11}... | collective-permute-start | bytes 294920 | tf_op jit(solution)/shard_map/ppermute | solution.py:340
  7.4 5.2 %collective-permute-start.3 = (bf16[64,768]{1,0:T(8,128)(2,1)S(1)}, bf16[64,768]{1,0:T(8,128)(2,1)S(1)}, u32[]{:S(2)}, u32[]{:S(2)}) collective-permute-start(bf16[64,768]{1,0:T(8,128)(2,1)S(1)} %get-tuple-element.31.refs_0_), channel_id=1, source_target_pairs={{0,4},{2,6},{4,0},{6,2},{8,12},{10,14},{12,8},{14,10},{1,5},{3,7},... | collective-permute-start | bytes 294920 | tf_op jit(solution)/shard_map/ppermute | solution.py:340
  9.0 1.3 %copy-start.2 = (s32[1024]{0:T(1024)S(1)}, s32[1024]{0:T(1024)}, u32[]{:S(2)}) copy-start(s32[1024]{0:T(1024)} %param.14) | copy-start | bytes 12292
  9.0 7.3 %collective-permute-start.1 = (bf16[64,768]{1,0:T(8,128)(2,1)S(1)}, bf16[64,768]{1,0:T(8,128)(2,1)S(1)}, u32[]{:S(2)}, u32[]{:S(2)}) collective-permute-start(bf16[64,768]{1,0:T(8,128)(2,1)S(1)} %shard_map.84.after_any), channel_id=1, source_target_pairs={{0,8},{2,10},{4,12},{6,14},{8,0},{10,2},{12,4},{14,6},{1,9},{3,11}... | collective-permute-start | bytes 294920 | tf_op jit(solution)/shard_map/ppermute | solution.py:340
  10.3 0.7 %copy-start.1 = (s32[1024]{0:T(1024)S(1)}, s32[1024]{0:T(1024)}, u32[]{:S(2)}) copy-start(s32[1024]{0:T(1024)} %param.13) | copy-start | bytes 12292
  10.3 0.7 %copy-start = (f32[1024]{0:T(1024)S(1)}, f32[1024]{0:T(1024)}, u32[]{:S(2)}) copy-start(f32[1024]{0:T(1024)} %param.12) | copy-start | bytes 12292
  10.3 0.7 %copy-start.3 = (f32[256]{0:T(256)S(1)}, f32[256]{0:T(256)}, u32[]{:S(2)}) copy-start(f32[256]{0:T(256)} %param.9) | copy-start | bytes 3076
  16.4 6.8 %collective-permute-start.5 = (bf16[64,1280]{1,0:T(8,128)(2,1)S(1)}, bf16[64,1280]{1,0:T(8,128)(2,1)S(1)}, u32[]{:S(2)}, u32[]{:S(2)}) collective-permute-start(bf16[64,1280]{1,0:T(8,128)(2,1)S(1)} %get-tuple-element.33), channel_id=1, source_target_pairs={{0,4},{2,6},{4,0},{6,2},{8,12},{10,14},{12,8},{14,10},{1,5},{3,7},... | collective-permute-start | bytes 491528 | tf_op jit(solution)/shard_map/ppermute | solution.py:340
  17.1 8.3 %collective-permute-start.7 = (bf16[64,2304]{1,0:T(8,128)(2,1)S(1)}, bf16[64,2304]{1,0:T(8,128)(2,1)S(1)}, u32[]{:S(2)}, u32[]{:S(2)}) collective-permute-start(bf16[64,2304]{1,0:T(8,128)(2,1)S(1)} %pad_maximum_fusion), channel_id=1, source_target_pairs={{0,2},{2,0},{4,6},{6,4},{8,10},{10,8},{12,14},{14,12},{1,3},{3,1},... | collective-permute-start | bytes 884744 | tf_op jit(solution)/shard_map/ppermute | solution.py:340
  17.7 6.8 %collective-permute-start.4 = (bf16[64,1536]{1,0:T(8,128)(2,1)S(1)}, bf16[64,1536]{1,0:T(8,128)(2,1)S(1)}, u32[]{:S(2)}, u32[]{:S(2)}) collective-permute-start(bf16[64,1536]{1,0:T(8,128)(2,1)S(1)} %get-tuple-element.32.mine_ref.kept_ref), channel_id=1, source_target_pairs={{0,1},{1,0},{2,3},{3,2},{4,5},{5,4},{6,7},{7,6},{8,9},{9,8},{10,11... | collective-permute-start | bytes 589832 | tf_op jit(solution)/shard_map/ppermute | solution.py:343
  17.7 6.5 %collective-permute-start.8 = (bf16[64,768]{1,0:T(8,128)(2,1)S(1)}, bf16[64,768]{1,0:T(8,128)(2,1)S(1)}, u32[]{:S(2)}, u32[]{:S(2)}) collective-permute-start(bf16[64,768]{1,0:T(8,128)(2,1)S(1)} %shard_map.85.far_any), channel_id=1, source_target_pairs={{0,4},{2,6},{4,0},{6,2},{8,12},{10,14},{12,8},{14,10},{1,5},{3,7},... | collective-permute-start | bytes 294920 | tf_op jit(solution)/shard_map/ppermute | solution.py:340
  23.1 3.3 %collective-permute-start.6 = (bf16[64,1280]{1,0:T(8,128)(2,1)S(1)}, bf16[64,1280]{1,0:T(8,128)(2,1)S(1)}, u32[]{:S(2)}, u32[]{:S(2)}) collective-permute-start(bf16[64,1280]{1,0:T(8,128)(2,1)S(1)} %collective-permute-done.5.mine_ref), channel_id=1, source_target_pairs={{0,1},{1,0},{2,3},{3,2},{4,5},{5,4},{6,7},{7,6},{8,9},{9,8},{10,11... | collective-permute-start | bytes 491528 | tf_op jit(solution)/shard_map/ppermute | solution.py:343
  24.2 4.6 %collective-permute-start.9 = (bf16[64,768]{1,0:T(8,128)(2,1)S(1)}, bf16[64,768]{1,0:T(8,128)(2,1)S(1)}, u32[]{:S(2)}, u32[]{:S(2)}) collective-permute-start(bf16[64,768]{1,0:T(8,128)(2,1)S(1)} %collective-permute-done.8.refs_4_), channel_id=1, source_target_pairs={{0,2},{2,0},{4,6},{6,4},{8,10},{10,8},{12,14},{14,12},{1,3},{3,1},... | collective-permute-start | bytes 294920 | tf_op jit(solution)/shard_map/ppermute | solution.py:340
  30.4 1.3 %collective-permute-start.10 = (f32[128,128]{1,0:T(8,128)S(1)}, f32[128,128]{1,0:T(8,128)S(1)}, u32[]{:S(2)}, u32[]{:S(2)}) collective-permute-start(f32[128,128]{1,0:T(8,128)S(1)} %get-tuple-element.42), channel_id=1, source_target_pairs={{0,1},{1,0},{2,3},{3,2},{4,5},{5,4},{6,7},{7,6},{8,9},{9,8},{10,11... | collective-permute-start | bytes 196616 | tf_op jit(solution)/shard_map/ppermute | solution.py:343

commit v15 on v10

--- a/solution.py
+++ b/solution.py
@@ -1,3 +1,5 @@
+import functools
+
 import jax
 import jax.numpy as jnp
 from jax import lax
@@ -8,7 +10,6 @@
 W = 256
 LANES = 128
 VMEM_LIMIT = 32 * 1024 * 1024
-ROUTE_LIMIT = 32 * 1024 * 1024
 NT = (((1,), (1,)), ((), ()))
 f32 = jnp.float32
 bf16 = jnp.bfloat16
@@ -193,7 +194,7 @@
     far_ref[...] = d4_ref[...]
 
 
-def third_kernel(ahead_ref, r1_ref, r4_ref, e2_ref, e0_ref, terms_ref, far_any, out_ref, kept_ref):
+def third_kernel(ahead_ref, r1_ref, r4_ref, e2_ref, e0_ref, terms_ref, far_any, d2_any, out_ref, kept_ref):
     half = terms_ref.shape[1]
     part = e0_ref.shape[0]
     for ref, own, at in ((out_ref, e2_ref, LANES), (kept_ref, e0_ref, 0)):
@@ -212,17 +213,19 @@
     kept_ref[terms:, width:] = jnp.zeros((kept_ref.shape[0] - terms, half), bf16)
 
 
-def rotate(place_ref, refs, turned_ref, data_scr):
+def rotate(place_ref, refs, turned_ref, data_scr, turned=(0, 1)):
     samples = refs[0].shape[0]
-    half = turned_ref.shape[0] // 2
+    half = turned_ref.shape[0] // len(turned)
     part = samples // 2
     core = place_ref[1]
     for c, ref in enumerate(refs):
         side = core if c == 0 else 1 - core
         for i in range(4):
-            turned_ref[c * half : (c + 1) * half, i * samples : (i + 1) * samples] = (
-                ref[:, i * half : (i + 1) * half].astype(f32).T.astype(bf16)
-            )
+            if c in turned:
+                at = turned.index(c) * half
+                turned_ref[at : at + half, i * samples : (i + 1) * samples] = (
+                    ref[:, i * half : (i + 1) * half].astype(f32).T.astype(bf16)
+                )
             at = 4 * half + i % 2 * LANES
             data_scr[pl.ds(pl.multiple_of(i * samples + side * part, part), part), :] = ref[
                 i // 2 * part : (i // 2 + 1) * part, at : at + LANES
@@ -235,6 +238,15 @@
     return shares
 
 
+def own_kernel(mine_ref, turned_ref):
+    samples = mine_ref.shape[0]
+    half = turned_ref.shape[0]
+    for i in range(4):
+        turned_ref[:, i * samples : (i + 1) * samples] = (
+            mine_ref[:, i * half : (i + 1) * half].astype(f32).T.astype(bf16)
+        )
+
+
 def half_kernel(place_ref, mine_ref, other_ref, d15_any, turned_ref, share_ref, data_scr):
     half = turned_ref.shape[0] // 2
     for c, share in enumerate(rotate(place_ref, (mine_ref, other_ref), turned_ref, data_scr)):
@@ -245,10 +257,10 @@
     place_ref, kept_ref, kept2_ref, mine_ref, other_ref, share_ref, gene_ref,
     turned_ref, weighted_ref, low_ref, power_ref, data_scr,
 ):
-    half = turned_ref.shape[0] // 2
+    half = turned_ref.shape[0]
     delta = gene_ref[:, 0:1]
     total = jnp.zeros((delta.shape[0], 1), f32)
-    shares = rotate(place_ref, (mine_ref, other_ref), turned_ref, data_scr)
+    shares = rotate(place_ref, (mine_ref, other_ref), turned_ref, data_scr, turned=(1,))
     width = mine_ref.shape[1]
     for c, (share, ref) in enumerate(zip(shares, (kept_ref, kept2_ref))):
         cols = slice(c * half, (c + 1) * half)
@@ -262,8 +274,33 @@
     power_ref[...] = jnp.broadcast_to(total, power_ref.shape)
 
 
-def score_kernel(place_ref, gene_ref, power_ref, turned_ref, turned2_ref, weighted_ref, low_ref, *refs):
-    *dose_refs, keep_ref, pass_ref, dose_scr = refs
+def window(place_ref, gene_ref, power_ref, cross, power, half, samples):
+    core = place_ref[1]
+    start = gene_ref[:, 1:2].astype(jnp.int32)
+    valid = gene_ref[:, 2:3].astype(jnp.int32)
+    genes = cross.shape[0]
+    lane = lax.broadcasted_iota(jnp.int32, (genes, LANES), 1)
+    own_power = power_ref[...]
+    scale = jnp.sqrt(f32(samples))
+    variants = cross.shape[1]
+    blocks = variants // LANES
+    offset = start + half * LANES - core * variants
+    block = offset >> 7
+    shift = offset & (LANES - 1)
+    need = block + (lane < shift).astype(jnp.int32)
+    products = [jnp.zeros((genes, LANES), f32)] * 2
+    for b in range(blocks):
+        here = need == b
+        parts = [array[:, b * LANES : (b + 1) * LANES] for array in (cross, power)]
+        products = [jnp.where(here, part, product) for part, product in zip(parts, products)]
+    inside = (need >= 0) & (need < blocks)
+    score = jnp.where(inside, scale * products[0] / jnp.sqrt(products[1] * own_power), 0.0)
+    score = jnp.take_along_axis(score, (lane + shift) & (LANES - 1), axis=1)
+    return jnp.where(lane + half * LANES < valid, score, 0.0)
+
+
+def score_kernel(place_ref, gene_ref, power_ref, turned_ref, own_ref, other_ref, weighted_ref, low_ref, *refs):
+    *dose_refs, cross_ref, product_ref, pass_ref, dose_scr = refs
     samples, variants = dose_refs[0].shape
     chunks = [(ref, at) for ref in dose_refs for at in range(0, ref.shape[1], variants)]
     order = [0, 1, 3, 2, 4, 5, 7, 6]
@@ -271,33 +308,20 @@
         dose_scr[m * samples : (m + 1) * samples, :] = ref[:, at : at + variants]
     line = turned_ref.shape[1]
     rotated = jnp.dot(turned_ref[...], dose_scr[:line], preferred_element_type=f32)
-    rotated += jnp.dot(turned2_ref[...], dose_scr[line:], preferred_element_type=f32)
+    rotated += jnp.dot(jnp.concatenate([own_ref[...], other_ref[...]], axis=0), dose_scr[line:], preferred_element_type=f32)
     rotated = rotated.astype(bf16)
     squared = jnp.square(rotated.astype(f32)).astype(bf16)
     cross = jnp.dot(weighted_ref[...], rotated, preferred_element_type=f32)
     power = jnp.dot(low_ref[...], squared, preferred_element_type=f32)
-    core = place_ref[1]
-    start = gene_ref[:, 1:2].astype(jnp.int32)
-    valid = gene_ref[:, 2:3].astype(jnp.int32)
-    genes = cross.shape[0]
-    lane = lax.broadcasted_iota(jnp.int32, (genes, LANES), 1)
-    own_power = power_ref[...]
-    scale = jnp.sqrt(f32(dose_scr.shape[0]))
-    blocks = variants // LANES
-    for out_ref, half in ((keep_ref, core), (pass_ref, 1 - core)):
-        offset = start + half * LANES - core * variants
-        block = offset >> 7
-        shift = offset & (LANES - 1)
-        need = block + (lane < shift).astype(jnp.int32)
-        products = [jnp.zeros((genes, LANES), f32)] * 2
-        for b in range(blocks):
-            here = need == b
-            parts = [array[:, b * LANES : (b + 1) * LANES] for array in (cross, power)]
-            products = [jnp.where(here, part, product) for part, product in zip(parts, products)]
-        inside = (need >= 0) & (need < blocks)
-        score = jnp.where(inside, scale * products[0] / jnp.sqrt(products[1] * own_power), 0.0)
-        score = jnp.take_along_axis(score, (lane + shift) & (LANES - 1), axis=1)
-        out_ref[...] = jnp.where(lane + half * LANES < valid, score, 0.0)
+    cross_ref[...] = cross
+    product_ref[...] = power
+    pass_ref[...] = window(place_ref, gene_ref, power_ref, cross, power, 1 - place_ref[1], dose_scr.shape[0])
+
+
+def keep_kernel(place_ref, gene_ref, power_ref, cross_ref, product_ref, keep_ref, *, samples):
+    keep_ref[...] = window(
+        place_ref, gene_ref, power_ref, cross_ref[...], product_ref[...], place_ref[1], samples
+    )
 
 
 def call(kernel, outs, count, scratch=(), smem=1, anywhere=0, limit=VMEM_LIMIT):
@@ -343,7 +367,7 @@
         scratch=[pltpu.VMEM((rows, LANES), kind) for kind in (jnp.int32, f32, jnp.int32, jnp.int32)]
         + [pltpu.VMEM((1, half), f32), pltpu.VMEM((part, expression.shape[1]), bf16), pltpu.SemaphoreType.DMA((8,))],
         anywhere=8,
-        limit=ROUTE_LIMIT,
+        limit=VMEM_LIMIT,
     )(
         place,
         *[
@@ -373,8 +397,8 @@
     d37 = swap(jnp.concatenate([d2, d6], axis=1), 1)
     width = 4 * half + 2 * LANES
     out, kept = call(
-        third_kernel, [((panel, width), bf16), ((panel, width + half), bf16)], 7, smem=0, anywhere=1
-    )(ahead, r1, r4, e2, e0, terms, far)
+        third_kernel, [((panel, width), bf16), ((panel, width + half), bf16)], 8, smem=0, anywhere=2
+    )(ahead, r1, r4, e2, e0, terms, far, d2)
     kept2 = other_core(kept)
     near = swap(out, 2)
     near2 = other_core(near)
@@ -386,18 +410,22 @@
         scratch=[pltpu.VMEM((samples // 2, LANES), bf16)],
         anywhere=1,
     )(place, kept, kept2, d15)
+    own = call(own_kernel, [((half, samples // 2), bf16)], 1, smem=0)(near)[0]
     turned2, weighted, low, power = call(
         weight_kernel,
-        [shape, ((LANES, 2 * half), bf16), ((LANES, 2 * half), bf16), ((LANES, LANES), f32)],
+        [((half, samples // 2), bf16), ((LANES, 2 * half), bf16), ((LANES, 2 * half), bf16), ((LANES, LANES), f32)],
         7,
         scratch=[pltpu.VMEM((samples // 2, LANES), bf16)],
     )(place, kept, kept2, near, near2, share, gene)
-    keep, passed = call(
+    cross, product, passed = call(
         score_kernel,
-        [((LANES, LANES), f32)] * 2,
-        13,
+        [((LANES, variants), f32)] * 2 + [((LANES, LANES), f32)],
+        14,
         scratch=[pltpu.VMEM((samples, variants), bf16)],
-    )(place, gene, power, turned, turned2, weighted, low, d0, d15, d4, d2, d37, d6)
+    )(place, gene, power, turned, own, turned2, weighted, low, d0, d15, d4, d2, d37, d6)
+    keep = call(functools.partial(keep_kernel, samples=samples), [((LANES, LANES), f32)], 5)(
+        place, gene, power, cross, product
+    )[0]
     return keep + other_core(passed)
 
 

time: 29.3 us -> 29.2 us (level)
  waiting for transfers between devices: 9.1 us -> 7.11 us
  starting transfers between devices: 13.6 us -> 14.6 us
  Pallas kernels: 5.71 us -> 6.52 us
    ppermute x3, waiting for transfers between devices: 1.56 us -> 0.4 us  [other_core(): return lax.ppermute(x, 'col', [(0, 1), (1, 0)])]
    ppermute x8, starting transfers between devices: 13.3 us -> 14.1 us  [swap(): return lax.ppermute(x, 'row', [(i, i ^ m) for i in range(rows)])]
    ppermute x8, waiting for transfers between devices: 7.54 us -> 6.71 us  [swap(): return lax.ppermute(x, 'row', [(i, i ^ m) for i in range(rows)])]
    pallas_call x2 -> x4, Pallas kernels: 2.8 us -> 3.6 us  [the longest x1 1.63 us: near_body(): call(score_kernel, [((LANES, variants), f32)] * 2 + [((LANES, LANES), f32...]
  transfers between devices with their start and end apart: 11 -> 11, of which waited for: 5 -> 6; matrix products, arithmetic and copies ran while one was open for 0% -> 0% of each run, Pallas kernels for 7% -> 10%
where the time goes in v15:
time: 29.2 us; the launch traced here: 29 us
  starting transfers between devices  14.6 us (50%)
  waiting for transfers between devices  7.11 us (24%)
  Pallas kernels  6.52 us (22%)
  other arithmetic  0.73 us (2%)
    ppermute x8, starting transfers between devices, swap(): return lax.ppermute(x, 'row', [(i, i ^ m) for i in range(rows)])  14.1 us
    ppermute x8, waiting for transfers between devices, swap(): return lax.ppermute(x, 'row', [(i, i ^ m) for i in range(rows)])  6.71 us
    pallas_call x1, Pallas kernels, near_body(): call(route_kernel, [((panel, half + 2 * LANES), bf16), ((part, 2 * LANES)...  1.93 us
    pallas_call x1, Pallas kernels, near_body(): call(score_kernel, [((LANES, variants), f32)] * 2 + [((LANES, LANES), f32...  1.63 us
    pallas_call x1, Pallas kernels, near_body(): call(weight_kernel, [((half, samples // 2), bf16), ((LANES, 2 * half), bf...  0.98 us
    pallas_call x1, Pallas kernels, near_body(): call(half_kernel, [shape, ((LANES, 2 * half), f32)], 4, scratch=[pltpu.VM...  0.93 us
    pallas_call x1, Pallas kernels, near_body(): call(functools.partial(keep_kernel, samples=samples), [((LANES, LANES), f...  0.78 us
    add x1, other arithmetic, near_body(): return keep + other_core(passed)  0.64 us
  transfers between devices with their start and end apart: 11, of which 6 were waited for; matrix products, arithmetic and copies ran while one was open for 0% of the time, Pallas kernels for 10%

profile of v15, /device:TPU:0, one launch (start us, length us, event | category | flops | bytes accessed | tf_op | source)
XLA Modules:
  0.0 29.0 jit_solution(15881625427795955046)
XLA Ops:
  0.0 0.1 pad_add_fusion.place_ref
  0.1 1.9 %shard_map.82 = (bf16[64,512]{1,0:T(8,128)(2,1)S(1)}, bf16[32,256]{1,0:T(8,128)(2,1)S(1)}, bf16[32,128]{1,0:T(8,128)(2,1)S(1)}, bf16[32,128]{1,0:T(8,128)(2,1)S(...) custom-call(s32[2]{0:T(128)S(1)} %pad_add_fusion.place_ref, ...), custom_call_target="tpu_custom_call" | custom-call | tf_op jit(solution)/shard_map/pallas_call | solution.py:355
  2.0 4.1 %collective-permute-start.2 = (bf16[64,768]{1,0:T(8,128)(2,1)S(1)}, bf16[64,768]{1,0:T(8,128)(2,1)S(1)}, u32[]{:S(2)}, u32[]{:S(2)}) collective-permute-start(bf16[64,768]{1,0:T(8,128)(2,1)S(1)} %get-tuple-element.31.d0_ref.refs_0_), channel_id=1, source_target_pairs={{0,8},{2,10},{4,12},{6,14},{8,0},{10,2},{12,4},{14,6},{1,9},{3,11}... | collective-permute-start | bytes 294920 | tf_op jit(solution)/shard_map/ppermute | solution.py:350
  6.1 1.5 %collective-permute-start = (bf16[64,512]{1,0:T(8,128)(2,1)S(1)}, bf16[64,512]{1,0:T(8,128)(2,1)S(1)}, u32[]{:S(2)}, u32[]{:S(2)}) collective-permute-start(bf16[64,512]{1,0:T(8,128)(2,1)S(1)} %get-tuple-element.26.ahead_ref), channel_id=1, source_target_pairs={{0,2},{2,0},{4,6},{6,4},{8,10},{10,8},{12,14},{14,12},{1,3},{3,1},... | collective-permute-start | bytes 196616 | tf_op jit(solution)/shard_map/ppermute | solution.py:350
  7.6 1.6 %collective-permute-start.3 = (bf16[64,768]{1,0:T(8,128)(2,1)S(1)}, bf16[64,768]{1,0:T(8,128)(2,1)S(1)}, u32[]{:S(2)}, u32[]{:S(2)}) collective-permute-start(bf16[64,768]{1,0:T(8,128)(2,1)S(1)} %get-tuple-element.31.d0_ref.refs_0_), channel_id=1, source_target_pairs={{0,4},{2,6},{4,0},{6,2},{8,12},{10,14},{12,8},{14,10},{1,5},{3,7},... | collective-permute-start | bytes 294920 | tf_op jit(solution)/shard_map/ppermute | solution.py:350
  9.2 1.2 %collective-permute-done.r1_ref = bf16[64,512]{1,0:T(8,128)(2,1)S(1)} collective-permute-done((bf16[64,512]{1,0:T(8,128)(2,1)S(1)}, bf16[64,512]{1,0:T(8,128)(2,1)S(1)}, u32[]{:S(2)}, u32[]{:S(2)}) %collective-permute-start) | collective-permute-done | bytes 65568 | tf_op jit(solution)/shard_map/ppermute | solution.py:350
  10.4 0.1 collective-permute-start.1
  10.5 0.6 %collective-permute-done.2.d4_ref.refs_2_ = bf16[64,768]{1,0:T(8,128)(2,1)S(1)} collective-permute-done((bf16[64,768]{1,0:T(8,128)(2,1)S(1)}, bf16[64,768]{1,0:T(8,128)(2,1)S(1)}, u32[]{:S(2)}, u32[]{:S(2)}) %collective-permute-start.2) | collective-permute-done | bytes 98336 | tf_op jit(solution)/shard_map/ppermute | solution.py:350
  11.1 1.8 %collective-permute-start.8 = (bf16[64,768]{1,0:T(8,128)(2,1)S(1)}, bf16[64,768]{1,0:T(8,128)(2,1)S(1)}, u32[]{:S(2)}, u32[]{:S(2)}) collective-permute-start(bf16[64,768]{1,0:T(8,128)(2,1)S(1)} %get-tuple-element.32.far_any), channel_id=1, source_target_pairs={{0,4},{2,6},{4,0},{6,2},{8,12},{10,14},{12,8},{14,10},{1,5},{3,7},... | collective-permute-start | bytes 294920 | tf_op jit(solution)/shard_map/ppermute | solution.py:350
  12.9 1.1 %collective-permute-start.7 = (bf16[64,1536]{1,0:T(8,128)(2,1)S(1)}, bf16[64,1536]{1,0:T(8,128)(2,1)S(1)}, u32[]{:S(2)}, u32[]{:S(2)}) collective-permute-start(bf16[64,1536]{1,0:T(8,128)(2,1)S(1)} %get-tuple-element.35), channel_id=1, source_target_pairs={{0,2},{2,0},{4,6},{6,4},{8,10},{10,8},{12,14},{14,12},{1,3},{3,1},... | collective-permute-start | bytes 589832 | tf_op jit(solution)/shard_map/ppermute | solution.py:350
  14.0 2.1 %collective-permute-done.1.r4_ref = bf16[64,768]{1,0:T(8,128)(2,1)S(1)} collective-permute-done((bf16[64,768]{1,0:T(8,128)(2,1)S(1)}, bf16[64,768]{1,0:T(8,128)(2,1)S(1)}, u32[]{:S(2)}, u32[]{:S(2)}) %collective-permute-start.1) | collective-permute-done | bytes 98336 | tf_op jit(solution)/shard_map/ppermute | solution.py:350
  16.1 0.1 collective-permute-start.4
  16.2 2.0 %collective-permute-start.5 = (bf16[64,1280]{1,0:T(8,128)(2,1)S(1)}, bf16[64,1280]{1,0:T(8,128)(2,1)S(1)}, u32[]{:S(2)}, u32[]{:S(2)}) collective-permute-start(bf16[64,1280]{1,0:T(8,128)(2,1)S(1)} %get-tuple-element.34), channel_id=1, source_target_pairs={{0,4},{2,6},{4,0},{6,2},{8,12},{10,14},{12,8},{14,10},{1,5},{3,7},... | collective-permute-start | bytes 491528 | tf_op jit(solution)/shard_map/ppermute | solution.py:350
  18.2 2.0 %collective-permute-start.9 = (bf16[64,1536]{1,0:T(8,128)(2,1)S(1)}, bf16[64,1536]{1,0:T(8,128)(2,1)S(1)}, u32[]{:S(2)}, u32[]{:S(2)}) collective-permute-start(bf16[64,1536]{1,0:T(8,128)(2,1)S(1)} %pad_maximum_fusion), channel_id=1, source_target_pairs={{0,2},{2,0},{4,6},{6,4},{8,10},{10,8},{12,14},{14,12},{1,3},{3,1},... | collective-permute-start | bytes 589832 | tf_op jit(solution)/shard_map/ppermute | solution.py:350
  20.2 2.8 %collective-permute-done.5.mine_ref = bf16[64,1280]{1,0:T(8,128)(2,1)S(1)} collective-permute-done((bf16[64,1280]{1,0:T(8,128)(2,1)S(1)}, bf16[64,1280]{1,0:T(8,128)(2,1)S(1)}, u32[]{:S(2)}, u32[]{:S(2)}) %collective-permute-start.5) | collective-permute-done | bytes 163872 | tf_op jit(solution)/shard_map/ppermute | solution.py:350
  23.0 0.2 shard_map.88.own_ref
  23.2 0.9 %shard_map.86 = (bf16[512,256]{1,0:T(8,128)(2,1)S(1)}, f32[128,512]{1,0:T(8,128)S(1)}) custom-call(s32[2]{0:T(128)S(1)} %pad_add_fusion.place_ref, bf16[64,1536]{1,0:T(8,128)(2,1)S(1)} %get-tuple-element.33.mine_ref.kept_ref, bf16[64,1536]{1,0:T(8,128)(2,1)S(1)} %collective-permute-done.4.other_ref.kept2_ref, ...), custom_call_target="tpu_custom_call" | custom-call | tf_op jit(solution)/shard_map/pallas_call | solution.py:406
  24.2 0.2 collective-permute-done.6.other_ref
  24.4 1.0 %shard_map.87 = (bf16[256,256]{1,0:T(8,128)(2,1)S(1)}, bf16[128,512]{1,0:T(8,128)(2,1)S(1)}, bf16[128,512]{1,0:T(8,128)(2,1)S(1)}, f32[128,128]{1,0:T(8,128)S(1)}) custom-call(s32[2]{0:T(128)S(1)} %pad_add_fusion.place_ref, bf16[64,1536]{1,0:T(8,128)(2,1)S(1)} %get-tuple-element.33.mine_ref.kept_ref, ...), custom_call_target="tpu_custom_call" | custom-call | tf_op jit(solution)/shard_map/pallas_call | solution.py:414
  25.4 1.6 %shard_map.89 = (f32[128,768]{1,0:T(8,128)S(1)}, f32[128,768]{1,0:T(8,128)S(1)}, f32[128,128]{1,0:T(8,128)S(1)}) custom-call(s32[2]{0:T(128)S(1)} %pad_add_fusion.place_ref, f32[128,128]{1,0:T(8,128)S(1)} %get-tuple-element.25.gene_ref, f32[128,128]{1,0:T(8,128)S(1)} %get-tuple-element.37.power_ref, bf16[512,256]{1,0:T(8,128)(2,1)S(1)} %get-tuple-element.38.turned_ref, ...), custom_call_target="tpu_custom_call" | custom-call | tf_op jit(solution)/shard_map/pallas_call | solution.py:420
  27.1 0.4 %collective-permute-start.10 = (f32[128,128]{1,0:T(8,128)S(1)}, f32[128,128]{1,0:T(8,128)S(1)}, u32[]{:S(2)}, u32[]{:S(2)}) collective-permute-start(f32[128,128]{1,0:T(8,128)S(1)} %get-tuple-element.44), channel_id=1, source_target_pairs={{0,1},{1,0},{2,3},{3,2},{4,5},{5,4},{6,7},{7,6},{8,9},{9,8},{10,11... | collective-permute-start | bytes 196616 | tf_op jit(solution)/shard_map/ppermute | solution.py:353
  27.4 0.8 %shard_map.90 = f32[128,128]{1,0:T(8,128)S(1)} custom-call(s32[2]{0:T(128)S(1)} %pad_add_fusion.place_ref, f32[128,128]{1,0:T(8,128)S(1)} %get-tuple-element.25.gene_ref, f32[128,128]{1,0:T(8,128)S(1)} %get-tuple-element.37.power_ref, f32[128,768]{1,0:T(8,128)S(1)} %get-tuple-element.42.cross_ref, f32[128,768]{1,0:T(8,128)S(1)} %get-tuple-element.43.product_ref), custom_call_target="tpu_custom_call" | custom-call | tf_op jit(solution)/shard_map/pallas_call | solution.py:426
  28.2 0.2 collective-permute-done.10
  28.4 0.6 %add.3 = f32[128,128]{1,0:T(8,128)} add(f32[128,128]{1,0:T(8,128)S(1)} %shard_map.90, f32[128,128]{1,0:T(8,128)S(1)} %collective-permute-done.10) | non-fusion elementwise | flops 16384 | bytes 196608 | tf_op jit(solution)/shard_map/add | solution.py:429
  (10 shorter events, 0.1 us)
Async XLA Ops:
  2.0 9.1 %collective-permute-start.2 = (bf16[64,768]{1,0:T(8,128)(2,1)S(1)}, bf16[64,768]{1,0:T(8,128)(2,1)S(1)}, u32[]{:S(2)}, u32[]{:S(2)}) collective-permute-start(bf16[64,768]{1,0:T(8,128)(2,1)S(1)} %get-tuple-element.31.d0_ref.refs_0_), channel_id=1, source_target_pairs={{0,8},{2,10},{4,12},{6,14},{8,0},{10,2},{12,4},{14,6},{1,9},{3,11}... | collective-permute-start | bytes 294920 | tf_op jit(solution)/shard_map/ppermute | solution.py:350
  6.1 4.3 %collective-permute-start = (bf16[64,512]{1,0:T(8,128)(2,1)S(1)}, bf16[64,512]{1,0:T(8,128)(2,1)S(1)}, u32[]{:S(2)}, u32[]{:S(2)}) collective-permute-start(bf16[64,512]{1,0:T(8,128)(2,1)S(1)} %get-tuple-element.26.ahead_ref), channel_id=1, source_target_pairs={{0,2},{2,0},{4,6},{6,4},{8,10},{10,8},{12,14},{14,12},{1,3},{3,1},... | collective-permute-start | bytes 196616 | tf_op jit(solution)/shard_map/ppermute | solution.py:350
  7.6 6.4 %collective-permute-start.3 = (bf16[64,768]{1,0:T(8,128)(2,1)S(1)}, bf16[64,768]{1,0:T(8,128)(2,1)S(1)}, u32[]{:S(2)}, u32[]{:S(2)}) collective-permute-start(bf16[64,768]{1,0:T(8,128)(2,1)S(1)} %get-tuple-element.31.d0_ref.refs_0_), channel_id=1, source_target_pairs={{0,4},{2,6},{4,0},{6,2},{8,12},{10,14},{12,8},{14,10},{1,5},{3,7},... | collective-permute-start | bytes 294920 | tf_op jit(solution)/shard_map/ppermute | solution.py:350
  10.4 5.7 %collective-permute-start.1 = (bf16[64,768]{1,0:T(8,128)(2,1)S(1)}, bf16[64,768]{1,0:T(8,128)(2,1)S(1)}, u32[]{:S(2)}, u32[]{:S(2)}) collective-permute-start(bf16[64,768]{1,0:T(8,128)(2,1)S(1)} %shard_map.83.after_any), channel_id=1, source_target_pairs={{0,8},{2,10},{4,12},{6,14},{8,0},{10,2},{12,4},{14,6},{1,9},{3,11}... | collective-permute-start | bytes 294920 | tf_op jit(solution)/shard_map/ppermute | solution.py:350
  11.1 7.1 %collective-permute-start.8 = (bf16[64,768]{1,0:T(8,128)(2,1)S(1)}, bf16[64,768]{1,0:T(8,128)(2,1)S(1)}, u32[]{:S(2)}, u32[]{:S(2)}) collective-permute-start(bf16[64,768]{1,0:T(8,128)(2,1)S(1)} %get-tuple-element.32.far_any), channel_id=1, source_target_pairs={{0,4},{2,6},{4,0},{6,2},{8,12},{10,14},{12,8},{14,10},{1,5},{3,7},... | collective-permute-start | bytes 294920 | tf_op jit(solution)/shard_map/ppermute | solution.py:350
  12.9 10.3 %collective-permute-start.7 = (bf16[64,1536]{1,0:T(8,128)(2,1)S(1)}, bf16[64,1536]{1,0:T(8,128)(2,1)S(1)}, u32[]{:S(2)}, u32[]{:S(2)}) collective-permute-start(bf16[64,1536]{1,0:T(8,128)(2,1)S(1)} %get-tuple-element.35), channel_id=1, source_target_pairs={{0,2},{2,0},{4,6},{6,4},{8,10},{10,8},{12,14},{14,12},{1,3},{3,1},... | collective-permute-start | bytes 589832 | tf_op jit(solution)/shard_map/ppermute | solution.py:350
  16.1 7.1 %collective-permute-start.4 = (bf16[64,1536]{1,0:T(8,128)(2,1)S(1)}, bf16[64,1536]{1,0:T(8,128)(2,1)S(1)}, u32[]{:S(2)}, u32[]{:S(2)}) collective-permute-start(bf16[64,1536]{1,0:T(8,128)(2,1)S(1)} %get-tuple-element.33.mine_ref.kept_ref), channel_id=1, source_target_pairs={{0,1},{1,0},{2,3},{3,2},{4,5},{5,4},{6,7},{7,6},{8,9},{9,8},{10,11... | collective-permute-start | bytes 589832 | tf_op jit(solution)/shard_map/ppermute | solution.py:353
  16.2 6.8 %collective-permute-start.5 = (bf16[64,1280]{1,0:T(8,128)(2,1)S(1)}, bf16[64,1280]{1,0:T(8,128)(2,1)S(1)}, u32[]{:S(2)}, u32[]{:S(2)}) collective-permute-start(bf16[64,1280]{1,0:T(8,128)(2,1)S(1)} %get-tuple-element.34), channel_id=1, source_target_pairs={{0,4},{2,6},{4,0},{6,2},{8,12},{10,14},{12,8},{14,10},{1,5},{3,7},... | collective-permute-start | bytes 491528 | tf_op jit(solution)/shard_map/ppermute | solution.py:350
  18.2 7.2 %collective-permute-start.9 = (bf16[64,1536]{1,0:T(8,128)(2,1)S(1)}, bf16[64,1536]{1,0:T(8,128)(2,1)S(1)}, u32[]{:S(2)}, u32[]{:S(2)}) collective-permute-start(bf16[64,1536]{1,0:T(8,128)(2,1)S(1)} %pad_maximum_fusion), channel_id=1, source_target_pairs={{0,2},{2,0},{4,6},{6,4},{8,10},{10,8},{12,14},{14,12},{1,3},{3,1},... | collective-permute-start | bytes 589832 | tf_op jit(solution)/shard_map/ppermute | solution.py:350
  23.0 1.4 %collective-permute-start.6 = (bf16[64,1280]{1,0:T(8,128)(2,1)S(1)}, bf16[64,1280]{1,0:T(8,128)(2,1)S(1)}, u32[]{:S(2)}, u32[]{:S(2)}) collective-permute-start(bf16[64,1280]{1,0:T(8,128)(2,1)S(1)} %collective-permute-done.5.mine_ref), channel_id=1, source_target_pairs={{0,1},{1,0},{2,3},{3,2},{4,5},{5,4},{6,7},{7,6},{8,9},{9,8},{10,11... | collective-permute-start | bytes 491528 | tf_op jit(solution)/shard_map/ppermute | solution.py:353
  27.1 1.3 %collective-permute-start.10 = (f32[128,128]{1,0:T(8,128)S(1)}, f32[128,128]{1,0:T(8,128)S(1)}, u32[]{:S(2)}, u32[]{:S(2)}) collective-permute-start(f32[128,128]{1,0:T(8,128)S(1)} %get-tuple-element.44), channel_id=1, source_target_pairs={{0,1},{1,0},{2,3},{3,2},{4,5},{5,4},{6,7},{7,6},{8,9},{9,8},{10,11... | collective-permute-start | bytes 196616 | tf_op jit(solution)/shard_map/ppermute | solution.py:353

commit v16 on v13

--- a/solution.py
+++ b/solution.py
@@ -198,26 +198,28 @@
     far_ref[...] = d4_ref[...]
 
 
-def third_kernel(ahead_ref, r1_ref, r4_ref, e2_ref, e0_ref, terms_ref, far_any, d2_any, out_ref, kept_ref):
+def third_kernel(ahead_ref, r1_ref, r4_ref, e2_ref, e0_ref, terms_ref, d2_ref, far_any, out_ref, kept_ref):
     half = terms_ref.shape[1]
     part = e0_ref.shape[0]
-    for ref, own, at in ((out_ref, e2_ref, LANES), (kept_ref, e0_ref, 0)):
-        ref[:, :half] = ahead_ref[:, :half]
-        ref[:, half : 2 * half] = r1_ref[:, :half]
-        ref[:, 2 * half : 4 * half] = r4_ref[:, : 2 * half]
+    kept_ref[:, :half] = ahead_ref[:, :half]
+    for ref, own, at, first in ((out_ref, e2_ref, LANES, 0), (kept_ref, e0_ref, 0, half)):
+        ref[:, first : first + half] = r1_ref[:, :half]
+        ref[:, first + half : first + 3 * half] = r4_ref[:, : 2 * half]
         side = slice(2 * half + at, 2 * half + at + LANES)
-        left, right = slice(4 * half, 4 * half + LANES), slice(4 * half + LANES, 4 * half + 2 * LANES)
+        middle = first + 3 * half + LANES
+        left, right = slice(middle - LANES, middle), slice(middle, middle + LANES)
         ref[:part, left] = own[...]
         ref[:part, right] = r1_ref[:part, half + at : half + at + LANES]
         ref[part:, left] = r4_ref[:part, side]
         ref[part:, right] = r4_ref[part:, side]
-    width = out_ref.shape[1]
+    width = out_ref.shape[1] + half
     terms = terms_ref.shape[0]
-    kept_ref[:terms, width:] = terms_ref[...]
-    kept_ref[terms:, width:] = jnp.zeros((kept_ref.shape[0] - terms, half), bf16)
-
-
-def rotate(place_ref, refs, turned_ref, data_scr):
+    kept_ref[:terms, width : width + half] = terms_ref[...]
+    kept_ref[terms:, width : width + half] = jnp.zeros((kept_ref.shape[0] - terms, half), bf16)
+    kept_ref[:, width + half :] = d2_ref[:, d2_ref.shape[1] - half :]
+
+
+def rotate(place_ref, refs, turned_ref, data_scr, panels, data_at):
     samples = refs[0].shape[0]
     half = turned_ref.shape[0] // 2
     part = samples // 2
@@ -225,24 +227,27 @@
     for c, ref in enumerate(refs):
         side = core if c == 0 else 1 - core
         for i in range(4):
+            panel, at = panels[c][i]
             turned_ref[c * half : (c + 1) * half, i * samples : (i + 1) * samples] = (
-                ref[:, i * half : (i + 1) * half].astype(f32).T.astype(bf16)
+                panel[:, at : at + half].astype(f32).T.astype(bf16)
             )
-            at = 4 * half + i % 2 * LANES
+            at = data_at + i % 2 * LANES
             data_scr[pl.ds(pl.multiple_of(i * samples + side * part, part), part), :] = ref[
                 i // 2 * part : (i // 2 + 1) * part, at : at + LANES
             ]
     data = data_scr[...].astype(f32).T.astype(bf16)
     shares = []
-    for ref in refs:
-        vecs = jnp.concatenate([ref[:, i * half : (i + 1) * half] for i in range(4)], axis=0)
+    for c in range(2):
+        vecs = jnp.concatenate([panel[:, at : at + half] for panel, at in panels[c]], axis=0)
         shares.append(jnp.dot(data, vecs, preferred_element_type=f32))
     return shares
 
 
 def half_kernel(place_ref, mine_ref, other_ref, d15_any, turned_ref, share_ref, data_scr):
     half = turned_ref.shape[0] // 2
-    for c, share in enumerate(rotate(place_ref, (mine_ref, other_ref), turned_ref, data_scr)):
+    refs = (mine_ref, other_ref)
+    panels = [[(ref, i * half) for i in range(4)] for ref in refs]
+    for c, share in enumerate(rotate(place_ref, refs, turned_ref, data_scr, panels, 4 * half)):
         share_ref[:, c * half : (c + 1) * half] = share
 
 
@@ -253,11 +258,15 @@
     half = turned_ref.shape[0] // 2
     delta = gene_ref[:, 0:1]
     total = jnp.zeros((delta.shape[0], 1), f32)
-    shares = rotate(place_ref, (mine_ref, other_ref), turned_ref, data_scr)
-    width = mine_ref.shape[1]
+    width = mine_ref.shape[1] + half
+    panels = [
+        [(kept, width + half)] + [(ref, i * half) for i in range(3)]
+        for kept, ref in ((kept_ref, mine_ref), (kept2_ref, other_ref))
+    ]
+    shares = rotate(place_ref, (mine_ref, other_ref), turned_ref, data_scr, panels, 3 * half)
     for c, (share, ref) in enumerate(zip(shares, (kept_ref, kept2_ref))):
         cols = slice(c * half, (c + 1) * half)
-        terms = ref[0:16, width:].astype(f32)
+        terms = ref[0:16, width : width + half].astype(f32)
         vals = terms[0:1] + terms[1:2] + terms[2:3]
         rotated = (share_ref[:, cols] + share).astype(bf16).astype(f32)
         weight = 1.0 / (vals + delta)
@@ -295,7 +304,7 @@
 def score_kernel(place_ref, gene_ref, power_ref, turned_ref, turned2_ref, weighted_ref, low_ref, *refs):
     *dose_refs, cross_ref, product_ref, pass_ref, dose_scr = refs
     samples, variants = dose_refs[0].shape
-    chunks = [(ref, at) for ref in dose_refs for at in range(0, ref.shape[1], variants)]
+    chunks = [(ref, at) for ref in dose_refs for at in range(0, ref.shape[1] - variants + 1, variants)]
     order = [0, 1, 3, 2, 4, 5, 7, 6]
     for m, (ref, at) in enumerate(chunks[i] for i in order):
         dose_scr[m * samples : (m + 1) * samples, :] = ref[:, at : at + variants]
@@ -378,7 +387,7 @@
     )
     r1 = swap(ahead, 1)
     d4 = swap(d0, 4)
-    d2 = swap(d0, 2)
+    d2 = swap(jnp.concatenate([d0, ahead[:, :half]], axis=1), 2)
     to4 = call(second_kernel, [((panel, 2 * half + 2 * LANES), bf16)], 3, smem=0)(ahead, r1, e46)[0]
     r4 = swap(to4, 4)
     pair, far = call(
@@ -386,11 +395,15 @@
     )(d0, d4, to4)
     d6 = swap(far, 2)
     d15 = swap(pair, 1)
-    d37 = swap(jnp.concatenate([d2, d6], axis=1), 1)
+    d37 = swap(jnp.concatenate([d2[:, :variants], d6], axis=1), 1)
     width = 4 * half + 2 * LANES
     out, kept = call(
-        third_kernel, [((panel, width), bf16), ((panel, width + half), bf16)], 8, smem=0, anywhere=2
-    )(ahead, r1, r4, e2, e0, terms, far, d2)
+        third_kernel,
+        [((panel, width - half), bf16), ((panel, width + 2 * half), bf16)],
+        8,
+        smem=0,
+        anywhere=1,
+    )(ahead, r1, r4, e2, e0, terms, d2, far)
     kept2 = other_core(kept)
     near = swap(out, 2)
     near2 = other_core(near)

time: 29 us -> 28.7 us (0.990)
  starting transfers between devices: 14.5 us -> 11.9 us
  waiting for transfers between devices: 6.48 us -> 8.72 us
    ppermute x8, starting transfers between devices: 14.2 us -> 11.6 us  [swap(): return lax.ppermute(x, 'row', [(i, i ^ m) for i in range(rows)])]
    ppermute x8, waiting for transfers between devices: 5.7 us -> 8 us  [swap(): return lax.ppermute(x, 'row', [(i, i ^ m) for i in range(rows)])]
  transfers between devices with their start and end apart: 11 -> 11, of which waited for: 6 -> 7; matrix products, arithmetic and copies ran while one was open for 0% -> 0% of each run, Pallas kernels for 10% -> 10%
where the time goes in v16:
time: 28.7 us; the launch traced here: 28.5 us
  starting transfers between devices  11.9 us (41%)
  waiting for transfers between devices  8.72 us (30%)
  Pallas kernels  6.33 us (22%)
  other arithmetic  0.74 us (3%)
  local copies, waits for them, and re-layouts  0.72 us (3%)
    ppermute x8, starting transfers between devices, swap(): return lax.ppermute(x, 'row', [(i, i ^ m) for i in range(rows)])  11.6 us
    ppermute x8, waiting for transfers between devices, swap(): return lax.ppermute(x, 'row', [(i, i ^ m) for i in range(rows)])  8 us
    pallas_call x1, Pallas kernels, near_body(): call(route_kernel, [((panel, half + 2 * LANES), bf16), ((part, 2 * LANES)...  1.73 us
    pallas_call x1, Pallas kernels, near_body(): call(score_kernel, [((LANES, variants), f32)] * 2 + [((LANES, LANES), f32...  1.64 us
    pallas_call x1, Pallas kernels, near_body(): call(weight_kernel, [shape, ((LANES, 2 * half), bf16), ((LANES, 2 * half)...  1.08 us
    pallas_call x1, Pallas kernels, near_body(): call(half_kernel, [shape, ((LANES, 2 * half), f32)], 4, scratch=[pltpu.VM...  0.93 us
    pallas_call x1, Pallas kernels, near_body(): call(functools.partial(keep_kernel, samples=samples), [((LANES, LANES), f...  0.78 us
    ppermute x3, waiting for transfers between devices, other_core(): return lax.ppermute(x, 'col', [(0, 1), (1, 0)])  0.73 us
  transfers between devices with their start and end apart: 11, of which 7 were waited for; matrix products, arithmetic and copies ran while one was open for 0% of the time, Pallas kernels for 10%

profile of v16, /device:TPU:0, one launch (start us, length us, event | category | flops | bytes accessed | tf_op | source)
XLA Modules:
  0.0 28.5 jit_solution(8863958395130722539)
XLA Ops:
  0.1 1.7 %shard_map.82 = (bf16[64,512]{1,0:T(8,128)(2,1)S(1)}, bf16[32,256]{1,0:T(8,128)(2,1)S(1)}, bf16[32,128]{1,0:T(8,128)(2,1)S(1)}, bf16[32,128]{1,0:T(8,128)(2,1)S(...) custom-call(s32[2]{0:T(128)S(1)} %pad_add_fusion.place_ref, s32[8,128]{1,0:T(8,128)} %bitcast.11, ...), custom_call_target="tpu_custom_call" | custom-call | tf_op jit(solution)/shard_map/pallas_call | solution.py:357
  1.8 3.0 %collective-permute-start = (bf16[64,512]{1,0:T(8,128)(2,1)S(1)}, bf16[64,512]{1,0:T(8,128)(2,1)S(1)}, u32[]{:S(2)}, u32[]{:S(2)}) collective-permute-start(bf16[64,512]{1,0:T(8,128)(2,1)S(1)} %get-tuple-element.28.ahead_ref), channel_id=1, source_target_pairs={{0,2},{2,0},{4,6},{6,4},{8,10},{10,8},{12,14},{14,12},{1,3},{3,1},... | collective-permute-start | bytes 196616 | tf_op jit(solution)/shard_map/ppermute | solution.py:352
  4.8 2.6 %collective-permute-start.3 = (bf16[64,768]{1,0:T(8,128)(2,1)S(1)}, bf16[64,768]{1,0:T(8,128)(2,1)S(1)}, u32[]{:S(2)}, u32[]{:S(2)}) collective-permute-start(bf16[64,768]{1,0:T(8,128)(2,1)S(1)} %get-tuple-element.33.d0_ref.refs_0_), channel_id=1, source_target_pairs={{0,8},{2,10},{4,12},{6,14},{8,0},{10,2},{12,4},{14,6},{1,9},{3,11}... | collective-permute-start | bytes 294920 | tf_op jit(solution)/shard_map/ppermute | solution.py:352
  7.5 1.6 %collective-permute-start.2 = (bf16[64,1024]{1,0:T(8,128)(2,1)S(1)}, bf16[64,1024]{1,0:T(8,128)(2,1)S(1)}, u32[]{:S(2)}, u32[]{:S(2)}) collective-permute-start(bf16[64,1024]{1,0:T(8,128)(2,1)S(1)} %pad_maximum_fusion.1), channel_id=1, source_target_pairs={{0,4},{2,6},{4,0},{6,2},{8,12},{10,14},{12,8},{14,10},{1,5},{3,7},... | collective-permute-start | bytes 393224 | tf_op jit(solution)/shard_map/ppermute | solution.py:352
  9.1 1.1 %collective-permute-start.1 = (bf16[64,768]{1,0:T(8,128)(2,1)S(1)}, bf16[64,768]{1,0:T(8,128)(2,1)S(1)}, u32[]{:S(2)}, u32[]{:S(2)}) collective-permute-start(bf16[64,768]{1,0:T(8,128)(2,1)S(1)} %shard_map.84.after_any), channel_id=1, source_target_pairs={{0,8},{2,10},{4,12},{6,14},{8,0},{10,2},{12,4},{14,6},{1,9},{3,11}... | collective-permute-start | bytes 294920 | tf_op jit(solution)/shard_map/ppermute | solution.py:352
  10.3 1.5 %collective-permute-done.3.d4_ref.refs_2_ = bf16[64,768]{1,0:T(8,128)(2,1)S(1)} collective-permute-done((bf16[64,768]{1,0:T(8,128)(2,1)S(1)}, bf16[64,768]{1,0:T(8,128)(2,1)S(1)}, u32[]{:S(2)}, u32[]{:S(2)}) %collective-permute-start.3) | collective-permute-done | bytes 98336 | tf_op jit(solution)/shard_map/ppermute | solution.py:352
  11.8 1.6 %collective-permute-start.8 = (bf16[64,768]{1,0:T(8,128)(2,1)S(1)}, bf16[64,768]{1,0:T(8,128)(2,1)S(1)}, u32[]{:S(2)}, u32[]{:S(2)}) collective-permute-start(bf16[64,768]{1,0:T(8,128)(2,1)S(1)} %get-tuple-element.34.far_any), channel_id=1, source_target_pairs={{0,4},{2,6},{4,0},{6,2},{8,12},{10,14},{12,8},{14,10},{1,5},{3,7},... | collective-permute-start | bytes 294920 | tf_op jit(solution)/shard_map/ppermute | solution.py:352
  13.4 0.7 %copy-done.1 = s32[1024]{0:T(1024)S(1)} copy-done((s32[1024]{0:T(1024)S(1)}, s32[1024]{0:T(1024)}, u32[]{:S(2)}) %copy-start.1) | copy-done | bytes 4120
  14.1 0.1 shard_map.83
  14.2 0.6 %collective-permute-start.7 = (bf16[64,1536]{1,0:T(8,128)(2,1)S(1)}, bf16[64,1536]{1,0:T(8,128)(2,1)S(1)}, u32[]{:S(2)}, u32[]{:S(2)}) collective-permute-start(bf16[64,1536]{1,0:T(8,128)(2,1)S(1)} %get-tuple-element.37), channel_id=1, source_target_pairs={{0,2},{2,0},{4,6},{6,4},{8,10},{10,8},{12,14},{14,12},{1,3},{3,1},... | collective-permute-start | bytes 589832 | tf_op jit(solution)/shard_map/ppermute | solution.py:352
  14.8 0.9 %collective-permute-done.2.d2_ref.refs_3_ = bf16[64,1024]{1,0:T(8,128)(2,1)S(1)} collective-permute-done((bf16[64,1024]{1,0:T(8,128)(2,1)S(1)}, bf16[64,1024]{1,0:T(8,128)(2,1)S(1)}, u32[]{:S(2)}, u32[]{:S(2)}) %collective-permute-start.2) | collective-permute-done | bytes 131104 | tf_op jit(solution)/shard_map/ppermute | solution.py:352
  15.7 0.7 %collective-permute-done.1.r4_ref = bf16[64,768]{1,0:T(8,128)(2,1)S(1)} collective-permute-done((bf16[64,768]{1,0:T(8,128)(2,1)S(1)}, bf16[64,768]{1,0:T(8,128)(2,1)S(1)}, u32[]{:S(2)}, u32[]{:S(2)}) %collective-permute-start.1) | collective-permute-done | bytes 98336 | tf_op jit(solution)/shard_map/ppermute | solution.py:352
  16.5 0.5 %collective-permute-start.5 = (bf16[64,1024]{1,0:T(8,128)(2,1)S(1)}, bf16[64,1024]{1,0:T(8,128)(2,1)S(1)}, u32[]{:S(2)}, u32[]{:S(2)}) collective-permute-start(bf16[64,1024]{1,0:T(8,128)(2,1)S(1)} %get-tuple-element.36), channel_id=1, source_target_pairs={{0,4},{2,6},{4,0},{6,2},{8,12},{10,14},{12,8},{14,10},{1,5},{3,7},... | collective-permute-start | bytes 393224 | tf_op jit(solution)/shard_map/ppermute | solution.py:352
  17.0 0.4 %collective-permute-done.8.refs_5_ = bf16[64,768]{1,0:T(8,128)(2,1)S(1)} collective-permute-done((bf16[64,768]{1,0:T(8,128)(2,1)S(1)}, bf16[64,768]{1,0:T(8,128)(2,1)S(1)}, u32[]{:S(2)}, u32[]{:S(2)}) %collective-permute-start.8) | collective-permute-done | bytes 98336 | tf_op jit(solution)/shard_map/ppermute | solution.py:352
  17.5 0.5 %collective-permute-start.9 = (bf16[64,1536]{1,0:T(8,128)(2,1)S(1)}, bf16[64,1536]{1,0:T(8,128)(2,1)S(1)}, u32[]{:S(2)}, u32[]{:S(2)}) collective-permute-start(bf16[64,1536]{1,0:T(8,128)(2,1)S(1)} %pad_maximum_fusion), channel_id=1, source_target_pairs={{0,2},{2,0},{4,6},{6,4},{8,10},{10,8},{12,14},{14,12},{1,3},{3,1},... | collective-permute-start | bytes 589832 | tf_op jit(solution)/shard_map/ppermute | solution.py:352
  18.0 4.4 %collective-permute-done.5.mine_ref = bf16[64,1024]{1,0:T(8,128)(2,1)S(1)} collective-permute-done((bf16[64,1024]{1,0:T(8,128)(2,1)S(1)}, bf16[64,1024]{1,0:T(8,128)(2,1)S(1)}, u32[]{:S(2)}, u32[]{:S(2)}) %collective-permute-start.5) | collective-permute-done | bytes 131104 | tf_op jit(solution)/shard_map/ppermute | solution.py:352
  22.5 0.9 %shard_map.87 = (bf16[512,256]{1,0:T(8,128)(2,1)S(1)}, f32[128,512]{1,0:T(8,128)S(1)}) custom-call(s32[2]{0:T(128)S(1)} %pad_add_fusion.place_ref, bf16[64,1792]{1,0:T(8,128)(2,1)S(1)} %get-tuple-element.35.mine_ref.kept_ref, bf16[64,1792]{1,0:T(8,128)(2,1)S(1)} %collective-permute-done.4.other_ref.kept2_ref, ...), custom_call_target="tpu_custom_call" | custom-call | tf_op jit(solution)/shard_map/pallas_call | solution.py:411
  23.4 0.4 %collective-permute-done.6.other_ref = bf16[64,1024]{1,0:T(8,128)(2,1)S(1)} collective-permute-done((bf16[64,1024]{1,0:T(8,128)(2,1)S(1)}, bf16[64,1024]{1,0:T(8,128)(2,1)S(1)}, u32[]{:S(2)}, u32[]{:S(2)}) %collective-permute-start.6) | collective-permute-done | bytes 131104 | tf_op jit(solution)/shard_map/ppermute | solution.py:355
  23.8 1.1 %shard_map.88 = (bf16[512,256]{1,0:T(8,128)(2,1)S(1)}, bf16[128,512]{1,0:T(8,128)(2,1)S(1)}, bf16[128,512]{1,0:T(8,128)(2,1)S(1)}, f32[128,128]{1,0:T(8,128)S(1)}) custom-call(s32[2]{0:T(128)S(1)} %pad_add_fusion.place_ref, bf16[64,1792]{1,0:T(8,128)(2,1)S(1)} %get-tuple-element.35.mine_ref.kept_ref, ...), custom_call_target="tpu_custom_call" | custom-call | tf_op jit(solution)/shard_map/pallas_call | solution.py:418
  24.9 1.6 %shard_map.89 = (f32[128,768]{1,0:T(8,128)S(1)}, f32[128,768]{1,0:T(8,128)S(1)}, f32[128,128]{1,0:T(8,128)S(1)}) custom-call(s32[2]{0:T(128)S(1)} %pad_add_fusion.place_ref, f32[128,128]{1,0:T(8,128)S(1)} %get-tuple-element.27.gene_ref, f32[128,128]{1,0:T(8,128)S(1)} %get-tuple-element.39.power_ref, bf16[512,256]{1,0:T(8,128)(2,1)S(1)} %get-tuple-element.40.turned_ref, ...), custom_call_target="tpu_custom_call" | custom-call | tf_op jit(solution)/shard_map/pallas_call | solution.py:424
  26.5 0.2 collective-permute-start.10
  26.8 0.8 %shard_map.90 = f32[128,128]{1,0:T(8,128)S(1)} custom-call(s32[2]{0:T(128)S(1)} %pad_add_fusion.place_ref, f32[128,128]{1,0:T(8,128)S(1)} %get-tuple-element.27.gene_ref, f32[128,128]{1,0:T(8,128)S(1)} %get-tuple-element.39.power_ref, f32[128,768]{1,0:T(8,128)S(1)} %get-tuple-element.44.cross_ref, f32[128,768]{1,0:T(8,128)S(1)} %get-tuple-element.45.product_ref), custom_call_target="tpu_custom_call" | custom-call | tf_op jit(solution)/shard_map/pallas_call | solution.py:430
  27.5 0.3 %collective-permute-done.10 = f32[128,128]{1,0:T(8,128)S(1)} collective-permute-done((f32[128,128]{1,0:T(8,128)S(1)}, f32[128,128]{1,0:T(8,128)S(1)}, u32[]{:S(2)}, u32[]{:S(2)}) %collective-permute-start.10) | collective-permute-done | bytes 65568 | tf_op jit(solution)/shard_map/ppermute | solution.py:355
  27.9 0.6 %add.3 = f32[128,128]{1,0:T(8,128)} add(f32[128,128]{1,0:T(8,128)S(1)} %shard_map.90, f32[128,128]{1,0:T(8,128)S(1)} %collective-permute-done.10) | non-fusion elementwise | flops 16384 | bytes 196608 | tf_op jit(solution)/shard_map/add | solution.py:433
  (21 shorter events, 0.3 us)
Async XLA Ops:
  1.8 7.3 %collective-permute-start = (bf16[64,512]{1,0:T(8,128)(2,1)S(1)}, bf16[64,512]{1,0:T(8,128)(2,1)S(1)}, u32[]{:S(2)}, u32[]{:S(2)}) collective-permute-start(bf16[64,512]{1,0:T(8,128)(2,1)S(1)} %get-tuple-element.28.ahead_ref), channel_id=1, source_target_pairs={{0,2},{2,0},{4,6},{6,4},{8,10},{10,8},{12,14},{14,12},{1,3},{3,1},... | collective-permute-start | bytes 196616 | tf_op jit(solution)/shard_map/ppermute | solution.py:352
  4.8 6.9 %collective-permute-start.3 = (bf16[64,768]{1,0:T(8,128)(2,1)S(1)}, bf16[64,768]{1,0:T(8,128)(2,1)S(1)}, u32[]{:S(2)}, u32[]{:S(2)}) collective-permute-start(bf16[64,768]{1,0:T(8,128)(2,1)S(1)} %get-tuple-element.33.d0_ref.refs_0_), channel_id=1, source_target_pairs={{0,8},{2,10},{4,12},{6,14},{8,0},{10,2},{12,4},{14,6},{1,9},{3,11}... | collective-permute-start | bytes 294920 | tf_op jit(solution)/shard_map/ppermute | solution.py:352
  7.5 8.2 %collective-permute-start.2 = (bf16[64,1024]{1,0:T(8,128)(2,1)S(1)}, bf16[64,1024]{1,0:T(8,128)(2,1)S(1)}, u32[]{:S(2)}, u32[]{:S(2)}) collective-permute-start(bf16[64,1024]{1,0:T(8,128)(2,1)S(1)} %pad_maximum_fusion.1), channel_id=1, source_target_pairs={{0,4},{2,6},{4,0},{6,2},{8,12},{10,14},{12,8},{14,10},{1,5},{3,7},... | collective-permute-start | bytes 393224 | tf_op jit(solution)/shard_map/ppermute | solution.py:352
  9.1 7.3 %collective-permute-start.1 = (bf16[64,768]{1,0:T(8,128)(2,1)S(1)}, bf16[64,768]{1,0:T(8,128)(2,1)S(1)}, u32[]{:S(2)}, u32[]{:S(2)}) collective-permute-start(bf16[64,768]{1,0:T(8,128)(2,1)S(1)} %shard_map.84.after_any), channel_id=1, source_target_pairs={{0,8},{2,10},{4,12},{6,14},{8,0},{10,2},{12,4},{14,6},{1,9},{3,11}... | collective-permute-start | bytes 294920 | tf_op jit(solution)/shard_map/ppermute | solution.py:352
  11.7 1.6 %copy-start.2 = (s32[1024]{0:T(1024)S(1)}, s32[1024]{0:T(1024)}, u32[]{:S(2)}) copy-start(s32[1024]{0:T(1024)} %param.14) | copy-start | bytes 12292
  11.8 5.7 %collective-permute-start.8 = (bf16[64,768]{1,0:T(8,128)(2,1)S(1)}, bf16[64,768]{1,0:T(8,128)(2,1)S(1)}, u32[]{:S(2)}, u32[]{:S(2)}) collective-permute-start(bf16[64,768]{1,0:T(8,128)(2,1)S(1)} %get-tuple-element.34.far_any), channel_id=1, source_target_pairs={{0,4},{2,6},{4,0},{6,2},{8,12},{10,14},{12,8},{14,10},{1,5},{3,7},... | collective-permute-start | bytes 294920 | tf_op jit(solution)/shard_map/ppermute | solution.py:352
  13.4 0.7 %copy-start.1 = (s32[1024]{0:T(1024)S(1)}, s32[1024]{0:T(1024)}, u32[]{:S(2)}) copy-start(s32[1024]{0:T(1024)} %param.13) | copy-start | bytes 12292
  13.4 0.7 %copy-start = (f32[1024]{0:T(1024)S(1)}, f32[1024]{0:T(1024)}, u32[]{:S(2)}) copy-start(f32[1024]{0:T(1024)} %param.12) | copy-start | bytes 12292
  13.4 0.7 %copy-start.3 = (f32[256]{0:T(256)S(1)}, f32[256]{0:T(256)}, u32[]{:S(2)}) copy-start(f32[256]{0:T(256)} %param.9) | copy-start | bytes 3076
  14.2 8.2 %collective-permute-start.7 = (bf16[64,1536]{1,0:T(8,128)(2,1)S(1)}, bf16[64,1536]{1,0:T(8,128)(2,1)S(1)}, u32[]{:S(2)}, u32[]{:S(2)}) collective-permute-start(bf16[64,1536]{1,0:T(8,128)(2,1)S(1)} %get-tuple-element.37), channel_id=1, source_target_pairs={{0,2},{2,0},{4,6},{6,4},{8,10},{10,8},{12,14},{14,12},{1,3},{3,1},... | collective-permute-start | bytes 589832 | tf_op jit(solution)/shard_map/ppermute | solution.py:352
  16.5 6.0 %collective-permute-start.4 = (bf16[64,1792]{1,0:T(8,128)(2,1)S(1)}, bf16[64,1792]{1,0:T(8,128)(2,1)S(1)}, u32[]{:S(2)}, u32[]{:S(2)}) collective-permute-start(bf16[64,1792]{1,0:T(8,128)(2,1)S(1)} %get-tuple-element.35.mine_ref.kept_ref), channel_id=1, source_target_pairs={{0,1},{1,0},{2,3},{3,2},{4,5},{5,4},{6,7},{7,6},{8,9},{9,8},{10,11... | collective-permute-start | bytes 688136 | tf_op jit(solution)/shard_map/ppermute | solution.py:355
  16.5 5.9 %collective-permute-start.5 = (bf16[64,1024]{1,0:T(8,128)(2,1)S(1)}, bf16[64,1024]{1,0:T(8,128)(2,1)S(1)}, u32[]{:S(2)}, u32[]{:S(2)}) collective-permute-start(bf16[64,1024]{1,0:T(8,128)(2,1)S(1)} %get-tuple-element.36), channel_id=1, source_target_pairs={{0,4},{2,6},{4,0},{6,2},{8,12},{10,14},{12,8},{14,10},{1,5},{3,7},... | collective-permute-start | bytes 393224 | tf_op jit(solution)/shard_map/ppermute | solution.py:352
  17.5 7.4 %collective-permute-start.9 = (bf16[64,1536]{1,0:T(8,128)(2,1)S(1)}, bf16[64,1536]{1,0:T(8,128)(2,1)S(1)}, u32[]{:S(2)}, u32[]{:S(2)}) collective-permute-start(bf16[64,1536]{1,0:T(8,128)(2,1)S(1)} %pad_maximum_fusion), channel_id=1, source_target_pairs={{0,2},{2,0},{4,6},{6,4},{8,10},{10,8},{12,14},{14,12},{1,3},{3,1},... | collective-permute-start | bytes 589832 | tf_op jit(solution)/shard_map/ppermute | solution.py:352
  22.5 1.3 %collective-permute-start.6 = (bf16[64,1024]{1,0:T(8,128)(2,1)S(1)}, bf16[64,1024]{1,0:T(8,128)(2,1)S(1)}, u32[]{:S(2)}, u32[]{:S(2)}) collective-permute-start(bf16[64,1024]{1,0:T(8,128)(2,1)S(1)} %collective-permute-done.5.mine_ref), channel_id=1, source_target_pairs={{0,1},{1,0},{2,3},{3,2},{4,5},{5,4},{6,7},{7,6},{8,9},{9,8},{10,11... | collective-permute-start | bytes 393224 | tf_op jit(solution)/shard_map/ppermute | solution.py:355
  26.5 1.3 %collective-permute-start.10 = (f32[128,128]{1,0:T(8,128)S(1)}, f32[128,128]{1,0:T(8,128)S(1)}, u32[]{:S(2)}, u32[]{:S(2)}) collective-permute-start(f32[128,128]{1,0:T(8,128)S(1)} %get-tuple-element.46), channel_id=1, source_target_pairs={{0,1},{1,0},{2,3},{3,2},{4,5},{5,4},{6,7},{7,6},{8,9},{9,8},{10,11... | collective-permute-start | bytes 196616 | tf_op jit(solution)/shard_map/ppermute | solution.py:355

commit v17 on v16

--- a/solution.py
+++ b/solution.py
@@ -103,9 +103,9 @@
 
 
 def route_kernel(
-    place_ref, owner_any, expr_any, vecs_any, dose_any,
-    ahead_ref, e46_ref, e2_ref, e0_ref, half_ref, bucket_ref,
-    owner_ref, expr_ref, sems,
+    place_ref, owner_any, delta_any, start_any, valid_any, vals_any, vecs_any, expr_any, dose_any,
+    ahead_ref, e46_ref, e2_ref, e0_ref, gene_ref, terms_ref, half_ref,
+    owner_ref, delta_ref, start_ref, valid_ref, vals_ref, expr_ref, sems,
 ):
     row, core = place_ref[0], place_ref[1]
     half = vecs_any.shape[1]
@@ -114,6 +114,10 @@
     pairs = (
         (owner_any, owner_ref),
         (expr_any.at[pl.ds(pl.multiple_of(core * part, part), part)], expr_ref),
+        (delta_any, delta_ref),
+        (start_any, start_ref),
+        (valid_any, valid_ref),
+        (vals_any, vals_ref),
         (vecs_any, ahead_ref.at[:, pl.ds(0, half)]),
         (dose_any.at[:, pl.ds(pl.multiple_of(core * variants, LANES), variants)], half_ref),
     )
@@ -127,6 +131,8 @@
     )
     before = before.astype(bf16)
     slot = lax.broadcasted_iota(jnp.int32, (LANES, LANES), 0)
+    own_slot = lax.broadcasted_iota(jnp.int32, (capacity, LANES), 0)
+    lane = lax.broadcasted_iota(jnp.int32, (capacity, LANES), 1)
     copies[0].wait()
     owner = owner_ref[...]
     rank = jnp.zeros(owner.shape, f32)
@@ -134,8 +140,8 @@
         same = (owner == o).astype(f32)
         rank += same * jnp.dot(same.astype(bf16), before, preferred_element_type=f32)
     bucket = (owner ^ row) * capacity + rank.astype(jnp.int32)
-    bucket_ref[...] = bucket
-    copies[1].wait()
+    for copy in copies[1:]:
+        copy.wait()
     sorted_slices = []
     for s in range(slices):
         here = bucket[s : s + 1, :]
@@ -143,6 +149,18 @@
         sorted_slices.append(
             lax.dot_general(pick, expr_ref[:, s * LANES : (s + 1) * LANES], NT, preferred_element_type=f32)
         )
+        mine = (own_slot == here).astype(f32)
+        figures = jnp.zeros((capacity, LANES), f32)
+        for i, ref in enumerate((delta_ref, start_ref, valid_ref)):
+            line = ref[s : s + 1, :].astype(f32)
+            figures = jnp.where(lane == i, jnp.sum(mine * line, axis=1, keepdims=True), figures)
+        gene_ref[s * capacity : (s + 1) * capacity, :] = figures
+    vals = vals_ref[...]
+    high = vals.astype(bf16).astype(f32)
+    middle = (vals - high).astype(bf16).astype(f32)
+    term = lax.broadcasted_iota(jnp.int32, terms_ref.shape, 0)
+    terms = jnp.where(term == 0, high, jnp.where(term == 1, middle, jnp.where(term == 2, vals - high - middle, 0.0)))
+    terms_ref[...] = terms.astype(bf16)
     left, right = slice(0, LANES), slice(LANES, 2 * LANES)
     upper, lower = slice(0, part), slice(part, 2 * part)
     targets = {
@@ -158,28 +176,6 @@
     for m, (ref, down, side) in targets.items():
         block = jnp.concatenate([x[m * capacity : (m + 1) * capacity, :] for x in sorted_slices], axis=0)
         ref[down, side] = block.T.astype(bf16)
-    for copy in copies[2:]:
-        copy.wait()
-
-
-def gene_kernel(bucket_ref, delta_ref, start_ref, valid_ref, vals_ref, gene_ref, terms_ref):
-    slices = bucket_ref.shape[0]
-    capacity = LANES // slices
-    own_slot = lax.broadcasted_iota(jnp.int32, (capacity, LANES), 0)
-    lane = lax.broadcasted_iota(jnp.int32, (capacity, LANES), 1)
-    for s in range(slices):
-        mine = (own_slot == bucket_ref[s : s + 1, :]).astype(f32)
-        figures = jnp.zeros((capacity, LANES), f32)
-        for i, ref in enumerate((delta_ref, start_ref, valid_ref)):
-            line = ref[s : s + 1, :].astype(f32)
-            figures = jnp.where(lane == i, jnp.sum(mine * line, axis=1, keepdims=True), figures)
-        gene_ref[s * capacity : (s + 1) * capacity, :] = figures
-    vals = vals_ref[...]
-    high = vals.astype(bf16).astype(f32)
-    middle = (vals - high).astype(bf16).astype(f32)
-    term = lax.broadcasted_iota(jnp.int32, terms_ref.shape, 0)
-    terms = jnp.where(term == 0, high, jnp.where(term == 1, middle, jnp.where(term == 2, vals - high - middle, 0.0)))
-    terms_ref[...] = terms.astype(bf16)
 
 
 def second_kernel(ahead_ref, r1_ref, e46_ref, out_ref):
@@ -354,36 +350,37 @@
     def other_core(x):
         return lax.ppermute(x, "col", [(0, 1), (1, 0)])
 
-    ahead, e46, e2, e0, d0, bucket = call(
+    ahead, e46, e2, e0, gene, terms, d0 = call(
         route_kernel,
         [
             ((panel, half + 2 * LANES), bf16),
             ((part, 2 * LANES), bf16),
             ((part, LANES), bf16),
             ((part, LANES), bf16),
+            ((LANES, LANES), f32),
+            ((16, half), bf16),
             ((panel, variants), bf16),
-            ((rows, LANES), jnp.int32),
         ],
-        5,
-        scratch=[
-            pltpu.VMEM((rows, LANES), jnp.int32),
-            pltpu.VMEM((part, expression.shape[1]), bf16),
-            pltpu.SemaphoreType.DMA((4,)),
-        ],
-        anywhere=4,
+        9,
+        scratch=[pltpu.VMEM((rows, LANES), kind) for kind in (jnp.int32, f32, jnp.int32, jnp.int32)]
+        + [pltpu.VMEM((1, half), f32), pltpu.VMEM((part, expression.shape[1]), bf16), pltpu.SemaphoreType.DMA((8,))],
+        anywhere=8,
+        limit=VMEM_LIMIT,
     )(
         place,
         *[
             pltpu.with_memory_space_constraint(x, pltpu.HBM)
-            for x in (gene_owner.reshape(rows, LANES), expression, eigvecs, dosage)
+            for x in (
+                gene_owner.reshape(rows, LANES),
+                delta.reshape(rows, LANES),
+                window_start.reshape(rows, LANES),
+                window_valid.reshape(rows, LANES),
+                eigvals[None, :],
+                eigvecs,
+                expression,
+                dosage,
+            )
         ],
-    )
-    gene, terms = call(gene_kernel, [((LANES, LANES), f32), ((16, half), bf16)], 5, smem=0)(
-        bucket,
-        delta.reshape(rows, LANES),
-        window_start.reshape(rows, LANES),
-        window_valid.reshape(rows, LANES),
-        eigvals[None, :],
     )
     r1 = swap(ahead, 1)
     d4 = swap(d0, 4)

time: 28.7 us -> 28.9 us (level)
  waiting for transfers between devices: 8.72 us -> 9.63 us
  local copies, waits for them, and re-layouts: 0.72 us -> 0.01 us
    ppermute x8, waiting for transfers between devices: 8 us -> 8.9 us  [swap(): return lax.ppermute(x, 'row', [(i, i ^ m) for i in range(rows)])]
    unnamed x8 -> x0, local copies, waits for them, and re-layouts: 0.71 us -> none
where the time goes in v17:
time: 28.9 us; the launch traced here: 28.7 us
  starting transfers between devices  11.8 us (41%)
  waiting for transfers between devices  9.63 us (33%)
  Pallas kernels  6.41 us (22%)
  other arithmetic  0.74 us (3%)
    ppermute x8, starting transfers between devices, swap(): return lax.ppermute(x, 'row', [(i, i ^ m) for i in range(rows)])  11.6 us
    ppermute x8, waiting for transfers between devices, swap(): return lax.ppermute(x, 'row', [(i, i ^ m) for i in range(rows)])  8.9 us
    pallas_call x1, Pallas kernels, near_body(): call(route_kernel, [((panel, half + 2 * LANES), bf16), ((part, 2 * LANES)...  1.93 us
    pallas_call x1, Pallas kernels, near_body(): call(score_kernel, [((LANES, variants), f32)] * 2 + [((LANES, LANES), f32...  1.64 us
    pallas_call x1, Pallas kernels, near_body(): call(weight_kernel, [shape, ((LANES, 2 * half), bf16), ((LANES, 2 * half)...  1.08 us
    pallas_call x1, Pallas kernels, near_body(): call(half_kernel, [shape, ((LANES, 2 * half), f32)], 4, scratch=[pltpu.VM...  0.93 us
    pallas_call x1, Pallas kernels, near_body(): call(functools.partial(keep_kernel, samples=samples), [((LANES, LANES), f...  0.78 us
    ppermute x3, waiting for transfers between devices, other_core(): return lax.ppermute(x, 'col', [(0, 1), (1, 0)])  0.73 us
  transfers between devices with their start and end apart: 11, of which 7 were waited for; matrix products, arithmetic and copies ran while one was open for 0% of the time, Pallas kernels for 10%

profile of v17, /device:TPU:0, one launch (start us, length us, event | category | flops | bytes accessed | tf_op | source)
XLA Modules:
  0.0 28.7 jit_solution(9124778809631571220)
XLA Ops:
  0.0 0.1 pad_add_fusion.place_ref
  0.1 1.9 %shard_map.82 = (bf16[64,512]{1,0:T(8,128)(2,1)S(1)}, bf16[32,256]{1,0:T(8,128)(2,1)S(1)}, bf16[32,128]{1,0:T(8,128)(2,1)S(1)}, bf16[32,128]{1,0:T(8,128)(2,1)S(...) custom-call(s32[2]{0:T(128)S(1)} %pad_add_fusion.place_ref, ...), custom_call_target="tpu_custom_call" | custom-call | tf_op jit(solution)/shard_map/pallas_call | solution.py:353
  2.0 3.0 %collective-permute-start = (bf16[64,512]{1,0:T(8,128)(2,1)S(1)}, bf16[64,512]{1,0:T(8,128)(2,1)S(1)}, u32[]{:S(2)}, u32[]{:S(2)}) collective-permute-start(bf16[64,512]{1,0:T(8,128)(2,1)S(1)} %get-tuple-element.26.ahead_ref), channel_id=1, source_target_pairs={{0,2},{2,0},{4,6},{6,4},{8,10},{10,8},{12,14},{14,12},{1,3},{3,1},... | collective-permute-start | bytes 196616 | tf_op jit(solution)/shard_map/ppermute | solution.py:348
  5.0 2.6 %collective-permute-start.3 = (bf16[64,768]{1,0:T(8,128)(2,1)S(1)}, bf16[64,768]{1,0:T(8,128)(2,1)S(1)}, u32[]{:S(2)}, u32[]{:S(2)}) collective-permute-start(bf16[64,768]{1,0:T(8,128)(2,1)S(1)} %get-tuple-element.31.d0_ref.refs_0_), channel_id=1, source_target_pairs={{0,8},{2,10},{4,12},{6,14},{8,0},{10,2},{12,4},{14,6},{1,9},{3,11}... | collective-permute-start | bytes 294920 | tf_op jit(solution)/shard_map/ppermute | solution.py:348
  7.7 1.6 %collective-permute-start.2 = (bf16[64,1024]{1,0:T(8,128)(2,1)S(1)}, bf16[64,1024]{1,0:T(8,128)(2,1)S(1)}, u32[]{:S(2)}, u32[]{:S(2)}) collective-permute-start(bf16[64,1024]{1,0:T(8,128)(2,1)S(1)} %pad_maximum_fusion.1), channel_id=1, source_target_pairs={{0,4},{2,6},{4,0},{6,2},{8,12},{10,14},{12,8},{14,10},{1,5},{3,7},... | collective-permute-start | bytes 393224 | tf_op jit(solution)/shard_map/ppermute | solution.py:348
  9.3 1.1 %collective-permute-start.1 = (bf16[64,768]{1,0:T(8,128)(2,1)S(1)}, bf16[64,768]{1,0:T(8,128)(2,1)S(1)}, u32[]{:S(2)}, u32[]{:S(2)}) collective-permute-start(bf16[64,768]{1,0:T(8,128)(2,1)S(1)} %shard_map.83.after_any), channel_id=1, source_target_pairs={{0,8},{2,10},{4,12},{6,14},{8,0},{10,2},{12,4},{14,6},{1,9},{3,11}... | collective-permute-start | bytes 294920 | tf_op jit(solution)/shard_map/ppermute | solution.py:348
  10.5 1.5 %collective-permute-done.3.d4_ref.refs_2_ = bf16[64,768]{1,0:T(8,128)(2,1)S(1)} collective-permute-done((bf16[64,768]{1,0:T(8,128)(2,1)S(1)}, bf16[64,768]{1,0:T(8,128)(2,1)S(1)}, u32[]{:S(2)}, u32[]{:S(2)}) %collective-permute-start.3) | collective-permute-done | bytes 98336 | tf_op jit(solution)/shard_map/ppermute | solution.py:348
  11.9 1.6 %collective-permute-start.8 = (bf16[64,768]{1,0:T(8,128)(2,1)S(1)}, bf16[64,768]{1,0:T(8,128)(2,1)S(1)}, u32[]{:S(2)}, u32[]{:S(2)}) collective-permute-start(bf16[64,768]{1,0:T(8,128)(2,1)S(1)} %get-tuple-element.32.far_any), channel_id=1, source_target_pairs={{0,4},{2,6},{4,0},{6,2},{8,12},{10,14},{12,8},{14,10},{1,5},{3,7},... | collective-permute-start | bytes 294920 | tf_op jit(solution)/shard_map/ppermute | solution.py:348
  13.6 0.5 %collective-permute-start.7 = (bf16[64,1536]{1,0:T(8,128)(2,1)S(1)}, bf16[64,1536]{1,0:T(8,128)(2,1)S(1)}, u32[]{:S(2)}, u32[]{:S(2)}) collective-permute-start(bf16[64,1536]{1,0:T(8,128)(2,1)S(1)} %get-tuple-element.35), channel_id=1, source_target_pairs={{0,2},{2,0},{4,6},{6,4},{8,10},{10,8},{12,14},{14,12},{1,3},{3,1},... | collective-permute-start | bytes 589832 | tf_op jit(solution)/shard_map/ppermute | solution.py:348
  14.1 1.8 %collective-permute-done.2.d2_ref.refs_3_ = bf16[64,1024]{1,0:T(8,128)(2,1)S(1)} collective-permute-done((bf16[64,1024]{1,0:T(8,128)(2,1)S(1)}, bf16[64,1024]{1,0:T(8,128)(2,1)S(1)}, u32[]{:S(2)}, u32[]{:S(2)}) %collective-permute-start.2) | collective-permute-done | bytes 131104 | tf_op jit(solution)/shard_map/ppermute | solution.py:348
  15.9 0.8 %collective-permute-done.1.r4_ref = bf16[64,768]{1,0:T(8,128)(2,1)S(1)} collective-permute-done((bf16[64,768]{1,0:T(8,128)(2,1)S(1)}, bf16[64,768]{1,0:T(8,128)(2,1)S(1)}, u32[]{:S(2)}, u32[]{:S(2)}) %collective-permute-start.1) | collective-permute-done | bytes 98336 | tf_op jit(solution)/shard_map/ppermute | solution.py:348
  16.7 0.1 collective-permute-start.4
  16.7 0.5 %collective-permute-start.5 = (bf16[64,1024]{1,0:T(8,128)(2,1)S(1)}, bf16[64,1024]{1,0:T(8,128)(2,1)S(1)}, u32[]{:S(2)}, u32[]{:S(2)}) collective-permute-start(bf16[64,1024]{1,0:T(8,128)(2,1)S(1)} %get-tuple-element.34), channel_id=1, source_target_pairs={{0,4},{2,6},{4,0},{6,2},{8,12},{10,14},{12,8},{14,10},{1,5},{3,7},... | collective-permute-start | bytes 393224 | tf_op jit(solution)/shard_map/ppermute | solution.py:348
  17.2 0.4 %collective-permute-done.8.refs_5_ = bf16[64,768]{1,0:T(8,128)(2,1)S(1)} collective-permute-done((bf16[64,768]{1,0:T(8,128)(2,1)S(1)}, bf16[64,768]{1,0:T(8,128)(2,1)S(1)}, u32[]{:S(2)}, u32[]{:S(2)}) %collective-permute-start.8) | collective-permute-done | bytes 98336 | tf_op jit(solution)/shard_map/ppermute | solution.py:348
  17.7 0.5 %collective-permute-start.9 = (bf16[64,1536]{1,0:T(8,128)(2,1)S(1)}, bf16[64,1536]{1,0:T(8,128)(2,1)S(1)}, u32[]{:S(2)}, u32[]{:S(2)}) collective-permute-start(bf16[64,1536]{1,0:T(8,128)(2,1)S(1)} %pad_maximum_fusion), channel_id=1, source_target_pairs={{0,2},{2,0},{4,6},{6,4},{8,10},{10,8},{12,14},{14,12},{1,3},{3,1},... | collective-permute-start | bytes 589832 | tf_op jit(solution)/shard_map/ppermute | solution.py:348
  18.2 4.4 %collective-permute-done.5.mine_ref = bf16[64,1024]{1,0:T(8,128)(2,1)S(1)} collective-permute-done((bf16[64,1024]{1,0:T(8,128)(2,1)S(1)}, bf16[64,1024]{1,0:T(8,128)(2,1)S(1)}, u32[]{:S(2)}, u32[]{:S(2)}) %collective-permute-start.5) | collective-permute-done | bytes 131104 | tf_op jit(solution)/shard_map/ppermute | solution.py:348
  22.7 0.9 %shard_map.86 = (bf16[512,256]{1,0:T(8,128)(2,1)S(1)}, f32[128,512]{1,0:T(8,128)S(1)}) custom-call(s32[2]{0:T(128)S(1)} %pad_add_fusion.place_ref, bf16[64,1792]{1,0:T(8,128)(2,1)S(1)} %get-tuple-element.33.mine_ref.kept_ref, bf16[64,1792]{1,0:T(8,128)(2,1)S(1)} %collective-permute-done.4.other_ref.kept2_ref, ...), custom_call_target="tpu_custom_call" | custom-call | tf_op jit(solution)/shard_map/pallas_call | solution.py:408
  23.6 0.4 %collective-permute-done.6.other_ref = bf16[64,1024]{1,0:T(8,128)(2,1)S(1)} collective-permute-done((bf16[64,1024]{1,0:T(8,128)(2,1)S(1)}, bf16[64,1024]{1,0:T(8,128)(2,1)S(1)}, u32[]{:S(2)}, u32[]{:S(2)}) %collective-permute-start.6) | collective-permute-done | bytes 131104 | tf_op jit(solution)/shard_map/ppermute | solution.py:351
  24.0 1.1 %shard_map.87 = (bf16[512,256]{1,0:T(8,128)(2,1)S(1)}, bf16[128,512]{1,0:T(8,128)(2,1)S(1)}, bf16[128,512]{1,0:T(8,128)(2,1)S(1)}, f32[128,128]{1,0:T(8,128)S(1)}) custom-call(s32[2]{0:T(128)S(1)} %pad_add_fusion.place_ref, bf16[64,1792]{1,0:T(8,128)(2,1)S(1)} %get-tuple-element.33.mine_ref.kept_ref, ...), custom_call_target="tpu_custom_call" | custom-call | tf_op jit(solution)/shard_map/pallas_call | solution.py:415
  25.1 1.6 %shard_map.88 = (f32[128,768]{1,0:T(8,128)S(1)}, f32[128,768]{1,0:T(8,128)S(1)}, f32[128,128]{1,0:T(8,128)S(1)}) custom-call(s32[2]{0:T(128)S(1)} %pad_add_fusion.place_ref, f32[128,128]{1,0:T(8,128)S(1)} %get-tuple-element.25.gene_ref, f32[128,128]{1,0:T(8,128)S(1)} %get-tuple-element.37.power_ref, bf16[512,256]{1,0:T(8,128)(2,1)S(1)} %get-tuple-element.38.turned_ref, ...), custom_call_target="tpu_custom_call" | custom-call | tf_op jit(solution)/shard_map/pallas_call | solution.py:421
  26.7 0.2 collective-permute-start.10
  27.0 0.8 %shard_map.89 = f32[128,128]{1,0:T(8,128)S(1)} custom-call(s32[2]{0:T(128)S(1)} %pad_add_fusion.place_ref, f32[128,128]{1,0:T(8,128)S(1)} %get-tuple-element.25.gene_ref, f32[128,128]{1,0:T(8,128)S(1)} %get-tuple-element.37.power_ref, f32[128,768]{1,0:T(8,128)S(1)} %get-tuple-element.42.cross_ref, f32[128,768]{1,0:T(8,128)S(1)} %get-tuple-element.43.product_ref), custom_call_target="tpu_custom_call" | custom-call | tf_op jit(solution)/shard_map/pallas_call | solution.py:427
  27.7 0.3 %collective-permute-done.10 = f32[128,128]{1,0:T(8,128)S(1)} collective-permute-done((f32[128,128]{1,0:T(8,128)S(1)}, f32[128,128]{1,0:T(8,128)S(1)}, u32[]{:S(2)}, u32[]{:S(2)}) %collective-permute-start.10) | collective-permute-done | bytes 65568 | tf_op jit(solution)/shard_map/ppermute | solution.py:351
  28.1 0.6 %add.3 = f32[128,128]{1,0:T(8,128)} add(f32[128,128]{1,0:T(8,128)S(1)} %shard_map.89, f32[128,128]{1,0:T(8,128)S(1)} %collective-permute-done.10) | non-fusion elementwise | flops 16384 | bytes 196608 | tf_op jit(solution)/shard_map/add | solution.py:430
  (12 shorter events, 0.1 us)
Async XLA Ops:
  2.0 7.3 %collective-permute-start = (bf16[64,512]{1,0:T(8,128)(2,1)S(1)}, bf16[64,512]{1,0:T(8,128)(2,1)S(1)}, u32[]{:S(2)}, u32[]{:S(2)}) collective-permute-start(bf16[64,512]{1,0:T(8,128)(2,1)S(1)} %get-tuple-element.26.ahead_ref), channel_id=1, source_target_pairs={{0,2},{2,0},{4,6},{6,4},{8,10},{10,8},{12,14},{14,12},{1,3},{3,1},... | collective-permute-start | bytes 196616 | tf_op jit(solution)/shard_map/ppermute | solution.py:348
  5.0 6.9 %collective-permute-start.3 = (bf16[64,768]{1,0:T(8,128)(2,1)S(1)}, bf16[64,768]{1,0:T(8,128)(2,1)S(1)}, u32[]{:S(2)}, u32[]{:S(2)}) collective-permute-start(bf16[64,768]{1,0:T(8,128)(2,1)S(1)} %get-tuple-element.31.d0_ref.refs_0_), channel_id=1, source_target_pairs={{0,8},{2,10},{4,12},{6,14},{8,0},{10,2},{12,4},{14,6},{1,9},{3,11}... | collective-permute-start | bytes 294920 | tf_op jit(solution)/shard_map/ppermute | solution.py:348
  7.7 8.2 %collective-permute-start.2 = (bf16[64,1024]{1,0:T(8,128)(2,1)S(1)}, bf16[64,1024]{1,0:T(8,128)(2,1)S(1)}, u32[]{:S(2)}, u32[]{:S(2)}) collective-permute-start(bf16[64,1024]{1,0:T(8,128)(2,1)S(1)} %pad_maximum_fusion.1), channel_id=1, source_target_pairs={{0,4},{2,6},{4,0},{6,2},{8,12},{10,14},{12,8},{14,10},{1,5},{3,7},... | collective-permute-start | bytes 393224 | tf_op jit(solution)/shard_map/ppermute | solution.py:348
  9.3 7.3 %collective-permute-start.1 = (bf16[64,768]{1,0:T(8,128)(2,1)S(1)}, bf16[64,768]{1,0:T(8,128)(2,1)S(1)}, u32[]{:S(2)}, u32[]{:S(2)}) collective-permute-start(bf16[64,768]{1,0:T(8,128)(2,1)S(1)} %shard_map.83.after_any), channel_id=1, source_target_pairs={{0,8},{2,10},{4,12},{6,14},{8,0},{10,2},{12,4},{14,6},{1,9},{3,11}... | collective-permute-start | bytes 294920 | tf_op jit(solution)/shard_map/ppermute | solution.py:348
  11.9 5.7 %collective-permute-start.8 = (bf16[64,768]{1,0:T(8,128)(2,1)S(1)}, bf16[64,768]{1,0:T(8,128)(2,1)S(1)}, u32[]{:S(2)}, u32[]{:S(2)}) collective-permute-start(bf16[64,768]{1,0:T(8,128)(2,1)S(1)} %get-tuple-element.32.far_any), channel_id=1, source_target_pairs={{0,4},{2,6},{4,0},{6,2},{8,12},{10,14},{12,8},{14,10},{1,5},{3,7},... | collective-permute-start | bytes 294920 | tf_op jit(solution)/shard_map/ppermute | solution.py:348
  13.6 9.1 %collective-permute-start.7 = (bf16[64,1536]{1,0:T(8,128)(2,1)S(1)}, bf16[64,1536]{1,0:T(8,128)(2,1)S(1)}, u32[]{:S(2)}, u32[]{:S(2)}) collective-permute-start(bf16[64,1536]{1,0:T(8,128)(2,1)S(1)} %get-tuple-element.35), channel_id=1, source_target_pairs={{0,2},{2,0},{4,6},{6,4},{8,10},{10,8},{12,14},{14,12},{1,3},{3,1},... | collective-permute-start | bytes 589832 | tf_op jit(solution)/shard_map/ppermute | solution.py:348
  16.7 6.0 %collective-permute-start.4 = (bf16[64,1792]{1,0:T(8,128)(2,1)S(1)}, bf16[64,1792]{1,0:T(8,128)(2,1)S(1)}, u32[]{:S(2)}, u32[]{:S(2)}) collective-permute-start(bf16[64,1792]{1,0:T(8,128)(2,1)S(1)} %get-tuple-element.33.mine_ref.kept_ref), channel_id=1, source_target_pairs={{0,1},{1,0},{2,3},{3,2},{4,5},{5,4},{6,7},{7,6},{8,9},{9,8},{10,11... | collective-permute-start | bytes 688136 | tf_op jit(solution)/shard_map/ppermute | solution.py:351
  16.7 5.9 %collective-permute-start.5 = (bf16[64,1024]{1,0:T(8,128)(2,1)S(1)}, bf16[64,1024]{1,0:T(8,128)(2,1)S(1)}, u32[]{:S(2)}, u32[]{:S(2)}) collective-permute-start(bf16[64,1024]{1,0:T(8,128)(2,1)S(1)} %get-tuple-element.34), channel_id=1, source_target_pairs={{0,4},{2,6},{4,0},{6,2},{8,12},{10,14},{12,8},{14,10},{1,5},{3,7},... | collective-permute-start | bytes 393224 | tf_op jit(solution)/shard_map/ppermute | solution.py:348
  17.7 7.4 %collective-permute-start.9 = (bf16[64,1536]{1,0:T(8,128)(2,1)S(1)}, bf16[64,1536]{1,0:T(8,128)(2,1)S(1)}, u32[]{:S(2)}, u32[]{:S(2)}) collective-permute-start(bf16[64,1536]{1,0:T(8,128)(2,1)S(1)} %pad_maximum_fusion), channel_id=1, source_target_pairs={{0,2},{2,0},{4,6},{6,4},{8,10},{10,8},{12,14},{14,12},{1,3},{3,1},... | collective-permute-start | bytes 589832 | tf_op jit(solution)/shard_map/ppermute | solution.py:348
  22.7 1.3 %collective-permute-start.6 = (bf16[64,1024]{1,0:T(8,128)(2,1)S(1)}, bf16[64,1024]{1,0:T(8,128)(2,1)S(1)}, u32[]{:S(2)}, u32[]{:S(2)}) collective-permute-start(bf16[64,1024]{1,0:T(8,128)(2,1)S(1)} %collective-permute-done.5.mine_ref), channel_id=1, source_target_pairs={{0,1},{1,0},{2,3},{3,2},{4,5},{5,4},{6,7},{7,6},{8,9},{9,8},{10,11... | collective-permute-start | bytes 393224 | tf_op jit(solution)/shard_map/ppermute | solution.py:351
  26.7 1.3 %collective-permute-start.10 = (f32[128,128]{1,0:T(8,128)S(1)}, f32[128,128]{1,0:T(8,128)S(1)}, u32[]{:S(2)}, u32[]{:S(2)}) collective-permute-start(f32[128,128]{1,0:T(8,128)S(1)} %get-tuple-element.44), channel_id=1, source_target_pairs={{0,1},{1,0},{2,3},{3,2},{4,5},{5,4},{6,7},{7,6},{8,9},{9,8},{10,11... | collective-permute-start | bytes 196616 | tf_op jit(solution)/shard_map/ppermute | solution.py:351

commit v18 on v17

--- a/solution.py
+++ b/solution.py
@@ -187,14 +187,11 @@
     out_ref[part:, 2 * half :] = r1_ref[part:, half:]
 
 
-def copy_kernel(d0_ref, d4_ref, after_any, pair_ref, far_ref):
-    variants = d0_ref.shape[1]
-    pair_ref[:, :variants] = d0_ref[...]
-    pair_ref[:, variants:] = d4_ref[...]
-    far_ref[...] = d4_ref[...]
-
-
-def third_kernel(ahead_ref, r1_ref, r4_ref, e2_ref, e0_ref, terms_ref, d2_ref, far_any, out_ref, kept_ref):
+def copy_kernel(dose_ref, after_any, out_ref):
+    out_ref[...] = dose_ref[...]
+
+
+def third_kernel(ahead_ref, r1_ref, r4_ref, e2_ref, e0_ref, terms_ref, d2_ref, far_any, d1_any, out_ref, kept_ref):
     half = terms_ref.shape[1]
     part = e0_ref.shape[0]
     kept_ref[:, :half] = ahead_ref[:, :half]
@@ -239,7 +236,7 @@
     return shares
 
 
-def half_kernel(place_ref, mine_ref, other_ref, d15_any, turned_ref, share_ref, data_scr):
+def half_kernel(place_ref, mine_ref, other_ref, d5_any, turned_ref, share_ref, data_scr):
     half = turned_ref.shape[0] // 2
     refs = (mine_ref, other_ref)
     panels = [[(ref, i * half) for i in range(4)] for ref in refs]
@@ -301,7 +298,7 @@
     *dose_refs, cross_ref, product_ref, pass_ref, dose_scr = refs
     samples, variants = dose_refs[0].shape
     chunks = [(ref, at) for ref in dose_refs for at in range(0, ref.shape[1] - variants + 1, variants)]
-    order = [0, 1, 3, 2, 4, 5, 7, 6]
+    order = [0, 1, 2, 3, 4, 5, 7, 6]
     for m, (ref, at) in enumerate(chunks[i] for i in order):
         dose_scr[m * samples : (m + 1) * samples, :] = ref[:, at : at + variants]
     line = turned_ref.shape[1]
@@ -387,20 +384,20 @@
     d2 = swap(jnp.concatenate([d0, ahead[:, :half]], axis=1), 2)
     to4 = call(second_kernel, [((panel, 2 * half + 2 * LANES), bf16)], 3, smem=0)(ahead, r1, e46)[0]
     r4 = swap(to4, 4)
-    pair, far = call(
-        copy_kernel, [((panel, 2 * variants), bf16), ((panel, variants), bf16)], 3, smem=0, anywhere=1
-    )(d0, d4, to4)
+    own = call(copy_kernel, [((panel, variants), bf16)], 2, smem=0, anywhere=1)(d0, to4)[0]
+    d1 = swap(own, 1)
+    far = call(copy_kernel, [((panel, variants), bf16)], 2, smem=0, anywhere=1)(d4, to4)[0]
     d6 = swap(far, 2)
-    d15 = swap(pair, 1)
+    d5 = swap(far, 1)
     d37 = swap(jnp.concatenate([d2[:, :variants], d6], axis=1), 1)
     width = 4 * half + 2 * LANES
     out, kept = call(
         third_kernel,
         [((panel, width - half), bf16), ((panel, width + 2 * half), bf16)],
-        8,
+        9,
         smem=0,
-        anywhere=1,
-    )(ahead, r1, r4, e2, e0, terms, d2, far)
+        anywhere=2,
+    )(ahead, r1, r4, e2, e0, terms, d2, far, d1)
     kept2 = other_core(kept)
     near = swap(out, 2)
     near2 = other_core(near)
@@ -411,7 +408,7 @@
         4,
         scratch=[pltpu.VMEM((samples // 2, LANES), bf16)],
         anywhere=1,
-    )(place, kept, kept2, d15)
+    )(place, kept, kept2, d5)
     turned2, weighted, low, power = call(
         weight_kernel,
         [shape, ((LANES, 2 * half), bf16), ((LANES, 2 * half), bf16), ((LANES, LANES), f32)],
@@ -421,9 +418,9 @@
     cross, product, passed = call(
         score_kernel,
         [((LANES, variants), f32)] * 2 + [((LANES, LANES), f32)],
-        13,
+        14,
         scratch=[pltpu.VMEM((samples, variants), bf16)],
-    )(place, gene, power, turned, turned2, weighted, low, d0, d15, d4, d2, d37, d6)
+    )(place, gene, power, turned, turned2, weighted, low, d0, d1, d4, d5, d2, d37, d6)
     keep = call(functools.partial(keep_kernel, samples=samples), [((LANES, LANES), f32)], 5)(
         place, gene, power, cross, product
     )[0]

time: 28.9 us -> 33.8 us (1.17)
  waiting for transfers between devices: 9.63 us -> 12.3 us
  starting transfers between devices: 11.8 us -> 14 us
    ppermute x8 -> x9, waiting for transfers between devices: 8.9 us -> 11.9 us  [swap(): return lax.ppermute(x, 'row', [(i, i ^ m) for i in range(rows)])]
    ppermute x8 -> x9, starting transfers between devices: 11.6 us -> 13.9 us  [swap(): return lax.ppermute(x, 'row', [(i, i ^ m) for i in range(rows)])]
  transfers between devices with their start and end apart: 11 -> 12, of which waited for: 7 -> 6; matrix products, arithmetic and copies ran while one was open for 0% -> 0% of each run, Pallas kernels for 10% -> 8%
where the time goes in v18:
time: 33.8 us; the launch traced here: 33.6 us
  starting transfers between devices  14 us (41%)
  waiting for transfers between devices  12.3 us (36%)
  Pallas kernels  6.41 us (19%)
  other arithmetic  0.74 us (2%)
    ppermute x9, starting transfers between devices, swap(): return lax.ppermute(x, 'row', [(i, i ^ m) for i in range(rows)])  13.9 us
    ppermute x9, waiting for transfers between devices, swap(): return lax.ppermute(x, 'row', [(i, i ^ m) for i in range(rows)])  11.9 us
    pallas_call x1, Pallas kernels, near_body(): call(route_kernel, [((panel, half + 2 * LANES), bf16), ((part, 2 * LANES)...  1.93 us
    pallas_call x1, Pallas kernels, near_body(): call(score_kernel, [((LANES, variants), f32)] * 2 + [((LANES, LANES), f32...  1.64 us
    pallas_call x1, Pallas kernels, near_body(): call(weight_kernel, [shape, ((LANES, 2 * half), bf16), ((LANES, 2 * half)...  1.08 us
    pallas_call x1, Pallas kernels, near_body(): call(half_kernel, [shape, ((LANES, 2 * half), f32)], 4, scratch=[pltpu.VM...  0.93 us
    pallas_call x1, Pallas kernels, near_body(): call(functools.partial(keep_kernel, samples=samples), [((LANES, LANES), f...  0.78 us
  transfers between devices with their start and end apart: 12, of which 6 were waited for; matrix products, arithmetic and copies ran while one was open for 0% of the time, Pallas kernels for 8%

profile of v18, /device:TPU:0, one launch (start us, length us, event | category | flops | bytes accessed | tf_op | source)
XLA Modules:
  0.0 33.6 jit_solution(8357614971540147798)
XLA Ops:
  0.0 0.1 pad_add_fusion.place_ref
  0.1 1.9 %shard_map.82 = (bf16[64,512]{1,0:T(8,128)(2,1)S(1)}, bf16[32,256]{1,0:T(8,128)(2,1)S(1)}, bf16[32,128]{1,0:T(8,128)(2,1)S(1)}, bf16[32,128]{1,0:T(8,128)(2,1)S(...) custom-call(s32[2]{0:T(128)S(1)} %pad_add_fusion.place_ref, ...), custom_call_target="tpu_custom_call" | custom-call | tf_op jit(solution)/shard_map/pallas_call | solution.py:350
  2.0 3.0 %collective-permute-start = (bf16[64,512]{1,0:T(8,128)(2,1)S(1)}, bf16[64,512]{1,0:T(8,128)(2,1)S(1)}, u32[]{:S(2)}, u32[]{:S(2)}) collective-permute-start(bf16[64,512]{1,0:T(8,128)(2,1)S(1)} %get-tuple-element.24.ahead_ref), channel_id=1, source_target_pairs={{0,2},{2,0},{4,6},{6,4},{8,10},{10,8},{12,14},{14,12},{1,3},{3,1},... | collective-permute-start | bytes 196616 | tf_op jit(solution)/shard_map/ppermute | solution.py:345
  5.0 2.6 %collective-permute-start.3 = (bf16[64,768]{1,0:T(8,128)(2,1)S(1)}, bf16[64,768]{1,0:T(8,128)(2,1)S(1)}, u32[]{:S(2)}, u32[]{:S(2)}) collective-permute-start(bf16[64,768]{1,0:T(8,128)(2,1)S(1)} %get-tuple-element.29.dose_ref.refs_0_), channel_id=1, source_target_pairs={{0,8},{2,10},{4,12},{6,14},{8,0},{10,2},{12,4},{14,6},{1,9},{3,11}... | collective-permute-start | bytes 294920 | tf_op jit(solution)/shard_map/ppermute | solution.py:345
  7.7 1.6 %collective-permute-start.2 = (bf16[64,1024]{1,0:T(8,128)(2,1)S(1)}, bf16[64,1024]{1,0:T(8,128)(2,1)S(1)}, u32[]{:S(2)}, u32[]{:S(2)}) collective-permute-start(bf16[64,1024]{1,0:T(8,128)(2,1)S(1)} %pad_maximum_fusion.1), channel_id=1, source_target_pairs={{0,4},{2,6},{4,0},{6,2},{8,12},{10,14},{12,8},{14,10},{1,5},{3,7},... | collective-permute-start | bytes 393224 | tf_op jit(solution)/shard_map/ppermute | solution.py:345
  9.3 0.6 %collective-permute-start.4 = (bf16[64,768]{1,0:T(8,128)(2,1)S(1)}, bf16[64,768]{1,0:T(8,128)(2,1)S(1)}, u32[]{:S(2)}, u32[]{:S(2)}) collective-permute-start(bf16[64,768]{1,0:T(8,128)(2,1)S(1)} %shard_map.85), channel_id=1, source_target_pairs={{0,2},{2,0},{4,6},{6,4},{8,10},{10,8},{12,14},{14,12},{1,3},{3,1},... | collective-permute-start | bytes 294920 | tf_op jit(solution)/shard_map/ppermute | solution.py:345
  9.9 2.1 %collective-permute-start.1 = (bf16[64,768]{1,0:T(8,128)(2,1)S(1)}, bf16[64,768]{1,0:T(8,128)(2,1)S(1)}, u32[]{:S(2)}, u32[]{:S(2)}) collective-permute-start(bf16[64,768]{1,0:T(8,128)(2,1)S(1)} %shard_map.83.after_any), channel_id=1, source_target_pairs={{0,8},{2,10},{4,12},{6,14},{8,0},{10,2},{12,4},{14,6},{1,9},{3,11}... | collective-permute-start | bytes 294920 | tf_op jit(solution)/shard_map/ppermute | solution.py:345
  12.0 1.6 %collective-permute-start.9 = (bf16[64,768]{1,0:T(8,128)(2,1)S(1)}, bf16[64,768]{1,0:T(8,128)(2,1)S(1)}, u32[]{:S(2)}, u32[]{:S(2)}) collective-permute-start(bf16[64,768]{1,0:T(8,128)(2,1)S(1)} %shard_map.84.far_any), channel_id=1, source_target_pairs={{0,4},{2,6},{4,0},{6,2},{8,12},{10,14},{12,8},{14,10},{1,5},{3,7},... | collective-permute-start | bytes 294920 | tf_op jit(solution)/shard_map/ppermute | solution.py:345
  13.6 2.1 %collective-permute-done.2.d2_ref.refs_4_ = bf16[64,1024]{1,0:T(8,128)(2,1)S(1)} collective-permute-done((bf16[64,1024]{1,0:T(8,128)(2,1)S(1)}, bf16[64,1024]{1,0:T(8,128)(2,1)S(1)}, u32[]{:S(2)}, u32[]{:S(2)}) %collective-permute-start.2) | collective-permute-done | bytes 131104 | tf_op jit(solution)/shard_map/ppermute | solution.py:345
  15.7 1.0 %collective-permute-done.1.r4_ref = bf16[64,768]{1,0:T(8,128)(2,1)S(1)} collective-permute-done((bf16[64,768]{1,0:T(8,128)(2,1)S(1)}, bf16[64,768]{1,0:T(8,128)(2,1)S(1)}, u32[]{:S(2)}, u32[]{:S(2)}) %collective-permute-start.1) | collective-permute-done | bytes 98336 | tf_op jit(solution)/shard_map/ppermute | solution.py:345
  16.8 0.1 collective-permute-start.5
  16.8 0.4 %collective-permute-start.6 = (bf16[64,1024]{1,0:T(8,128)(2,1)S(1)}, bf16[64,1024]{1,0:T(8,128)(2,1)S(1)}, u32[]{:S(2)}, u32[]{:S(2)}) collective-permute-start(bf16[64,1024]{1,0:T(8,128)(2,1)S(1)} %get-tuple-element.31), channel_id=1, source_target_pairs={{0,4},{2,6},{4,0},{6,2},{8,12},{10,14},{12,8},{14,10},{1,5},{3,7},... | collective-permute-start | bytes 393224 | tf_op jit(solution)/shard_map/ppermute | solution.py:345
  17.2 0.4 %collective-permute-done.9.refs_6_ = bf16[64,768]{1,0:T(8,128)(2,1)S(1)} collective-permute-done((bf16[64,768]{1,0:T(8,128)(2,1)S(1)}, bf16[64,768]{1,0:T(8,128)(2,1)S(1)}, u32[]{:S(2)}, u32[]{:S(2)}) %collective-permute-start.9) | collective-permute-done | bytes 98336 | tf_op jit(solution)/shard_map/ppermute | solution.py:345
  17.7 0.7 %collective-permute-start.10 = (bf16[64,1536]{1,0:T(8,128)(2,1)S(1)}, bf16[64,1536]{1,0:T(8,128)(2,1)S(1)}, u32[]{:S(2)}, u32[]{:S(2)}) collective-permute-start(bf16[64,1536]{1,0:T(8,128)(2,1)S(1)} %pad_maximum_fusion), channel_id=1, source_target_pairs={{0,2},{2,0},{4,6},{6,4},{8,10},{10,8},{12,14},{14,12},{1,3},{3,1},... | collective-permute-start | bytes 589832 | tf_op jit(solution)/shard_map/ppermute | solution.py:345
  18.3 4.4 %collective-permute-done.6.mine_ref = bf16[64,1024]{1,0:T(8,128)(2,1)S(1)} collective-permute-done((bf16[64,1024]{1,0:T(8,128)(2,1)S(1)}, bf16[64,1024]{1,0:T(8,128)(2,1)S(1)}, u32[]{:S(2)}, u32[]{:S(2)}) %collective-permute-start.6) | collective-permute-done | bytes 131104 | tf_op jit(solution)/shard_map/ppermute | solution.py:345
  22.7 1.3 %collective-permute-start.8 = (bf16[64,768]{1,0:T(8,128)(2,1)S(1)}, bf16[64,768]{1,0:T(8,128)(2,1)S(1)}, u32[]{:S(2)}, u32[]{:S(2)}) collective-permute-start(bf16[64,768]{1,0:T(8,128)(2,1)S(1)} %shard_map.84.far_any), channel_id=1, source_target_pairs={{0,2},{2,0},{4,6},{6,4},{8,10},{10,8},{12,14},{14,12},{1,3},{3,1},... | collective-permute-start | bytes 294920 | tf_op jit(solution)/shard_map/ppermute | solution.py:345
  24.0 3.9 %collective-permute-done.8.d5_any.refs_3_ = bf16[64,768]{1,0:T(8,128)(2,1)S(1)} collective-permute-done((bf16[64,768]{1,0:T(8,128)(2,1)S(1)}, bf16[64,768]{1,0:T(8,128)(2,1)S(1)}, u32[]{:S(2)}, u32[]{:S(2)}) %collective-permute-start.8) | collective-permute-done | bytes 98336 | tf_op jit(solution)/shard_map/ppermute | solution.py:345
  28.0 0.9 %shard_map.87 = (bf16[512,256]{1,0:T(8,128)(2,1)S(1)}, f32[128,512]{1,0:T(8,128)S(1)}) custom-call(s32[2]{0:T(128)S(1)} %pad_add_fusion.place_ref, bf16[64,1792]{1,0:T(8,128)(2,1)S(1)} %get-tuple-element.30.mine_ref.kept_ref, bf16[64,1792]{1,0:T(8,128)(2,1)S(1)} %collective-permute-done.5.other_ref.kept2_ref, ...), custom_call_target="tpu_custom_call" | custom-call | tf_op jit(solution)/shard_map/pallas_call | solution.py:405
  28.9 1.1 %shard_map.88 = (bf16[512,256]{1,0:T(8,128)(2,1)S(1)}, bf16[128,512]{1,0:T(8,128)(2,1)S(1)}, bf16[128,512]{1,0:T(8,128)(2,1)S(1)}, f32[128,128]{1,0:T(8,128)S(1)}) custom-call(s32[2]{0:T(128)S(1)} %pad_add_fusion.place_ref, bf16[64,1792]{1,0:T(8,128)(2,1)S(1)} %get-tuple-element.30.mine_ref.kept_ref, ...), custom_call_target="tpu_custom_call" | custom-call | tf_op jit(solution)/shard_map/pallas_call | solution.py:412
  30.0 1.6 %shard_map.89 = (f32[128,768]{1,0:T(8,128)S(1)}, f32[128,768]{1,0:T(8,128)S(1)}, f32[128,128]{1,0:T(8,128)S(1)}) custom-call(s32[2]{0:T(128)S(1)} %pad_add_fusion.place_ref, f32[128,128]{1,0:T(8,128)S(1)} %get-tuple-element.23.gene_ref, f32[128,128]{1,0:T(8,128)S(1)} %get-tuple-element.33.power_ref, bf16[512,256]{1,0:T(8,128)(2,1)S(1)} %get-tuple-element.34.turned_ref, ...), custom_call_target="tpu_custom_call" | custom-call | tf_op jit(solution)/shard_map/pallas_call | solution.py:418
  31.6 0.1 collective-permute-start.11
  31.7 0.8 %shard_map.90 = f32[128,128]{1,0:T(8,128)S(1)} custom-call(s32[2]{0:T(128)S(1)} %pad_add_fusion.place_ref, f32[128,128]{1,0:T(8,128)S(1)} %get-tuple-element.23.gene_ref, f32[128,128]{1,0:T(8,128)S(1)} %get-tuple-element.33.power_ref, f32[128,768]{1,0:T(8,128)S(1)} %get-tuple-element.38.cross_ref, f32[128,768]{1,0:T(8,128)S(1)} %get-tuple-element.39.product_ref), custom_call_target="tpu_custom_call" | custom-call | tf_op jit(solution)/shard_map/pallas_call | solution.py:424
  32.5 0.5 %collective-permute-done.11 = f32[128,128]{1,0:T(8,128)S(1)} collective-permute-done((f32[128,128]{1,0:T(8,128)S(1)}, f32[128,128]{1,0:T(8,128)S(1)}, u32[]{:S(2)}, u32[]{:S(2)}) %collective-permute-start.11) | collective-permute-done | bytes 65568 | tf_op jit(solution)/shard_map/ppermute | solution.py:348
  33.0 0.6 %add.3 = f32[128,128]{1,0:T(8,128)} add(f32[128,128]{1,0:T(8,128)S(1)} %shard_map.90, f32[128,128]{1,0:T(8,128)S(1)} %collective-permute-done.11) | non-fusion elementwise | flops 16384 | bytes 196608 | tf_op jit(solution)/shard_map/add | solution.py:427
  (15 shorter events, 0.1 us)
Async XLA Ops:
  2.0 7.3 %collective-permute-start = (bf16[64,512]{1,0:T(8,128)(2,1)S(1)}, bf16[64,512]{1,0:T(8,128)(2,1)S(1)}, u32[]{:S(2)}, u32[]{:S(2)}) collective-permute-start(bf16[64,512]{1,0:T(8,128)(2,1)S(1)} %get-tuple-element.24.ahead_ref), channel_id=1, source_target_pairs={{0,2},{2,0},{4,6},{6,4},{8,10},{10,8},{12,14},{14,12},{1,3},{3,1},... | collective-permute-start | bytes 196616 | tf_op jit(solution)/shard_map/ppermute | solution.py:345
  5.0 7.0 %collective-permute-start.3 = (bf16[64,768]{1,0:T(8,128)(2,1)S(1)}, bf16[64,768]{1,0:T(8,128)(2,1)S(1)}, u32[]{:S(2)}, u32[]{:S(2)}) collective-permute-start(bf16[64,768]{1,0:T(8,128)(2,1)S(1)} %get-tuple-element.29.dose_ref.refs_0_), channel_id=1, source_target_pairs={{0,8},{2,10},{4,12},{6,14},{8,0},{10,2},{12,4},{14,6},{1,9},{3,11}... | collective-permute-start | bytes 294920 | tf_op jit(solution)/shard_map/ppermute | solution.py:345
  7.7 8.1 %collective-permute-start.2 = (bf16[64,1024]{1,0:T(8,128)(2,1)S(1)}, bf16[64,1024]{1,0:T(8,128)(2,1)S(1)}, u32[]{:S(2)}, u32[]{:S(2)}) collective-permute-start(bf16[64,1024]{1,0:T(8,128)(2,1)S(1)} %pad_maximum_fusion.1), channel_id=1, source_target_pairs={{0,4},{2,6},{4,0},{6,2},{8,12},{10,14},{12,8},{14,10},{1,5},{3,7},... | collective-permute-start | bytes 393224 | tf_op jit(solution)/shard_map/ppermute | solution.py:345
  9.3 6.4 %collective-permute-start.4 = (bf16[64,768]{1,0:T(8,128)(2,1)S(1)}, bf16[64,768]{1,0:T(8,128)(2,1)S(1)}, u32[]{:S(2)}, u32[]{:S(2)}) collective-permute-start(bf16[64,768]{1,0:T(8,128)(2,1)S(1)} %shard_map.85), channel_id=1, source_target_pairs={{0,2},{2,0},{4,6},{6,4},{8,10},{10,8},{12,14},{14,12},{1,3},{3,1},... | collective-permute-start | bytes 294920 | tf_op jit(solution)/shard_map/ppermute | solution.py:345
  9.9 6.8 %collective-permute-start.1 = (bf16[64,768]{1,0:T(8,128)(2,1)S(1)}, bf16[64,768]{1,0:T(8,128)(2,1)S(1)}, u32[]{:S(2)}, u32[]{:S(2)}) collective-permute-start(bf16[64,768]{1,0:T(8,128)(2,1)S(1)} %shard_map.83.after_any), channel_id=1, source_target_pairs={{0,8},{2,10},{4,12},{6,14},{8,0},{10,2},{12,4},{14,6},{1,9},{3,11}... | collective-permute-start | bytes 294920 | tf_op jit(solution)/shard_map/ppermute | solution.py:345
  12.0 5.6 %collective-permute-start.9 = (bf16[64,768]{1,0:T(8,128)(2,1)S(1)}, bf16[64,768]{1,0:T(8,128)(2,1)S(1)}, u32[]{:S(2)}, u32[]{:S(2)}) collective-permute-start(bf16[64,768]{1,0:T(8,128)(2,1)S(1)} %shard_map.84.far_any), channel_id=1, source_target_pairs={{0,4},{2,6},{4,0},{6,2},{8,12},{10,14},{12,8},{14,10},{1,5},{3,7},... | collective-permute-start | bytes 294920 | tf_op jit(solution)/shard_map/ppermute | solution.py:345
  16.8 11.2 %collective-permute-start.5 = (bf16[64,1792]{1,0:T(8,128)(2,1)S(1)}, bf16[64,1792]{1,0:T(8,128)(2,1)S(1)}, u32[]{:S(2)}, u32[]{:S(2)}) collective-permute-start(bf16[64,1792]{1,0:T(8,128)(2,1)S(1)} %get-tuple-element.30.mine_ref.kept_ref), channel_id=1, source_target_pairs={{0,1},{1,0},{2,3},{3,2},{4,5},{5,4},{6,7},{7,6},{8,9},{9,8},{10,11... | collective-permute-start | bytes 688136 | tf_op jit(solution)/shard_map/ppermute | solution.py:348
  16.8 5.9 %collective-permute-start.6 = (bf16[64,1024]{1,0:T(8,128)(2,1)S(1)}, bf16[64,1024]{1,0:T(8,128)(2,1)S(1)}, u32[]{:S(2)}, u32[]{:S(2)}) collective-permute-start(bf16[64,1024]{1,0:T(8,128)(2,1)S(1)} %get-tuple-element.31), channel_id=1, source_target_pairs={{0,4},{2,6},{4,0},{6,2},{8,12},{10,14},{12,8},{14,10},{1,5},{3,7},... | collective-permute-start | bytes 393224 | tf_op jit(solution)/shard_map/ppermute | solution.py:345
  17.7 12.3 %collective-permute-start.10 = (bf16[64,1536]{1,0:T(8,128)(2,1)S(1)}, bf16[64,1536]{1,0:T(8,128)(2,1)S(1)}, u32[]{:S(2)}, u32[]{:S(2)}) collective-permute-start(bf16[64,1536]{1,0:T(8,128)(2,1)S(1)} %pad_maximum_fusion), channel_id=1, source_target_pairs={{0,2},{2,0},{4,6},{6,4},{8,10},{10,8},{12,14},{14,12},{1,3},{3,1},... | collective-permute-start | bytes 589832 | tf_op jit(solution)/shard_map/ppermute | solution.py:345
  22.7 6.2 %collective-permute-start.7 = (bf16[64,1024]{1,0:T(8,128)(2,1)S(1)}, bf16[64,1024]{1,0:T(8,128)(2,1)S(1)}, u32[]{:S(2)}, u32[]{:S(2)}) collective-permute-start(bf16[64,1024]{1,0:T(8,128)(2,1)S(1)} %collective-permute-done.6.mine_ref), channel_id=1, source_target_pairs={{0,1},{1,0},{2,3},{3,2},{4,5},{5,4},{6,7},{7,6},{8,9},{9,8},{10,11... | collective-permute-start | bytes 393224 | tf_op jit(solution)/shard_map/ppermute | solution.py:348
  22.7 5.2 %collective-permute-start.8 = (bf16[64,768]{1,0:T(8,128)(2,1)S(1)}, bf16[64,768]{1,0:T(8,128)(2,1)S(1)}, u32[]{:S(2)}, u32[]{:S(2)}) collective-permute-start(bf16[64,768]{1,0:T(8,128)(2,1)S(1)} %shard_map.84.far_any), channel_id=1, source_target_pairs={{0,2},{2,0},{4,6},{6,4},{8,10},{10,8},{12,14},{14,12},{1,3},{3,1},... | collective-permute-start | bytes 294920 | tf_op jit(solution)/shard_map/ppermute | solution.py:345
  31.6 1.3 %collective-permute-start.11 = (f32[128,128]{1,0:T(8,128)S(1)}, f32[128,128]{1,0:T(8,128)S(1)}, u32[]{:S(2)}, u32[]{:S(2)}) collective-permute-start(f32[128,128]{1,0:T(8,128)S(1)} %get-tuple-element.40), channel_id=1, source_target_pairs={{0,1},{1,0},{2,3},{3,2},{4,5},{5,4},{6,7},{7,6},{8,9},{9,8},{10,11... | collective-permute-start | bytes 196616 | tf_op jit(solution)/shard_map/ppermute | solution.py:348

commit v19 on v16

--- a/solution.py
+++ b/solution.py
@@ -243,12 +243,18 @@
     return shares
 
 
-def half_kernel(place_ref, mine_ref, other_ref, d15_any, turned_ref, share_ref, data_scr):
+def half_kernel(place_ref, mine_ref, other_ref, d0_ref, d15_ref, d4_ref, line_ref, share_ref, data_scr, turned_ref, dose_scr):
     half = turned_ref.shape[0] // 2
     refs = (mine_ref, other_ref)
     panels = [[(ref, i * half) for i in range(4)] for ref in refs]
     for c, share in enumerate(rotate(place_ref, refs, turned_ref, data_scr, panels, 4 * half)):
         share_ref[:, c * half : (c + 1) * half] = share
+    samples, variants = d0_ref.shape
+    dose_scr[:samples, :] = d0_ref[...]
+    dose_scr[samples : 2 * samples, :] = d15_ref[:, :variants]
+    dose_scr[2 * samples : 3 * samples, :] = d4_ref[...]
+    dose_scr[3 * samples :, :] = d15_ref[:, variants:]
+    line_ref[...] = jnp.dot(turned_ref[...], dose_scr[...], preferred_element_type=f32)
 
 
 def weight_kernel(
@@ -301,23 +307,21 @@
     return jnp.where(lane + half * LANES < valid, score, 0.0)
 
 
-def score_kernel(place_ref, gene_ref, power_ref, turned_ref, turned2_ref, weighted_ref, low_ref, *refs):
+def score_kernel(place_ref, gene_ref, power_ref, line_ref, turned_ref, weighted_ref, low_ref, *refs):
     *dose_refs, cross_ref, product_ref, pass_ref, dose_scr = refs
-    samples, variants = dose_refs[0].shape
+    samples, variants = dose_refs[2].shape
     chunks = [(ref, at) for ref in dose_refs for at in range(0, ref.shape[1] - variants + 1, variants)]
-    order = [0, 1, 3, 2, 4, 5, 7, 6]
+    order = [0, 1, 3, 2]
     for m, (ref, at) in enumerate(chunks[i] for i in order):
         dose_scr[m * samples : (m + 1) * samples, :] = ref[:, at : at + variants]
-    line = turned_ref.shape[1]
-    rotated = jnp.dot(turned_ref[...], dose_scr[:line], preferred_element_type=f32)
-    rotated += jnp.dot(turned2_ref[...], dose_scr[line:], preferred_element_type=f32)
+    rotated = line_ref[...] + jnp.dot(turned_ref[...], dose_scr[...], preferred_element_type=f32)
     rotated = rotated.astype(bf16)
     squared = jnp.square(rotated.astype(f32)).astype(bf16)
     cross = jnp.dot(weighted_ref[...], rotated, preferred_element_type=f32)
     power = jnp.dot(low_ref[...], squared, preferred_element_type=f32)
     cross_ref[...] = cross
     product_ref[...] = power
-    pass_ref[...] = window(place_ref, gene_ref, power_ref, cross, power, 1 - place_ref[1], dose_scr.shape[0])
+    pass_ref[...] = window(place_ref, gene_ref, power_ref, cross, power, 1 - place_ref[1], line_ref.shape[0])
 
 
 def keep_kernel(place_ref, gene_ref, power_ref, cross_ref, product_ref, keep_ref, *, samples):
@@ -408,13 +412,16 @@
     near = swap(out, 2)
     near2 = other_core(near)
     shape = ((2 * half, samples // 2), bf16)
-    turned, share = call(
+    line, share = call(
         half_kernel,
-        [shape, ((LANES, 2 * half), f32)],
-        4,
-        scratch=[pltpu.VMEM((samples // 2, LANES), bf16)],
-        anywhere=1,
-    )(place, kept, kept2, d15)
+        [((2 * half, variants), f32), ((LANES, 2 * half), f32)],
+        6,
+        scratch=[
+            pltpu.VMEM((samples // 2, LANES), bf16),
+            pltpu.VMEM((2 * half, samples // 2), bf16),
+            pltpu.VMEM((samples // 2, variants), bf16),
+        ],
+    )(place, kept, kept2, d0, d15, d4)
     turned2, weighted, low, power = call(
         weight_kernel,
         [shape, ((LANES, 2 * half), bf16), ((LANES, 2 * half), bf16), ((LANES, LANES), f32)],
@@ -424,9 +431,9 @@
     cross, product, passed = call(
         score_kernel,
         [((LANES, variants), f32)] * 2 + [((LANES, LANES), f32)],
-        13,
-        scratch=[pltpu.VMEM((samples, variants), bf16)],
-    )(place, gene, power, turned, turned2, weighted, low, d0, d15, d4, d2, d37, d6)
+        10,
+        scratch=[pltpu.VMEM((samples // 2, variants), bf16)],
+    )(place, gene, power, line, turned2, weighted, low, d2, d37, d6)
     keep = call(functools.partial(keep_kernel, samples=samples), [((LANES, LANES), f32)], 5)(
         place, gene, power, cross, product
     )[0]

time: 28.7 us -> 29.9 us (1.042)
  local copies, waits for them, and re-layouts: 0.72 us -> 2.75 us
  waiting for transfers between devices: 8.72 us -> 6.69 us
  starting transfers between devices: 11.9 us -> 12.8 us
    unnamed x8, local copies, waits for them, and re-layouts: 0.71 us -> 2.74 us
    ppermute x8, waiting for transfers between devices: 8 us -> 6.23 us  [swap(): return lax.ppermute(x, 'row', [(i, i ^ m) for i in range(rows)])]
    ppermute x8, starting transfers between devices: 11.6 us -> 12.7 us  [swap(): return lax.ppermute(x, 'row', [(i, i ^ m) for i in range(rows)])]
    pallas_call x1, Pallas kernels: 0.93 us -> 1.26 us  [near_body(): call(half_kernel, [((2 * half, variants), f32), ((LANES, 2 * half), f32)]...]
  transfers between devices with their start and end apart: 11 -> 11, of which waited for: 7 -> 4; matrix products, arithmetic and copies ran while one was open for 0% -> 0% of each run, Pallas kernels for 10% -> 11%
where the time goes in v19:
time: 29.9 us; the launch traced here: 29.5 us
  starting transfers between devices  12.8 us (43%)
  waiting for transfers between devices  6.69 us (22%)
  Pallas kernels  6.39 us (21%)
  local copies, waits for them, and re-layouts  2.75 us (9%)
  other arithmetic  0.74 us (2%)
    ppermute x8, starting transfers between devices, swap(): return lax.ppermute(x, 'row', [(i, i ^ m) for i in range(rows)])  12.7 us
    ppermute x8, waiting for transfers between devices, swap(): return lax.ppermute(x, 'row', [(i, i ^ m) for i in range(rows)])  6.23 us
    unnamed x8, local copies, waits for them, and re-layouts  2.74 us
    pallas_call x1, Pallas kernels, near_body(): call(route_kernel, [((panel, half + 2 * LANES), bf16), ((part, 2 * LANES)...  1.73 us
    pallas_call x1, Pallas kernels, near_body(): call(score_kernel, [((LANES, variants), f32)] * 2 + [((LANES, LANES), f32...  1.34 us
    pallas_call x1, Pallas kernels, near_body(): call(half_kernel, [((2 * half, variants), f32), ((LANES, 2 * half), f32)]...  1.26 us
    pallas_call x1, Pallas kernels, near_body(): call(weight_kernel, [shape, ((LANES, 2 * half), bf16), ((LANES, 2 * half)...  1.08 us
    pallas_call x1, Pallas kernels, near_body(): call(functools.partial(keep_kernel, samples=samples), [((LANES, LANES), f...  0.79 us
  transfers between devices with their start and end apart: 11, of which 4 were waited for; matrix products, arithmetic and copies ran while one was open for 0% of the time, Pallas kernels for 11%

profile of v19, /device:TPU:0, one launch (start us, length us, event | category | flops | bytes accessed | tf_op | source)
XLA Modules:
  0.0 29.5 jit_solution(3081915788131093794)
XLA Ops:
  0.0 0.1 pad_add_fusion.place_ref
  0.1 1.7 %shard_map.82 = (bf16[64,512]{1,0:T(8,128)(2,1)S(1)}, bf16[32,256]{1,0:T(8,128)(2,1)S(1)}, bf16[32,128]{1,0:T(8,128)(2,1)S(1)}, bf16[32,128]{1,0:T(8,128)(2,1)S(...) custom-call(s32[2]{0:T(128)S(1)} %pad_add_fusion.place_ref, s32[8,128]{1,0:T(8,128)} %bitcast.11, ...), custom_call_target="tpu_custom_call" | custom-call | tf_op jit(solution)/shard_map/pallas_call | solution.py:361
  1.8 3.0 %collective-permute-start = (bf16[64,512]{1,0:T(8,128)(2,1)S(1)}, bf16[64,512]{1,0:T(8,128)(2,1)S(1)}, u32[]{:S(2)}, u32[]{:S(2)}) collective-permute-start(bf16[64,512]{1,0:T(8,128)(2,1)S(1)} %get-tuple-element.28.ahead_ref), channel_id=1, source_target_pairs={{0,2},{2,0},{4,6},{6,4},{8,10},{10,8},{12,14},{14,12},{1,3},{3,1},... | collective-permute-start | bytes 196616 | tf_op jit(solution)/shard_map/ppermute | solution.py:356
  4.8 2.6 %collective-permute-start.3 = (bf16[64,768]{1,0:T(8,128)(2,1)S(1)}, bf16[64,768]{1,0:T(8,128)(2,1)S(1)}, u32[]{:S(2)}, u32[]{:S(2)}) collective-permute-start(bf16[64,768]{1,0:T(8,128)(2,1)S(1)} %get-tuple-element.33.d0_ref), channel_id=1, source_target_pairs={{0,8},{2,10},{4,12},{6,14},{8,0},{10,2},{12,4},{14,6},{1,9},{3,11}... | collective-permute-start | bytes 294920 | tf_op jit(solution)/shard_map/ppermute | solution.py:356
  7.5 1.6 %collective-permute-start.2 = (bf16[64,1024]{1,0:T(8,128)(2,1)S(1)}, bf16[64,1024]{1,0:T(8,128)(2,1)S(1)}, u32[]{:S(2)}, u32[]{:S(2)}) collective-permute-start(bf16[64,1024]{1,0:T(8,128)(2,1)S(1)} %pad_maximum_fusion.1), channel_id=1, source_target_pairs={{0,4},{2,6},{4,0},{6,2},{8,12},{10,14},{12,8},{14,10},{1,5},{3,7},... | collective-permute-start | bytes 393224 | tf_op jit(solution)/shard_map/ppermute | solution.py:356
  9.1 1.1 %collective-permute-start.1 = (bf16[64,768]{1,0:T(8,128)(2,1)S(1)}, bf16[64,768]{1,0:T(8,128)(2,1)S(1)}, u32[]{:S(2)}, u32[]{:S(2)}) collective-permute-start(bf16[64,768]{1,0:T(8,128)(2,1)S(1)} %shard_map.84.after_any), channel_id=1, source_target_pairs={{0,8},{2,10},{4,12},{6,14},{8,0},{10,2},{12,4},{14,6},{1,9},{3,11}... | collective-permute-start | bytes 294920 | tf_op jit(solution)/shard_map/ppermute | solution.py:356
  10.3 1.5 %collective-permute-done.3.d4_ref = bf16[64,768]{1,0:T(8,128)(2,1)S(1)} collective-permute-done((bf16[64,768]{1,0:T(8,128)(2,1)S(1)}, bf16[64,768]{1,0:T(8,128)(2,1)S(1)}, u32[]{:S(2)}, u32[]{:S(2)}) %collective-permute-start.3) | collective-permute-done | bytes 98336 | tf_op jit(solution)/shard_map/ppermute | solution.py:356
  11.8 1.6 %collective-permute-start.8 = (bf16[64,768]{1,0:T(8,128)(2,1)S(1)}, bf16[64,768]{1,0:T(8,128)(2,1)S(1)}, u32[]{:S(2)}, u32[]{:S(2)}) collective-permute-start(bf16[64,768]{1,0:T(8,128)(2,1)S(1)} %get-tuple-element.34.far_any), channel_id=1, source_target_pairs={{0,4},{2,6},{4,0},{6,2},{8,12},{10,14},{12,8},{14,10},{1,5},{3,7},... | collective-permute-start | bytes 294920 | tf_op jit(solution)/shard_map/ppermute | solution.py:356
  13.4 0.7 %copy-done = f32[1024]{0:T(1024)S(1)} copy-done((f32[1024]{0:T(1024)S(1)}, f32[1024]{0:T(1024)}, u32[]{:S(2)}) %copy-start) | copy-done | bytes 4120
  14.1 0.7 %copy-done.1 = s32[1024]{0:T(1024)S(1)} copy-done((s32[1024]{0:T(1024)S(1)}, s32[1024]{0:T(1024)}, u32[]{:S(2)}) %copy-start.1) | copy-done | bytes 4120
  14.8 0.7 %copy-done.2 = s32[1024]{0:T(1024)S(1)} copy-done((s32[1024]{0:T(1024)S(1)}, s32[1024]{0:T(1024)}, u32[]{:S(2)}) %copy-start.2) | copy-done | bytes 4120
  15.4 0.7 %copy-done.3 = f32[256]{0:T(256)S(1)} copy-done((f32[256]{0:T(256)S(1)}, f32[256]{0:T(256)}, u32[]{:S(2)}) %copy-start.3) | copy-done | bytes 1048
  16.1 0.1 shard_map.83
  16.2 0.6 %collective-permute-start.7 = (bf16[64,1536]{1,0:T(8,128)(2,1)S(1)}, bf16[64,1536]{1,0:T(8,128)(2,1)S(1)}, u32[]{:S(2)}, u32[]{:S(2)}) collective-permute-start(bf16[64,1536]{1,0:T(8,128)(2,1)S(1)} %get-tuple-element.37), channel_id=1, source_target_pairs={{0,2},{2,0},{4,6},{6,4},{8,10},{10,8},{12,14},{14,12},{1,3},{3,1},... | collective-permute-start | bytes 589832 | tf_op jit(solution)/shard_map/ppermute | solution.py:356
  17.0 0.5 %collective-permute-start.5 = (bf16[64,1024]{1,0:T(8,128)(2,1)S(1)}, bf16[64,1024]{1,0:T(8,128)(2,1)S(1)}, u32[]{:S(2)}, u32[]{:S(2)}) collective-permute-start(bf16[64,1024]{1,0:T(8,128)(2,1)S(1)} %get-tuple-element.36), channel_id=1, source_target_pairs={{0,4},{2,6},{4,0},{6,2},{8,12},{10,14},{12,8},{14,10},{1,5},{3,7},... | collective-permute-start | bytes 393224 | tf_op jit(solution)/shard_map/ppermute | solution.py:356
  17.5 1.6 %collective-permute-start.9 = (bf16[64,1536]{1,0:T(8,128)(2,1)S(1)}, bf16[64,1536]{1,0:T(8,128)(2,1)S(1)}, u32[]{:S(2)}, u32[]{:S(2)}) collective-permute-start(bf16[64,1536]{1,0:T(8,128)(2,1)S(1)} %pad_maximum_fusion), channel_id=1, source_target_pairs={{0,2},{2,0},{4,6},{6,4},{8,10},{10,8},{12,14},{14,12},{1,3},{3,1},... | collective-permute-start | bytes 589832 | tf_op jit(solution)/shard_map/ppermute | solution.py:356
  19.1 3.8 %collective-permute-done.5.mine_ref = bf16[64,1024]{1,0:T(8,128)(2,1)S(1)} collective-permute-done((bf16[64,1024]{1,0:T(8,128)(2,1)S(1)}, bf16[64,1024]{1,0:T(8,128)(2,1)S(1)}, u32[]{:S(2)}, u32[]{:S(2)}) %collective-permute-start.5) | collective-permute-done | bytes 131104 | tf_op jit(solution)/shard_map/ppermute | solution.py:356
  22.9 0.9 %collective-permute-done.7.d15_ref = bf16[64,1536]{1,0:T(8,128)(2,1)S(1)} collective-permute-done((bf16[64,1536]{1,0:T(8,128)(2,1)S(1)}, bf16[64,1536]{1,0:T(8,128)(2,1)S(1)}, u32[]{:S(2)}, u32[]{:S(2)}) %collective-permute-start.7) | collective-permute-done | bytes 196640 | tf_op jit(solution)/shard_map/ppermute | solution.py:356
  23.8 1.3 %shard_map.87 = (f32[512,768]{1,0:T(8,128)S(1)}, f32[128,512]{1,0:T(8,128)S(1)}) custom-call(s32[2]{0:T(128)S(1)} %pad_add_fusion.place_ref, bf16[64,1792]{1,0:T(8,128)(2,1)S(1)} %get-tuple-element.35.mine_ref.kept_ref, bf16[64,1792]{1,0:T(8,128)(2,1)S(1)} %collective-permute-done.4.other_ref.kept2_ref, bf16[64,768]{1,0:T(8,128)(2,1)S(1)} %get-tuple-element.33.d0_ref, ...), custom_call_target="tpu_custom_call" | custom-call | tf_op jit(solution)/shard_map/pallas_call | solution.py:415
  25.1 1.1 %shard_map.88 = (bf16[512,256]{1,0:T(8,128)(2,1)S(1)}, bf16[128,512]{1,0:T(8,128)(2,1)S(1)}, bf16[128,512]{1,0:T(8,128)(2,1)S(1)}, f32[128,128]{1,0:T(8,128)S(1)}) custom-call(s32[2]{0:T(128)S(1)} %pad_add_fusion.place_ref, bf16[64,1792]{1,0:T(8,128)(2,1)S(1)} %get-tuple-element.35.mine_ref.kept_ref, ...), custom_call_target="tpu_custom_call" | custom-call | tf_op jit(solution)/shard_map/pallas_call | solution.py:425
  26.2 1.3 %shard_map.89 = (f32[128,768]{1,0:T(8,128)S(1)}, f32[128,768]{1,0:T(8,128)S(1)}, f32[128,128]{1,0:T(8,128)S(1)}) custom-call(s32[2]{0:T(128)S(1)} %pad_add_fusion.place_ref, f32[128,128]{1,0:T(8,128)S(1)} %get-tuple-element.27.gene_ref, f32[128,128]{1,0:T(8,128)S(1)} %get-tuple-element.39.power_ref, f32[512,768]{1,0:T(8,128)S(1)} %get-tuple-element.40.line_ref, ...), custom_call_target="tpu_custom_call" | custom-call | tf_op jit(solution)/shard_map/pallas_call | solution.py:431
  27.6 0.8 %shard_map.90 = f32[128,128]{1,0:T(8,128)S(1)} custom-call(s32[2]{0:T(128)S(1)} %pad_add_fusion.place_ref, f32[128,128]{1,0:T(8,128)S(1)} %get-tuple-element.27.gene_ref, f32[128,128]{1,0:T(8,128)S(1)} %get-tuple-element.39.power_ref, f32[128,768]{1,0:T(8,128)S(1)} %get-tuple-element.44.cross_ref, f32[128,768]{1,0:T(8,128)S(1)} %get-tuple-element.45.product_ref), custom_call_target="tpu_custom_call" | custom-call | tf_op jit(solution)/shard_map/pallas_call | solution.py:437
  28.4 0.4 %collective-permute-done.10 = f32[128,128]{1,0:T(8,128)S(1)} collective-permute-done((f32[128,128]{1,0:T(8,128)S(1)}, f32[128,128]{1,0:T(8,128)S(1)}, u32[]{:S(2)}, u32[]{:S(2)}) %collective-permute-start.10) | collective-permute-done | bytes 65568 | tf_op jit(solution)/shard_map/ppermute | solution.py:359
  28.9 0.6 %add.3 = f32[128,128]{1,0:T(8,128)} add(f32[128,128]{1,0:T(8,128)S(1)} %shard_map.90, f32[128,128]{1,0:T(8,128)S(1)} %collective-permute-done.10) | non-fusion elementwise | flops 16384 | bytes 196608 | tf_op jit(solution)/shard_map/add | solution.py:440
  (21 shorter events, 0.3 us)
Async XLA Ops:
  1.8 7.3 %collective-permute-start = (bf16[64,512]{1,0:T(8,128)(2,1)S(1)}, bf16[64,512]{1,0:T(8,128)(2,1)S(1)}, u32[]{:S(2)}, u32[]{:S(2)}) collective-permute-start(bf16[64,512]{1,0:T(8,128)(2,1)S(1)} %get-tuple-element.28.ahead_ref), channel_id=1, source_target_pairs={{0,2},{2,0},{4,6},{6,4},{8,10},{10,8},{12,14},{14,12},{1,3},{3,1},... | collective-permute-start | bytes 196616 | tf_op jit(solution)/shard_map/ppermute | solution.py:356
  4.8 6.9 %collective-permute-start.3 = (bf16[64,768]{1,0:T(8,128)(2,1)S(1)}, bf16[64,768]{1,0:T(8,128)(2,1)S(1)}, u32[]{:S(2)}, u32[]{:S(2)}) collective-permute-start(bf16[64,768]{1,0:T(8,128)(2,1)S(1)} %get-tuple-element.33.d0_ref), channel_id=1, source_target_pairs={{0,8},{2,10},{4,12},{6,14},{8,0},{10,2},{12,4},{14,6},{1,9},{3,11}... | collective-permute-start | bytes 294920 | tf_op jit(solution)/shard_map/ppermute | solution.py:356
  7.5 9.4 %collective-permute-start.2 = (bf16[64,1024]{1,0:T(8,128)(2,1)S(1)}, bf16[64,1024]{1,0:T(8,128)(2,1)S(1)}, u32[]{:S(2)}, u32[]{:S(2)}) collective-permute-start(bf16[64,1024]{1,0:T(8,128)(2,1)S(1)} %pad_maximum_fusion.1), channel_id=1, source_target_pairs={{0,4},{2,6},{4,0},{6,2},{8,12},{10,14},{12,8},{14,10},{1,5},{3,7},... | collective-permute-start | bytes 393224 | tf_op jit(solution)/shard_map/ppermute | solution.py:356
  9.1 7.7 %collective-permute-start.1 = (bf16[64,768]{1,0:T(8,128)(2,1)S(1)}, bf16[64,768]{1,0:T(8,128)(2,1)S(1)}, u32[]{:S(2)}, u32[]{:S(2)}) collective-permute-start(bf16[64,768]{1,0:T(8,128)(2,1)S(1)} %shard_map.84.after_any), channel_id=1, source_target_pairs={{0,8},{2,10},{4,12},{6,14},{8,0},{10,2},{12,4},{14,6},{1,9},{3,11}... | collective-permute-start | bytes 294920 | tf_op jit(solution)/shard_map/ppermute | solution.py:356
  11.8 5.7 %collective-permute-start.8 = (bf16[64,768]{1,0:T(8,128)(2,1)S(1)}, bf16[64,768]{1,0:T(8,128)(2,1)S(1)}, u32[]{:S(2)}, u32[]{:S(2)}) collective-permute-start(bf16[64,768]{1,0:T(8,128)(2,1)S(1)} %get-tuple-element.34.far_any), channel_id=1, source_target_pairs={{0,4},{2,6},{4,0},{6,2},{8,12},{10,14},{12,8},{14,10},{1,5},{3,7},... | collective-permute-start | bytes 294920 | tf_op jit(solution)/shard_map/ppermute | solution.py:356
  13.4 0.7 %copy-start = (f32[1024]{0:T(1024)S(1)}, f32[1024]{0:T(1024)}, u32[]{:S(2)}) copy-start(f32[1024]{0:T(1024)} %param.12) | copy-start | bytes 12292
  14.1 0.7 %copy-start.1 = (s32[1024]{0:T(1024)S(1)}, s32[1024]{0:T(1024)}, u32[]{:S(2)}) copy-start(s32[1024]{0:T(1024)} %param.13) | copy-start | bytes 12292
  14.7 0.7 %copy-start.2 = (s32[1024]{0:T(1024)S(1)}, s32[1024]{0:T(1024)}, u32[]{:S(2)}) copy-start(s32[1024]{0:T(1024)} %param.14) | copy-start | bytes 12292
  15.4 0.7 %copy-start.3 = (f32[256]{0:T(256)S(1)}, f32[256]{0:T(256)}, u32[]{:S(2)}) copy-start(f32[256]{0:T(256)} %param.9) | copy-start | bytes 3076
  16.2 7.5 %collective-permute-start.7 = (bf16[64,1536]{1,0:T(8,128)(2,1)S(1)}, bf16[64,1536]{1,0:T(8,128)(2,1)S(1)}, u32[]{:S(2)}, u32[]{:S(2)}) collective-permute-start(bf16[64,1536]{1,0:T(8,128)(2,1)S(1)} %get-tuple-element.37), channel_id=1, source_target_pairs={{0,2},{2,0},{4,6},{6,4},{8,10},{10,8},{12,14},{14,12},{1,3},{3,1},... | collective-permute-start | bytes 589832 | tf_op jit(solution)/shard_map/ppermute | solution.py:356
  16.9 6.9 %collective-permute-start.4 = (bf16[64,1792]{1,0:T(8,128)(2,1)S(1)}, bf16[64,1792]{1,0:T(8,128)(2,1)S(1)}, u32[]{:S(2)}, u32[]{:S(2)}) collective-permute-start(bf16[64,1792]{1,0:T(8,128)(2,1)S(1)} %get-tuple-element.35.mine_ref.kept_ref), channel_id=1, source_target_pairs={{0,1},{1,0},{2,3},{3,2},{4,5},{5,4},{6,7},{7,6},{8,9},{9,8},{10,11... | collective-permute-start | bytes 688136 | tf_op jit(solution)/shard_map/ppermute | solution.py:359
  17.0 5.9 %collective-permute-start.5 = (bf16[64,1024]{1,0:T(8,128)(2,1)S(1)}, bf16[64,1024]{1,0:T(8,128)(2,1)S(1)}, u32[]{:S(2)}, u32[]{:S(2)}) collective-permute-start(bf16[64,1024]{1,0:T(8,128)(2,1)S(1)} %get-tuple-element.36), channel_id=1, source_target_pairs={{0,4},{2,6},{4,0},{6,2},{8,12},{10,14},{12,8},{14,10},{1,5},{3,7},... | collective-permute-start | bytes 393224 | tf_op jit(solution)/shard_map/ppermute | solution.py:356
  17.5 8.7 %collective-permute-start.9 = (bf16[64,1536]{1,0:T(8,128)(2,1)S(1)}, bf16[64,1536]{1,0:T(8,128)(2,1)S(1)}, u32[]{:S(2)}, u32[]{:S(2)}) collective-permute-start(bf16[64,1536]{1,0:T(8,128)(2,1)S(1)} %pad_maximum_fusion), channel_id=1, source_target_pairs={{0,2},{2,0},{4,6},{6,4},{8,10},{10,8},{12,14},{14,12},{1,3},{3,1},... | collective-permute-start | bytes 589832 | tf_op jit(solution)/shard_map/ppermute | solution.py:356
  22.9 2.2 %collective-permute-start.6 = (bf16[64,1024]{1,0:T(8,128)(2,1)S(1)}, bf16[64,1024]{1,0:T(8,128)(2,1)S(1)}, u32[]{:S(2)}, u32[]{:S(2)}) collective-permute-start(bf16[64,1024]{1,0:T(8,128)(2,1)S(1)} %collective-permute-done.5.mine_ref), channel_id=1, source_target_pairs={{0,1},{1,0},{2,3},{3,2},{4,5},{5,4},{6,7},{7,6},{8,9},{9,8},{10,11... | collective-permute-start | bytes 393224 | tf_op jit(solution)/shard_map/ppermute | solution.py:359
  27.5 1.3 %collective-permute-start.10 = (f32[128,128]{1,0:T(8,128)S(1)}, f32[128,128]{1,0:T(8,128)S(1)}, u32[]{:S(2)}, u32[]{:S(2)}) collective-permute-start(f32[128,128]{1,0:T(8,128)S(1)} %get-tuple-element.46), channel_id=1, source_target_pairs={{0,1},{1,0},{2,3},{3,2},{4,5},{5,4},{6,7},{7,6},{8,9},{9,8},{10,11... | collective-permute-start | bytes 196616 | tf_op jit(solution)/shard_map/ppermute | solution.py:359
